TPU v7x, 32 devices: a whole 2x2x4 slice. The times are simulated.
32 devices in a mesh: species: 4 (over y, core), tile: 8 (over z, x).
Axes of the slice: x: 2, y: 2, z: 4, core: 2. Of those that a mesh axis runs over, the one named last changes fastest.
Arguments:
- tracers: float32 [64, 16, 64, 128], P('species', None, 'tile'), may hold values from 0.1 to 4
- fluxes: float32 [4, 3, 16, 64, 128], P(None, None, 'species', 'tile'), may hold values from -0.15 to 0.15
- weight_in: bfloat16 [512, 64], replicated, may hold values from -0.75 to 0.75
- weight_out: bfloat16 [64, 512], replicated, may hold values from -0.25 to 0.25
Outputs:
- tracers_out: float32 [64, 16, 64, 128], P('species', None, 'tile')
All inputs are finite; a program needn't handle non-finite values.
Results may differ from a plain program's by a relative error of at most 0.0035.
Values may be sent and summed in bfloat16 or wider, within the bound.
No kernel may reach another device: no remote copies, remote signals or barrier semaphores. Data moves between devices by JAX's collectives and lax.ppermute only.
A program may use at most 64 MiB of HBM per device.

v0:
```python
import jax
import jax.numpy as jnp
from jax import lax
from jax.sharding import PartitionSpec as P

STEPS = 4


def extended(cells, sides, width):
    for axis, dim in sides:
        count = lax.axis_size(axis)
        ends = count - 1
        head = lax.slice_in_dim(cells, 0, width, axis=dim)
        tail = lax.slice_in_dim(cells, cells.shape[dim] - width, cells.shape[dim], axis=dim)
        cells = jnp.concatenate(
            [
                lax.ppermute(tail, axis, [(i, (i + 1) % count) for i in range(ends)]),
                cells,
                lax.ppermute(head, axis, [((i + 1) % count, i) for i in range(ends)]),
            ],
            axis=dim,
        )
    return cells


def positive(value):
    return jnp.maximum(value, 0.0)


def negative(value):
    return jnp.minimum(value, 0.0)


def advance(padded_state, padded_x, flux_y, padded_z):
    inner = padded_state[:, 1:-1, 1:-1]
    along_x = padded_state[:, 1:-1]
    face_x = padded_x[:, 1:]
    faces_x = positive(face_x) * along_x[:, :, :-1] + negative(face_x) * along_x[:, :, 1:]
    along_z = padded_state[:, :, 1:-1]
    face_z = padded_z[1:]
    faces_z = positive(face_z) * along_z[:, :-1] + negative(face_z) * along_z[:, 1:]
    faces_y = positive(flux_y) * jnp.roll(inner, 1, 3) + negative(flux_y) * inner
    return (
        inner
        + faces_x[:, :, :-1]
        - faces_x[:, :, 1:]
        + faces_y
        - jnp.roll(faces_y, -1, 3)
        + faces_z[:, :-1]
        - faces_z[:, 1:]
    )


def per_device(tracers, fluxes, weight_in, weight_out):
    spec_loc, depth_all, width_x, width_y = tracers.shape
    tile_at = lax.axis_index("tile")
    state = lax.all_to_all(tracers, "species", split_axis=1, concat_axis=0, tiled=True)
    spec_all, lev_loc = (state.shape[0], state.shape[1])
    grid_shape = (lev_loc, width_x, width_y)
    column = tile_at * width_x + lax.broadcasted_iota(jnp.int32, grid_shape, 1)
    level_at = lax.axis_index("species") * lev_loc + lax.broadcasted_iota(jnp.int32, grid_shape, 0)
    for interval in range(STEPS):
        own_flux = fluxes[interval]
        flux_x = jnp.where(column == 0, 0.0, own_flux[0])
        flux_y = own_flux[1]
        flux_z = jnp.where(level_at == 0, 0.0, own_flux[2])
        stacked = jnp.concatenate([state, flux_x[None], flux_z[None]], 0)
        padded = extended(stacked, (("species", 1), ("tile", 2)), 1)
        padded_state = padded[:spec_all]
        padded_x = padded[spec_all, 1:-1]
        padded_z = padded[spec_all + 1, :, 1:-1]
        state = advance(padded_state, padded_x, flux_y, padded_z)
        flattened = state.astype(jnp.bfloat16).reshape(spec_all, lev_loc, width_x * width_y)
        hidden = jax.nn.silu(
            jnp.einsum("hs,szc->hzc", weight_in, flattened, preferred_element_type=jnp.float32)
        ).astype(jnp.bfloat16)
        tendency = (
            0.5 * jnp.einsum("sh,hzc->szc", weight_out, hidden, preferred_element_type=jnp.float32)
        ).astype(jnp.bfloat16)
        state = state + tendency.reshape(state.shape).astype(jnp.float32)
    return lax.all_to_all(state, "species", split_axis=0, concat_axis=1, tiled=True)


def solution(mesh):
    placed = (P("species", None, "tile", None), P(None, None, "species", "tile", None), P(), P())
    return jax.shard_map(
        per_device,
        mesh=mesh,
        in_specs=placed,
        out_specs=P("species", None, "tile", None),
        check_vma=False,
    )
```

profile of v0, /device:TPU:0, one launch (start us, length us, event | category | flops | bytes accessed | tf_op | source)
XLA Modules:
  0.0 153.6 jit_solution(681662531189179415)
XLA Ops:
  0.0 2.3 %copy.32 = f32[16,16,8,128]{3,2,0,1:T(8,128)} copy(f32[16,16,8,128]{3,2,1,0:T(8,128)} %param.4) | data formatting | bytes 2097152 | tf_op args[0]
  2.3 4.2 %all-to-all-start = ((f32[16,16,8,128]{3,2,0,1:T(8,128)}), f32[16,16,8,128]{3,2,0,1:T(8,128)S(1)}, u32[]{:S(2)}, u32[]{:S(2)}) async-start(f32[16,16,8,128]{3,2,0,1:T(8,128)} %copy.32), calls=%async_computation | async-start | bytes 2097152 | tf_op jit(solution)/shard_map/all_to_all | solution.py:57
  6.7 14.3 %all-to-all-done = f32[16,16,8,128]{3,2,0,1:T(8,128)S(1)} async-done(((f32[16,16,8,128]{3,2,0,1:T(8,128)}), f32[16,16,8,128]{3,2,0,1:T(8,128)S(1)}, u32[]{:S(2)}, u32[]{:S(2)}) %all-to-all-start) | async-done | bytes 1048608 | tf_op jit(solution)/shard_map/all_to_all | solution.py:57
  22.9 3.0 %collective-permute-start = (f32[66,1,8,128]{3,2,1,0:T(8,128)S(1)}, f32[66,1,8,128]{3,2,1,0:T(8,128)S(1)}, u32[]{:S(2)}, u32[]{:S(2)}) collective-permute-start(f32[66,1,8,128]{3,2,1,0:T(8,128)S(1)} %get-tuple-element.35), channel_id=1, source_target_pairs={{0,8},{8,16},{16,24},{1,9},{9,17},{17,25},{2,10},{10,18},{18,26},{... | collective-permute-start | bytes 811016 | tf_op jit(solution)/shard_map/ppermute | solution.py:17
  27.3 4.1 %collective-permute-start.2 = (f32[66,6,1,128]{3,2,1,0:T(1,128)S(1)}, f32[66,6,1,128]{3,2,1,0:T(1,128)S(1)}, u32[]{:S(2)}, u32[]{:S(2)}) collective-permute-start(f32[66,6,1,128]{3,2,1,0:T(1,128)S(1)} %get-tuple-element.27), channel_id=1, source_target_pairs={{0,1},{1,2},{2,3},{3,4},{4,5},{5,6},{6,7},{8,9},{9,10},{10,11},{11... | collective-permute-start | bytes 608264 | tf_op jit(solution)/shard_map/ppermute | solution.py:17
  34.7 4.7 %collective-permute-done.3 = f32[66,6,1,128]{3,2,1,0:T(1,128)S(1)} collective-permute-done((f32[66,6,1,128]{3,2,1,0:T(1,128)S(1)}, f32[66,6,1,128]{3,2,1,0:T(1,128)S(1)}, u32[]{:S(2)}, u32[]{:S(2)}) %collective-permute-start.3) | collective-permute-done | bytes 202784 | tf_op jit(solution)/shard_map/ppermute | solution.py:19
  42.2 3.6 %fusion.89 = f32[4,1024,64]{1,2,0:T(8,128)S(1)} fusion(bf16[64,4,1024]{2,1,0:T(4,128)(2,1)S(1)} %reshape.196, bf16[64,512]{1,0:T(8,128)(2,1)S(1)} %copy-done, bf16[512,64]{0,1:T(8,128)(2,1)S(1)} %copy-done.2), kind=kOutput, calls=%fused_computation.131 | convolution fusion | flops 548143104 | bytes 1703936 | tf_op jit(solution)/shard_map/sh,hzc->szc/dot_general | solution.py:78
  46.5 3.7 %collective-permute-start.4 = (f32[66,1,8,128]{3,2,1,0:T(8,128)S(1)}, f32[66,1,8,128]{3,2,1,0:T(8,128)S(1)}, u32[]{:S(2)}, u32[]{:S(2)}) collective-permute-start(f32[66,1,8,128]{3,2,1,0:T(8,128)S(1)} %get-tuple-element.33), channel_id=1, source_target_pairs={{0,8},{8,16},{16,24},{1,9},{9,17},{17,25},{2,10},{10,18},{18,26},{... | collective-permute-start | bytes 811016 | tf_op jit(solution)/shard_map/ppermute | solution.py:17
  52.2 4.5 %collective-permute-done.5 = f32[66,1,8,128]{3,2,1,0:T(8,128)S(1)} collective-permute-done((f32[66,1,8,128]{3,2,1,0:T(8,128)S(1)}, f32[66,1,8,128]{3,2,1,0:T(8,128)S(1)}, u32[]{:S(2)}, u32[]{:S(2)}) %collective-permute-start.5) | collective-permute-done | bytes 270368 | tf_op jit(solution)/shard_map/ppermute | solution.py:19
  57.0 4.4 %collective-permute-start.6 = (f32[66,6,1,128]{3,2,1,0:T(1,128)S(1)}, f32[66,6,1,128]{3,2,1,0:T(1,128)S(1)}, u32[]{:S(2)}, u32[]{:S(2)}) collective-permute-start(f32[66,6,1,128]{3,2,1,0:T(1,128)S(1)} %get-tuple-element.25), channel_id=1, source_target_pairs={{0,1},{1,2},{2,3},{3,4},{4,5},{5,6},{6,7},{8,9},{9,10},{10,11},{11... | collective-permute-start | bytes 608264 | tf_op jit(solution)/shard_map/ppermute | solution.py:17
  64.6 4.4 %collective-permute-done.7 = f32[66,6,1,128]{3,2,1,0:T(1,128)S(1)} collective-permute-done((f32[66,6,1,128]{3,2,1,0:T(1,128)S(1)}, f32[66,6,1,128]{3,2,1,0:T(1,128)S(1)}, u32[]{:S(2)}, u32[]{:S(2)}) %collective-permute-start.7) | collective-permute-done | bytes 202784 | tf_op jit(solution)/shard_map/ppermute | solution.py:19
  69.0 2.0 %fusion.39 = f32[64,4,9,128]{3,2,1,0:T(8,128)S(1)} fusion(f32[66,6,1,128]{3,2,1,0:T(1,128)S(1)} %collective-permute-done.7, f32[66,1,8,128]{3,2,1,0:T(8,128)S(1)} %collective-permute-done.5, f32[66,1,8,128]{3,2,1,0:T(8,128)S(1)} %collective-permute-done.4, f32[1,4,8,128]{3,2,1,0:T(8,128)S(1)} %get-tuple-element.54, ...), kind=kLoop, calls=%fused_computation.60 | loop fusion | flops 3833856 | bytes 3244032 | tf_op jit(solution)/shard_map/add | solution.py:38
  71.7 3.6 %fusion.83 = f32[4,1024,64]{1,2,0:T(8,128)S(1)} fusion(bf16[64,4,1024]{2,1,0:T(4,128)(2,1)S(1)} %reshape.197, bf16[64,512]{1,0:T(8,128)(2,1)S(1)} %copy-done, bf16[512,64]{0,1:T(8,128)(2,1)S(1)} %copy-done.2), kind=kOutput, calls=%fused_computation.129 | convolution fusion | flops 548143104 | bytes 1703936 | tf_op jit(solution)/shard_map/sh,hzc->szc/dot_general | solution.py:78
  76.1 5.4 %collective-permute-start.8 = (f32[66,1,8,128]{3,2,1,0:T(8,128)S(1)}, f32[66,1,8,128]{3,2,1,0:T(8,128)S(1)}, u32[]{:S(2)}, u32[]{:S(2)}) collective-permute-start(f32[66,1,8,128]{3,2,1,0:T(8,128)S(1)} %get-tuple-element.31), channel_id=1, source_target_pairs={{0,8},{8,16},{16,24},{1,9},{9,17},{17,25},{2,10},{10,18},{18,26},{... | collective-permute-start | bytes 811016 | tf_op jit(solution)/shard_map/ppermute | solution.py:17
  83.5 2.1 %collective-permute-done.9 = f32[66,1,8,128]{3,2,1,0:T(8,128)S(1)} collective-permute-done((f32[66,1,8,128]{3,2,1,0:T(8,128)S(1)}, f32[66,1,8,128]{3,2,1,0:T(8,128)S(1)}, u32[]{:S(2)}, u32[]{:S(2)}) %collective-permute-start.9) | collective-permute-done | bytes 270368 | tf_op jit(solution)/shard_map/ppermute | solution.py:19
  85.9 3.4 %collective-permute-start.10 = (f32[66,6,1,128]{3,2,1,0:T(1,128)S(1)}, f32[66,6,1,128]{3,2,1,0:T(1,128)S(1)}, u32[]{:S(2)}, u32[]{:S(2)}) collective-permute-start(f32[66,6,1,128]{3,2,1,0:T(1,128)S(1)} %get-tuple-element.23), channel_id=1, source_target_pairs={{0,1},{1,2},{2,3},{3,4},{4,5},{5,6},{6,7},{8,9},{9,10},{10,11},{11... | collective-permute-start | bytes 608264 | tf_op jit(solution)/shard_map/ppermute | solution.py:17
  92.5 4.4 %collective-permute-done.11 = f32[66,6,1,128]{3,2,1,0:T(1,128)S(1)} collective-permute-done((f32[66,6,1,128]{3,2,1,0:T(1,128)S(1)}, f32[66,6,1,128]{3,2,1,0:T(1,128)S(1)}, u32[]{:S(2)}, u32[]{:S(2)}) %collective-permute-start.11) | collective-permute-done | bytes 202784 | tf_op jit(solution)/shard_map/ppermute | solution.py:19
  99.6 3.6 %fusion.77 = f32[4,1024,64]{1,2,0:T(8,128)S(1)} fusion(bf16[64,4,1024]{2,1,0:T(4,128)(2,1)S(1)} %reshape.198, bf16[64,512]{1,0:T(8,128)(2,1)S(1)} %copy-done, bf16[512,64]{0,1:T(8,128)(2,1)S(1)} %copy-done.2), kind=kOutput, calls=%fused_computation.127 | convolution fusion | flops 548143104 | bytes 1703936 | tf_op jit(solution)/shard_map/sh,hzc->szc/dot_general | solution.py:78
  104.0 5.3 %collective-permute-start.12 = (f32[66,1,8,128]{3,2,1,0:T(8,128)S(1)}, f32[66,1,8,128]{3,2,1,0:T(8,128)S(1)}, u32[]{:S(2)}, u32[]{:S(2)}) collective-permute-start(f32[66,1,8,128]{3,2,1,0:T(8,128)S(1)} %get-tuple-element.29), channel_id=1, source_target_pairs={{0,8},{8,16},{16,24},{1,9},{9,17},{17,25},{2,10},{10,18},{18,26},{... | collective-permute-start | bytes 811016 | tf_op jit(solution)/shard_map/ppermute | solution.py:17
  111.3 2.2 %collective-permute-done.13 = f32[66,1,8,128]{3,2,1,0:T(8,128)S(1)} collective-permute-done((f32[66,1,8,128]{3,2,1,0:T(8,128)S(1)}, f32[66,1,8,128]{3,2,1,0:T(8,128)S(1)}, u32[]{:S(2)}, u32[]{:S(2)}) %collective-permute-start.13) | collective-permute-done | bytes 270368 | tf_op jit(solution)/shard_map/ppermute | solution.py:19
  113.8 4.4 %collective-permute-start.14 = (f32[66,6,1,128]{3,2,1,0:T(1,128)S(1)}, f32[66,6,1,128]{3,2,1,0:T(1,128)S(1)}, u32[]{:S(2)}, u32[]{:S(2)}) collective-permute-start(f32[66,6,1,128]{3,2,1,0:T(1,128)S(1)} %get-tuple-element.21), channel_id=1, source_target_pairs={{0,1},{1,2},{2,3},{3,4},{4,5},{5,6},{6,7},{8,9},{9,10},{10,11},{11... | collective-permute-start | bytes 608264 | tf_op jit(solution)/shard_map/ppermute | solution.py:17
  121.4 4.4 %collective-permute-done.15 = f32[66,6,1,128]{3,2,1,0:T(1,128)S(1)} collective-permute-done((f32[66,6,1,128]{3,2,1,0:T(1,128)S(1)}, f32[66,6,1,128]{3,2,1,0:T(1,128)S(1)}, u32[]{:S(2)}, u32[]{:S(2)}) %collective-permute-start.15) | collective-permute-done | bytes 202784 | tf_op jit(solution)/shard_map/ppermute | solution.py:19
  128.5 3.6 %fusion.71 = f32[4,1024,64]{1,2,0:T(8,128)S(1)} fusion(bf16[64,4,1024]{2,1,0:T(4,128)(2,1)S(1)} %reshape.199, bf16[64,512]{1,0:T(8,128)(2,1)S(1)} %copy-done, bf16[512,64]{0,1:T(8,128)(2,1)S(1)} %copy-done.2), kind=kOutput, calls=%fused_computation.125 | convolution fusion | flops 548143104 | bytes 1703936 | tf_op jit(solution)/shard_map/sh,hzc->szc/dot_general | solution.py:78
  132.5 20.1 %all_to_all.36 = f32[64,4,8,128]{3,2,1,0:T(8,128)S(1)} all-to-all(f32[64,4,8,128]{3,2,1,0:T(8,128)S(1)} %copy_add_fusion), channel_id=1, replica_groups=mesh['species'=4,'tile'=8] {'species'}, dimensions={0} | all-to-all | bytes 2097152 | tf_op jit(solution)/shard_map/all_to_all | solution.py:81
  (88 shorter events, 35.2 us)
Async XLA Ops:
  0.0 42.1 %copy-start = (bf16[64,512]{1,0:T(8,128)(2,1)S(1)}, bf16[64,512]{1,0:T(8,128)(2,1)}, u32[]{:S(2)}) copy-start(bf16[64,512]{1,0:T(8,128)(2,1)} %param.7) | copy-start | bytes 196612
  0.0 6.6 %copy-start.1 = (f32[4,3,4,8,128]{4,3,2,1,0:T(8,128)S(1)}, f32[4,3,4,8,128]{4,3,2,1,0:T(8,128)}, u32[]{:S(2)}) copy-start(f32[4,3,4,8,128]{4,3,2,1,0:T(8,128)} %param.5) | copy-start | bytes 589828
  2.3 18.7 %all-to-all-start = ((f32[16,16,8,128]{3,2,0,1:T(8,128)}), f32[16,16,8,128]{3,2,0,1:T(8,128)S(1)}, u32[]{:S(2)}, u32[]{:S(2)}) async-start(f32[16,16,8,128]{3,2,0,1:T(8,128)} %copy.32), calls=%async_computation | async-start | bytes 2097152 | tf_op jit(solution)/shard_map/all_to_all | solution.py:57
  21.6 5.1 %collective-permute-start.1 = (f32[66,1,8,128]{3,2,1,0:T(8,128)S(1)}, f32[66,1,8,128]{3,2,1,0:T(8,128)S(1)}, u32[]{:S(2)}, u32[]{:S(2)}) collective-permute-start(f32[66,1,8,128]{3,2,1,0:T(8,128)S(1)} %get-tuple-element.36), channel_id=1, source_target_pairs={{8,0},{16,8},{24,16},{9,1},{17,9},{25,17},{10,2},{18,10},{26,18},{... | collective-permute-start | bytes 811016 | tf_op jit(solution)/shard_map/ppermute | solution.py:19
  22.9 4.2 %collective-permute-start = (f32[66,1,8,128]{3,2,1,0:T(8,128)S(1)}, f32[66,1,8,128]{3,2,1,0:T(8,128)S(1)}, u32[]{:S(2)}, u32[]{:S(2)}) collective-permute-start(f32[66,1,8,128]{3,2,1,0:T(8,128)S(1)} %get-tuple-element.35), channel_id=1, source_target_pairs={{0,8},{8,16},{16,24},{1,9},{9,17},{17,25},{2,10},{10,18},{18,26},{... | collective-permute-start | bytes 811016 | tf_op jit(solution)/shard_map/ppermute | solution.py:17
  27.3 7.3 %collective-permute-start.2 = (f32[66,6,1,128]{3,2,1,0:T(1,128)S(1)}, f32[66,6,1,128]{3,2,1,0:T(1,128)S(1)}, u32[]{:S(2)}, u32[]{:S(2)}) collective-permute-start(f32[66,6,1,128]{3,2,1,0:T(1,128)S(1)} %get-tuple-element.27), channel_id=1, source_target_pairs={{0,1},{1,2},{2,3},{3,4},{4,5},{5,6},{6,7},{8,9},{9,10},{10,11},{11... | collective-permute-start | bytes 608264 | tf_op jit(solution)/shard_map/ppermute | solution.py:17
  31.4 7.9 %collective-permute-start.3 = (f32[66,6,1,128]{3,2,1,0:T(1,128)S(1)}, f32[66,6,1,128]{3,2,1,0:T(1,128)S(1)}, u32[]{:S(2)}, u32[]{:S(2)}) collective-permute-start(f32[66,6,1,128]{3,2,1,0:T(1,128)S(1)} %get-tuple-element.28), channel_id=1, source_target_pairs={{1,0},{2,1},{3,2},{4,3},{5,4},{6,5},{7,6},{9,8},{10,9},{11,10},{12... | collective-permute-start | bytes 608264 | tf_op jit(solution)/shard_map/ppermute | solution.py:19
  41.3 0.8 copy-start.2
  46.5 5.7 %collective-permute-start.4 = (f32[66,1,8,128]{3,2,1,0:T(8,128)S(1)}, f32[66,1,8,128]{3,2,1,0:T(8,128)S(1)}, u32[]{:S(2)}, u32[]{:S(2)}) collective-permute-start(f32[66,1,8,128]{3,2,1,0:T(8,128)S(1)} %get-tuple-element.33), channel_id=1, source_target_pairs={{0,8},{8,16},{16,24},{1,9},{9,17},{17,25},{2,10},{10,18},{18,26},{... | collective-permute-start | bytes 811016 | tf_op jit(solution)/shard_map/ppermute | solution.py:17
  50.2 6.5 %collective-permute-start.5 = (f32[66,1,8,128]{3,2,1,0:T(8,128)S(1)}, f32[66,1,8,128]{3,2,1,0:T(8,128)S(1)}, u32[]{:S(2)}, u32[]{:S(2)}) collective-permute-start(f32[66,1,8,128]{3,2,1,0:T(8,128)S(1)} %get-tuple-element.34), channel_id=1, source_target_pairs={{8,0},{16,8},{24,16},{9,1},{17,9},{25,17},{10,2},{18,10},{26,18},{... | collective-permute-start | bytes 811016 | tf_op jit(solution)/shard_map/ppermute | solution.py:19
  57.0 7.6 %collective-permute-start.6 = (f32[66,6,1,128]{3,2,1,0:T(1,128)S(1)}, f32[66,6,1,128]{3,2,1,0:T(1,128)S(1)}, u32[]{:S(2)}, u32[]{:S(2)}) collective-permute-start(f32[66,6,1,128]{3,2,1,0:T(1,128)S(1)} %get-tuple-element.25), channel_id=1, source_target_pairs={{0,1},{1,2},{2,3},{3,4},{4,5},{5,6},{6,7},{8,9},{9,10},{10,11},{11... | collective-permute-start | bytes 608264 | tf_op jit(solution)/shard_map/ppermute | solution.py:17
  61.3 7.6 %collective-permute-start.7 = (f32[66,6,1,128]{3,2,1,0:T(1,128)S(1)}, f32[66,6,1,128]{3,2,1,0:T(1,128)S(1)}, u32[]{:S(2)}, u32[]{:S(2)}) collective-permute-start(f32[66,6,1,128]{3,2,1,0:T(1,128)S(1)} %get-tuple-element.26), channel_id=1, source_target_pairs={{1,0},{2,1},{3,2},{4,3},{5,4},{6,5},{7,6},{9,8},{10,9},{11,10},{12... | collective-permute-start | bytes 608264 | tf_op jit(solution)/shard_map/ppermute | solution.py:19
  76.1 7.4 %collective-permute-start.8 = (f32[66,1,8,128]{3,2,1,0:T(8,128)S(1)}, f32[66,1,8,128]{3,2,1,0:T(8,128)S(1)}, u32[]{:S(2)}, u32[]{:S(2)}) collective-permute-start(f32[66,1,8,128]{3,2,1,0:T(8,128)S(1)} %get-tuple-element.31), channel_id=1, source_target_pairs={{0,8},{8,16},{16,24},{1,9},{9,17},{17,25},{2,10},{10,18},{18,26},{... | collective-permute-start | bytes 811016 | tf_op jit(solution)/shard_map/ppermute | solution.py:17
  81.5 4.1 %collective-permute-start.9 = (f32[66,1,8,128]{3,2,1,0:T(8,128)S(1)}, f32[66,1,8,128]{3,2,1,0:T(8,128)S(1)}, u32[]{:S(2)}, u32[]{:S(2)}) collective-permute-start(f32[66,1,8,128]{3,2,1,0:T(8,128)S(1)} %get-tuple-element.32), channel_id=1, source_target_pairs={{8,0},{16,8},{24,16},{9,1},{17,9},{25,17},{10,2},{18,10},{26,18},{... | collective-permute-start | bytes 811016 | tf_op jit(solution)/shard_map/ppermute | solution.py:19
  85.9 6.6 %collective-permute-start.10 = (f32[66,6,1,128]{3,2,1,0:T(1,128)S(1)}, f32[66,6,1,128]{3,2,1,0:T(1,128)S(1)}, u32[]{:S(2)}, u32[]{:S(2)}) collective-permute-start(f32[66,6,1,128]{3,2,1,0:T(1,128)S(1)} %get-tuple-element.23), channel_id=1, source_target_pairs={{0,1},{1,2},{2,3},{3,4},{4,5},{5,6},{6,7},{8,9},{9,10},{10,11},{11... | collective-permute-start | bytes 608264 | tf_op jit(solution)/shard_map/ppermute | solution.py:17
  89.3 7.6 %collective-permute-start.11 = (f32[66,6,1,128]{3,2,1,0:T(1,128)S(1)}, f32[66,6,1,128]{3,2,1,0:T(1,128)S(1)}, u32[]{:S(2)}, u32[]{:S(2)}) collective-permute-start(f32[66,6,1,128]{3,2,1,0:T(1,128)S(1)} %get-tuple-element.24), channel_id=1, source_target_pairs={{1,0},{2,1},{3,2},{4,3},{5,4},{6,5},{7,6},{9,8},{10,9},{11,10},{12... | collective-permute-start | bytes 608264 | tf_op jit(solution)/shard_map/ppermute | solution.py:19
  104.0 7.3 %collective-permute-start.12 = (f32[66,1,8,128]{3,2,1,0:T(8,128)S(1)}, f32[66,1,8,128]{3,2,1,0:T(8,128)S(1)}, u32[]{:S(2)}, u32[]{:S(2)}) collective-permute-start(f32[66,1,8,128]{3,2,1,0:T(8,128)S(1)} %get-tuple-element.29), channel_id=1, source_target_pairs={{0,8},{8,16},{16,24},{1,9},{9,17},{17,25},{2,10},{10,18},{18,26},{... | collective-permute-start | bytes 811016 | tf_op jit(solution)/shard_map/ppermute | solution.py:17
  109.3 4.2 %collective-permute-start.13 = (f32[66,1,8,128]{3,2,1,0:T(8,128)S(1)}, f32[66,1,8,128]{3,2,1,0:T(8,128)S(1)}, u32[]{:S(2)}, u32[]{:S(2)}) collective-permute-start(f32[66,1,8,128]{3,2,1,0:T(8,128)S(1)} %get-tuple-element.30), channel_id=1, source_target_pairs={{8,0},{16,8},{24,16},{9,1},{17,9},{25,17},{10,2},{18,10},{26,18},{... | collective-permute-start | bytes 811016 | tf_op jit(solution)/shard_map/ppermute | solution.py:19
  113.8 7.6 %collective-permute-start.14 = (f32[66,6,1,128]{3,2,1,0:T(1,128)S(1)}, f32[66,6,1,128]{3,2,1,0:T(1,128)S(1)}, u32[]{:S(2)}, u32[]{:S(2)}) collective-permute-start(f32[66,6,1,128]{3,2,1,0:T(1,128)S(1)} %get-tuple-element.21), channel_id=1, source_target_pairs={{0,1},{1,2},{2,3},{3,4},{4,5},{5,6},{6,7},{8,9},{9,10},{10,11},{11... | collective-permute-start | bytes 608264 | tf_op jit(solution)/shard_map/ppermute | solution.py:17
  118.1 7.6 %collective-permute-start.15 = (f32[66,6,1,128]{3,2,1,0:T(1,128)S(1)}, f32[66,6,1,128]{3,2,1,0:T(1,128)S(1)}, u32[]{:S(2)}, u32[]{:S(2)}) collective-permute-start(f32[66,6,1,128]{3,2,1,0:T(1,128)S(1)} %get-tuple-element.22), channel_id=1, source_target_pairs={{1,0},{2,1},{3,2},{4,3},{5,4},{6,5},{7,6},{9,8},{10,9},{11,10},{12... | collective-permute-start | bytes 608264 | tf_op jit(solution)/shard_map/ppermute | solution.py:19
where the time goes:
time: 154 us
  starting transfers between devices  48.9 us (32%)
  waiting for transfers between devices  47.7 us (31%)
  blocking collectives  20.1 us (13%)
  matrix products  14.5 us (9%)
  other arithmetic  14.3 us (9%)
  local copies, waits for them, and re-layouts  7.61 us (5%)
    ppermute x8, starting transfers between devices, extended(): lax.ppermute(tail, axis, [(i, (i + 1) % count) for i in range(ends)])  33.6 us
    ppermute x8, waiting for transfers between devices, extended(): lax.ppermute(head, axis, [((i + 1) % count, i) for i in range(ends)])  26.7 us
    all_to_all x1, blocking collectives, per_device(): lax.all_to_all(state, 'species', split_axis=0, concat_axis=1, tiled=True)  20.1 us
    dot_general x4, matrix products, per_device(): jnp.einsum('sh,hzc->szc', weight_out, hidden, preferred_element_type=jnp....  14.5 us
    all_to_all x1, waiting for transfers between devices, per_device(): lax.all_to_all(tracers, 'species', split_axis=1, concat_axis=0, tiled=True)  14.3 us
    ppermute x8, starting transfers between devices, extended(): lax.ppermute(head, axis, [((i + 1) % count, i) for i in range(ends)])  11 us
    add x4, other arithmetic, advance(): positive(face_x) * along_x[:, :, :-1] + negative(face_x) * along_x[:, :, 1:]  7.89 us
    ppermute x8, waiting for transfers between devices, extended(): lax.ppermute(tail, axis, [(i, (i + 1) % count) for i in range(ends)])  6.59 us
  transfers between devices with their start and end apart: 17, of which 13 were waited for; matrix products, arithmetic and copies ran while one was open for 2% of the time, Pallas kernels for 0%

commit v1 on v0

--- a/solution.py
+++ b/solution.py
@@ -1,9 +1,26 @@
+import functools
+
 import jax
 import jax.numpy as jnp
 from jax import lax
+from jax.experimental import pallas as pl
+from jax.experimental.pallas import tpu as pltpu
 from jax.sharding import PartitionSpec as P
 
 STEPS = 4
+AXES = ("species", "tile")
+PACK = 16
+VMEM = pl.BlockSpec(memory_space=pltpu.VMEM)
+SMEM = pl.BlockSpec(memory_space=pltpu.SMEM)
+LIMIT = 24 * 1024 * 1024
+
+
+def positive(value):
+    return jnp.maximum(value, 0.0)
+
+
+def negative(value):
+    return jnp.minimum(value, 0.0)
 
 
 def extended(cells, sides, width):
@@ -21,14 +38,6 @@
             axis=dim,
         )
     return cells
-
-
-def positive(value):
-    return jnp.maximum(value, 0.0)
-
-
-def negative(value):
-    return jnp.minimum(value, 0.0)
 
 
 def advance(padded_state, padded_x, flux_y, padded_z):
@@ -51,7 +60,7 @@
     )
 
 
-def per_device(tracers, fluxes, weight_in, weight_out):
+def by_levels(tracers, fluxes, weight_in, weight_out):
     spec_loc, depth_all, width_x, width_y = tracers.shape
     tile_at = lax.axis_index("tile")
     state = lax.all_to_all(tracers, "species", split_axis=1, concat_axis=0, tiled=True)
@@ -81,6 +90,275 @@
     return lax.all_to_all(state, "species", split_axis=0, concat_axis=1, tiled=True)
 
 
+def pack_kernel(count, depth, width, tile_ref, tracers_ref, fluxes_ref, out_ref):
+    tile = tile_ref[0]
+    odd = lax.rem(tile, 2)
+    spec = tracers_ref.shape[0] // (depth * width)
+    rows = fluxes_ref.shape[0] // width
+    lev = depth // count
+    parts = rows // PACK
+    at = lax.broadcasted_iota(jnp.int32, (rows, 1), 0)
+    is_x = lax.rem(lax.div(at, lev), 3) == 0
+    for place in range(count):
+        target = jnp.where(odd == 1, count - 1 - place, place)
+        for side in range(2):
+            x = 2 * place + side
+            base = side * (depth + 2 * parts)
+            for k in range(depth):
+                cells = tracers_ref[pl.ds(k * width + x, spec, stride=depth * width), :]
+                out_ref[target, base + k] = cells.astype(jnp.bfloat16)
+            flux = fluxes_ref[pl.ds(x, rows, stride=width), :]
+            if x == 0:
+                flux = jnp.where(jnp.logical_and(is_x, tile == 0), 0.0, flux)
+            flux = flux.astype(jnp.bfloat16)
+            for part in range(parts):
+                out_ref[target, depth + side * parts + part] = flux[part * PACK : (part + 1) * PACK]
+
+
+def flux_rows(ref, first, parts, count, lev):
+    blocks = []
+    for source in range(count):
+        tiles = [ref[source, first + part].astype(jnp.float32) for part in range(parts)]
+        blocks.append(jnp.concatenate(tiles, 0))
+    return [
+        [
+            jnp.concatenate(
+                [b[(t * 3 + d) * lev : (t * 3 + d + 1) * lev] for b in blocks], 0
+            )
+            for d in range(3)
+        ]
+        for t in range(STEPS)
+    ]
+
+
+def unpack_kernel(depth, parts, got_ref, left_ref, right_ref, flux_left_ref, flux_right_ref):
+    count = got_ref.shape[0]
+    lev = depth // count
+    spec = got_ref.shape[2]
+    for side, (state_ref, flux_ref) in enumerate(
+        ((left_ref, flux_left_ref), (right_ref, flux_right_ref))
+    ):
+        base = side * (depth + 2 * parts)
+        for source in range(count):
+            for k in range(depth):
+                state_ref[k, source * spec : (source + 1) * spec] = got_ref[
+                    source, base + k
+                ].astype(jnp.float32)
+        flux = flux_rows(got_ref, depth + side * parts, parts, count, lev)
+        for t in range(STEPS):
+            for d in range(3):
+                flux_ref[t, d] = flux[t][d]
+
+
+def step_kernel(
+    t, is_left, first, parts, own_ref, side_ref, halo_ref, flux_ref, upper_ref, w_in_ref, w_out_ref, *rest
+):
+    depth, spec_all, width_y = own_ref.shape
+    count, spec = halo_ref.shape[0], halo_ref.shape[2]
+    lev = depth // count
+    rest = list(rest)
+    coef = rest.pop()
+    send_ref = rest.pop(0)
+    new_ref = rest.pop(0) if t < STEPS - 1 else None
+    if first and not is_left:
+        edge_ref = rest.pop(0)
+        edge = flux_rows(halo_ref, depth, parts, count, lev)
+        for i in range(STEPS):
+            edge_ref[i] = edge[i][0]
+        fx_hi = edge[t][0]
+    elif is_left:
+        fx_hi = upper_ref[t, 0]
+    else:
+        fx_hi = upper_ref[t]
+    fx = flux_ref[t, 0]
+    fy = flux_ref[t, 1]
+    fy_hi = pltpu.roll(fy, width_y - 1, 1)
+    fz = flux_ref[t, 2]
+    fz = jnp.where(lax.broadcasted_iota(jnp.int32, fz.shape, 0) == 0, 0.0, fz)
+    fz_hi = jnp.concatenate([fz[1:], jnp.zeros_like(fz[:1])], 0)
+    coef[0] = (
+        1.0
+        + (negative(fx) - positive(fx_hi))
+        + (negative(fy) - positive(fy_hi))
+        + (negative(fz) - positive(fz_hi))
+    )
+    coef[1] = positive(fx) if is_left else -negative(fx_hi)
+    coef[2] = -negative(fx_hi) if is_left else positive(fx)
+    coef[3] = positive(fy)
+    coef[4] = -negative(fy_hi)
+    coef[5] = positive(fz)
+    coef[6] = -negative(fz_hi)
+    w_in = w_in_ref[...]
+    w_out = w_out_ref[...]
+    group = 2
+    for k0 in range(0, depth, group):
+        moved = []
+        for k in range(k0, k0 + group):
+            own = own_ref[k]
+            halo = jnp.concatenate([halo_ref[s, k].astype(jnp.float32) for s in range(count)], 0)
+            out = coef[0, pl.ds(k, 1)] * own
+            out += coef[1, pl.ds(k, 1)] * halo
+            out += coef[2, pl.ds(k, 1)] * side_ref[k]
+            out += coef[3, pl.ds(k, 1)] * pltpu.roll(own, 1, 1)
+            out += coef[4, pl.ds(k, 1)] * pltpu.roll(own, width_y - 1, 1)
+            if k > 0:
+                out += coef[5, pl.ds(k, 1)] * own_ref[k - 1]
+            if k < depth - 1:
+                out += coef[6, pl.ds(k, 1)] * own_ref[k + 1]
+            moved.append(out)
+        cells = jnp.concatenate([m.astype(jnp.bfloat16) for m in moved], 1)
+        half = jnp.dot(w_in, cells, preferred_element_type=jnp.float32)
+        hidden = (half + half * jnp.tanh(half)).astype(jnp.bfloat16)
+        change = jnp.dot(w_out, hidden, preferred_element_type=jnp.float32)
+        for i in range(group):
+            new = moved[i] + change[:, i * width_y : (i + 1) * width_y]
+            if new_ref is not None:
+                new_ref[k0 + i] = new
+            for s in range(count):
+                send_ref[s, k0 + i] = new[s * spec : (s + 1) * spec].astype(jnp.bfloat16)
+
+
+def finish_kernel(depth, width, tile_ref, got_ref, out_ref):
+    odd = lax.rem(tile_ref[0], 2)
+    count, spec = got_ref.shape[0], got_ref.shape[3]
+    for place in range(count):
+        source = jnp.where(odd == 1, count - 1 - place, place)
+        for side in range(2):
+            for k in range(depth):
+                out_ref[pl.ds(k * width + 2 * place + side, spec, stride=depth * width), :] = got_ref[
+                    source, side, k
+                ].astype(jnp.float32)
+
+
+def call(kernel, out_shape, in_specs, args, scratch=(), flops=0, trans=0):
+    many = isinstance(out_shape, (list, tuple))
+    moved = sum(a.size * a.dtype.itemsize for a in args)
+    moved += sum(o.size * o.dtype.itemsize for o in (out_shape if many else [out_shape]))
+    return pl.pallas_call(
+        kernel,
+        out_shape=out_shape,
+        in_specs=in_specs,
+        out_specs=[VMEM] * len(out_shape) if many else VMEM,
+        scratch_shapes=scratch,
+        compiler_params=pltpu.CompilerParams(vmem_limit_bytes=LIMIT),
+        cost_estimate=pl.CostEstimate(flops=flops, bytes_accessed=moved, transcendentals=trans),
+    )(*args)
+
+
+def by_columns(tracers, fluxes, weight_in, weight_out):
+    spec, depth, width, width_y = tracers.shape
+    count, tiles = lax.axis_size("species"), lax.axis_size("tile")
+    spec_all, hid, lev = spec * count, weight_in.shape[0], depth // count
+    parts = STEPS * 3 * lev // PACK
+    f32, bf16 = jnp.float32, jnp.bfloat16
+    shape = jax.ShapeDtypeStruct
+
+    chain = []
+    for t in range(tiles):
+        for place in range(count):
+            s = place if t % 2 == 0 else count - 1 - place
+            chain.append(s * tiles + t)
+    to_left = [(chain[i + 1], chain[i]) for i in range(len(chain) - 1)]
+    to_right = [(chain[i], chain[i + 1]) for i in range(len(chain) - 1)]
+
+    tile = lax.axis_index("tile").astype(jnp.int32).reshape(1)
+    w_in = weight_in * jnp.asarray(0.5, bf16)
+    w_out = weight_out * jnp.asarray(0.5, bf16)
+
+    pieces = 2 * depth + 2 * parts
+    packed = call(
+        functools.partial(pack_kernel, count, depth, width),
+        shape((count, pieces, spec, width_y), bf16),
+        [SMEM, VMEM, VMEM],
+        (tile, tracers.reshape(-1, width_y), fluxes.reshape(-1, width_y)),
+    )
+    got = lax.all_to_all(packed, "species", split_axis=0, concat_axis=0, tiled=True)
+    from_right = lax.ppermute(got[:, : depth + parts], AXES, to_left)
+    from_left = lax.ppermute(got[:, depth + 2 * parts :], AXES, to_right)
+    row = shape((depth, spec_all, width_y), f32)
+    flux = shape((STEPS, 3, depth, width_y), f32)
+    left, right, flux_left, flux_right = call(
+        functools.partial(unpack_kernel, depth, parts), [row, row, flux, flux], [VMEM], (got,)
+    )
+    sent = shape((count, depth, spec, width_y), bf16)
+    edge = flux_right
+    flops = 4 * depth * width_y * spec_all * hid
+    trans = depth * width_y * hid
+
+    def step(t, is_left, own, side, halo):
+        nonlocal edge
+        first = t == 0
+        outs = [sent] + ([row] if t < STEPS - 1 else [])
+        if first and not is_left:
+            outs.append(shape((STEPS, depth, width_y), f32))
+        args = (
+            own,
+            side,
+            halo,
+            flux_left if is_left else flux_right,
+            flux_right if is_left else edge,
+            w_in,
+            w_out,
+        )
+        outs = call(
+            functools.partial(step_kernel, t, is_left, first, parts),
+            outs,
+            [VMEM] * len(args),
+            args,
+            scratch=[pltpu.VMEM((7, depth, width_y), f32)],
+            flops=flops,
+            trans=trans,
+        )
+        if first and not is_left:
+            edge = outs[-1]
+        return outs[0], (outs[1] if t < STEPS - 1 else None)
+
+    for t in range(STEPS):
+        last = t == STEPS - 1
+        old_left, old_right = left, right
+        if t % 2 == 0:
+            send_right, right = step(t, False, old_right, old_left, from_right)
+            left_in = from_left
+            if not last:
+                from_left = lax.ppermute(send_right, AXES, to_right)
+            send_left, left = step(t, True, old_left, old_right, left_in)
+            if not last:
+                from_right = lax.ppermute(send_left, AXES, to_left)
+        else:
+            send_left, left = step(t, True, old_left, old_right, from_left)
+            right_in = from_right
+            if not last:
+                from_right = lax.ppermute(send_left, AXES, to_left)
+            send_right, right = step(t, False, old_right, old_left, right_in)
+            if not last:
+                from_left = lax.ppermute(send_right, AXES, to_right)
+    done = lax.all_to_all(
+        jnp.stack([send_left, send_right], 1), "species", split_axis=0, concat_axis=0, tiled=True
+    )
+    out = call(
+        functools.partial(finish_kernel, depth, width),
+        shape((spec * depth * width, width_y), f32),
+        [SMEM, VMEM],
+        (tile, done),
+    )
+    return out.reshape(tracers.shape)
+
+
+def per_device(tracers, fluxes, weight_in, weight_out):
+    spec, depth, width, width_y = tracers.shape
+    count = lax.axis_size("species")
+    fits = (
+        width == 2 * count
+        and depth % (2 * count) == 0
+        and spec == PACK
+        and width_y % 128 == 0
+        and width % 8 == 0
+        and (STEPS * 3 * depth // count) % PACK == 0
+    )
+    chosen = by_columns if fits else by_levels
+    return chosen(tracers, fluxes, weight_in, weight_out)
+
+
 def solution(mesh):
     placed = (P("species", None, "tile", None), P(None, None, "species", "tile", None), P(), P())
     return jax.shard_map(

time: 154 us -> 78.1 us (0.51)
  the two profiles are of different devices: /device:TPU:0 before, /device:TPU:17 now
where the time goes in v1:
time: 78.1 us; the launch traced here: 77.2 us
  blocking collectives  25.2 us (32%)
  starting transfers between devices  25.2 us (32%)
  Pallas kernels  22.4 us (29%)
  local copies, waits for them, and re-layouts  2.32 us (3%)
  waiting for transfers between devices  1.69 us (2%)
    pallas_call x11, Pallas kernels, call(): pl.pallas_call(kernel, out_shape=out_shape, in_specs=in_specs, out_specs=...  22.4 us
    ppermute x3, starting transfers between devices, by_columns(): from_right = lax.ppermute(send_left, AXES, to_left)  13.3 us
    all_to_all x1, blocking collectives, by_columns(): lax.all_to_all(jnp.stack([send_left, send_right], 1), 'species', split_ax...  13 us
    all_to_all x1, blocking collectives, by_columns(): lax.all_to_all(packed, 'species', split_axis=0, concat_axis=0, tiled=True)  12.2 us
    ppermute x3, starting transfers between devices, by_columns(): from_left = lax.ppermute(send_right, AXES, to_right)  6.89 us
    ppermute x1, starting transfers between devices, by_columns(): from_left = lax.ppermute(got[:, depth + 2 * parts:], AXES, to_right)  2.96 us
    unnamed x9, local copies, waits for them, and re-layouts  2.28 us
    ppermute x1, starting transfers between devices, by_columns(): from_right = lax.ppermute(got[:, :depth + parts], AXES, to_left)  2.09 us
  transfers between devices with their start and end apart: 8, of which 2 were waited for; matrix products, arithmetic and copies ran while one was open for 0% of the time, Pallas kernels for 23%

profile of v1, /device:TPU:17, one launch (start us, length us, event | category | flops | bytes accessed | tf_op | source)
XLA Modules:
  0.0 77.2 jit_solution(10565868635741681769)
XLA Ops:
  0.0 1.2 %copy-done = f32[16,16,8,128]{3,2,1,0:T(8,128)S(1)} copy-done((f32[16,16,8,128]{3,2,1,0:T(8,128)S(1)}, f32[16,16,8,128]{3,2,1,0:T(8,128)}, u32[]{:S(2)}) %copy-start) | copy-done | bytes 1048600
  1.2 0.9 %copy-done.1 = f32[4,3,4,8,128]{4,3,2,1,0:T(8,128)S(1)} copy-done((f32[4,3,4,8,128]{4,3,2,1,0:T(8,128)S(1)}, f32[4,3,4,8,128]{4,3,2,1,0:T(8,128)}, u32[]{:S(2)}) %copy-start.1) | copy-done | bytes 196632
  2.2 0.6 shard_map.46
  2.8 12.2 %all_to_all.10.got_ref = bf16[4,38,16,128]{3,2,1,0:T(8,128)(2,1)S(1)} all-to-all(bf16[4,38,16,128]{3,2,1,0:T(8,128)(2,1)S(1)} %shard_map.46), channel_id=1, replica_groups=mesh['species'=4,'tile'=8] {'species'}, dimensions={0} | all-to-all | bytes 1245184 | tf_op jit(solution)/shard_map/all_to_all | solution.py:275
  15.0 3.0 %collective-permute-start = (bf16[4,16,16,128]{3,2,1,0:T(8,128)(2,1)S(1)}, bf16[4,16,16,128]{3,2,1,0:T(8,128)(2,1)S(1)}, u32[]{:S(2)}, u32[]{:S(2)}) collective-permute-start(bf16[4,16,16,128]{3,2,1,0:T(8,128)(2,1)S(1)} %slice.8), channel_id=1, source_target_pairs={{0,8},{8,16},{16,24},{24,25},{25,17},{17,9},{9,1},{1,2},{2,10},{10... | collective-permute-start | bytes 786440 | tf_op jit(solution)/shard_map/ppermute | solution.py:277
  18.0 2.1 %collective-permute-start.1 = (bf16[4,19,16,128]{3,2,1,0:T(8,128)(2,1)S(1)}, bf16[4,19,16,128]{3,2,1,0:T(8,128)(2,1)S(1)}, u32[]{:S(2)}, u32[]{:S(2)}) collective-permute-start(bf16[4,19,16,128]{3,2,1,0:T(8,128)(2,1)S(1)} %slice.9), channel_id=1, source_target_pairs={{8,0},{16,8},{24,16},{25,24},{17,25},{9,17},{1,9},{2,1},{10,2},{18... | collective-permute-start | bytes 933896 | tf_op jit(solution)/shard_map/ppermute | solution.py:276
  20.4 0.9 %collective-permute-done.halo_ref = bf16[4,16,16,128]{3,2,1,0:T(8,128)(2,1)S(1)} collective-permute-done((bf16[4,16,16,128]{3,2,1,0:T(8,128)(2,1)S(1)}, bf16[4,16,16,128]{3,2,1,0:T(8,128)(2,1)S(1)}, u32[]{:S(2)}, u32[]{:S(2)}) %collective-permute-start) | collective-permute-done | bytes 262176 | tf_op jit(solution)/shard_map/ppermute | solution.py:277
  21.3 2.5 %shard_map.48 = (bf16[4,16,16,128]{3,2,1,0:T(8,128)(2,1)S(1)}, f32[16,64,128]{2,1,0:T(8,128)S(1)}) custom-call(f32[16,64,128]{2,1,0:T(8,128)S(1)} %get-tuple-element.22.own_ref.side_ref, f32[16,64,128]{2,1,0:T(8,128)S(1)} %get-tuple-element.23.side_ref.own_ref, bf16[4,16,16,128]{3,2,1,0:T(8,128)(2,1)S(1)} %collective-permute-done.halo_ref, ...), custom_call_target="tpu_custom_call" | custom-call | flops 268435456 | bytes 2424832 | tf_op jit(solution)/shard_map/pallas_call | solution.py:237
  23.8 5.9 %collective-permute-start.3 = (bf16[4,16,16,128]{3,2,1,0:T(8,128)(2,1)S(1)}, bf16[4,16,16,128]{3,2,1,0:T(8,128)(2,1)S(1)}, u32[]{:S(2)}, u32[]{:S(2)}) collective-permute-start(bf16[4,16,16,128]{3,2,1,0:T(8,128)(2,1)S(1)} %get-tuple-element.30), channel_id=1, source_target_pairs={{8,0},{16,8},{24,16},{25,24},{17,25},{9,17},{1,9},{2,1},{10,2},{18... | collective-permute-start | bytes 786440 | tf_op jit(solution)/shard_map/ppermute | solution.py:326
  29.7 2.5 %shard_map.49 = (bf16[4,16,16,128]{3,2,1,0:T(8,128)(2,1)S(1)}, f32[16,64,128]{2,1,0:T(8,128)S(1)}, f32[4,16,128]{2,1,0:T(8,128)S(1)}) custom-call(f32[16,64,128]{2,1,0:T(8,128)S(1)} %get-tuple-element.23.side_ref.own_ref, f32[16,64,128]{2,1,0:T(8,128)S(1)} %get-tuple-element.22.own_ref.side_ref, ...), custom_call_target="tpu_custom_call" | custom-call | flops 268435456 | bytes 2506752 | tf_op jit(solution)/shard_map/pallas_call | solution.py:237
  32.2 1.9 %collective-permute-start.2 = (bf16[4,16,16,128]{3,2,1,0:T(8,128)(2,1)S(1)}, bf16[4,16,16,128]{3,2,1,0:T(8,128)(2,1)S(1)}, u32[]{:S(2)}, u32[]{:S(2)}) collective-permute-start(bf16[4,16,16,128]{3,2,1,0:T(8,128)(2,1)S(1)} %get-tuple-element.28), channel_id=1, source_target_pairs={{0,8},{8,16},{16,24},{24,25},{25,17},{17,9},{9,1},{1,2},{2,10},{10... | collective-permute-start | bytes 786440 | tf_op jit(solution)/shard_map/ppermute | solution.py:323
  34.1 2.5 %shard_map.51 = (bf16[4,16,16,128]{3,2,1,0:T(8,128)(2,1)S(1)}, f32[16,64,128]{2,1,0:T(8,128)S(1)}) custom-call(f32[16,64,128]{2,1,0:T(8,128)S(1)} %get-tuple-element.27.side_ref.own_ref, f32[16,64,128]{2,1,0:T(8,128)S(1)} %get-tuple-element.26.own_ref.side_ref, bf16[4,16,16,128]{3,2,1,0:T(8,128)(2,1)S(1)} %collective-permute-done.3.halo_ref, ...), custom_call_target="tpu_custom_call" | custom-call | flops 268435456 | bytes 2359296 | tf_op jit(solution)/shard_map/pallas_call | solution.py:237
  36.6 1.9 %collective-permute-start.4 = (bf16[4,16,16,128]{3,2,1,0:T(8,128)(2,1)S(1)}, bf16[4,16,16,128]{3,2,1,0:T(8,128)(2,1)S(1)}, u32[]{:S(2)}, u32[]{:S(2)}) collective-permute-start(bf16[4,16,16,128]{3,2,1,0:T(8,128)(2,1)S(1)} %get-tuple-element.33), channel_id=1, source_target_pairs={{0,8},{8,16},{16,24},{24,25},{25,17},{17,9},{9,1},{1,2},{2,10},{10... | collective-permute-start | bytes 786440 | tf_op jit(solution)/shard_map/ppermute | solution.py:334
  38.6 2.5 %shard_map.50 = (bf16[4,16,16,128]{3,2,1,0:T(8,128)(2,1)S(1)}, f32[16,64,128]{2,1,0:T(8,128)S(1)}) custom-call(f32[16,64,128]{2,1,0:T(8,128)S(1)} %get-tuple-element.26.own_ref.side_ref, f32[16,64,128]{2,1,0:T(8,128)S(1)} %get-tuple-element.27.side_ref.own_ref, bf16[4,16,16,128]{3,2,1,0:T(8,128)(2,1)S(1)} %collective-permute-done.2.halo_ref, ...), custom_call_target="tpu_custom_call" | custom-call | flops 268435456 | bytes 2424832 | tf_op jit(solution)/shard_map/pallas_call | solution.py:237
  41.0 4.7 %collective-permute-start.5 = (bf16[4,16,16,128]{3,2,1,0:T(8,128)(2,1)S(1)}, bf16[4,16,16,128]{3,2,1,0:T(8,128)(2,1)S(1)}, u32[]{:S(2)}, u32[]{:S(2)}) collective-permute-start(bf16[4,16,16,128]{3,2,1,0:T(8,128)(2,1)S(1)} %get-tuple-element.35), channel_id=1, source_target_pairs={{8,0},{16,8},{24,16},{25,24},{17,25},{9,17},{1,9},{2,1},{10,2},{18... | collective-permute-start | bytes 786440 | tf_op jit(solution)/shard_map/ppermute | solution.py:331
  45.8 2.5 %shard_map.52 = (bf16[4,16,16,128]{3,2,1,0:T(8,128)(2,1)S(1)}, f32[16,64,128]{2,1,0:T(8,128)S(1)}) custom-call(f32[16,64,128]{2,1,0:T(8,128)S(1)} %get-tuple-element.29.own_ref.side_ref, f32[16,64,128]{2,1,0:T(8,128)S(1)} %get-tuple-element.32.side_ref.own_ref, bf16[4,16,16,128]{3,2,1,0:T(8,128)(2,1)S(1)} %collective-permute-done.4.halo_ref, ...), custom_call_target="tpu_custom_call" | custom-call | flops 268435456 | bytes 2424832 | tf_op jit(solution)/shard_map/pallas_call | solution.py:237
  48.3 2.7 %collective-permute-start.7 = (bf16[4,16,16,128]{3,2,1,0:T(8,128)(2,1)S(1)}, bf16[4,16,16,128]{3,2,1,0:T(8,128)(2,1)S(1)}, u32[]{:S(2)}, u32[]{:S(2)}) collective-permute-start(bf16[4,16,16,128]{3,2,1,0:T(8,128)(2,1)S(1)} %get-tuple-element.38), channel_id=1, source_target_pairs={{8,0},{16,8},{24,16},{25,24},{17,25},{9,17},{1,9},{2,1},{10,2},{18... | collective-permute-start | bytes 786440 | tf_op jit(solution)/shard_map/ppermute | solution.py:326
  51.0 2.5 %shard_map.53 = (bf16[4,16,16,128]{3,2,1,0:T(8,128)(2,1)S(1)}, f32[16,64,128]{2,1,0:T(8,128)S(1)}) custom-call(f32[16,64,128]{2,1,0:T(8,128)S(1)} %get-tuple-element.32.side_ref.own_ref, f32[16,64,128]{2,1,0:T(8,128)S(1)} %get-tuple-element.29.own_ref.side_ref, bf16[4,16,16,128]{3,2,1,0:T(8,128)(2,1)S(1)} %collective-permute-done.5.halo_ref, ...), custom_call_target="tpu_custom_call" | custom-call | flops 268435456 | bytes 2359296 | tf_op jit(solution)/shard_map/pallas_call | solution.py:237
  53.5 3.0 %collective-permute-start.6 = (bf16[4,16,16,128]{3,2,1,0:T(8,128)(2,1)S(1)}, bf16[4,16,16,128]{3,2,1,0:T(8,128)(2,1)S(1)}, u32[]{:S(2)}, u32[]{:S(2)}) collective-permute-start(bf16[4,16,16,128]{3,2,1,0:T(8,128)(2,1)S(1)} %get-tuple-element.37), channel_id=1, source_target_pairs={{0,8},{8,16},{16,24},{24,25},{25,17},{17,9},{9,1},{1,2},{2,10},{10... | collective-permute-start | bytes 786440 | tf_op jit(solution)/shard_map/ppermute | solution.py:323
  56.5 2.5 %shard_map.55 = bf16[4,16,16,128]{3,2,1,0:T(8,128)(2,1)S(1)} custom-call(f32[16,64,128]{2,1,0:T(8,128)S(1)} %get-tuple-element.36.side_ref.own_ref, f32[16,64,128]{2,1,0:T(8,128)S(1)} %get-tuple-element.34.own_ref.side_ref, bf16[4,16,16,128]{3,2,1,0:T(8,128)(2,1)S(1)} %collective-permute-done.7.halo_ref, ...), custom_call_target="tpu_custom_call" | custom-call | flops 268435456 | bytes 1835008 | tf_op jit(solution)/shard_map/pallas_call | solution.py:237
  59.0 0.8 %collective-permute-done.6.halo_ref = bf16[4,16,16,128]{3,2,1,0:T(8,128)(2,1)S(1)} collective-permute-done((bf16[4,16,16,128]{3,2,1,0:T(8,128)(2,1)S(1)}, bf16[4,16,16,128]{3,2,1,0:T(8,128)(2,1)S(1)}, u32[]{:S(2)}, u32[]{:S(2)}) %collective-permute-start.6) | collective-permute-done | bytes 262176 | tf_op jit(solution)/shard_map/ppermute | solution.py:323
  59.8 2.5 %shard_map.54 = bf16[4,16,16,128]{3,2,1,0:T(8,128)(2,1)S(1)} custom-call(f32[16,64,128]{2,1,0:T(8,128)S(1)} %get-tuple-element.34.own_ref.side_ref, f32[16,64,128]{2,1,0:T(8,128)S(1)} %get-tuple-element.36.side_ref.own_ref, bf16[4,16,16,128]{3,2,1,0:T(8,128)(2,1)S(1)} %collective-permute-done.6.halo_ref, f32[4,3,16,128]{3,2,1,0:T(8,128)S(1)} %get-tuple-element.24.flux_ref, ...), custom_call_target="tpu_custom_call" | custom-call | flops 268435456 | bytes 1900544 | tf_op jit(solution)/shard_map/pallas_call | solution.py:237
  62.4 13.0 %all_to_all.11.got_ref = bf16[4,2,16,16,128]{4,3,2,1,0:T(8,128)(2,1)S(1)} all-to-all(bf16[4,2,16,16,128]{4,3,2,1,0:T(8,128)(2,1)S(1)} %pad_maximum_fusion), channel_id=1, replica_groups=mesh['species'=4,'tile'=8] {'species'}, dimensions={0} | all-to-all | bytes 1048576 | tf_op jit(solution)/shard_map/all_to_all | solution.py:335
  75.4 1.8 %shard_map.56 = f32[2048,128]{1,0:T(8,128)} custom-call(s32[1]{0:T(128)} %bitcast.tile_ref, bf16[4,2,16,16,128]{4,3,2,1,0:T(8,128)(2,1)S(1)} %all_to_all.11.got_ref), custom_call_target="tpu_custom_call" | custom-call | bytes 1572868 | tf_op jit(solution)/shard_map/pallas_call | solution.py:237
  (19 shorter events, 0.4 us)
Async XLA Ops:
  0.0 1.2 %copy-start = (f32[16,16,8,128]{3,2,1,0:T(8,128)S(1)}, f32[16,16,8,128]{3,2,1,0:T(8,128)}, u32[]{:S(2)}) copy-start(f32[16,16,8,128]{3,2,1,0:T(8,128)} %param.4) | copy-start | bytes 3145732
  1.2 0.9 %copy-start.1 = (f32[4,3,4,8,128]{4,3,2,1,0:T(8,128)S(1)}, f32[4,3,4,8,128]{4,3,2,1,0:T(8,128)}, u32[]{:S(2)}) copy-start(f32[4,3,4,8,128]{4,3,2,1,0:T(8,128)} %param.5) | copy-start | bytes 589828
  15.0 5.1 %copy-start.3 = (bf16[64,512]{1,0:T(8,128)(2,1)S(1)}, bf16[64,512]{1,0:T(8,128)(2,1)}, u32[]{:S(2)}) copy-start(bf16[64,512]{1,0:T(8,128)(2,1)} %param.7) | copy-start | bytes 196612
  15.0 6.3 %collective-permute-start = (bf16[4,16,16,128]{3,2,1,0:T(8,128)(2,1)S(1)}, bf16[4,16,16,128]{3,2,1,0:T(8,128)(2,1)S(1)}, u32[]{:S(2)}, u32[]{:S(2)}) collective-permute-start(bf16[4,16,16,128]{3,2,1,0:T(8,128)(2,1)S(1)} %slice.8), channel_id=1, source_target_pairs={{0,8},{8,16},{16,24},{24,25},{25,17},{17,9},{9,1},{1,2},{2,10},{10... | collective-permute-start | bytes 786440 | tf_op jit(solution)/shard_map/ppermute | solution.py:277
  18.0 2.1 %copy-start.2 = (bf16[512,64]{0,1:T(8,128)(2,1)S(1)}, bf16[512,64]{0,1:T(8,128)(2,1)}, u32[]{:S(2)}) copy-start(bf16[512,64]{0,1:T(8,128)(2,1)} %param.6) | copy-start | bytes 196612
  18.0 11.6 %collective-permute-start.1 = (bf16[4,19,16,128]{3,2,1,0:T(8,128)(2,1)S(1)}, bf16[4,19,16,128]{3,2,1,0:T(8,128)(2,1)S(1)}, u32[]{:S(2)}, u32[]{:S(2)}) collective-permute-start(bf16[4,19,16,128]{3,2,1,0:T(8,128)(2,1)S(1)} %slice.9), channel_id=1, source_target_pairs={{8,0},{16,8},{24,16},{25,24},{17,25},{9,17},{1,9},{2,1},{10,2},{18... | collective-permute-start | bytes 933896 | tf_op jit(solution)/shard_map/ppermute | solution.py:276
  23.8 10.3 %collective-permute-start.3 = (bf16[4,16,16,128]{3,2,1,0:T(8,128)(2,1)S(1)}, bf16[4,16,16,128]{3,2,1,0:T(8,128)(2,1)S(1)}, u32[]{:S(2)}, u32[]{:S(2)}) collective-permute-start(bf16[4,16,16,128]{3,2,1,0:T(8,128)(2,1)S(1)} %get-tuple-element.30), channel_id=1, source_target_pairs={{8,0},{16,8},{24,16},{25,24},{17,25},{9,17},{1,9},{2,1},{10,2},{18... | collective-permute-start | bytes 786440 | tf_op jit(solution)/shard_map/ppermute | solution.py:326
  32.2 6.4 %collective-permute-start.2 = (bf16[4,16,16,128]{3,2,1,0:T(8,128)(2,1)S(1)}, bf16[4,16,16,128]{3,2,1,0:T(8,128)(2,1)S(1)}, u32[]{:S(2)}, u32[]{:S(2)}) collective-permute-start(bf16[4,16,16,128]{3,2,1,0:T(8,128)(2,1)S(1)} %get-tuple-element.28), channel_id=1, source_target_pairs={{0,8},{8,16},{16,24},{24,25},{25,17},{17,9},{9,1},{1,2},{2,10},{10... | collective-permute-start | bytes 786440 | tf_op jit(solution)/shard_map/ppermute | solution.py:323
  36.6 9.2 %collective-permute-start.4 = (bf16[4,16,16,128]{3,2,1,0:T(8,128)(2,1)S(1)}, bf16[4,16,16,128]{3,2,1,0:T(8,128)(2,1)S(1)}, u32[]{:S(2)}, u32[]{:S(2)}) collective-permute-start(bf16[4,16,16,128]{3,2,1,0:T(8,128)(2,1)S(1)} %get-tuple-element.33), channel_id=1, source_target_pairs={{0,8},{8,16},{16,24},{24,25},{25,17},{17,9},{9,1},{1,2},{2,10},{10... | collective-permute-start | bytes 786440 | tf_op jit(solution)/shard_map/ppermute | solution.py:334
  41.0 9.9 %collective-permute-start.5 = (bf16[4,16,16,128]{3,2,1,0:T(8,128)(2,1)S(1)}, bf16[4,16,16,128]{3,2,1,0:T(8,128)(2,1)S(1)}, u32[]{:S(2)}, u32[]{:S(2)}) collective-permute-start(bf16[4,16,16,128]{3,2,1,0:T(8,128)(2,1)S(1)} %get-tuple-element.35), channel_id=1, source_target_pairs={{8,0},{16,8},{24,16},{25,24},{17,25},{9,17},{1,9},{2,1},{10,2},{18... | collective-permute-start | bytes 786440 | tf_op jit(solution)/shard_map/ppermute | solution.py:331
  48.3 8.3 %collective-permute-start.7 = (bf16[4,16,16,128]{3,2,1,0:T(8,128)(2,1)S(1)}, bf16[4,16,16,128]{3,2,1,0:T(8,128)(2,1)S(1)}, u32[]{:S(2)}, u32[]{:S(2)}) collective-permute-start(bf16[4,16,16,128]{3,2,1,0:T(8,128)(2,1)S(1)} %get-tuple-element.38), channel_id=1, source_target_pairs={{8,0},{16,8},{24,16},{25,24},{17,25},{9,17},{1,9},{2,1},{10,2},{18... | collective-permute-start | bytes 786440 | tf_op jit(solution)/shard_map/ppermute | solution.py:326
  53.5 6.4 %collective-permute-start.6 = (bf16[4,16,16,128]{3,2,1,0:T(8,128)(2,1)S(1)}, bf16[4,16,16,128]{3,2,1,0:T(8,128)(2,1)S(1)}, u32[]{:S(2)}, u32[]{:S(2)}) collective-permute-start(bf16[4,16,16,128]{3,2,1,0:T(8,128)(2,1)S(1)} %get-tuple-element.37), channel_id=1, source_target_pairs={{0,8},{8,16},{16,24},{24,25},{25,17},{17,9},{9,1},{1,2},{2,10},{10... | collective-permute-start | bytes 786440 | tf_op jit(solution)/shard_map/ppermute | solution.py:323

commit v2 on v0

--- a/solution.py
+++ b/solution.py
@@ -1,9 +1,27 @@
+import functools
+
 import jax
 import jax.numpy as jnp
 from jax import lax
+from jax.experimental import pallas as pl
+from jax.experimental.pallas import tpu as pltpu
 from jax.sharding import PartitionSpec as P
 
 STEPS = 4
+AXES = ("species", "tile")
+PACK = 16
+GROUP = 4
+VMEM = pl.BlockSpec(memory_space=pltpu.VMEM)
+SMEM = pl.BlockSpec(memory_space=pltpu.SMEM)
+LIMIT = 24 * 1024 * 1024
+
+
+def positive(value):
+    return jnp.maximum(value, 0.0)
+
+
+def negative(value):
+    return jnp.minimum(value, 0.0)
 
 
 def extended(cells, sides, width):
@@ -21,14 +39,6 @@
             axis=dim,
         )
     return cells
-
-
-def positive(value):
-    return jnp.maximum(value, 0.0)
-
-
-def negative(value):
-    return jnp.minimum(value, 0.0)
 
 
 def advance(padded_state, padded_x, flux_y, padded_z):
@@ -51,7 +61,7 @@
     )
 
 
-def per_device(tracers, fluxes, weight_in, weight_out):
+def by_levels(tracers, fluxes, weight_in, weight_out):
     spec_loc, depth_all, width_x, width_y = tracers.shape
     tile_at = lax.axis_index("tile")
     state = lax.all_to_all(tracers, "species", split_axis=1, concat_axis=0, tiled=True)
@@ -81,6 +91,286 @@
     return lax.all_to_all(state, "species", split_axis=0, concat_axis=1, tiled=True)
 
 
+def place_of(species, tile, count):
+    return jnp.where(lax.rem(tile, 2) == 1, count - 1 - species, species)
+
+
+def pack_kernel(count, depth, width, at_ref, tracers_ref, fluxes_ref, *out_refs):
+    tile, species = at_ref[0], at_ref[1]
+    spec = tracers_ref.shape[0] // (depth * width)
+    lev = depth // count
+    for d, out_ref in enumerate(out_refs):
+        place = place_of(species ^ d, tile, count)
+        low = 2 * place
+        b_at = low + lax.rem(place, 2)
+        a_at = low + 1 - lax.rem(place, 2)
+        for base, x in ((0, b_at), (depth + 1, a_at)):
+            for k in range(depth):
+                cells = tracers_ref[pl.ds(k * width + x, spec, stride=depth * width), :]
+                out_ref[base + k] = cells.astype(jnp.bfloat16)
+
+        def tile_of(direction, x):
+            return jnp.concatenate(
+                [
+                    fluxes_ref[pl.ds((t * 3 + direction) * lev * width + x, lev, stride=width), :]
+                    for t in range(STEPS)
+                ],
+                0,
+            )
+
+        outer = jnp.logical_and(tile == 0, place == 0)
+        tiles = [jnp.where(outer, 0.0, tile_of(0, low)), tile_of(0, low + 1)]
+        tiles += [tile_of(1, b_at), tile_of(1, a_at), tile_of(2, b_at), tile_of(2, a_at)]
+        out_ref[depth] = tiles[0].astype(jnp.bfloat16)
+        for i, part in enumerate(tiles[1:]):
+            out_ref[2 * depth + 1 + i] = part.astype(jnp.bfloat16)
+
+
+def unpack_kernel(depth, at_ref, *refs):
+    count = len(refs) - 5
+    got, (b_ref, a_ref, msg_b_ref, msg_a_ref, flux_ref) = refs[:count], refs[count:]
+    lev = depth // count
+    spec = got[0].shape[1]
+    for d in range(count):
+        source = at_ref[1] ^ d
+        rows = pl.ds(pl.multiple_of(source * spec, spec), spec)
+        for base, state_ref, msg_ref in ((0, b_ref, msg_b_ref), (depth + 1, a_ref, msg_a_ref)):
+            first = 0 if base == 0 else 1
+            for k in range(depth):
+                cells = got[d][base + k]
+                state_ref[k, rows] = cells.astype(jnp.float32)
+                msg_ref[source, k] = cells
+            msg_ref[source, depth] = got[d][depth]
+        for i in range(6):
+            part = got[d][depth if i == 0 else 2 * depth + i].astype(jnp.float32)
+            for t in range(STEPS):
+                flux_ref[t, i, source] = part[t * lev : (t + 1) * lev]
+
+
+def step_kernel(t, is_a, group, at_ref, own_ref, other_ref, halo_ref, flux_ref, edge_ref, w_in_ref, w_out_ref, *rest):
+    rest = list(rest)
+    first, last = t == 0, t == STEPS - 1
+    depth, spec_all, width_y = own_ref.shape
+    count, spec = halo_ref.shape[0], halo_ref.shape[2]
+    lev = depth // count
+    coef, cells_ref = rest[-2:]
+    if last and is_a:
+        send_ref = rest[0]
+    elif last:
+        sent_a_ref, outs, send_ref = rest[0], rest[1 : 1 + count], rest[1 + count]
+    else:
+        send_ref, new_ref = rest[:2]
+
+    def whole(index):
+        return jnp.concatenate([flux_ref[t, index, s] for s in range(count)], 0)
+
+    if first:
+        parts = [halo_ref[s, depth].astype(jnp.float32) for s in range(count)]
+        for i in range(STEPS):
+            rest[2][i] = jnp.concatenate([p[i * lev : (i + 1) * lev] for p in parts], 0)
+        beyond = rest[2][t]
+    else:
+        beyond = edge_ref[t]
+    is_first = lax.rem(at_ref[2], 2) == (1 if is_a else 0)
+    fx_first, fx_second = whole(0), whole(1)
+    fx = jnp.where(is_first, fx_first, fx_second)
+    fx_hi = jnp.where(is_first, fx_second, beyond)
+    fy = whole(3 if is_a else 2)
+    fy_hi = pltpu.roll(fy, width_y - 1, 1)
+    fz = whole(5 if is_a else 4)
+    fz = jnp.where(lax.broadcasted_iota(jnp.int32, fz.shape, 0) == 0, 0.0, fz)
+    fz_hi = jnp.concatenate([fz[1:], jnp.zeros_like(fz[:1])], 0)
+    low, high = positive(fx), -negative(fx_hi)
+    coef[0] = (
+        1.0
+        + (negative(fx) - positive(fx_hi))
+        + (negative(fy) - positive(fy_hi))
+        + (negative(fz) - positive(fz_hi))
+    )
+    coef[1] = jnp.where(is_first, low, high)
+    coef[2] = jnp.where(is_first, high, low)
+    coef[3] = positive(fy)
+    coef[4] = -negative(fy_hi)
+    coef[5] = positive(fz)
+    coef[6] = -negative(fz_hi)
+    w_in = w_in_ref[...]
+    w_out = w_out_ref[...]
+
+    def transport(k0):
+        moved = []
+        for k in range(k0, k0 + group):
+            own = own_ref[k]
+            halo = jnp.concatenate([halo_ref[s, k].astype(jnp.float32) for s in range(count)], 0)
+            out = coef[0, pl.ds(k, 1)] * own
+            out += coef[1, pl.ds(k, 1)] * halo
+            out += coef[2, pl.ds(k, 1)] * other_ref[k]
+            out += coef[3, pl.ds(k, 1)] * pltpu.roll(own, 1, 1)
+            out += coef[4, pl.ds(k, 1)] * pltpu.roll(own, width_y - 1, 1)
+            if k > 0:
+                out += coef[5, pl.ds(k, 1)] * own_ref[k - 1]
+            if k < depth - 1:
+                out += coef[6, pl.ds(k, 1)] * own_ref[k + 1]
+            cells_ref[k] = out
+            moved.append(out.astype(jnp.bfloat16))
+        cells = jnp.concatenate(moved, 1)
+        return jnp.dot(w_in, cells, preferred_element_type=jnp.float32)
+
+    def activate(half):
+        return (half + half * jnp.tanh(half)).astype(jnp.bfloat16)
+
+    def finish(k0, hidden):
+        change = jnp.dot(w_out, hidden, preferred_element_type=jnp.float32)
+        for i in range(group):
+            new = cells_ref[k0 + i] + change[:, i * width_y : (i + 1) * width_y]
+            if not last:
+                new_ref[k0 + i] = new
+            for s in range(count):
+                send_ref[s, k0 + i] = new[s * spec : (s + 1) * spec].astype(jnp.bfloat16)
+
+    half = transport(0)
+    for k0 in range(0, depth, group):
+        ahead = transport(k0 + group) if k0 + group < depth else None
+        finish(k0, activate(half))
+        half = ahead
+    if last and not is_a:
+        for d in range(count):
+            outs[d][0] = send_ref[at_ref[1] ^ d]
+            outs[d][1] = sent_a_ref[at_ref[1] ^ d]
+
+
+def finish_kernel(depth, width, at_ref, *refs):
+    out_ref = refs[-1]
+    count, spec = len(refs) - 1, refs[0].shape[2]
+    for d in range(count):
+        place = place_of(at_ref[1] ^ d, at_ref[0], count)
+        b_at = 2 * place + lax.rem(place, 2)
+        a_at = 2 * place + 1 - lax.rem(place, 2)
+        for side, x in enumerate((b_at, a_at)):
+            for k in range(depth):
+                out_ref[pl.ds(k * width + x, spec, stride=depth * width), :] = refs[d][side, k].astype(
+                    jnp.float32
+                )
+
+
+def call(kernel, out_shape, args, scratch=(), limit=LIMIT, flops=0, trans=0):
+    many = isinstance(out_shape, (list, tuple))
+    moved = sum(a.size * a.dtype.itemsize for a in args)
+    moved += sum(o.size * o.dtype.itemsize for o in (out_shape if many else [out_shape]))
+    return pl.pallas_call(
+        kernel,
+        out_shape=out_shape,
+        in_specs=[SMEM if a.dtype == jnp.int32 else VMEM for a in args],
+        out_specs=[VMEM] * len(out_shape) if many else VMEM,
+        scratch_shapes=scratch,
+        compiler_params=pltpu.CompilerParams(vmem_limit_bytes=limit),
+        cost_estimate=pl.CostEstimate(flops=flops, bytes_accessed=moved, transcendentals=trans),
+    )(*args)
+
+
+def by_columns(tracers, fluxes, weight_in, weight_out):
+    spec, depth, width, width_y = tracers.shape
+    count, tiles = lax.axis_size("species"), lax.axis_size("tile")
+    spec_all, hid = spec * count, weight_in.shape[0]
+    f32, bf16 = jnp.float32, jnp.bfloat16
+    shape = jax.ShapeDtypeStruct
+
+    chain = []
+    for t in range(tiles):
+        for place in range(count):
+            s = place if t % 2 == 0 else count - 1 - place
+            chain.append(s * tiles + t)
+    swap_a, swap_b = [], []
+    for i in range(len(chain) - 1):
+        (swap_a if i % 2 == 0 else swap_b).extend(
+            [(chain[i], chain[i + 1]), (chain[i + 1], chain[i])]
+        )
+
+    tile = lax.axis_index("tile").astype(jnp.int32)
+    species = lax.axis_index("species").astype(jnp.int32)
+    at = jnp.stack([tile, species, place_of(species, tile, count)])
+    w_in = weight_in * jnp.asarray(0.5, bf16)
+    w_out = weight_out * jnp.asarray(0.5, bf16)
+
+    def exchange(pieces):
+        got = list(pieces)
+        for d in [*range(2, count), 1]:
+            got[d] = lax.ppermute(pieces[d], "species", [(s, s ^ d) for s in range(count)])
+        return got
+
+    piece = shape((2 * depth + 6, spec, width_y), bf16)
+    packed = call(
+        functools.partial(pack_kernel, count, depth, width),
+        [piece] * count,
+        (at, tracers.reshape(-1, width_y), fluxes.reshape(-1, width_y)),
+    )
+    got = exchange(packed)
+    row = shape((depth, spec_all, width_y), f32)
+    message = shape((count, depth + 1, spec, width_y), bf16)
+    sent = shape((count, depth, spec, width_y), bf16)
+    edges = shape((STEPS, depth, width_y), f32)
+    b, a, send_b, send_a, flux = call(
+        functools.partial(unpack_kernel, depth),
+        [row, row, message, message, shape((STEPS, 6, count, depth // count, width_y), f32)],
+        (at, *got),
+    )
+    halo_b = lax.ppermute(send_b, AXES, swap_b)
+    halo_a = lax.ppermute(send_a, AXES, swap_a)
+
+    def step(t, is_a, own, other, halo, edge, more=()):
+        last = t == STEPS - 1
+        outs = [sent, row, edges][: 3 if t == 0 else 2]
+        scratch = []
+        if last:
+            outs = [sent] if is_a else [shape((2, depth, spec, width_y), bf16)] * count
+            scratch = [] if is_a else [pltpu.VMEM(sent.shape, bf16)]
+        return call(
+            functools.partial(step_kernel, t, is_a, GROUP),
+            outs,
+            (at, own, other, halo, flux, edge, w_in, w_out, *more),
+            scratch=[*scratch, pltpu.VMEM((7, depth, width_y), f32), pltpu.VMEM(row.shape, f32)],
+            flops=4 * depth * width_y * spec_all * hid,
+            trans=depth * width_y * hid,
+        )
+
+    edge_a = edge_b = flux
+    for t in range(STEPS):
+        first, last = t == 0, t == STEPS - 1
+        made_a = step(t, True, a, b, halo_a, edge_a)
+        if last:
+            pieces = step(t, False, b, a, halo_b, edge_b, made_a)
+            break
+        halo_a = lax.ppermute(made_a[0], AXES, swap_a)
+        made_b = step(t, False, b, a, halo_b, edge_b)
+        halo_b = lax.ppermute(made_b[0], AXES, swap_b)
+        if first:
+            edge_a, edge_b = made_a[2], made_b[2]
+        a, b = made_a[1], made_b[1]
+    out = call(
+        functools.partial(finish_kernel, depth, width),
+        shape((spec * depth * width, width_y), f32),
+        (at, *exchange(pieces)),
+    )
+    return out.reshape(tracers.shape)
+
+
+def per_device(tracers, fluxes, weight_in, weight_out):
+    spec, depth, width, width_y = tracers.shape
+    count = lax.axis_size("species")
+    fits = (
+        width == 2 * count
+        and count % 2 == 0
+        and count & (count - 1) == 0
+        and depth % count == 0
+        and depth % GROUP == 0
+        and spec == PACK
+        and width_y % 128 == 0
+        and width % 8 == 0
+        and STEPS * (depth // count) == PACK
+    )
+    chosen = by_columns if fits else by_levels
+    return chosen(tracers, fluxes, weight_in, weight_out)
+
+
 def solution(mesh):
     placed = (P("species", None, "tile", None), P(None, None, "species", "tile", None), P(), P())
     return jax.shard_map(

time: 154 us -> 69.7 us (0.45)
  the two profiles are of different devices: /device:TPU:0 before, /device:TPU:17 now
where the time goes in v2:
time: 69.7 us; the launch traced here: 69.4 us
  starting transfers between devices  27 us (39%)
  waiting for transfers between devices  20.8 us (30%)
  Pallas kernels  19.1 us (27%)
  local copies, waits for them, and re-layouts  2.28 us (3%)
    pallas_call x11, Pallas kernels, call(): pl.pallas_call(kernel, out_shape=out_shape, in_specs=[SMEM if a.dtype ==...  19.1 us
    ppermute x6, waiting for transfers between devices, exchange(): lax.ppermute(pieces[d], 'species', [(s, s ^ d) for s in range(count)])  13.7 us
    ppermute x6, starting transfers between devices, exchange(): lax.ppermute(pieces[d], 'species', [(s, s ^ d) for s in range(count)])  9.64 us
    ppermute x3, starting transfers between devices, by_columns(): halo_b = lax.ppermute(made_b[0], AXES, swap_b)  8.27 us
    ppermute x3, starting transfers between devices, by_columns(): halo_a = lax.ppermute(made_a[0], AXES, swap_a)  5.37 us
    ppermute x3, waiting for transfers between devices, by_columns(): halo_b = lax.ppermute(made_b[0], AXES, swap_b)  4.59 us
    ppermute x1, starting transfers between devices, by_columns(): halo_b = lax.ppermute(send_b, AXES, swap_b)  3.43 us
    ppermute x1, waiting for transfers between devices, by_columns(): halo_b = lax.ppermute(send_b, AXES, swap_b)  2.48 us
  transfers between devices with their start and end apart: 14, of which 7 were waited for; matrix products, arithmetic and copies ran while one was open for 0% of the time, Pallas kernels for 19%

profile of v2, /device:TPU:17, one launch (start us, length us, event | category | flops | bytes accessed | tf_op | source)
XLA Modules:
  0.0 69.4 jit_solution(9856516463285689130)
XLA Ops:
  5.9 3.9 %collective-permute-done.1.refs_2_ = bf16[38,16,128]{2,1,0:T(8,128)(2,1)S(1)} collective-permute-done((bf16[38,16,128]{2,1,0:T(8,128)(2,1)S(1)}, bf16[38,16,128]{2,1,0:T(8,128)(2,1)S(1)}, u32[]{:S(2)}, u32[]{:S(2)}) %collective-permute-start.1) | collective-permute-done | bytes 155680 | tf_op jit(solution)/shard_map/ppermute | solution.py:297
  9.8 3.5 %collective-permute-done.2.refs_3_ = bf16[38,16,128]{2,1,0:T(8,128)(2,1)S(1)} collective-permute-done((bf16[38,16,128]{2,1,0:T(8,128)(2,1)S(1)}, bf16[38,16,128]{2,1,0:T(8,128)(2,1)S(1)}, u32[]{:S(2)}, u32[]{:S(2)}) %collective-permute-start.2) | collective-permute-done | bytes 155680 | tf_op jit(solution)/shard_map/ppermute | solution.py:297
  14.3 3.4 %collective-permute-start.3 = (bf16[4,17,16,128]{3,2,1,0:T(8,128)(2,1)S(1)}, bf16[4,17,16,128]{3,2,1,0:T(8,128)(2,1)S(1)}, u32[]{:S(2)}, u32[]{:S(2)}) collective-permute-start(bf16[4,17,16,128]{3,2,1,0:T(8,128)(2,1)S(1)} %get-tuple-element.38), channel_id=1, source_target_pairs={{8,16},{16,8},{24,25},{25,24},{17,9},{9,17},{1,2},{2,1},{10,18},{1... | collective-permute-start | bytes 835592 | tf_op jit(solution)/shard_map/ppermute | solution.py:316
  17.9 1.9 %shard_map.49 = (bf16[4,16,16,128]{3,2,1,0:T(8,128)(2,1)S(1)}, f32[16,64,128]{2,1,0:T(8,128)S(1)}, f32[4,16,128]{2,1,0:T(8,128)S(1)}) custom-call(s32[3]{0:T(128)S(1)} %pad_add_fusion.at_ref, f32[16,64,128]{2,1,0:T(8,128)S(1)} %get-tuple-element.37.other_ref.own_ref, f32[16,64,128]{2,1,0:T(8,128)S(1)} %get-tuple-element.36.own_ref.other_ref, ...), custom_call_target="tpu_custom_call" | custom-call | flops 268435456 | bytes 2670604 | tf_op jit(solution)/shard_map/pallas_call | solution.py:259
  20.1 2.5 %collective-permute-done.3.halo_ref = bf16[4,17,16,128]{3,2,1,0:T(8,128)(2,1)S(1)} collective-permute-done((bf16[4,17,16,128]{3,2,1,0:T(8,128)(2,1)S(1)}, bf16[4,17,16,128]{3,2,1,0:T(8,128)(2,1)S(1)}, u32[]{:S(2)}, u32[]{:S(2)}) %collective-permute-start.3) | collective-permute-done | bytes 278560 | tf_op jit(solution)/shard_map/ppermute | solution.py:316
  22.6 1.9 %shard_map.48 = (bf16[4,16,16,128]{3,2,1,0:T(8,128)(2,1)S(1)}, f32[16,64,128]{2,1,0:T(8,128)S(1)}, f32[4,16,128]{2,1,0:T(8,128)S(1)}) custom-call(s32[3]{0:T(128)S(1)} %pad_add_fusion.at_ref, f32[16,64,128]{2,1,0:T(8,128)S(1)} %get-tuple-element.36.own_ref.other_ref, f32[16,64,128]{2,1,0:T(8,128)S(1)} %get-tuple-element.37.other_ref.own_ref, ...), custom_call_target="tpu_custom_call" | custom-call | flops 268435456 | bytes 2670604 | tf_op jit(solution)/shard_map/pallas_call | solution.py:259
  24.4 3.0 %collective-permute-start.5 = (bf16[4,16,16,128]{3,2,1,0:T(8,128)(2,1)S(1)}, bf16[4,16,16,128]{3,2,1,0:T(8,128)(2,1)S(1)}, u32[]{:S(2)}, u32[]{:S(2)}) collective-permute-start(bf16[4,16,16,128]{3,2,1,0:T(8,128)(2,1)S(1)} %get-tuple-element.43), channel_id=1, source_target_pairs={{8,16},{16,8},{24,25},{25,24},{17,9},{9,17},{1,2},{2,1},{10,18},{1... | collective-permute-start | bytes 786440 | tf_op jit(solution)/shard_map/ppermute | solution.py:344
  27.4 1.9 %shard_map.51 = (bf16[4,16,16,128]{3,2,1,0:T(8,128)(2,1)S(1)}, f32[16,64,128]{2,1,0:T(8,128)S(1)}) custom-call(s32[3]{0:T(128)S(1)} %pad_add_fusion.at_ref, f32[16,64,128]{2,1,0:T(8,128)S(1)} %get-tuple-element.42.other_ref.own_ref, f32[16,64,128]{2,1,0:T(8,128)S(1)} %get-tuple-element.40.own_ref.other_ref, ...), custom_call_target="tpu_custom_call" | custom-call | flops 268435456 | bytes 2457612 | tf_op jit(solution)/shard_map/pallas_call | solution.py:259
  29.3 1.8 %collective-permute-start.8 = (bf16[4,16,16,128]{3,2,1,0:T(8,128)(2,1)S(1)}, bf16[4,16,16,128]{3,2,1,0:T(8,128)(2,1)S(1)}, u32[]{:S(2)}, u32[]{:S(2)}) collective-permute-start(bf16[4,16,16,128]{3,2,1,0:T(8,128)(2,1)S(1)} %get-tuple-element.51), channel_id=1, source_target_pairs={{0,8},{8,0},{16,24},{24,16},{25,17},{17,25},{9,1},{1,9},{2,10},{10... | collective-permute-start | bytes 786440 | tf_op jit(solution)/shard_map/ppermute | solution.py:342
  31.1 1.3 %collective-permute-done.5.halo_ref = bf16[4,16,16,128]{3,2,1,0:T(8,128)(2,1)S(1)} collective-permute-done((bf16[4,16,16,128]{3,2,1,0:T(8,128)(2,1)S(1)}, bf16[4,16,16,128]{3,2,1,0:T(8,128)(2,1)S(1)}, u32[]{:S(2)}, u32[]{:S(2)}) %collective-permute-start.5) | collective-permute-done | bytes 262176 | tf_op jit(solution)/shard_map/ppermute | solution.py:344
  32.4 1.9 %shard_map.50 = (bf16[4,16,16,128]{3,2,1,0:T(8,128)(2,1)S(1)}, f32[16,64,128]{2,1,0:T(8,128)S(1)}) custom-call(s32[3]{0:T(128)S(1)} %pad_add_fusion.at_ref, f32[16,64,128]{2,1,0:T(8,128)S(1)} %get-tuple-element.40.own_ref.other_ref, f32[16,64,128]{2,1,0:T(8,128)S(1)} %get-tuple-element.42.other_ref.own_ref, ...), custom_call_target="tpu_custom_call" | custom-call | flops 268435456 | bytes 2457612 | tf_op jit(solution)/shard_map/pallas_call | solution.py:259
  34.2 2.7 %collective-permute-start.7 = (bf16[4,16,16,128]{3,2,1,0:T(8,128)(2,1)S(1)}, bf16[4,16,16,128]{3,2,1,0:T(8,128)(2,1)S(1)}, u32[]{:S(2)}, u32[]{:S(2)}) collective-permute-start(bf16[4,16,16,128]{3,2,1,0:T(8,128)(2,1)S(1)} %get-tuple-element.49), channel_id=1, source_target_pairs={{8,16},{16,8},{24,25},{25,24},{17,9},{9,17},{1,2},{2,1},{10,18},{1... | collective-permute-start | bytes 786440 | tf_op jit(solution)/shard_map/ppermute | solution.py:344
  37.0 1.9 %shard_map.53 = (bf16[4,16,16,128]{3,2,1,0:T(8,128)(2,1)S(1)}, f32[16,64,128]{2,1,0:T(8,128)S(1)}) custom-call(s32[3]{0:T(128)S(1)} %pad_add_fusion.at_ref, f32[16,64,128]{2,1,0:T(8,128)S(1)} %get-tuple-element.48.other_ref.own_ref, f32[16,64,128]{2,1,0:T(8,128)S(1)} %get-tuple-element.45.own_ref.other_ref, ...), custom_call_target="tpu_custom_call" | custom-call | flops 268435456 | bytes 2457612 | tf_op jit(solution)/shard_map/pallas_call | solution.py:259
  38.8 3.3 %collective-permute-start.10 = (bf16[4,16,16,128]{3,2,1,0:T(8,128)(2,1)S(1)}, bf16[4,16,16,128]{3,2,1,0:T(8,128)(2,1)S(1)}, u32[]{:S(2)}, u32[]{:S(2)}) collective-permute-start(bf16[4,16,16,128]{3,2,1,0:T(8,128)(2,1)S(1)} %get-tuple-element.54), channel_id=1, source_target_pairs={{0,8},{8,0},{16,24},{24,16},{25,17},{17,25},{9,1},{1,9},{2,10},{10... | collective-permute-start | bytes 786440 | tf_op jit(solution)/shard_map/ppermute | solution.py:342
  42.1 1.9 %shard_map.52 = (bf16[4,16,16,128]{3,2,1,0:T(8,128)(2,1)S(1)}, f32[16,64,128]{2,1,0:T(8,128)S(1)}) custom-call(s32[3]{0:T(128)S(1)} %pad_add_fusion.at_ref, f32[16,64,128]{2,1,0:T(8,128)S(1)} %get-tuple-element.45.own_ref.other_ref, f32[16,64,128]{2,1,0:T(8,128)S(1)} %get-tuple-element.48.other_ref.own_ref, ...), custom_call_target="tpu_custom_call" | custom-call | flops 268435456 | bytes 2457612 | tf_op jit(solution)/shard_map/pallas_call | solution.py:259
  43.9 2.6 %collective-permute-start.9 = (bf16[4,16,16,128]{3,2,1,0:T(8,128)(2,1)S(1)}, bf16[4,16,16,128]{3,2,1,0:T(8,128)(2,1)S(1)}, u32[]{:S(2)}, u32[]{:S(2)}) collective-permute-start(bf16[4,16,16,128]{3,2,1,0:T(8,128)(2,1)S(1)} %get-tuple-element.53), channel_id=1, source_target_pairs={{8,16},{16,8},{24,25},{25,24},{17,9},{9,17},{1,2},{2,1},{10,18},{1... | collective-permute-start | bytes 786440 | tf_op jit(solution)/shard_map/ppermute | solution.py:344
  46.5 1.8 %shard_map.54.rest_0_ = bf16[4,16,16,128]{3,2,1,0:T(8,128)(2,1)S(1)} custom-call(s32[3]{0:T(128)S(1)} %pad_add_fusion.at_ref, f32[16,64,128]{2,1,0:T(8,128)S(1)} %get-tuple-element.52.own_ref.other_ref, f32[16,64,128]{2,1,0:T(8,128)S(1)} %get-tuple-element.50.other_ref.own_ref, bf16[4,16,16,128]{3,2,1,0:T(8,128)(2,1)S(1)} %collective-permute-done.10.halo_ref, ...), custom_call_target="tpu_custom_call" | custom-call | flops 268435456 | bytes 1933324 | tf_op jit(solution)/shard_map/pallas_call | solution.py:259
  48.4 3.3 %collective-permute-done.9.halo_ref = bf16[4,16,16,128]{3,2,1,0:T(8,128)(2,1)S(1)} collective-permute-done((bf16[4,16,16,128]{3,2,1,0:T(8,128)(2,1)S(1)}, bf16[4,16,16,128]{3,2,1,0:T(8,128)(2,1)S(1)}, u32[]{:S(2)}, u32[]{:S(2)}) %collective-permute-start.9) | collective-permute-done | bytes 262176 | tf_op jit(solution)/shard_map/ppermute | solution.py:344
  51.6 1.9 %shard_map.55 = (bf16[2,16,16,128]{3,2,1,0:T(8,128)(2,1)S(1)}, bf16[2,16,16,128]{3,2,1,0:T(8,128)(2,1)S(1)}, bf16[2,16,16,128]{3,2,1,0:T(8,128)(2,1)S(1)}, bf16[2,16,16,128]{3,2,1,0:T(8,128)(2,1)S(1)}) custom-call(s32[3]{0:T(128)S(1)} %pad_add_fusion.at_ref, f32[16,64,128]{2,1,0:T(8,128)S(1)} %get-tuple-element.50.other_ref.own_ref, ...), custom_call_target="tpu_custom_call" | custom-call | flops 268435456 | bytes 2457612 | tf_op jit(solution)/shard_map/pallas_call | solution.py:259
  53.5 5.5 %collective-permute-start.11 = (bf16[2,16,16,128]{3,2,1,0:T(8,128)(2,1)S(1)}, bf16[2,16,16,128]{3,2,1,0:T(8,128)(2,1)S(1)}, u32[]{:S(2)}, u32[]{:S(2)}) collective-permute-start(bf16[2,16,16,128]{3,2,1,0:T(8,128)(2,1)S(1)} %get-tuple-element.56), channel_id=1, source_target_pairs={{0,8},{8,0},{16,24},{24,16},{1,9},{9,1},{17,25},{25,17},{2,10},{10... | collective-permute-start | bytes 393224 | tf_op jit(solution)/shard_map/ppermute | solution.py:297
  59.0 1.7 %collective-permute-start.13 = (bf16[2,16,16,128]{3,2,1,0:T(8,128)(2,1)S(1)}, bf16[2,16,16,128]{3,2,1,0:T(8,128)(2,1)S(1)}, u32[]{:S(2)}, u32[]{:S(2)}) collective-permute-start(bf16[2,16,16,128]{3,2,1,0:T(8,128)(2,1)S(1)} %get-tuple-element.58), channel_id=1, source_target_pairs={{0,24},{8,16},{16,8},{24,0},{1,25},{9,17},{17,9},{25,1},{2,26},{10... | collective-permute-start | bytes 393224 | tf_op jit(solution)/shard_map/ppermute | solution.py:297
  60.7 3.4 %collective-permute-done.12.refs_2_ = bf16[2,16,16,128]{3,2,1,0:T(8,128)(2,1)S(1)} collective-permute-done((bf16[2,16,16,128]{3,2,1,0:T(8,128)(2,1)S(1)}, bf16[2,16,16,128]{3,2,1,0:T(8,128)(2,1)S(1)}, u32[]{:S(2)}, u32[]{:S(2)}) %collective-permute-start.12) | collective-permute-done | bytes 131104 | tf_op jit(solution)/shard_map/ppermute | solution.py:297
  64.1 3.0 %collective-permute-done.13.refs_3_ = bf16[2,16,16,128]{3,2,1,0:T(8,128)(2,1)S(1)} collective-permute-done((bf16[2,16,16,128]{3,2,1,0:T(8,128)(2,1)S(1)}, bf16[2,16,16,128]{3,2,1,0:T(8,128)(2,1)S(1)}, u32[]{:S(2)}, u32[]{:S(2)}) %collective-permute-start.13) | collective-permute-done | bytes 131104 | tf_op jit(solution)/shard_map/ppermute | solution.py:297
  67.0 2.4 %shard_map.56 = f32[2048,128]{1,0:T(8,128)} custom-call(s32[3]{0:T(128)S(1)} %pad_add_fusion.at_ref, bf16[2,16,16,128]{3,2,1,0:T(8,128)(2,1)S(1)} %get-tuple-element.55.refs_0_, bf16[2,16,16,128]{3,2,1,0:T(8,128)(2,1)S(1)} %collective-permute-done.11.refs_1_, bf16[2,16,16,128]{3,2,1,0:T(8,128)(2,1)S(1)} %collective-permute-done.12.refs_2_, ...), custom_call_target="tpu_custom_call" | custom-call | bytes 1572876 | tf_op jit(solution)/shard_map/pallas_call | solution.py:259
  (27 shorter events, 7.4 us)
Async XLA Ops:
  0.1 1.2 %copy-start = (f32[16,16,8,128]{3,2,1,0:T(8,128)S(1)}, f32[16,16,8,128]{3,2,1,0:T(8,128)}, u32[]{:S(2)}) copy-start(f32[16,16,8,128]{3,2,1,0:T(8,128)} %param.4) | copy-start | bytes 3145732
  1.3 0.9 %copy-start.1 = (f32[4,3,4,8,128]{4,3,2,1,0:T(8,128)S(1)}, f32[4,3,4,8,128]{4,3,2,1,0:T(8,128)}, u32[]{:S(2)}) copy-start(f32[4,3,4,8,128]{4,3,2,1,0:T(8,128)} %param.5) | copy-start | bytes 589828
  3.4 2.5 %collective-permute-start = (bf16[38,16,128]{2,1,0:T(8,128)(2,1)S(1)}, bf16[38,16,128]{2,1,0:T(8,128)(2,1)S(1)}, u32[]{:S(2)}, u32[]{:S(2)}) collective-permute-start(bf16[38,16,128]{2,1,0:T(8,128)(2,1)S(1)} %get-tuple-element.33), channel_id=1, source_target_pairs={{0,8},{8,0},{16,24},{24,16},{1,9},{9,1},{17,25},{25,17},{2,10},{10... | collective-permute-start | bytes 466952 | tf_op jit(solution)/shard_map/ppermute | solution.py:297
  4.2 5.6 %collective-permute-start.1 = (bf16[38,16,128]{2,1,0:T(8,128)(2,1)S(1)}, bf16[38,16,128]{2,1,0:T(8,128)(2,1)S(1)}, u32[]{:S(2)}, u32[]{:S(2)}) collective-permute-start(bf16[38,16,128]{2,1,0:T(8,128)(2,1)S(1)} %get-tuple-element.34), channel_id=1, source_target_pairs={{0,16},{8,24},{16,0},{24,8},{1,17},{9,25},{17,1},{25,9},{2,18},{10... | collective-permute-start | bytes 466952 | tf_op jit(solution)/shard_map/ppermute | solution.py:297
  5.4 7.8 %collective-permute-start.2 = (bf16[38,16,128]{2,1,0:T(8,128)(2,1)S(1)}, bf16[38,16,128]{2,1,0:T(8,128)(2,1)S(1)}, u32[]{:S(2)}, u32[]{:S(2)}) collective-permute-start(bf16[38,16,128]{2,1,0:T(8,128)(2,1)S(1)} %get-tuple-element.35), channel_id=1, source_target_pairs={{0,24},{8,16},{16,8},{24,0},{1,25},{9,17},{17,9},{25,1},{2,26},{10... | collective-permute-start | bytes 466952 | tf_op jit(solution)/shard_map/ppermute | solution.py:297
  13.3 4.5 %copy-start.3 = (bf16[64,512]{1,0:T(8,128)(2,1)S(1)}, bf16[64,512]{1,0:T(8,128)(2,1)}, u32[]{:S(2)}) copy-start(bf16[64,512]{1,0:T(8,128)(2,1)} %param.7) | copy-start | bytes 196612
  14.0 3.9 %collective-permute-start.4 = (bf16[4,17,16,128]{3,2,1,0:T(8,128)(2,1)S(1)}, bf16[4,17,16,128]{3,2,1,0:T(8,128)(2,1)S(1)}, u32[]{:S(2)}, u32[]{:S(2)}) collective-permute-start(bf16[4,17,16,128]{3,2,1,0:T(8,128)(2,1)S(1)} %get-tuple-element.41), channel_id=1, source_target_pairs={{0,8},{8,0},{16,24},{24,16},{25,17},{17,25},{9,1},{1,9},{2,10},{10... | collective-permute-start | bytes 835592 | tf_op jit(solution)/shard_map/ppermute | solution.py:317
  14.3 3.5 %copy-start.2 = (bf16[512,64]{0,1:T(8,128)(2,1)S(1)}, bf16[512,64]{0,1:T(8,128)(2,1)}, u32[]{:S(2)}) copy-start(bf16[512,64]{0,1:T(8,128)(2,1)} %param.6) | copy-start | bytes 196612
  14.3 8.3 %collective-permute-start.3 = (bf16[4,17,16,128]{3,2,1,0:T(8,128)(2,1)S(1)}, bf16[4,17,16,128]{3,2,1,0:T(8,128)(2,1)S(1)}, u32[]{:S(2)}, u32[]{:S(2)}) collective-permute-start(bf16[4,17,16,128]{3,2,1,0:T(8,128)(2,1)S(1)} %get-tuple-element.38), channel_id=1, source_target_pairs={{8,16},{16,8},{24,25},{25,24},{17,9},{9,17},{1,2},{2,1},{10,18},{1... | collective-permute-start | bytes 835592 | tf_op jit(solution)/shard_map/ppermute | solution.py:316
  19.8 7.7 %collective-permute-start.6 = (bf16[4,16,16,128]{3,2,1,0:T(8,128)(2,1)S(1)}, bf16[4,16,16,128]{3,2,1,0:T(8,128)(2,1)S(1)}, u32[]{:S(2)}, u32[]{:S(2)}) collective-permute-start(bf16[4,16,16,128]{3,2,1,0:T(8,128)(2,1)S(1)} %get-tuple-element.46), channel_id=1, source_target_pairs={{0,8},{8,0},{16,24},{24,16},{25,17},{17,25},{9,1},{1,9},{2,10},{10... | collective-permute-start | bytes 786440 | tf_op jit(solution)/shard_map/ppermute | solution.py:342
  24.4 8.0 %collective-permute-start.5 = (bf16[4,16,16,128]{3,2,1,0:T(8,128)(2,1)S(1)}, bf16[4,16,16,128]{3,2,1,0:T(8,128)(2,1)S(1)}, u32[]{:S(2)}, u32[]{:S(2)}) collective-permute-start(bf16[4,16,16,128]{3,2,1,0:T(8,128)(2,1)S(1)} %get-tuple-element.43), channel_id=1, source_target_pairs={{8,16},{16,8},{24,25},{25,24},{17,9},{9,17},{1,2},{2,1},{10,18},{1... | collective-permute-start | bytes 786440 | tf_op jit(solution)/shard_map/ppermute | solution.py:344
  29.3 7.7 %collective-permute-start.8 = (bf16[4,16,16,128]{3,2,1,0:T(8,128)(2,1)S(1)}, bf16[4,16,16,128]{3,2,1,0:T(8,128)(2,1)S(1)}, u32[]{:S(2)}, u32[]{:S(2)}) collective-permute-start(bf16[4,16,16,128]{3,2,1,0:T(8,128)(2,1)S(1)} %get-tuple-element.51), channel_id=1, source_target_pairs={{0,8},{8,0},{16,24},{24,16},{25,17},{17,25},{9,1},{1,9},{2,10},{10... | collective-permute-start | bytes 786440 | tf_op jit(solution)/shard_map/ppermute | solution.py:342
  34.2 7.9 %collective-permute-start.7 = (bf16[4,16,16,128]{3,2,1,0:T(8,128)(2,1)S(1)}, bf16[4,16,16,128]{3,2,1,0:T(8,128)(2,1)S(1)}, u32[]{:S(2)}, u32[]{:S(2)}) collective-permute-start(bf16[4,16,16,128]{3,2,1,0:T(8,128)(2,1)S(1)} %get-tuple-element.49), channel_id=1, source_target_pairs={{8,16},{16,8},{24,25},{25,24},{17,9},{9,17},{1,2},{2,1},{10,18},{1... | collective-permute-start | bytes 786440 | tf_op jit(solution)/shard_map/ppermute | solution.py:344
  38.8 7.7 %collective-permute-start.10 = (bf16[4,16,16,128]{3,2,1,0:T(8,128)(2,1)S(1)}, bf16[4,16,16,128]{3,2,1,0:T(8,128)(2,1)S(1)}, u32[]{:S(2)}, u32[]{:S(2)}) collective-permute-start(bf16[4,16,16,128]{3,2,1,0:T(8,128)(2,1)S(1)} %get-tuple-element.54), channel_id=1, source_target_pairs={{0,8},{8,0},{16,24},{24,16},{25,17},{17,25},{9,1},{1,9},{2,10},{10... | collective-permute-start | bytes 786440 | tf_op jit(solution)/shard_map/ppermute | solution.py:342
  43.9 7.7 %collective-permute-start.9 = (bf16[4,16,16,128]{3,2,1,0:T(8,128)(2,1)S(1)}, bf16[4,16,16,128]{3,2,1,0:T(8,128)(2,1)S(1)}, u32[]{:S(2)}, u32[]{:S(2)}) collective-permute-start(bf16[4,16,16,128]{3,2,1,0:T(8,128)(2,1)S(1)} %get-tuple-element.53), channel_id=1, source_target_pairs={{8,16},{16,8},{24,25},{25,24},{17,9},{9,17},{1,2},{2,1},{10,18},{1... | collective-permute-start | bytes 786440 | tf_op jit(solution)/shard_map/ppermute | solution.py:344
  53.5 7.2 %collective-permute-start.11 = (bf16[2,16,16,128]{3,2,1,0:T(8,128)(2,1)S(1)}, bf16[2,16,16,128]{3,2,1,0:T(8,128)(2,1)S(1)}, u32[]{:S(2)}, u32[]{:S(2)}) collective-permute-start(bf16[2,16,16,128]{3,2,1,0:T(8,128)(2,1)S(1)} %get-tuple-element.56), channel_id=1, source_target_pairs={{0,8},{8,0},{16,24},{24,16},{1,9},{9,1},{17,25},{25,17},{2,10},{10... | collective-permute-start | bytes 393224 | tf_op jit(solution)/shard_map/ppermute | solution.py:297
  59.0 5.1 %collective-permute-start.12 = (bf16[2,16,16,128]{3,2,1,0:T(8,128)(2,1)S(1)}, bf16[2,16,16,128]{3,2,1,0:T(8,128)(2,1)S(1)}, u32[]{:S(2)}, u32[]{:S(2)}) collective-permute-start(bf16[2,16,16,128]{3,2,1,0:T(8,128)(2,1)S(1)} %get-tuple-element.57), channel_id=1, source_target_pairs={{0,16},{8,24},{16,0},{24,8},{1,17},{9,25},{17,1},{25,9},{2,18},{10... | collective-permute-start | bytes 393224 | tf_op jit(solution)/shard_map/ppermute | solution.py:297
  59.0 8.0 %collective-permute-start.13 = (bf16[2,16,16,128]{3,2,1,0:T(8,128)(2,1)S(1)}, bf16[2,16,16,128]{3,2,1,0:T(8,128)(2,1)S(1)}, u32[]{:S(2)}, u32[]{:S(2)}) collective-permute-start(bf16[2,16,16,128]{3,2,1,0:T(8,128)(2,1)S(1)} %get-tuple-element.58), channel_id=1, source_target_pairs={{0,24},{8,16},{16,8},{24,0},{1,25},{9,17},{17,9},{25,1},{2,26},{10... | collective-permute-start | bytes 393224 | tf_op jit(solution)/shard_map/ppermute | solution.py:297

commit v3 on v2

--- a/solution.py
+++ b/solution.py
@@ -11,9 +11,11 @@
 AXES = ("species", "tile")
 PACK = 16
 GROUP = 4
+PARTS = 4
 VMEM = pl.BlockSpec(memory_space=pltpu.VMEM)
 SMEM = pl.BlockSpec(memory_space=pltpu.SMEM)
 LIMIT = 24 * 1024 * 1024
+FULL = 56 * 1024 * 1024
 
 
 def positive(value):
@@ -95,35 +97,68 @@
     return jnp.where(lax.rem(tile, 2) == 1, count - 1 - species, species)
 
 
-def pack_kernel(count, depth, width, at_ref, tracers_ref, fluxes_ref, *out_refs):
-    tile, species = at_ref[0], at_ref[1]
-    spec = tracers_ref.shape[0] // (depth * width)
-    lev = depth // count
-    for d, out_ref in enumerate(out_refs):
-        place = place_of(species ^ d, tile, count)
-        low = 2 * place
-        b_at = low + lax.rem(place, 2)
-        a_at = low + 1 - lax.rem(place, 2)
-        for base, x in ((0, b_at), (depth + 1, a_at)):
-            for k in range(depth):
-                cells = tracers_ref[pl.ds(k * width + x, spec, stride=depth * width), :]
-                out_ref[base + k] = cells.astype(jnp.bfloat16)
-
-        def tile_of(direction, x):
-            return jnp.concatenate(
-                [
-                    fluxes_ref[pl.ds((t * 3 + direction) * lev * width + x, lev, stride=width), :]
-                    for t in range(STEPS)
-                ],
-                0,
-            )
-
-        outer = jnp.logical_and(tile == 0, place == 0)
-        tiles = [jnp.where(outer, 0.0, tile_of(0, low)), tile_of(0, low + 1)]
-        tiles += [tile_of(1, b_at), tile_of(1, a_at), tile_of(2, b_at), tile_of(2, a_at)]
-        out_ref[depth] = tiles[0].astype(jnp.bfloat16)
-        for i, part in enumerate(tiles[1:]):
-            out_ref[2 * depth + 1 + i] = part.astype(jnp.bfloat16)
+def columns_of(place):
+    return (2 * place, 2 * place + 1) if place % 2 == 0 else (2 * place + 1, 2 * place)
+
+
+def for_each_place(at_ref, count, act):
+    for own in range(count):
+        pl.when(at_ref[2] == own)(functools.partial(act, own))
+
+
+def pack_kernel(count, at_ref, tracers_ref, fluxes_ref, *refs):
+    out_refs, (held, flux_ref, sems) = refs[:count], refs[count:]
+    parts, spec, rows, width_y = held.shape
+    width = 2 * count
+    lev = rows // width
+    depth = parts * lev
+    lev_own = fluxes_ref.shape[0] // (STEPS * 3 * width)
+    copies = [pltpu.make_async_copy(fluxes_ref, flux_ref, sems.at[parts])]
+    for part in range(parts):
+        source = tracers_ref.at[:, pl.ds(part * rows, rows), :]
+        copies.append(pltpu.make_async_copy(source, held.at[part], sems.at[part]))
+    for copy in copies:
+        copy.start()
+    outer = at_ref[0] == 0
+
+    def fluxes(own):
+        for d in range(count):
+            place = own ^ d
+            b_at, a_at = columns_of(place)
+
+            def tile_of(direction, x):
+                return jnp.concatenate(
+                    [
+                        flux_ref[
+                            pl.ds((t * 3 + direction) * lev_own * width + x, lev_own, stride=width), :
+                        ]
+                        for t in range(STEPS)
+                    ],
+                    0,
+                )
+
+            first = tile_of(0, 2 * place)
+            if place == 0:
+                first = jnp.where(outer, 0.0, first)
+            out_refs[d][depth] = first.astype(jnp.bfloat16)
+            others = ((0, 2 * place + 1), (1, b_at), (1, a_at), (2, b_at), (2, a_at))
+            for i, (direction, x) in enumerate(others):
+                out_refs[d][2 * depth + 1 + i] = tile_of(direction, x).astype(jnp.bfloat16)
+
+    def tracers(part, own):
+        flat = held.at[part].reshape(spec * rows, width_y)
+        for d in range(count):
+            b_at, a_at = columns_of(own ^ d)
+            for base, x in ((0, b_at), (depth + 1, a_at)):
+                for k in range(lev):
+                    cells = flat[pl.ds(k * width + x, spec, stride=rows), :]
+                    out_refs[d][base + part * lev + k] = cells.astype(jnp.bfloat16)
+
+    copies[0].wait()
+    for_each_place(at_ref, count, fluxes)
+    for part in range(parts):
+        copies[1 + part].wait()
+        for_each_place(at_ref, count, functools.partial(tracers, part))
 
 
 def unpack_kernel(depth, at_ref, *refs):
@@ -147,7 +182,7 @@
                 flux_ref[t, i, source] = part[t * lev : (t + 1) * lev]
 
 
-def step_kernel(t, is_a, group, at_ref, own_ref, other_ref, halo_ref, flux_ref, edge_ref, w_in_ref, w_out_ref, *rest):
+def step_kernel(t, is_a, group, tiles, at_ref, own_ref, other_ref, halo_ref, flux_ref, edge_ref, w_in_ref, w_out_ref, *rest):
     rest = list(rest)
     first, last = t == 0, t == STEPS - 1
     depth, spec_all, width_y = own_ref.shape
@@ -168,6 +203,10 @@
         parts = [halo_ref[s, depth].astype(jnp.float32) for s in range(count)]
         for i in range(STEPS):
             rest[2][i] = jnp.concatenate([p[i * lev : (i + 1) * lev] for p in parts], 0)
+        if not is_a:
+            is_end = jnp.logical_and(at_ref[0] == tiles - 1, at_ref[2] == count - 1)
+            for i in range(STEPS):
+                rest[2][i] = jnp.where(is_end, 0.0, rest[2][i])
         beyond = rest[2][t]
     else:
         beyond = edge_ref[t]
@@ -216,7 +255,8 @@
         return jnp.dot(w_in, cells, preferred_element_type=jnp.float32)
 
     def activate(half):
-        return (half + half * jnp.tanh(half)).astype(jnp.bfloat16)
+        half = half.astype(jnp.bfloat16)
+        return half + half * jnp.tanh(half)
 
     def finish(k0, hidden):
         change = jnp.dot(w_out, hidden, preferred_element_type=jnp.float32)
@@ -238,29 +278,44 @@
             outs[d][1] = sent_a_ref[at_ref[1] ^ d]
 
 
-def finish_kernel(depth, width, at_ref, *refs):
-    out_ref = refs[-1]
-    count, spec = len(refs) - 1, refs[0].shape[2]
-    for d in range(count):
-        place = place_of(at_ref[1] ^ d, at_ref[0], count)
-        b_at = 2 * place + lax.rem(place, 2)
-        a_at = 2 * place + 1 - lax.rem(place, 2)
-        for side, x in enumerate((b_at, a_at)):
-            for k in range(depth):
-                out_ref[pl.ds(k * width + x, spec, stride=depth * width), :] = refs[d][side, k].astype(
-                    jnp.float32
-                )
-
-
-def call(kernel, out_shape, args, scratch=(), limit=LIMIT, flops=0, trans=0):
+def finish_kernel(at_ref, *refs):
+    out_ref, held, sems = refs[-3:]
+    count, depth, spec = len(refs) - 3, refs[0].shape[1], refs[0].shape[2]
+    parts, _, rows, width_y = held.shape
+    width = 2 * count
+    lev = rows // width
+
+    def store(part, own):
+        flat = held.at[part].reshape(spec * rows, width_y)
+        for d in range(count):
+            for side, x in enumerate(columns_of(own ^ d)):
+                for k in range(lev):
+                    cells = refs[d][side, part * lev + k].astype(jnp.float32)
+                    flat[pl.ds(k * width + x, spec, stride=rows), :] = cells
+
+    copies = []
+    for part in range(parts):
+        for_each_place(at_ref, count, functools.partial(store, part))
+        target = out_ref.at[:, pl.ds(part * rows, rows), :]
+        copies.append(pltpu.make_async_copy(held.at[part], target, sems.at[part]))
+        copies[-1].start()
+    for copy in copies:
+        copy.wait()
+
+
+def call(kernel, out_shape, args, scratch=(), limit=LIMIT, far=(), far_out=False, flops=0, trans=0):
     many = isinstance(out_shape, (list, tuple))
     moved = sum(a.size * a.dtype.itemsize for a in args)
     moved += sum(o.size * o.dtype.itemsize for o in (out_shape if many else [out_shape]))
+    anywhere = pl.BlockSpec(memory_space=pl.ANY)
     return pl.pallas_call(
         kernel,
         out_shape=out_shape,
-        in_specs=[SMEM if a.dtype == jnp.int32 else VMEM for a in args],
-        out_specs=[VMEM] * len(out_shape) if many else VMEM,
+        in_specs=[
+            anywhere if i in far else SMEM if a.dtype == jnp.int32 else VMEM
+            for i, a in enumerate(args)
+        ],
+        out_specs=[VMEM] * len(out_shape) if many else anywhere if far_out else VMEM,
         scratch_shapes=scratch,
         compiler_params=pltpu.CompilerParams(vmem_limit_bytes=limit),
         cost_estimate=pl.CostEstimate(flops=flops, bytes_accessed=moved, transcendentals=trans),
@@ -279,7 +334,7 @@
         for place in range(count):
             s = place if t % 2 == 0 else count - 1 - place
             chain.append(s * tiles + t)
-    swap_a, swap_b = [], []
+    swap_a, swap_b = [], [(chain[0], chain[0]), (chain[-1], chain[-1])]
     for i in range(len(chain) - 1):
         (swap_a if i % 2 == 0 else swap_b).extend(
             [(chain[i], chain[i + 1]), (chain[i + 1], chain[i])]
@@ -298,10 +353,19 @@
         return got
 
     piece = shape((2 * depth + 6, spec, width_y), bf16)
+    held = pltpu.VMEM((PARTS, spec, depth * width // PARTS, width_y), f32)
+    flux_rows = fluxes.reshape(-1, width_y)
     packed = call(
-        functools.partial(pack_kernel, count, depth, width),
+        functools.partial(pack_kernel, count),
         [piece] * count,
-        (at, tracers.reshape(-1, width_y), fluxes.reshape(-1, width_y)),
+        (at, tracers.reshape(spec, depth * width, width_y), flux_rows),
+        scratch=[
+            held,
+            pltpu.VMEM(flux_rows.shape, f32),
+            pltpu.SemaphoreType.DMA((PARTS + 1,)),
+        ],
+        limit=FULL,
+        far=(1, 2),
     )
     got = exchange(packed)
     row = shape((depth, spec_all, width_y), f32)
@@ -324,7 +388,7 @@
             outs = [sent] if is_a else [shape((2, depth, spec, width_y), bf16)] * count
             scratch = [] if is_a else [pltpu.VMEM(sent.shape, bf16)]
         return call(
-            functools.partial(step_kernel, t, is_a, GROUP),
+            functools.partial(step_kernel, t, is_a, GROUP, tiles),
             outs,
             (at, own, other, halo, flux, edge, w_in, w_out, *more),
             scratch=[*scratch, pltpu.VMEM((7, depth, width_y), f32), pltpu.VMEM(row.shape, f32)],
@@ -346,9 +410,11 @@
             edge_a, edge_b = made_a[2], made_b[2]
         a, b = made_a[1], made_b[1]
     out = call(
-        functools.partial(finish_kernel, depth, width),
-        shape((spec * depth * width, width_y), f32),
+        finish_kernel,
+        shape((spec, depth * width, width_y), f32),
         (at, *exchange(pieces)),
+        scratch=[held, pltpu.SemaphoreType.DMA((PARTS,))],
+        far_out=True,
     )
     return out.reshape(tracers.shape)
 
@@ -362,6 +428,7 @@
         and count & (count - 1) == 0
         and depth % count == 0
         and depth % GROUP == 0
+        and depth % PARTS == 0
         and spec == PACK
         and width_y % 128 == 0
         and width % 8 == 0

time: 69.7 us -> 71.7 us (1.029)
  Pallas kernels: 19.1 us -> 21.7 us
  local copies, waits for them, and re-layouts: 2.28 us -> 1.04 us
    pallas_call x11, Pallas kernels: 19.1 us -> 21.7 us  [call(): pl.pallas_call(kernel, out_shape=out_shape, in_specs=[anywhere if i in fa...]
    unnamed x9, local copies, waits for them, and re-layouts: 2.28 us -> 1.04 us
where the time goes in v3:
time: 71.7 us; the launch traced here: 71.4 us
  starting transfers between devices  27 us (38%)
  Pallas kernels  21.7 us (30%)
  waiting for transfers between devices  20.7 us (29%)
  local copies, waits for them, and re-layouts  1.04 us (1%)
    pallas_call x11, Pallas kernels, call(): pl.pallas_call(kernel, out_shape=out_shape, in_specs=[anywhere if i in fa...  21.7 us
    ppermute x6, waiting for transfers between devices, exchange(): lax.ppermute(pieces[d], 'species', [(s, s ^ d) for s in range(count)])  13.9 us
    ppermute x6, starting transfers between devices, exchange(): lax.ppermute(pieces[d], 'species', [(s, s ^ d) for s in range(count)])  9.6 us
    ppermute x3, starting transfers between devices, by_columns(): halo_b = lax.ppermute(made_b[0], AXES, swap_b)  8.34 us
    ppermute x3, starting transfers between devices, by_columns(): halo_a = lax.ppermute(made_a[0], AXES, swap_a)  5.34 us
    ppermute x3, waiting for transfers between devices, by_columns(): halo_b = lax.ppermute(made_b[0], AXES, swap_b)  4.34 us
    ppermute x1, starting transfers between devices, by_columns(): halo_b = lax.ppermute(send_b, AXES, swap_b)  3.41 us
    ppermute x1, waiting for transfers between devices, by_columns(): halo_b = lax.ppermute(send_b, AXES, swap_b)  2.41 us
  transfers between devices with their start and end apart: 14, of which 7 were waited for; matrix products, arithmetic and copies ran while one was open for 0% of the time, Pallas kernels for 19%

profile of v3, /device:TPU:17, one launch (start us, length us, event | category | flops | bytes accessed | tf_op | source)
XLA Modules:
  0.0 71.4 jit_solution(4678236184387296783)
XLA Ops:
  0.7 3.3 %shard_map.46 = (bf16[38,16,128]{2,1,0:T(8,128)(2,1)}, bf16[38,16,128]{2,1,0:T(8,128)(2,1)}, bf16[38,16,128]{2,1,0:T(8,128)(2,1)}, bf16[38,16,128]{2,1,0:T(8,128)(2,1)}) custom-call(s32[3]{0:T(128)} %pad_add_fusion.at_ref, f32[16,128,128]{2,1,0:T(8,128)} %bitcast.6, f32[384,128]{1,0:T(8,128)} %bitcast.7), custom_call_target="tpu_custom_call" | custom-call | bytes 1867788 | tf_op jit(solution)/shard_map/pallas_call | solution.py:311
  6.4 4.1 %collective-permute-done.1.refs_2_ = bf16[38,16,128]{2,1,0:T(8,128)(2,1)S(1)} collective-permute-done((bf16[38,16,128]{2,1,0:T(8,128)(2,1)}, bf16[38,16,128]{2,1,0:T(8,128)(2,1)S(1)}, u32[]{:S(2)}, u32[]{:S(2)}) %collective-permute-start.1) | collective-permute-done | bytes 155680 | tf_op jit(solution)/shard_map/ppermute | solution.py:352
  10.5 3.5 %collective-permute-done.2.refs_3_ = bf16[38,16,128]{2,1,0:T(8,128)(2,1)S(1)} collective-permute-done((bf16[38,16,128]{2,1,0:T(8,128)(2,1)}, bf16[38,16,128]{2,1,0:T(8,128)(2,1)S(1)}, u32[]{:S(2)}, u32[]{:S(2)}) %collective-permute-start.2) | collective-permute-done | bytes 155680 | tf_op jit(solution)/shard_map/ppermute | solution.py:352
  15.9 3.4 %collective-permute-start.3 = (bf16[4,17,16,128]{3,2,1,0:T(8,128)(2,1)S(1)}, bf16[4,17,16,128]{3,2,1,0:T(8,128)(2,1)S(1)}, u32[]{:S(2)}, u32[]{:S(2)}) collective-permute-start(bf16[4,17,16,128]{3,2,1,0:T(8,128)(2,1)S(1)} %get-tuple-element.38), channel_id=1, source_target_pairs={{0,0},{7,7},{8,16},{16,8},{24,25},{25,24},{17,9},{9,17},{1,2},{2,1... | collective-permute-start | bytes 835592 | tf_op jit(solution)/shard_map/ppermute | solution.py:380
  19.5 1.9 %shard_map.49 = (bf16[4,16,16,128]{3,2,1,0:T(8,128)(2,1)S(1)}, f32[16,64,128]{2,1,0:T(8,128)S(1)}, f32[4,16,128]{2,1,0:T(8,128)S(1)}) custom-call(s32[3]{0:T(128)S(1)} %copy-done.1, f32[16,64,128]{2,1,0:T(8,128)S(1)} %get-tuple-element.37.other_ref.own_ref, f32[16,64,128]{2,1,0:T(8,128)S(1)} %get-tuple-element.36.own_ref.other_ref, ...), custom_call_target="tpu_custom_call" | custom-call | flops 268435456 | bytes 2670604 | tf_op jit(solution)/shard_map/pallas_call | solution.py:311
  21.8 2.4 %collective-permute-done.3.halo_ref = bf16[4,17,16,128]{3,2,1,0:T(8,128)(2,1)S(1)} collective-permute-done((bf16[4,17,16,128]{3,2,1,0:T(8,128)(2,1)S(1)}, bf16[4,17,16,128]{3,2,1,0:T(8,128)(2,1)S(1)}, u32[]{:S(2)}, u32[]{:S(2)}) %collective-permute-start.3) | collective-permute-done | bytes 278560 | tf_op jit(solution)/shard_map/ppermute | solution.py:380
  24.2 1.9 %shard_map.48 = (bf16[4,16,16,128]{3,2,1,0:T(8,128)(2,1)S(1)}, f32[16,64,128]{2,1,0:T(8,128)S(1)}, f32[4,16,128]{2,1,0:T(8,128)S(1)}) custom-call(s32[3]{0:T(128)S(1)} %copy-done.1, f32[16,64,128]{2,1,0:T(8,128)S(1)} %get-tuple-element.36.own_ref.other_ref, f32[16,64,128]{2,1,0:T(8,128)S(1)} %get-tuple-element.37.other_ref.own_ref, ...), custom_call_target="tpu_custom_call" | custom-call | flops 268435456 | bytes 2670604 | tf_op jit(solution)/shard_map/pallas_call | solution.py:311
  26.1 3.0 %collective-permute-start.5 = (bf16[4,16,16,128]{3,2,1,0:T(8,128)(2,1)S(1)}, bf16[4,16,16,128]{3,2,1,0:T(8,128)(2,1)S(1)}, u32[]{:S(2)}, u32[]{:S(2)}) collective-permute-start(bf16[4,16,16,128]{3,2,1,0:T(8,128)(2,1)S(1)} %get-tuple-element.43), channel_id=1, source_target_pairs={{0,0},{7,7},{8,16},{16,8},{24,25},{25,24},{17,9},{9,17},{1,2},{2,1... | collective-permute-start | bytes 786440 | tf_op jit(solution)/shard_map/ppermute | solution.py:408
  29.2 1.9 %shard_map.51 = (bf16[4,16,16,128]{3,2,1,0:T(8,128)(2,1)S(1)}, f32[16,64,128]{2,1,0:T(8,128)S(1)}) custom-call(s32[3]{0:T(128)S(1)} %copy-done.1, f32[16,64,128]{2,1,0:T(8,128)S(1)} %get-tuple-element.42.other_ref.own_ref, f32[16,64,128]{2,1,0:T(8,128)S(1)} %get-tuple-element.40.own_ref.other_ref, ...), custom_call_target="tpu_custom_call" | custom-call | flops 268435456 | bytes 2457612 | tf_op jit(solution)/shard_map/pallas_call | solution.py:311
  31.1 1.8 %collective-permute-start.8 = (bf16[4,16,16,128]{3,2,1,0:T(8,128)(2,1)S(1)}, bf16[4,16,16,128]{3,2,1,0:T(8,128)(2,1)S(1)}, u32[]{:S(2)}, u32[]{:S(2)}) collective-permute-start(bf16[4,16,16,128]{3,2,1,0:T(8,128)(2,1)S(1)} %get-tuple-element.51), channel_id=1, source_target_pairs={{0,8},{8,0},{16,24},{24,16},{25,17},{17,25},{9,1},{1,9},{2,10},{10... | collective-permute-start | bytes 786440 | tf_op jit(solution)/shard_map/ppermute | solution.py:406
  34.1 1.9 %shard_map.50 = (bf16[4,16,16,128]{3,2,1,0:T(8,128)(2,1)S(1)}, f32[16,64,128]{2,1,0:T(8,128)S(1)}) custom-call(s32[3]{0:T(128)S(1)} %copy-done.1, f32[16,64,128]{2,1,0:T(8,128)S(1)} %get-tuple-element.40.own_ref.other_ref, f32[16,64,128]{2,1,0:T(8,128)S(1)} %get-tuple-element.42.other_ref.own_ref, ...), custom_call_target="tpu_custom_call" | custom-call | flops 268435456 | bytes 2457612 | tf_op jit(solution)/shard_map/pallas_call | solution.py:311
  36.1 2.7 %collective-permute-start.7 = (bf16[4,16,16,128]{3,2,1,0:T(8,128)(2,1)S(1)}, bf16[4,16,16,128]{3,2,1,0:T(8,128)(2,1)S(1)}, u32[]{:S(2)}, u32[]{:S(2)}) collective-permute-start(bf16[4,16,16,128]{3,2,1,0:T(8,128)(2,1)S(1)} %get-tuple-element.49), channel_id=1, source_target_pairs={{0,0},{7,7},{8,16},{16,8},{24,25},{25,24},{17,9},{9,17},{1,2},{2,1... | collective-permute-start | bytes 786440 | tf_op jit(solution)/shard_map/ppermute | solution.py:408
  38.8 1.9 %shard_map.53 = (bf16[4,16,16,128]{3,2,1,0:T(8,128)(2,1)S(1)}, f32[16,64,128]{2,1,0:T(8,128)S(1)}) custom-call(s32[3]{0:T(128)S(1)} %copy-done.1, f32[16,64,128]{2,1,0:T(8,128)S(1)} %get-tuple-element.48.other_ref.own_ref, f32[16,64,128]{2,1,0:T(8,128)S(1)} %get-tuple-element.45.own_ref.other_ref, ...), custom_call_target="tpu_custom_call" | custom-call | flops 268435456 | bytes 2457612 | tf_op jit(solution)/shard_map/pallas_call | solution.py:311
  40.7 3.3 %collective-permute-start.10 = (bf16[4,16,16,128]{3,2,1,0:T(8,128)(2,1)S(1)}, bf16[4,16,16,128]{3,2,1,0:T(8,128)(2,1)S(1)}, u32[]{:S(2)}, u32[]{:S(2)}) collective-permute-start(bf16[4,16,16,128]{3,2,1,0:T(8,128)(2,1)S(1)} %get-tuple-element.54), channel_id=1, source_target_pairs={{0,8},{8,0},{16,24},{24,16},{25,17},{17,25},{9,1},{1,9},{2,10},{10... | collective-permute-start | bytes 786440 | tf_op jit(solution)/shard_map/ppermute | solution.py:406
  44.0 1.9 %shard_map.52 = (bf16[4,16,16,128]{3,2,1,0:T(8,128)(2,1)S(1)}, f32[16,64,128]{2,1,0:T(8,128)S(1)}) custom-call(s32[3]{0:T(128)S(1)} %copy-done.1, f32[16,64,128]{2,1,0:T(8,128)S(1)} %get-tuple-element.45.own_ref.other_ref, f32[16,64,128]{2,1,0:T(8,128)S(1)} %get-tuple-element.48.other_ref.own_ref, ...), custom_call_target="tpu_custom_call" | custom-call | flops 268435456 | bytes 2457612 | tf_op jit(solution)/shard_map/pallas_call | solution.py:311
  45.9 2.7 %collective-permute-start.9 = (bf16[4,16,16,128]{3,2,1,0:T(8,128)(2,1)S(1)}, bf16[4,16,16,128]{3,2,1,0:T(8,128)(2,1)S(1)}, u32[]{:S(2)}, u32[]{:S(2)}) collective-permute-start(bf16[4,16,16,128]{3,2,1,0:T(8,128)(2,1)S(1)} %get-tuple-element.53), channel_id=1, source_target_pairs={{0,0},{7,7},{8,16},{16,8},{24,25},{25,24},{17,9},{9,17},{1,2},{2,1... | collective-permute-start | bytes 786440 | tf_op jit(solution)/shard_map/ppermute | solution.py:408
  48.6 1.9 %shard_map.54.rest_0_ = bf16[4,16,16,128]{3,2,1,0:T(8,128)(2,1)S(1)} custom-call(s32[3]{0:T(128)S(1)} %copy-done.1, f32[16,64,128]{2,1,0:T(8,128)S(1)} %get-tuple-element.52.own_ref.other_ref, f32[16,64,128]{2,1,0:T(8,128)S(1)} %get-tuple-element.50.other_ref.own_ref, bf16[4,16,16,128]{3,2,1,0:T(8,128)(2,1)S(1)} %collective-permute-done.10.halo_ref, ...), custom_call_target="tpu_custom_call" | custom-call | flops 268435456 | bytes 1933324 | tf_op jit(solution)/shard_map/pallas_call | solution.py:311
  50.5 3.1 %collective-permute-done.9.halo_ref = bf16[4,16,16,128]{3,2,1,0:T(8,128)(2,1)S(1)} collective-permute-done((bf16[4,16,16,128]{3,2,1,0:T(8,128)(2,1)S(1)}, bf16[4,16,16,128]{3,2,1,0:T(8,128)(2,1)S(1)}, u32[]{:S(2)}, u32[]{:S(2)}) %collective-permute-start.9) | collective-permute-done | bytes 262176 | tf_op jit(solution)/shard_map/ppermute | solution.py:408
  53.6 2.0 %shard_map.55 = (bf16[2,16,16,128]{3,2,1,0:T(8,128)(2,1)S(1)}, bf16[2,16,16,128]{3,2,1,0:T(8,128)(2,1)S(1)}, bf16[2,16,16,128]{3,2,1,0:T(8,128)(2,1)S(1)}, bf16[2,16,16,128]{3,2,1,0:T(8,128)(2,1)S(1)}) custom-call(s32[3]{0:T(128)S(1)} %copy-done.1, f32[16,64,128]{2,1,0:T(8,128)S(1)} %get-tuple-element.50.other_ref.own_ref, ...), custom_call_target="tpu_custom_call" | custom-call | flops 268435456 | bytes 2457612 | tf_op jit(solution)/shard_map/pallas_call | solution.py:311
  55.6 5.4 %collective-permute-start.11 = (bf16[2,16,16,128]{3,2,1,0:T(8,128)(2,1)S(1)}, bf16[2,16,16,128]{3,2,1,0:T(8,128)(2,1)S(1)}, u32[]{:S(2)}, u32[]{:S(2)}) collective-permute-start(bf16[2,16,16,128]{3,2,1,0:T(8,128)(2,1)S(1)} %get-tuple-element.56), channel_id=1, source_target_pairs={{0,8},{8,0},{16,24},{24,16},{1,9},{9,1},{17,25},{25,17},{2,10},{10... | collective-permute-start | bytes 393224 | tf_op jit(solution)/shard_map/ppermute | solution.py:352
  61.0 1.7 %collective-permute-start.13 = (bf16[2,16,16,128]{3,2,1,0:T(8,128)(2,1)S(1)}, bf16[2,16,16,128]{3,2,1,0:T(8,128)(2,1)S(1)}, u32[]{:S(2)}, u32[]{:S(2)}) collective-permute-start(bf16[2,16,16,128]{3,2,1,0:T(8,128)(2,1)S(1)} %get-tuple-element.58), channel_id=1, source_target_pairs={{0,24},{8,16},{16,8},{24,0},{1,25},{9,17},{17,9},{25,1},{2,26},{10... | collective-permute-start | bytes 393224 | tf_op jit(solution)/shard_map/ppermute | solution.py:352
  62.7 3.4 %collective-permute-done.12.refs_2_ = bf16[2,16,16,128]{3,2,1,0:T(8,128)(2,1)S(1)} collective-permute-done((bf16[2,16,16,128]{3,2,1,0:T(8,128)(2,1)S(1)}, bf16[2,16,16,128]{3,2,1,0:T(8,128)(2,1)S(1)}, u32[]{:S(2)}, u32[]{:S(2)}) %collective-permute-start.12) | collective-permute-done | bytes 131104 | tf_op jit(solution)/shard_map/ppermute | solution.py:352
  66.1 3.0 %collective-permute-done.13.refs_3_ = bf16[2,16,16,128]{3,2,1,0:T(8,128)(2,1)S(1)} collective-permute-done((bf16[2,16,16,128]{3,2,1,0:T(8,128)(2,1)S(1)}, bf16[2,16,16,128]{3,2,1,0:T(8,128)(2,1)S(1)}, u32[]{:S(2)}, u32[]{:S(2)}) %collective-permute-start.13) | collective-permute-done | bytes 131104 | tf_op jit(solution)/shard_map/ppermute | solution.py:352
  69.0 2.2 %shard_map.56 = f32[16,128,128]{2,1,0:T(8,128)} custom-call(s32[3]{0:T(128)S(1)} %copy-done.1, bf16[2,16,16,128]{3,2,1,0:T(8,128)(2,1)S(1)} %get-tuple-element.55.refs_0_, bf16[2,16,16,128]{3,2,1,0:T(8,128)(2,1)S(1)} %collective-permute-done.11.refs_1_, bf16[2,16,16,128]{3,2,1,0:T(8,128)(2,1)S(1)} %collective-permute-done.12.refs_2_, ...), custom_call_target="tpu_custom_call" | custom-call | bytes 1572876 | tf_op jit(solution)/shard_map/pallas_call | solution.py:311
  (27 shorter events, 6.8 us)
Async XLA Ops:
  3.9 2.5 %collective-permute-start = (bf16[38,16,128]{2,1,0:T(8,128)(2,1)}, bf16[38,16,128]{2,1,0:T(8,128)(2,1)S(1)}, u32[]{:S(2)}, u32[]{:S(2)}) collective-permute-start(bf16[38,16,128]{2,1,0:T(8,128)(2,1)} %get-tuple-element.33), channel_id=1, source_target_pairs={{0,8},{8,0},{16,24},{24,16},{1,9},{9,1},{17,25},{25,17},{2,10},{10... | collective-permute-start | bytes 466952 | tf_op jit(solution)/shard_map/ppermute | solution.py:352
  4.7 5.8 %collective-permute-start.1 = (bf16[38,16,128]{2,1,0:T(8,128)(2,1)}, bf16[38,16,128]{2,1,0:T(8,128)(2,1)S(1)}, u32[]{:S(2)}, u32[]{:S(2)}) collective-permute-start(bf16[38,16,128]{2,1,0:T(8,128)(2,1)} %get-tuple-element.34), channel_id=1, source_target_pairs={{0,16},{8,24},{16,0},{24,8},{1,17},{9,25},{17,1},{25,9},{2,18},{10... | collective-permute-start | bytes 466952 | tf_op jit(solution)/shard_map/ppermute | solution.py:352
  5.9 8.1 %copy-start.1 = (s32[3]{0:T(128)S(1)}, s32[3]{0:T(128)}, u32[]{:S(2)}) copy-start(s32[3]{0:T(128)} %pad_add_fusion.at_ref) | copy-start | bytes 40
  5.9 8.1 %collective-permute-start.2 = (bf16[38,16,128]{2,1,0:T(8,128)(2,1)}, bf16[38,16,128]{2,1,0:T(8,128)(2,1)S(1)}, u32[]{:S(2)}, u32[]{:S(2)}) collective-permute-start(bf16[38,16,128]{2,1,0:T(8,128)(2,1)} %get-tuple-element.35), channel_id=1, source_target_pairs={{0,24},{8,16},{16,8},{24,0},{1,25},{9,17},{17,9},{25,1},{2,26},{10... | collective-permute-start | bytes 466952 | tf_op jit(solution)/shard_map/ppermute | solution.py:352
  14.0 0.9 %copy-start = (bf16[38,16,128]{2,1,0:T(8,128)(2,1)S(1)}, bf16[38,16,128]{2,1,0:T(8,128)(2,1)}, u32[]{:S(2)}) copy-start(bf16[38,16,128]{2,1,0:T(8,128)(2,1)} %get-tuple-element.32.refs_0_) | copy-start | bytes 466948
  14.9 4.4 %copy-start.3 = (bf16[64,512]{1,0:T(8,128)(2,1)S(1)}, bf16[64,512]{1,0:T(8,128)(2,1)}, u32[]{:S(2)}) copy-start(bf16[64,512]{1,0:T(8,128)(2,1)} %param.7) | copy-start | bytes 196612
  15.6 3.9 %collective-permute-start.4 = (bf16[4,17,16,128]{3,2,1,0:T(8,128)(2,1)S(1)}, bf16[4,17,16,128]{3,2,1,0:T(8,128)(2,1)S(1)}, u32[]{:S(2)}, u32[]{:S(2)}) collective-permute-start(bf16[4,17,16,128]{3,2,1,0:T(8,128)(2,1)S(1)} %get-tuple-element.41), channel_id=1, source_target_pairs={{0,8},{8,0},{16,24},{24,16},{25,17},{17,25},{9,1},{1,9},{2,10},{10... | collective-permute-start | bytes 835592 | tf_op jit(solution)/shard_map/ppermute | solution.py:381
  15.9 3.5 %copy-start.2 = (bf16[512,64]{0,1:T(8,128)(2,1)S(1)}, bf16[512,64]{0,1:T(8,128)(2,1)}, u32[]{:S(2)}) copy-start(bf16[512,64]{0,1:T(8,128)(2,1)} %param.6) | copy-start | bytes 196612
  15.9 8.3 %collective-permute-start.3 = (bf16[4,17,16,128]{3,2,1,0:T(8,128)(2,1)S(1)}, bf16[4,17,16,128]{3,2,1,0:T(8,128)(2,1)S(1)}, u32[]{:S(2)}, u32[]{:S(2)}) collective-permute-start(bf16[4,17,16,128]{3,2,1,0:T(8,128)(2,1)S(1)} %get-tuple-element.38), channel_id=1, source_target_pairs={{0,0},{7,7},{8,16},{16,8},{24,25},{25,24},{17,9},{9,17},{1,2},{2,1... | collective-permute-start | bytes 835592 | tf_op jit(solution)/shard_map/ppermute | solution.py:380
  21.5 7.7 %collective-permute-start.6 = (bf16[4,16,16,128]{3,2,1,0:T(8,128)(2,1)S(1)}, bf16[4,16,16,128]{3,2,1,0:T(8,128)(2,1)S(1)}, u32[]{:S(2)}, u32[]{:S(2)}) collective-permute-start(bf16[4,16,16,128]{3,2,1,0:T(8,128)(2,1)S(1)} %get-tuple-element.46), channel_id=1, source_target_pairs={{0,8},{8,0},{16,24},{24,16},{25,17},{17,25},{9,1},{1,9},{2,10},{10... | collective-permute-start | bytes 786440 | tf_op jit(solution)/shard_map/ppermute | solution.py:406
  26.1 8.0 %collective-permute-start.5 = (bf16[4,16,16,128]{3,2,1,0:T(8,128)(2,1)S(1)}, bf16[4,16,16,128]{3,2,1,0:T(8,128)(2,1)S(1)}, u32[]{:S(2)}, u32[]{:S(2)}) collective-permute-start(bf16[4,16,16,128]{3,2,1,0:T(8,128)(2,1)S(1)} %get-tuple-element.43), channel_id=1, source_target_pairs={{0,0},{7,7},{8,16},{16,8},{24,25},{25,24},{17,9},{9,17},{1,2},{2,1... | collective-permute-start | bytes 786440 | tf_op jit(solution)/shard_map/ppermute | solution.py:408
  31.1 7.7 %collective-permute-start.8 = (bf16[4,16,16,128]{3,2,1,0:T(8,128)(2,1)S(1)}, bf16[4,16,16,128]{3,2,1,0:T(8,128)(2,1)S(1)}, u32[]{:S(2)}, u32[]{:S(2)}) collective-permute-start(bf16[4,16,16,128]{3,2,1,0:T(8,128)(2,1)S(1)} %get-tuple-element.51), channel_id=1, source_target_pairs={{0,8},{8,0},{16,24},{24,16},{25,17},{17,25},{9,1},{1,9},{2,10},{10... | collective-permute-start | bytes 786440 | tf_op jit(solution)/shard_map/ppermute | solution.py:406
  36.1 7.9 %collective-permute-start.7 = (bf16[4,16,16,128]{3,2,1,0:T(8,128)(2,1)S(1)}, bf16[4,16,16,128]{3,2,1,0:T(8,128)(2,1)S(1)}, u32[]{:S(2)}, u32[]{:S(2)}) collective-permute-start(bf16[4,16,16,128]{3,2,1,0:T(8,128)(2,1)S(1)} %get-tuple-element.49), channel_id=1, source_target_pairs={{0,0},{7,7},{8,16},{16,8},{24,25},{25,24},{17,9},{9,17},{1,2},{2,1... | collective-permute-start | bytes 786440 | tf_op jit(solution)/shard_map/ppermute | solution.py:408
  40.7 7.9 %collective-permute-start.10 = (bf16[4,16,16,128]{3,2,1,0:T(8,128)(2,1)S(1)}, bf16[4,16,16,128]{3,2,1,0:T(8,128)(2,1)S(1)}, u32[]{:S(2)}, u32[]{:S(2)}) collective-permute-start(bf16[4,16,16,128]{3,2,1,0:T(8,128)(2,1)S(1)} %get-tuple-element.54), channel_id=1, source_target_pairs={{0,8},{8,0},{16,24},{24,16},{25,17},{17,25},{9,1},{1,9},{2,10},{10... | collective-permute-start | bytes 786440 | tf_op jit(solution)/shard_map/ppermute | solution.py:406
  45.9 7.7 %collective-permute-start.9 = (bf16[4,16,16,128]{3,2,1,0:T(8,128)(2,1)S(1)}, bf16[4,16,16,128]{3,2,1,0:T(8,128)(2,1)S(1)}, u32[]{:S(2)}, u32[]{:S(2)}) collective-permute-start(bf16[4,16,16,128]{3,2,1,0:T(8,128)(2,1)S(1)} %get-tuple-element.53), channel_id=1, source_target_pairs={{0,0},{7,7},{8,16},{16,8},{24,25},{25,24},{17,9},{9,17},{1,2},{2,1... | collective-permute-start | bytes 786440 | tf_op jit(solution)/shard_map/ppermute | solution.py:408
  55.6 7.1 %collective-permute-start.11 = (bf16[2,16,16,128]{3,2,1,0:T(8,128)(2,1)S(1)}, bf16[2,16,16,128]{3,2,1,0:T(8,128)(2,1)S(1)}, u32[]{:S(2)}, u32[]{:S(2)}) collective-permute-start(bf16[2,16,16,128]{3,2,1,0:T(8,128)(2,1)S(1)} %get-tuple-element.56), channel_id=1, source_target_pairs={{0,8},{8,0},{16,24},{24,16},{1,9},{9,1},{17,25},{25,17},{2,10},{10... | collective-permute-start | bytes 393224 | tf_op jit(solution)/shard_map/ppermute | solution.py:352
  61.0 5.1 %collective-permute-start.12 = (bf16[2,16,16,128]{3,2,1,0:T(8,128)(2,1)S(1)}, bf16[2,16,16,128]{3,2,1,0:T(8,128)(2,1)S(1)}, u32[]{:S(2)}, u32[]{:S(2)}) collective-permute-start(bf16[2,16,16,128]{3,2,1,0:T(8,128)(2,1)S(1)} %get-tuple-element.57), channel_id=1, source_target_pairs={{0,16},{8,24},{16,0},{24,8},{1,17},{9,25},{17,1},{25,9},{2,18},{10... | collective-permute-start | bytes 393224 | tf_op jit(solution)/shard_map/ppermute | solution.py:352
  61.0 8.0 %collective-permute-start.13 = (bf16[2,16,16,128]{3,2,1,0:T(8,128)(2,1)S(1)}, bf16[2,16,16,128]{3,2,1,0:T(8,128)(2,1)S(1)}, u32[]{:S(2)}, u32[]{:S(2)}) collective-permute-start(bf16[2,16,16,128]{3,2,1,0:T(8,128)(2,1)S(1)} %get-tuple-element.58), channel_id=1, source_target_pairs={{0,24},{8,16},{16,8},{24,0},{1,25},{9,17},{17,9},{25,1},{2,26},{10... | collective-permute-start | bytes 393224 | tf_op jit(solution)/shard_map/ppermute | solution.py:352

commit v4 on v3

--- a/solution.py
+++ b/solution.py
@@ -13,7 +13,6 @@
 GROUP = 4
 PARTS = 4
 VMEM = pl.BlockSpec(memory_space=pltpu.VMEM)
-SMEM = pl.BlockSpec(memory_space=pltpu.SMEM)
 LIMIT = 24 * 1024 * 1024
 FULL = 56 * 1024 * 1024
 
@@ -93,88 +92,93 @@
     return lax.all_to_all(state, "species", split_axis=0, concat_axis=1, tiled=True)
 
 
-def place_of(species, tile, count):
-    return jnp.where(lax.rem(tile, 2) == 1, count - 1 - species, species)
+def place_and_species(count):
+    species = lax.axis_index("species")
+    return jnp.where(lax.rem(lax.axis_index("tile"), 2) == 1, count - 1 - species, species), species
 
 
 def columns_of(place):
-    return (2 * place, 2 * place + 1) if place % 2 == 0 else (2 * place + 1, 2 * place)
-
-
-def for_each_place(at_ref, count, act):
-    for own in range(count):
-        pl.when(at_ref[2] == own)(functools.partial(act, own))
-
-
-def pack_kernel(count, at_ref, tracers_ref, fluxes_ref, *refs):
+    odd = lax.rem(place, 2)
+    return 2 * place + odd, 2 * place + 1 - odd
+
+
+def pack_kernel(count, tracers_ref, fluxes_ref, *refs):
     out_refs, (held, flux_ref, sems) = refs[:count], refs[count:]
     parts, spec, rows, width_y = held.shape
     width = 2 * count
     lev = rows // width
     depth = parts * lev
     lev_own = fluxes_ref.shape[0] // (STEPS * 3 * width)
-    copies = [pltpu.make_async_copy(fluxes_ref, flux_ref, sems.at[parts])]
+    own, _ = place_and_species(count)
+    outer = lax.axis_index("tile") == 0
+    copies = []
     for part in range(parts):
         source = tracers_ref.at[:, pl.ds(part * rows, rows), :]
         copies.append(pltpu.make_async_copy(source, held.at[part], sems.at[part]))
+    copies.append(pltpu.make_async_copy(fluxes_ref, flux_ref, sems.at[parts]))
     for copy in copies:
         copy.start()
-    outer = at_ref[0] == 0
-
-    def fluxes(own):
-        for d in range(count):
-            place = own ^ d
-            b_at, a_at = columns_of(place)
-
-            def tile_of(direction, x):
-                return jnp.concatenate(
-                    [
-                        flux_ref[
-                            pl.ds((t * 3 + direction) * lev_own * width + x, lev_own, stride=width), :
-                        ]
-                        for t in range(STEPS)
-                    ],
-                    0,
-                )
-
-            first = tile_of(0, 2 * place)
-            if place == 0:
-                first = jnp.where(outer, 0.0, first)
-            out_refs[d][depth] = first.astype(jnp.bfloat16)
-            others = ((0, 2 * place + 1), (1, b_at), (1, a_at), (2, b_at), (2, a_at))
-            for i, (direction, x) in enumerate(others):
-                out_refs[d][2 * depth + 1 + i] = tile_of(direction, x).astype(jnp.bfloat16)
-
-    def tracers(part, own):
+
+    columns = [columns_of(own ^ d) for d in range(count)]
+    for part in range(parts):
+        copies[part].wait()
         flat = held.at[part].reshape(spec * rows, width_y)
-        for d in range(count):
-            b_at, a_at = columns_of(own ^ d)
-            for base, x in ((0, b_at), (depth + 1, a_at)):
-                for k in range(lev):
+
+        def level(k, carry):
+            for d in range(count):
+                for base, x in zip((0, depth + 1), columns[d]):
                     cells = flat[pl.ds(k * width + x, spec, stride=rows), :]
                     out_refs[d][base + part * lev + k] = cells.astype(jnp.bfloat16)
-
-    copies[0].wait()
-    for_each_place(at_ref, count, fluxes)
-    for part in range(parts):
-        copies[1 + part].wait()
-        for_each_place(at_ref, count, functools.partial(tracers, part))
-
-
-def unpack_kernel(depth, at_ref, *refs):
-    count = len(refs) - 5
-    got, (b_ref, a_ref, msg_b_ref, msg_a_ref, flux_ref) = refs[:count], refs[count:]
+            return carry
+
+        lax.fori_loop(0, lev, level, 0)
+
+    copies[parts].wait()
+    for d in range(count):
+        b_at, a_at = columns[d]
+        low = jnp.minimum(b_at, a_at)
+
+        def tile_of(direction, x):
+            return jnp.concatenate(
+                [
+                    flux_ref[pl.ds((t * 3 + direction) * lev_own * width + x, lev_own, stride=width), :]
+                    for t in range(STEPS)
+                ],
+                0,
+            )
+
+        first = jnp.where(jnp.logical_and(outer, low == 0), 0.0, tile_of(0, low))
+        out_refs[d][depth] = first.astype(jnp.bfloat16)
+        others = ((0, low + 1), (1, b_at), (1, a_at), (2, b_at), (2, a_at))
+        for i, (direction, x) in enumerate(others):
+            out_refs[d][2 * depth + 1 + i] = tile_of(direction, x).astype(jnp.bfloat16)
+
+
+def unpack_kernel(depth, *refs):
+    count = len(refs) - 7
+    got, refs = refs[:count], refs[count:]
+    b_ref, a_ref, msg_b_ref, msg_a_ref, flux_ref, kept, sem = refs
+    copy = pltpu.make_async_copy(got[0], kept, sem)
+    copy.start()
+    got = [kept, *got[1:]]
     lev = depth // count
     spec = got[0].shape[1]
-    for d in range(count):
-        source = at_ref[1] ^ d
-        rows = pl.ds(pl.multiple_of(source * spec, spec), spec)
+    _, species = place_and_species(count)
+
+    def level(d, k, carry):
+        rows = pl.ds(pl.multiple_of((species ^ d) * spec, spec), spec)
         for base, state_ref, msg_ref in ((0, b_ref, msg_b_ref), (depth + 1, a_ref, msg_a_ref)):
-            first = 0 if base == 0 else 1
-            for k in range(depth):
-                cells = got[d][base + k]
-                state_ref[k, rows] = cells.astype(jnp.float32)
-                msg_ref[source, k] = cells
+            cells = got[d][base + k]
+            state_ref[k, rows] = cells.astype(jnp.float32)
+            msg_ref[species ^ d, k] = cells
+        return carry
+
+    for d in [*range(1, count), 0]:
+        if d == 0:
+            copy.wait()
+        lax.fori_loop(0, depth, functools.partial(level, d), 0, unroll=4)
+        source = species ^ d
+        for msg_ref in (msg_b_ref, msg_a_ref):
             msg_ref[source, depth] = got[d][depth]
         for i in range(6):
             part = got[d][depth if i == 0 else 2 * depth + i].astype(jnp.float32)
@@ -182,13 +186,14 @@
                 flux_ref[t, i, source] = part[t * lev : (t + 1) * lev]
 
 
-def step_kernel(t, is_a, group, tiles, at_ref, own_ref, other_ref, halo_ref, flux_ref, edge_ref, w_in_ref, w_out_ref, *rest):
+def step_kernel(t, is_a, group, own_ref, other_ref, halo_ref, flux_ref, edge_ref, w_in_ref, w_out_ref, *rest):
     rest = list(rest)
     first, last = t == 0, t == STEPS - 1
     depth, spec_all, width_y = own_ref.shape
     count, spec = halo_ref.shape[0], halo_ref.shape[2]
     lev = depth // count
-    coef, cells_ref = rest[-2:]
+    place, species = place_and_species(count)
+    coef, moved_ref, cells_ref = rest[-3:]
     if last and is_a:
         send_ref = rest[0]
     elif last:
@@ -203,14 +208,10 @@
         parts = [halo_ref[s, depth].astype(jnp.float32) for s in range(count)]
         for i in range(STEPS):
             rest[2][i] = jnp.concatenate([p[i * lev : (i + 1) * lev] for p in parts], 0)
-        if not is_a:
-            is_end = jnp.logical_and(at_ref[0] == tiles - 1, at_ref[2] == count - 1)
-            for i in range(STEPS):
-                rest[2][i] = jnp.where(is_end, 0.0, rest[2][i])
         beyond = rest[2][t]
     else:
         beyond = edge_ref[t]
-    is_first = lax.rem(at_ref[2], 2) == (1 if is_a else 0)
+    is_first = lax.rem(place, 2) == (1 if is_a else 0)
     fx_first, fx_second = whole(0), whole(1)
     fx = jnp.where(is_first, fx_first, fx_second)
     fx_hi = jnp.where(is_first, fx_second, beyond)
@@ -235,67 +236,67 @@
     w_in = w_in_ref[...]
     w_out = w_out_ref[...]
 
-    def transport(k0):
-        moved = []
-        for k in range(k0, k0 + group):
-            own = own_ref[k]
-            halo = jnp.concatenate([halo_ref[s, k].astype(jnp.float32) for s in range(count)], 0)
-            out = coef[0, pl.ds(k, 1)] * own
-            out += coef[1, pl.ds(k, 1)] * halo
-            out += coef[2, pl.ds(k, 1)] * other_ref[k]
-            out += coef[3, pl.ds(k, 1)] * pltpu.roll(own, 1, 1)
-            out += coef[4, pl.ds(k, 1)] * pltpu.roll(own, width_y - 1, 1)
-            if k > 0:
-                out += coef[5, pl.ds(k, 1)] * own_ref[k - 1]
-            if k < depth - 1:
-                out += coef[6, pl.ds(k, 1)] * own_ref[k + 1]
-            cells_ref[k] = out
-            moved.append(out.astype(jnp.bfloat16))
-        cells = jnp.concatenate(moved, 1)
-        return jnp.dot(w_in, cells, preferred_element_type=jnp.float32)
-
-    def activate(half):
-        half = half.astype(jnp.bfloat16)
-        return half + half * jnp.tanh(half)
-
-    def finish(k0, hidden):
+    def level(k, slot, column):
+        own = own_ref[k]
+        halo = jnp.concatenate([halo_ref[s, k].astype(jnp.float32) for s in range(count)], 0)
+        out = coef[0, pl.ds(k, 1)] * own
+        out += coef[1, pl.ds(k, 1)] * halo
+        out += coef[2, pl.ds(k, 1)] * other_ref[k]
+        out += coef[3, pl.ds(k, 1)] * pltpu.roll(own, 1, 1)
+        out += coef[4, pl.ds(k, 1)] * pltpu.roll(own, width_y - 1, 1)
+        out += coef[5, pl.ds(k, 1)] * own_ref[jnp.maximum(k - 1, 0)]
+        out += coef[6, pl.ds(k, 1)] * own_ref[jnp.minimum(k + 1, depth - 1)]
+        moved_ref[k] = out
+        cells_ref[slot, :, column * width_y : (column + 1) * width_y] = out.astype(jnp.bfloat16)
+
+    groups = depth // group
+
+    def body(g, carry):
+        slot = lax.rem(g, 2)
+        half = jnp.dot(w_in, cells_ref[slot], preferred_element_type=jnp.float32)
+        ahead = jnp.minimum(g + 1, groups - 1)
+        for i in range(group):
+            level(ahead * group + i, 1 - slot, i)
+        hidden = (half + half * jnp.tanh(half)).astype(jnp.bfloat16)
         change = jnp.dot(w_out, hidden, preferred_element_type=jnp.float32)
         for i in range(group):
-            new = cells_ref[k0 + i] + change[:, i * width_y : (i + 1) * width_y]
+            k = g * group + i
+            new = moved_ref[k] + change[:, i * width_y : (i + 1) * width_y]
             if not last:
-                new_ref[k0 + i] = new
+                new_ref[k] = new
             for s in range(count):
-                send_ref[s, k0 + i] = new[s * spec : (s + 1) * spec].astype(jnp.bfloat16)
-
-    half = transport(0)
-    for k0 in range(0, depth, group):
-        ahead = transport(k0 + group) if k0 + group < depth else None
-        finish(k0, activate(half))
-        half = ahead
+                send_ref[s, k] = new[s * spec : (s + 1) * spec].astype(jnp.bfloat16)
+        return carry
+
+    for i in range(group):
+        level(i, 0, i)
+    lax.fori_loop(0, groups, body, 0)
     if last and not is_a:
         for d in range(count):
-            outs[d][0] = send_ref[at_ref[1] ^ d]
-            outs[d][1] = sent_a_ref[at_ref[1] ^ d]
-
-
-def finish_kernel(at_ref, *refs):
+            outs[d][0] = send_ref[species ^ d]
+            outs[d][1] = sent_a_ref[species ^ d]
+
+
+def finish_kernel(*refs):
     out_ref, held, sems = refs[-3:]
-    count, depth, spec = len(refs) - 3, refs[0].shape[1], refs[0].shape[2]
+    count, spec = len(refs) - 3, refs[0].shape[2]
     parts, _, rows, width_y = held.shape
     width = 2 * count
     lev = rows // width
-
-    def store(part, own):
+    own, _ = place_and_species(count)
+    columns = [columns_of(own ^ d) for d in range(count)]
+    copies = []
+    for part in range(parts):
         flat = held.at[part].reshape(spec * rows, width_y)
-        for d in range(count):
-            for side, x in enumerate(columns_of(own ^ d)):
-                for k in range(lev):
+
+        def level(k, carry):
+            for d in range(count):
+                for side, x in enumerate(columns[d]):
                     cells = refs[d][side, part * lev + k].astype(jnp.float32)
                     flat[pl.ds(k * width + x, spec, stride=rows), :] = cells
-
-    copies = []
-    for part in range(parts):
-        for_each_place(at_ref, count, functools.partial(store, part))
+            return carry
+
+        lax.fori_loop(0, lev, level, 0)
         target = out_ref.at[:, pl.ds(part * rows, rows), :]
         copies.append(pltpu.make_async_copy(held.at[part], target, sems.at[part]))
         copies[-1].start()
@@ -312,8 +313,8 @@
         kernel,
         out_shape=out_shape,
         in_specs=[
-            anywhere if i in far else SMEM if a.dtype == jnp.int32 else VMEM
-            for i, a in enumerate(args)
+            anywhere if i in far else VMEM
+            for i in range(len(args))
         ],
         out_specs=[VMEM] * len(out_shape) if many else anywhere if far_out else VMEM,
         scratch_shapes=scratch,
@@ -334,15 +335,12 @@
         for place in range(count):
             s = place if t % 2 == 0 else count - 1 - place
             chain.append(s * tiles + t)
-    swap_a, swap_b = [], [(chain[0], chain[0]), (chain[-1], chain[-1])]
+    swap_a, swap_b = [], []
     for i in range(len(chain) - 1):
         (swap_a if i % 2 == 0 else swap_b).extend(
             [(chain[i], chain[i + 1]), (chain[i + 1], chain[i])]
         )
 
-    tile = lax.axis_index("tile").astype(jnp.int32)
-    species = lax.axis_index("species").astype(jnp.int32)
-    at = jnp.stack([tile, species, place_of(species, tile, count)])
     w_in = weight_in * jnp.asarray(0.5, bf16)
     w_out = weight_out * jnp.asarray(0.5, bf16)
 
@@ -358,14 +356,14 @@
     packed = call(
         functools.partial(pack_kernel, count),
         [piece] * count,
-        (at, tracers.reshape(spec, depth * width, width_y), flux_rows),
+        (tracers.reshape(spec, depth * width, width_y), flux_rows),
         scratch=[
             held,
             pltpu.VMEM(flux_rows.shape, f32),
             pltpu.SemaphoreType.DMA((PARTS + 1,)),
         ],
         limit=FULL,
-        far=(1, 2),
+        far=(0, 1),
     )
     got = exchange(packed)
     row = shape((depth, spec_all, width_y), f32)
@@ -375,10 +373,18 @@
     b, a, send_b, send_a, flux = call(
         functools.partial(unpack_kernel, depth),
         [row, row, message, message, shape((STEPS, 6, count, depth // count, width_y), f32)],
-        (at, *got),
+        got,
+        scratch=[pltpu.VMEM(piece.shape, bf16), pltpu.SemaphoreType.DMA],
+        far=(0,),
     )
     halo_b = lax.ppermute(send_b, AXES, swap_b)
     halo_a = lax.ppermute(send_a, AXES, swap_a)
+
+    common = [
+        pltpu.VMEM((7, depth, width_y), f32),
+        pltpu.VMEM(row.shape, f32),
+        pltpu.VMEM((2, spec_all, GROUP * width_y), bf16),
+    ]
 
     def step(t, is_a, own, other, halo, edge, more=()):
         last = t == STEPS - 1
@@ -388,10 +394,10 @@
             outs = [sent] if is_a else [shape((2, depth, spec, width_y), bf16)] * count
             scratch = [] if is_a else [pltpu.VMEM(sent.shape, bf16)]
         return call(
-            functools.partial(step_kernel, t, is_a, GROUP, tiles),
+            functools.partial(step_kernel, t, is_a, GROUP),
             outs,
-            (at, own, other, halo, flux, edge, w_in, w_out, *more),
-            scratch=[*scratch, pltpu.VMEM((7, depth, width_y), f32), pltpu.VMEM(row.shape, f32)],
+            (own, other, halo, flux, edge, w_in, w_out, *more),
+            scratch=[*scratch, *common],
             flops=4 * depth * width_y * spec_all * hid,
             trans=depth * width_y * hid,
         )
@@ -412,7 +418,7 @@
     out = call(
         finish_kernel,
         shape((spec, depth * width, width_y), f32),
-        (at, *exchange(pieces)),
+        exchange(pieces),
         scratch=[held, pltpu.SemaphoreType.DMA((PARTS,))],
         far_out=True,
     )

time: 71.7 us -> 69.6 us (0.971)
  Pallas kernels: 21.7 us -> 20.3 us
    pallas_call x11, Pallas kernels: 21.7 us -> 20.3 us  [call(): pl.pallas_call(kernel, out_shape=out_shape, in_specs=[anywhere if i in fa...]
where the time goes in v4:
time: 69.6 us; the launch traced here: 69.4 us
  starting transfers between devices  26.9 us (39%)
  waiting for transfers between devices  20.9 us (30%)
  Pallas kernels  20.3 us (29%)
  local copies, waits for them, and re-layouts  1.04 us (1%)
    pallas_call x11, Pallas kernels, call(): pl.pallas_call(kernel, out_shape=out_shape, in_specs=[anywhere if i in fa...  20.3 us
    ppermute x6, waiting for transfers between devices, exchange(): lax.ppermute(pieces[d], 'species', [(s, s ^ d) for s in range(count)])  13.9 us
    ppermute x6, starting transfers between devices, exchange(): lax.ppermute(pieces[d], 'species', [(s, s ^ d) for s in range(count)])  9.57 us
    ppermute x3, starting transfers between devices, by_columns(): halo_b = lax.ppermute(made_b[0], AXES, swap_b)  8.22 us
    ppermute x3, starting transfers between devices, by_columns(): halo_a = lax.ppermute(made_a[0], AXES, swap_a)  5.37 us
    ppermute x3, waiting for transfers between devices, by_columns(): halo_b = lax.ppermute(made_b[0], AXES, swap_b)  4.52 us
    ppermute x1, starting transfers between devices, by_columns(): halo_b = lax.ppermute(send_b, AXES, swap_b)  3.43 us
    ppermute x1, waiting for transfers between devices, by_columns(): halo_b = lax.ppermute(send_b, AXES, swap_b)  2.41 us
  transfers between devices with their start and end apart: 14, of which 7 were waited for; matrix products, arithmetic and copies ran while one was open for 0% of the time, Pallas kernels for 19%

profile of v4, /device:TPU:17, one launch (start us, length us, event | category | flops | bytes accessed | tf_op | source)
XLA Modules:
  0.0 69.4 jit_solution(16098184647337836820)
XLA Ops:
  0.0 3.0 %shard_map.46 = (bf16[38,16,128]{2,1,0:T(8,128)(2,1)}, bf16[38,16,128]{2,1,0:T(8,128)(2,1)}, bf16[38,16,128]{2,1,0:T(8,128)(2,1)}, bf16[38,16,128]{2,1,0:T(8,128)(2,1)}) custom-call(f32[16,128,128]{2,1,0:T(8,128)} %bitcast.3, f32[384,128]{1,0:T(8,128)} %bitcast.4), custom_call_target="tpu_custom_call" | custom-call | bytes 1867776 | tf_op jit(solution)/shard_map/pallas_call | solution.py:312
  5.5 4.1 %collective-permute-done.1.refs_2_ = bf16[38,16,128]{2,1,0:T(8,128)(2,1)S(1)} collective-permute-done((bf16[38,16,128]{2,1,0:T(8,128)(2,1)}, bf16[38,16,128]{2,1,0:T(8,128)(2,1)S(1)}, u32[]{:S(2)}, u32[]{:S(2)}) %collective-permute-start.1) | collective-permute-done | bytes 155680 | tf_op jit(solution)/shard_map/ppermute | solution.py:350
  9.6 3.5 %collective-permute-done.2.refs_3_ = bf16[38,16,128]{2,1,0:T(8,128)(2,1)S(1)} collective-permute-done((bf16[38,16,128]{2,1,0:T(8,128)(2,1)}, bf16[38,16,128]{2,1,0:T(8,128)(2,1)S(1)}, u32[]{:S(2)}, u32[]{:S(2)}) %collective-permute-start.2) | collective-permute-done | bytes 155680 | tf_op jit(solution)/shard_map/ppermute | solution.py:350
  14.7 3.4 %collective-permute-start.3 = (bf16[4,17,16,128]{3,2,1,0:T(8,128)(2,1)S(1)}, bf16[4,17,16,128]{3,2,1,0:T(8,128)(2,1)S(1)}, u32[]{:S(2)}, u32[]{:S(2)}) collective-permute-start(bf16[4,17,16,128]{3,2,1,0:T(8,128)(2,1)S(1)} %get-tuple-element.38), channel_id=1, source_target_pairs={{8,16},{16,8},{24,25},{25,24},{17,9},{9,17},{1,2},{2,1},{10,18},{1... | collective-permute-start | bytes 835592 | tf_op jit(solution)/shard_map/ppermute | solution.py:380
  18.3 1.9 %shard_map.49 = (bf16[4,16,16,128]{3,2,1,0:T(8,128)(2,1)S(1)}, f32[16,64,128]{2,1,0:T(8,128)S(1)}, f32[4,16,128]{2,1,0:T(8,128)S(1)}) custom-call(f32[16,64,128]{2,1,0:T(8,128)S(1)} %get-tuple-element.37.other_ref.own_ref, f32[16,64,128]{2,1,0:T(8,128)S(1)} %get-tuple-element.36.own_ref.other_ref, ...), custom_call_target="tpu_custom_call" | custom-call | flops 268435456 | bytes 2670592 | tf_op jit(solution)/shard_map/pallas_call | solution.py:312
  20.6 2.4 %collective-permute-done.3.halo_ref = bf16[4,17,16,128]{3,2,1,0:T(8,128)(2,1)S(1)} collective-permute-done((bf16[4,17,16,128]{3,2,1,0:T(8,128)(2,1)S(1)}, bf16[4,17,16,128]{3,2,1,0:T(8,128)(2,1)S(1)}, u32[]{:S(2)}, u32[]{:S(2)}) %collective-permute-start.3) | collective-permute-done | bytes 278560 | tf_op jit(solution)/shard_map/ppermute | solution.py:380
  23.0 1.9 %shard_map.48 = (bf16[4,16,16,128]{3,2,1,0:T(8,128)(2,1)S(1)}, f32[16,64,128]{2,1,0:T(8,128)S(1)}, f32[4,16,128]{2,1,0:T(8,128)S(1)}) custom-call(f32[16,64,128]{2,1,0:T(8,128)S(1)} %get-tuple-element.36.own_ref.other_ref, f32[16,64,128]{2,1,0:T(8,128)S(1)} %get-tuple-element.37.other_ref.own_ref, ...), custom_call_target="tpu_custom_call" | custom-call | flops 268435456 | bytes 2670592 | tf_op jit(solution)/shard_map/pallas_call | solution.py:312
  24.9 3.0 %collective-permute-start.5 = (bf16[4,16,16,128]{3,2,1,0:T(8,128)(2,1)S(1)}, bf16[4,16,16,128]{3,2,1,0:T(8,128)(2,1)S(1)}, u32[]{:S(2)}, u32[]{:S(2)}) collective-permute-start(bf16[4,16,16,128]{3,2,1,0:T(8,128)(2,1)S(1)} %get-tuple-element.43), channel_id=1, source_target_pairs={{8,16},{16,8},{24,25},{25,24},{17,9},{9,17},{1,2},{2,1},{10,18},{1... | collective-permute-start | bytes 786440 | tf_op jit(solution)/shard_map/ppermute | solution.py:414
  27.9 1.9 %shard_map.51 = (bf16[4,16,16,128]{3,2,1,0:T(8,128)(2,1)S(1)}, f32[16,64,128]{2,1,0:T(8,128)S(1)}) custom-call(f32[16,64,128]{2,1,0:T(8,128)S(1)} %get-tuple-element.42.other_ref.own_ref, f32[16,64,128]{2,1,0:T(8,128)S(1)} %get-tuple-element.40.own_ref.other_ref, bf16[4,16,16,128]{3,2,1,0:T(8,128)(2,1)S(1)} %collective-permute-done.6.halo_ref, ...), custom_call_target="tpu_custom_call" | custom-call | flops 268435456 | bytes 2457600 | tf_op jit(solution)/shard_map/pallas_call | solution.py:312
  29.9 1.8 %collective-permute-start.8 = (bf16[4,16,16,128]{3,2,1,0:T(8,128)(2,1)S(1)}, bf16[4,16,16,128]{3,2,1,0:T(8,128)(2,1)S(1)}, u32[]{:S(2)}, u32[]{:S(2)}) collective-permute-start(bf16[4,16,16,128]{3,2,1,0:T(8,128)(2,1)S(1)} %get-tuple-element.51), channel_id=1, source_target_pairs={{0,8},{8,0},{16,24},{24,16},{25,17},{17,25},{9,1},{1,9},{2,10},{10... | collective-permute-start | bytes 786440 | tf_op jit(solution)/shard_map/ppermute | solution.py:412
  32.9 1.9 %shard_map.50 = (bf16[4,16,16,128]{3,2,1,0:T(8,128)(2,1)S(1)}, f32[16,64,128]{2,1,0:T(8,128)S(1)}) custom-call(f32[16,64,128]{2,1,0:T(8,128)S(1)} %get-tuple-element.40.own_ref.other_ref, f32[16,64,128]{2,1,0:T(8,128)S(1)} %get-tuple-element.42.other_ref.own_ref, bf16[4,16,16,128]{3,2,1,0:T(8,128)(2,1)S(1)} %collective-permute-done.5.halo_ref, ...), custom_call_target="tpu_custom_call" | custom-call | flops 268435456 | bytes 2457600 | tf_op jit(solution)/shard_map/pallas_call | solution.py:312
  34.8 2.7 %collective-permute-start.7 = (bf16[4,16,16,128]{3,2,1,0:T(8,128)(2,1)S(1)}, bf16[4,16,16,128]{3,2,1,0:T(8,128)(2,1)S(1)}, u32[]{:S(2)}, u32[]{:S(2)}) collective-permute-start(bf16[4,16,16,128]{3,2,1,0:T(8,128)(2,1)S(1)} %get-tuple-element.49), channel_id=1, source_target_pairs={{8,16},{16,8},{24,25},{25,24},{17,9},{9,17},{1,2},{2,1},{10,18},{1... | collective-permute-start | bytes 786440 | tf_op jit(solution)/shard_map/ppermute | solution.py:414
  37.5 1.9 %shard_map.53 = (bf16[4,16,16,128]{3,2,1,0:T(8,128)(2,1)S(1)}, f32[16,64,128]{2,1,0:T(8,128)S(1)}) custom-call(f32[16,64,128]{2,1,0:T(8,128)S(1)} %get-tuple-element.48.other_ref.own_ref, f32[16,64,128]{2,1,0:T(8,128)S(1)} %get-tuple-element.45.own_ref.other_ref, bf16[4,16,16,128]{3,2,1,0:T(8,128)(2,1)S(1)} %collective-permute-done.8.halo_ref, ...), custom_call_target="tpu_custom_call" | custom-call | flops 268435456 | bytes 2457600 | tf_op jit(solution)/shard_map/pallas_call | solution.py:312
  39.5 3.3 %collective-permute-start.10 = (bf16[4,16,16,128]{3,2,1,0:T(8,128)(2,1)S(1)}, bf16[4,16,16,128]{3,2,1,0:T(8,128)(2,1)S(1)}, u32[]{:S(2)}, u32[]{:S(2)}) collective-permute-start(bf16[4,16,16,128]{3,2,1,0:T(8,128)(2,1)S(1)} %get-tuple-element.54), channel_id=1, source_target_pairs={{0,8},{8,0},{16,24},{24,16},{25,17},{17,25},{9,1},{1,9},{2,10},{10... | collective-permute-start | bytes 786440 | tf_op jit(solution)/shard_map/ppermute | solution.py:412
  42.7 1.9 %shard_map.52 = (bf16[4,16,16,128]{3,2,1,0:T(8,128)(2,1)S(1)}, f32[16,64,128]{2,1,0:T(8,128)S(1)}) custom-call(f32[16,64,128]{2,1,0:T(8,128)S(1)} %get-tuple-element.45.own_ref.other_ref, f32[16,64,128]{2,1,0:T(8,128)S(1)} %get-tuple-element.48.other_ref.own_ref, bf16[4,16,16,128]{3,2,1,0:T(8,128)(2,1)S(1)} %collective-permute-done.7.halo_ref, ...), custom_call_target="tpu_custom_call" | custom-call | flops 268435456 | bytes 2457600 | tf_op jit(solution)/shard_map/pallas_call | solution.py:312
  44.7 2.5 %collective-permute-start.9 = (bf16[4,16,16,128]{3,2,1,0:T(8,128)(2,1)S(1)}, bf16[4,16,16,128]{3,2,1,0:T(8,128)(2,1)S(1)}, u32[]{:S(2)}, u32[]{:S(2)}) collective-permute-start(bf16[4,16,16,128]{3,2,1,0:T(8,128)(2,1)S(1)} %get-tuple-element.53), channel_id=1, source_target_pairs={{8,16},{16,8},{24,25},{25,24},{17,9},{9,17},{1,2},{2,1},{10,18},{1... | collective-permute-start | bytes 786440 | tf_op jit(solution)/shard_map/ppermute | solution.py:414
  47.2 1.9 %shard_map.54.rest_0_ = bf16[4,16,16,128]{3,2,1,0:T(8,128)(2,1)S(1)} custom-call(f32[16,64,128]{2,1,0:T(8,128)S(1)} %get-tuple-element.52.own_ref.other_ref, f32[16,64,128]{2,1,0:T(8,128)S(1)} %get-tuple-element.50.other_ref.own_ref, bf16[4,16,16,128]{3,2,1,0:T(8,128)(2,1)S(1)} %collective-permute-done.10.halo_ref, ...), custom_call_target="tpu_custom_call" | custom-call | flops 268435456 | bytes 1933312 | tf_op jit(solution)/shard_map/pallas_call | solution.py:312
  49.1 3.3 %collective-permute-done.9.halo_ref = bf16[4,16,16,128]{3,2,1,0:T(8,128)(2,1)S(1)} collective-permute-done((bf16[4,16,16,128]{3,2,1,0:T(8,128)(2,1)S(1)}, bf16[4,16,16,128]{3,2,1,0:T(8,128)(2,1)S(1)}, u32[]{:S(2)}, u32[]{:S(2)}) %collective-permute-start.9) | collective-permute-done | bytes 262176 | tf_op jit(solution)/shard_map/ppermute | solution.py:414
  52.3 1.9 %shard_map.55 = (bf16[2,16,16,128]{3,2,1,0:T(8,128)(2,1)S(1)}, bf16[2,16,16,128]{3,2,1,0:T(8,128)(2,1)S(1)}, bf16[2,16,16,128]{3,2,1,0:T(8,128)(2,1)S(1)}, bf16[2,16,16,128]{3,2,1,0:T(8,128)(2,1)S(1)}) custom-call(f32[16,64,128]{2,1,0:T(8,128)S(1)} %get-tuple-element.50.other_ref.own_ref, f32[16,64,128]{2,1,0:T(8,128)S(1)} %get-tuple-element.52.own_ref.other_ref, ...), custom_call_target="tpu_custom_call" | custom-call | flops 268435456 | bytes 2457600 | tf_op jit(solution)/shard_map/pallas_call | solution.py:312
  54.3 5.4 %collective-permute-start.11 = (bf16[2,16,16,128]{3,2,1,0:T(8,128)(2,1)S(1)}, bf16[2,16,16,128]{3,2,1,0:T(8,128)(2,1)S(1)}, u32[]{:S(2)}, u32[]{:S(2)}) collective-permute-start(bf16[2,16,16,128]{3,2,1,0:T(8,128)(2,1)S(1)} %get-tuple-element.56), channel_id=1, source_target_pairs={{0,8},{8,0},{16,24},{24,16},{1,9},{9,1},{17,25},{25,17},{2,10},{10... | collective-permute-start | bytes 393224 | tf_op jit(solution)/shard_map/ppermute | solution.py:350
  59.7 1.7 %collective-permute-start.13 = (bf16[2,16,16,128]{3,2,1,0:T(8,128)(2,1)S(1)}, bf16[2,16,16,128]{3,2,1,0:T(8,128)(2,1)S(1)}, u32[]{:S(2)}, u32[]{:S(2)}) collective-permute-start(bf16[2,16,16,128]{3,2,1,0:T(8,128)(2,1)S(1)} %get-tuple-element.58), channel_id=1, source_target_pairs={{0,24},{8,16},{16,8},{24,0},{1,25},{9,17},{17,9},{25,1},{2,26},{10... | collective-permute-start | bytes 393224 | tf_op jit(solution)/shard_map/ppermute | solution.py:350
  61.4 3.4 %collective-permute-done.12.refs_2_ = bf16[2,16,16,128]{3,2,1,0:T(8,128)(2,1)S(1)} collective-permute-done((bf16[2,16,16,128]{3,2,1,0:T(8,128)(2,1)S(1)}, bf16[2,16,16,128]{3,2,1,0:T(8,128)(2,1)S(1)}, u32[]{:S(2)}, u32[]{:S(2)}) %collective-permute-start.12) | collective-permute-done | bytes 131104 | tf_op jit(solution)/shard_map/ppermute | solution.py:350
  64.8 3.0 %collective-permute-done.13.refs_3_ = bf16[2,16,16,128]{3,2,1,0:T(8,128)(2,1)S(1)} collective-permute-done((bf16[2,16,16,128]{3,2,1,0:T(8,128)(2,1)S(1)}, bf16[2,16,16,128]{3,2,1,0:T(8,128)(2,1)S(1)}, u32[]{:S(2)}, u32[]{:S(2)}) %collective-permute-start.13) | collective-permute-done | bytes 131104 | tf_op jit(solution)/shard_map/ppermute | solution.py:350
  67.8 1.6 %shard_map.56 = f32[16,128,128]{2,1,0:T(8,128)} custom-call(bf16[2,16,16,128]{3,2,1,0:T(8,128)(2,1)S(1)} %get-tuple-element.55.refs_0_, bf16[2,16,16,128]{3,2,1,0:T(8,128)(2,1)S(1)} %collective-permute-done.11.refs_1_, bf16[2,16,16,128]{3,2,1,0:T(8,128)(2,1)S(1)} %collective-permute-done.12.refs_2_, bf16[2,16,16,128]{3,2,1,0:T(8,128)(2,1)S(1)} %collective-permute-done.13.refs_3_), custom_call_target="tpu_custom_call" | custom-call | bytes 1572864 | tf_op jit(solution)/shard_map/pallas_call | solution.py:312
  (24 shorter events, 5.8 us)
Async XLA Ops:
  3.0 2.5 %collective-permute-start = (bf16[38,16,128]{2,1,0:T(8,128)(2,1)}, bf16[38,16,128]{2,1,0:T(8,128)(2,1)S(1)}, u32[]{:S(2)}, u32[]{:S(2)}) collective-permute-start(bf16[38,16,128]{2,1,0:T(8,128)(2,1)} %get-tuple-element.33), channel_id=1, source_target_pairs={{0,8},{8,0},{16,24},{24,16},{1,9},{9,1},{17,25},{25,17},{2,10},{10... | collective-permute-start | bytes 466952 | tf_op jit(solution)/shard_map/ppermute | solution.py:350
  3.8 5.8 %collective-permute-start.1 = (bf16[38,16,128]{2,1,0:T(8,128)(2,1)}, bf16[38,16,128]{2,1,0:T(8,128)(2,1)S(1)}, u32[]{:S(2)}, u32[]{:S(2)}) collective-permute-start(bf16[38,16,128]{2,1,0:T(8,128)(2,1)} %get-tuple-element.34), channel_id=1, source_target_pairs={{0,16},{8,24},{16,0},{24,8},{1,17},{9,25},{17,1},{25,9},{2,18},{10... | collective-permute-start | bytes 466952 | tf_op jit(solution)/shard_map/ppermute | solution.py:350
  5.0 8.1 %collective-permute-start.2 = (bf16[38,16,128]{2,1,0:T(8,128)(2,1)}, bf16[38,16,128]{2,1,0:T(8,128)(2,1)S(1)}, u32[]{:S(2)}, u32[]{:S(2)}) collective-permute-start(bf16[38,16,128]{2,1,0:T(8,128)(2,1)} %get-tuple-element.35), channel_id=1, source_target_pairs={{0,24},{8,16},{16,8},{24,0},{1,25},{9,17},{17,9},{25,1},{2,26},{10... | collective-permute-start | bytes 466952 | tf_op jit(solution)/shard_map/ppermute | solution.py:350
  13.1 0.9 %copy-start = (bf16[38,16,128]{2,1,0:T(8,128)(2,1)S(1)}, bf16[38,16,128]{2,1,0:T(8,128)(2,1)}, u32[]{:S(2)}) copy-start(bf16[38,16,128]{2,1,0:T(8,128)(2,1)} %get-tuple-element.32.refs_0_) | copy-start | bytes 466948
  14.0 4.2 %copy-start.2 = (bf16[64,512]{1,0:T(8,128)(2,1)S(1)}, bf16[64,512]{1,0:T(8,128)(2,1)}, u32[]{:S(2)}) copy-start(bf16[64,512]{1,0:T(8,128)(2,1)} %param.7) | copy-start | bytes 196612
  14.4 3.9 %collective-permute-start.4 = (bf16[4,17,16,128]{3,2,1,0:T(8,128)(2,1)S(1)}, bf16[4,17,16,128]{3,2,1,0:T(8,128)(2,1)S(1)}, u32[]{:S(2)}, u32[]{:S(2)}) collective-permute-start(bf16[4,17,16,128]{3,2,1,0:T(8,128)(2,1)S(1)} %get-tuple-element.41), channel_id=1, source_target_pairs={{0,8},{8,0},{16,24},{24,16},{25,17},{17,25},{9,1},{1,9},{2,10},{10... | collective-permute-start | bytes 835592 | tf_op jit(solution)/shard_map/ppermute | solution.py:381
  14.7 3.5 %copy-start.1 = (bf16[512,64]{0,1:T(8,128)(2,1)S(1)}, bf16[512,64]{0,1:T(8,128)(2,1)}, u32[]{:S(2)}) copy-start(bf16[512,64]{0,1:T(8,128)(2,1)} %param.6) | copy-start | bytes 196612
  14.7 8.3 %collective-permute-start.3 = (bf16[4,17,16,128]{3,2,1,0:T(8,128)(2,1)S(1)}, bf16[4,17,16,128]{3,2,1,0:T(8,128)(2,1)S(1)}, u32[]{:S(2)}, u32[]{:S(2)}) collective-permute-start(bf16[4,17,16,128]{3,2,1,0:T(8,128)(2,1)S(1)} %get-tuple-element.38), channel_id=1, source_target_pairs={{8,16},{16,8},{24,25},{25,24},{17,9},{9,17},{1,2},{2,1},{10,18},{1... | collective-permute-start | bytes 835592 | tf_op jit(solution)/shard_map/ppermute | solution.py:380
  20.3 7.7 %collective-permute-start.6 = (bf16[4,16,16,128]{3,2,1,0:T(8,128)(2,1)S(1)}, bf16[4,16,16,128]{3,2,1,0:T(8,128)(2,1)S(1)}, u32[]{:S(2)}, u32[]{:S(2)}) collective-permute-start(bf16[4,16,16,128]{3,2,1,0:T(8,128)(2,1)S(1)} %get-tuple-element.46), channel_id=1, source_target_pairs={{0,8},{8,0},{16,24},{24,16},{25,17},{17,25},{9,1},{1,9},{2,10},{10... | collective-permute-start | bytes 786440 | tf_op jit(solution)/shard_map/ppermute | solution.py:412
  24.9 8.0 %collective-permute-start.5 = (bf16[4,16,16,128]{3,2,1,0:T(8,128)(2,1)S(1)}, bf16[4,16,16,128]{3,2,1,0:T(8,128)(2,1)S(1)}, u32[]{:S(2)}, u32[]{:S(2)}) collective-permute-start(bf16[4,16,16,128]{3,2,1,0:T(8,128)(2,1)S(1)} %get-tuple-element.43), channel_id=1, source_target_pairs={{8,16},{16,8},{24,25},{25,24},{17,9},{9,17},{1,2},{2,1},{10,18},{1... | collective-permute-start | bytes 786440 | tf_op jit(solution)/shard_map/ppermute | solution.py:414
  29.9 7.7 %collective-permute-start.8 = (bf16[4,16,16,128]{3,2,1,0:T(8,128)(2,1)S(1)}, bf16[4,16,16,128]{3,2,1,0:T(8,128)(2,1)S(1)}, u32[]{:S(2)}, u32[]{:S(2)}) collective-permute-start(bf16[4,16,16,128]{3,2,1,0:T(8,128)(2,1)S(1)} %get-tuple-element.51), channel_id=1, source_target_pairs={{0,8},{8,0},{16,24},{24,16},{25,17},{17,25},{9,1},{1,9},{2,10},{10... | collective-permute-start | bytes 786440 | tf_op jit(solution)/shard_map/ppermute | solution.py:412
  34.8 7.9 %collective-permute-start.7 = (bf16[4,16,16,128]{3,2,1,0:T(8,128)(2,1)S(1)}, bf16[4,16,16,128]{3,2,1,0:T(8,128)(2,1)S(1)}, u32[]{:S(2)}, u32[]{:S(2)}) collective-permute-start(bf16[4,16,16,128]{3,2,1,0:T(8,128)(2,1)S(1)} %get-tuple-element.49), channel_id=1, source_target_pairs={{8,16},{16,8},{24,25},{25,24},{17,9},{9,17},{1,2},{2,1},{10,18},{1... | collective-permute-start | bytes 786440 | tf_op jit(solution)/shard_map/ppermute | solution.py:414
  39.5 7.7 %collective-permute-start.10 = (bf16[4,16,16,128]{3,2,1,0:T(8,128)(2,1)S(1)}, bf16[4,16,16,128]{3,2,1,0:T(8,128)(2,1)S(1)}, u32[]{:S(2)}, u32[]{:S(2)}) collective-permute-start(bf16[4,16,16,128]{3,2,1,0:T(8,128)(2,1)S(1)} %get-tuple-element.54), channel_id=1, source_target_pairs={{0,8},{8,0},{16,24},{24,16},{25,17},{17,25},{9,1},{1,9},{2,10},{10... | collective-permute-start | bytes 786440 | tf_op jit(solution)/shard_map/ppermute | solution.py:412
  44.7 7.7 %collective-permute-start.9 = (bf16[4,16,16,128]{3,2,1,0:T(8,128)(2,1)S(1)}, bf16[4,16,16,128]{3,2,1,0:T(8,128)(2,1)S(1)}, u32[]{:S(2)}, u32[]{:S(2)}) collective-permute-start(bf16[4,16,16,128]{3,2,1,0:T(8,128)(2,1)S(1)} %get-tuple-element.53), channel_id=1, source_target_pairs={{8,16},{16,8},{24,25},{25,24},{17,9},{9,17},{1,2},{2,1},{10,18},{1... | collective-permute-start | bytes 786440 | tf_op jit(solution)/shard_map/ppermute | solution.py:414
  54.3 7.1 %collective-permute-start.11 = (bf16[2,16,16,128]{3,2,1,0:T(8,128)(2,1)S(1)}, bf16[2,16,16,128]{3,2,1,0:T(8,128)(2,1)S(1)}, u32[]{:S(2)}, u32[]{:S(2)}) collective-permute-start(bf16[2,16,16,128]{3,2,1,0:T(8,128)(2,1)S(1)} %get-tuple-element.56), channel_id=1, source_target_pairs={{0,8},{8,0},{16,24},{24,16},{1,9},{9,1},{17,25},{25,17},{2,10},{10... | collective-permute-start | bytes 393224 | tf_op jit(solution)/shard_map/ppermute | solution.py:350
  59.7 5.1 %collective-permute-start.12 = (bf16[2,16,16,128]{3,2,1,0:T(8,128)(2,1)S(1)}, bf16[2,16,16,128]{3,2,1,0:T(8,128)(2,1)S(1)}, u32[]{:S(2)}, u32[]{:S(2)}) collective-permute-start(bf16[2,16,16,128]{3,2,1,0:T(8,128)(2,1)S(1)} %get-tuple-element.57), channel_id=1, source_target_pairs={{0,16},{8,24},{16,0},{24,8},{1,17},{9,25},{17,1},{25,9},{2,18},{10... | collective-permute-start | bytes 393224 | tf_op jit(solution)/shard_map/ppermute | solution.py:350
  59.7 8.0 %collective-permute-start.13 = (bf16[2,16,16,128]{3,2,1,0:T(8,128)(2,1)S(1)}, bf16[2,16,16,128]{3,2,1,0:T(8,128)(2,1)S(1)}, u32[]{:S(2)}, u32[]{:S(2)}) collective-permute-start(bf16[2,16,16,128]{3,2,1,0:T(8,128)(2,1)S(1)} %get-tuple-element.58), channel_id=1, source_target_pairs={{0,24},{8,16},{16,8},{24,0},{1,25},{9,17},{17,9},{25,1},{2,26},{10... | collective-permute-start | bytes 393224 | tf_op jit(solution)/shard_map/ppermute | solution.py:350

commit v5 on v4

--- a/solution.py
+++ b/solution.py
@@ -126,7 +126,7 @@
 
         def level(k, carry):
             for d in range(count):
-                for base, x in zip((0, depth + 1), columns[d]):
+                for base, x in zip((depth + 4, 0), columns[d]):
                     cells = flat[pl.ds(k * width + x, spec, stride=rows), :]
                     out_refs[d][base + part * lev + k] = cells.astype(jnp.bfloat16)
             return carry
@@ -149,9 +149,9 @@
 
         first = jnp.where(jnp.logical_and(outer, low == 0), 0.0, tile_of(0, low))
         out_refs[d][depth] = first.astype(jnp.bfloat16)
-        others = ((0, low + 1), (1, b_at), (1, a_at), (2, b_at), (2, a_at))
-        for i, (direction, x) in enumerate(others):
-            out_refs[d][2 * depth + 1 + i] = tile_of(direction, x).astype(jnp.bfloat16)
+        others = ((0, low + 1, 1), (1, b_at, 2), (2, b_at, 3), (1, a_at, depth + 4), (2, a_at, depth + 5))
+        for direction, x, to in others:
+            out_refs[d][depth + to] = tile_of(direction, x).astype(jnp.bfloat16)
 
 
 def unpack_kernel(depth, *refs):
@@ -167,7 +167,7 @@
 
     def level(d, k, carry):
         rows = pl.ds(pl.multiple_of((species ^ d) * spec, spec), spec)
-        for base, state_ref, msg_ref in ((0, b_ref, msg_b_ref), (depth + 1, a_ref, msg_a_ref)):
+        for base, state_ref, msg_ref in ((depth + 4, b_ref, msg_b_ref), (0, a_ref, msg_a_ref)):
             cells = got[d][base + k]
             state_ref[k, rows] = cells.astype(jnp.float32)
             msg_ref[species ^ d, k] = cells
@@ -178,46 +178,58 @@
             copy.wait()
         lax.fori_loop(0, depth, functools.partial(level, d), 0, unroll=4)
         source = species ^ d
-        for msg_ref in (msg_b_ref, msg_a_ref):
-            msg_ref[source, depth] = got[d][depth]
+        msg_a_ref[source, depth] = got[d][depth]
+        for i in range(4):
+            msg_b_ref[source, depth + i] = got[d][depth + i]
         for i in range(6):
-            part = got[d][depth if i == 0 else 2 * depth + i].astype(jnp.float32)
+            part = got[d][depth + i if i < 4 else 2 * depth + i].astype(jnp.float32)
             for t in range(STEPS):
                 flux_ref[t, i, source] = part[t * lev : (t + 1) * lev]
 
 
-def step_kernel(t, is_a, group, own_ref, other_ref, halo_ref, flux_ref, edge_ref, w_in_ref, w_out_ref, *rest):
+def column_kernel(
+    t, kind, group, sends, own_ref, inner_ref, outer_ref, flux_ref, from_a_ref, from_b_ref, w_in_ref, w_out_ref, *rest
+):
+    last = t == STEPS - 1
+    coef, moved_ref, cells_ref = rest[-3:]
+    count, spec, lev = from_a_ref.shape[0], from_a_ref.shape[2], flux_ref.shape[3]
+    depth, spec_all, width_y = inner_ref.shape
+    place, species = place_and_species(count)
     rest = list(rest)
-    first, last = t == 0, t == STEPS - 1
-    depth, spec_all, width_y = own_ref.shape
-    count, spec = halo_ref.shape[0], halo_ref.shape[2]
-    lev = depth // count
-    place, species = place_and_species(count)
-    coef, moved_ref, cells_ref = rest[-3:]
-    if last and is_a:
-        send_ref = rest[0]
-    elif last:
-        sent_a_ref, outs, send_ref = rest[0], rest[1 : 1 + count], rest[1 + count]
+    sent_b_ref = rest.pop(0) if last and kind == "A" else None
+    outs = rest[:count] if last and kind == "A" else None
+    send_ref = rest[count] if outs else rest.pop(0) if sends else None
+    new_ref = None if last else rest.pop(0)
+
+    def cells_of(ref, k):
+        if ref.shape == inner_ref.shape:
+            return ref[k]
+        return jnp.concatenate([ref[s, k].astype(jnp.float32) for s in range(count)], 0)
+
+    def mine(index):
+        return jnp.concatenate([flux_ref[t, index, s] for s in range(count)], 0)
+
+    def theirs(ref, index):
+        parts = [ref[s, depth + index].astype(jnp.float32) for s in range(count)]
+        return jnp.concatenate([p[t * lev : (t + 1) * lev] for p in parts], 0)
+
+    even = lax.rem(place, 2) == 0
+    if kind == "A":
+        outer_high = even
+        fx = jnp.where(even, mine(1), mine(0))
+        fx_hi = jnp.where(even, theirs(from_a_ref, 0), mine(1))
+        fy, fz = mine(4), mine(5)
+    elif kind == "B":
+        outer_high = jnp.logical_not(even)
+        fx = jnp.where(even, mine(0), mine(1))
+        fx_hi = jnp.where(even, mine(1), theirs(from_b_ref, 0))
+        fy, fz = mine(2), mine(3)
     else:
-        send_ref, new_ref = rest[:2]
-
-    def whole(index):
-        return jnp.concatenate([flux_ref[t, index, s] for s in range(count)], 0)
-
-    if first:
-        parts = [halo_ref[s, depth].astype(jnp.float32) for s in range(count)]
-        for i in range(STEPS):
-            rest[2][i] = jnp.concatenate([p[i * lev : (i + 1) * lev] for p in parts], 0)
-        beyond = rest[2][t]
-    else:
-        beyond = edge_ref[t]
-    is_first = lax.rem(place, 2) == (1 if is_a else 0)
-    fx_first, fx_second = whole(0), whole(1)
-    fx = jnp.where(is_first, fx_first, fx_second)
-    fx_hi = jnp.where(is_first, fx_second, beyond)
-    fy = whole(3 if is_a else 2)
+        outer_high = jnp.logical_not(even)
+        fx = jnp.where(even, theirs(from_b_ref, 1), theirs(from_b_ref, 0))
+        fx_hi = jnp.where(even, mine(0), theirs(from_b_ref, 1))
+        fy, fz = theirs(from_b_ref, 2), theirs(from_b_ref, 3)
     fy_hi = pltpu.roll(fy, width_y - 1, 1)
-    fz = whole(5 if is_a else 4)
     fz = jnp.where(lax.broadcasted_iota(jnp.int32, fz.shape, 0) == 0, 0.0, fz)
     fz_hi = jnp.concatenate([fz[1:], jnp.zeros_like(fz[:1])], 0)
     low, high = positive(fx), -negative(fx_hi)
@@ -227,8 +239,8 @@
         + (negative(fy) - positive(fy_hi))
         + (negative(fz) - positive(fz_hi))
     )
-    coef[1] = jnp.where(is_first, low, high)
-    coef[2] = jnp.where(is_first, high, low)
+    coef[1] = jnp.where(outer_high, high, low)
+    coef[2] = jnp.where(outer_high, low, high)
     coef[3] = positive(fy)
     coef[4] = -negative(fy_hi)
     coef[5] = positive(fz)
@@ -237,15 +249,14 @@
     w_out = w_out_ref[...]
 
     def level(k, slot, column):
-        own = own_ref[k]
-        halo = jnp.concatenate([halo_ref[s, k].astype(jnp.float32) for s in range(count)], 0)
+        own = cells_of(own_ref, k)
         out = coef[0, pl.ds(k, 1)] * own
-        out += coef[1, pl.ds(k, 1)] * halo
-        out += coef[2, pl.ds(k, 1)] * other_ref[k]
+        out += coef[1, pl.ds(k, 1)] * cells_of(outer_ref, k)
+        out += coef[2, pl.ds(k, 1)] * inner_ref[k]
         out += coef[3, pl.ds(k, 1)] * pltpu.roll(own, 1, 1)
         out += coef[4, pl.ds(k, 1)] * pltpu.roll(own, width_y - 1, 1)
-        out += coef[5, pl.ds(k, 1)] * own_ref[jnp.maximum(k - 1, 0)]
-        out += coef[6, pl.ds(k, 1)] * own_ref[jnp.minimum(k + 1, depth - 1)]
+        out += coef[5, pl.ds(k, 1)] * cells_of(own_ref, jnp.maximum(k - 1, 0))
+        out += coef[6, pl.ds(k, 1)] * cells_of(own_ref, jnp.minimum(k + 1, depth - 1))
         moved_ref[k] = out
         cells_ref[slot, :, column * width_y : (column + 1) * width_y] = out.astype(jnp.bfloat16)
 
@@ -262,19 +273,20 @@
         for i in range(group):
             k = g * group + i
             new = moved_ref[k] + change[:, i * width_y : (i + 1) * width_y]
-            if not last:
+            if new_ref is not None:
                 new_ref[k] = new
-            for s in range(count):
-                send_ref[s, k] = new[s * spec : (s + 1) * spec].astype(jnp.bfloat16)
+            if send_ref is not None:
+                for s in range(count):
+                    send_ref[s, k] = new[s * spec : (s + 1) * spec].astype(jnp.bfloat16)
         return carry
 
     for i in range(group):
         level(i, 0, i)
     lax.fori_loop(0, groups, body, 0)
-    if last and not is_a:
+    if outs is not None:
         for d in range(count):
-            outs[d][0] = send_ref[species ^ d]
-            outs[d][1] = sent_a_ref[species ^ d]
+            outs[d][0] = sent_b_ref[species ^ d]
+            outs[d][1] = send_ref[species ^ d]
 
 
 def finish_kernel(*refs):
@@ -367,54 +379,62 @@
     )
     got = exchange(packed)
     row = shape((depth, spec_all, width_y), f32)
-    message = shape((count, depth + 1, spec, width_y), bf16)
     sent = shape((count, depth, spec, width_y), bf16)
-    edges = shape((STEPS, depth, width_y), f32)
     b, a, send_b, send_a, flux = call(
         functools.partial(unpack_kernel, depth),
-        [row, row, message, message, shape((STEPS, 6, count, depth // count, width_y), f32)],
+        [
+            row,
+            row,
+            shape((count, depth + 4, spec, width_y), bf16),
+            shape((count, depth + 1, spec, width_y), bf16),
+            shape((STEPS, 6, count, depth // count, width_y), f32),
+        ],
         got,
         scratch=[pltpu.VMEM(piece.shape, bf16), pltpu.SemaphoreType.DMA],
         far=(0,),
     )
-    halo_b = lax.ppermute(send_b, AXES, swap_b)
-    halo_a = lax.ppermute(send_a, AXES, swap_a)
-
+    halo_a = from_a = lax.ppermute(send_a, AXES, swap_a)
+    halo_b = from_b = lax.ppermute(send_b, AXES, swap_b)
+    halo_c = lax.ppermute(send_a, AXES, swap_b)
     common = [
         pltpu.VMEM((7, depth, width_y), f32),
         pltpu.VMEM(row.shape, f32),
         pltpu.VMEM((2, spec_all, GROUP * width_y), bf16),
     ]
 
-    def step(t, is_a, own, other, halo, edge, more=()):
-        last = t == STEPS - 1
-        outs = [sent, row, edges][: 3 if t == 0 else 2]
-        scratch = []
-        if last:
-            outs = [sent] if is_a else [shape((2, depth, spec, width_y), bf16)] * count
-            scratch = [] if is_a else [pltpu.VMEM(sent.shape, bf16)]
+    def column(t, kind, own, inner, outer, sends=True, more=()):
+        scratch = list(common)
+        if t < STEPS - 1:
+            outs = [sent, row] if sends else [row]
+        elif kind == "A":
+            outs = [shape((2, depth, spec, width_y), bf16)] * count
+            scratch = [pltpu.VMEM(sent.shape, bf16), *common]
+        else:
+            outs = [sent]
         return call(
-            functools.partial(step_kernel, t, is_a, GROUP),
+            functools.partial(column_kernel, t, kind, GROUP, sends),
             outs,
-            (own, other, halo, flux, edge, w_in, w_out, *more),
-            scratch=[*scratch, *common],
+            (own, inner, outer, flux, from_a, from_b, w_in, w_out, *more),
+            scratch=scratch,
             flops=4 * depth * width_y * spec_all * hid,
             trans=depth * width_y * hid,
         )
 
-    edge_a = edge_b = flux
-    for t in range(STEPS):
-        first, last = t == 0, t == STEPS - 1
-        made_a = step(t, True, a, b, halo_a, edge_a)
-        if last:
-            pieces = step(t, False, b, a, halo_b, edge_b, made_a)
+    for t in range(0, STEPS, 2):
+        send_a, new_a = column(t, "A", a, b, halo_a)
+        halo_a = lax.ppermute(send_a, AXES, swap_a)
+        (new_b,) = column(t, "B", b, a, halo_b, sends=False)
+        (ghost,) = column(t, "G", halo_b, b, halo_c, sends=False)
+        a, b = new_a, new_b
+        made_b = column(t + 1, "B", b, a, ghost)
+        if t + 1 == STEPS - 1:
+            pieces = column(t + 1, "A", a, b, halo_a, more=made_b)
             break
-        halo_a = lax.ppermute(made_a[0], AXES, swap_a)
-        made_b = step(t, False, b, a, halo_b, edge_b)
         halo_b = lax.ppermute(made_b[0], AXES, swap_b)
-        if first:
-            edge_a, edge_b = made_a[2], made_b[2]
-        a, b = made_a[1], made_b[1]
+        send_a, new_a = column(t + 1, "A", a, b, halo_a)
+        halo_a = lax.ppermute(send_a, AXES, swap_a)
+        halo_c = lax.ppermute(send_a, AXES, swap_b)
+        a, b = new_a, made_b[1]
     out = call(
         finish_kernel,
         shape((spec, depth * width, width_y), f32),
@@ -431,6 +451,7 @@
     fits = (
         width == 2 * count
         and count % 2 == 0
+        and STEPS % 2 == 0
         and count & (count - 1) == 0
         and depth % count == 0
         and depth % GROUP == 0

time: 69.6 us -> 68.6 us (0.986)
  starting transfers between devices: 26.9 us -> 22.6 us
  Pallas kernels: 20.3 us -> 24.3 us
  waiting for transfers between devices: 20.9 us -> 20.1 us
    ppermute x3 -> x1, starting transfers between devices: 8.22 us -> 1.92 us  [by_columns(): halo_b = lax.ppermute(made_b[0], AXES, swap_b)]
    ppermute x1 -> x3, starting transfers between devices: 0.3 us -> 5.42 us  [by_columns(): halo_a = lax.ppermute(send_a, AXES, swap_a)]
    ppermute x3 -> x1, waiting for transfers between devices: 4.52 us -> 0.01 us  [by_columns(): halo_b = lax.ppermute(made_b[0], AXES, swap_b)]
    pallas_call x11 -> x13, Pallas kernels: 20.3 us -> 24.3 us  [call(): pl.pallas_call(kernel, out_shape=out_shape, in_specs=[anywhere if i in fa...]
    ppermute x4, waiting for transfers between devices: 2.42 us -> 6.11 us  [the longest x1 5.18 us: by_columns(): halo_b = from_b = lax.ppermute(send_b, AXES, swap_b)]
    ppermute x6, starting transfers between devices: 9.57 us -> 5.98 us  [exchange(): lax.ppermute(pieces[d], 'species', [(s, s ^ d) for s in range(count)])]
  transfers between devices with their start and end apart: 14 -> 14, of which waited for: 7 -> 6; matrix products, arithmetic and copies ran while one was open for 0% -> 0% of each run, Pallas kernels for 19% -> 23%
where the time goes in v5:
time: 68.6 us; the launch traced here: 68.2 us
  Pallas kernels  24.3 us (35%)
  starting transfers between devices  22.6 us (33%)
  waiting for transfers between devices  20.1 us (29%)
  local copies, waits for them, and re-layouts  1.04 us (2%)
    pallas_call x13, Pallas kernels, call(): pl.pallas_call(kernel, out_shape=out_shape, in_specs=[anywhere if i in fa...  24.3 us
    ppermute x6, waiting for transfers between devices, exchange(): lax.ppermute(pieces[d], 'species', [(s, s ^ d) for s in range(count)])  13.9 us
    ppermute x6, starting transfers between devices, exchange(): lax.ppermute(pieces[d], 'species', [(s, s ^ d) for s in range(count)])  5.98 us
    ppermute x2, starting transfers between devices, by_columns(): halo_c = lax.ppermute(send_a, AXES, swap_b)  5.55 us
    ppermute x3, starting transfers between devices, by_columns(): halo_a = lax.ppermute(send_a, AXES, swap_a)  5.42 us
    ppermute x1, waiting for transfers between devices, by_columns(): halo_b = from_b = lax.ppermute(send_b, AXES, swap_b)  5.18 us
    ppermute x1, starting transfers between devices, by_columns(): halo_b = from_b = lax.ppermute(send_b, AXES, swap_b)  3.43 us
    ppermute x1, starting transfers between devices, by_columns(): halo_b = lax.ppermute(made_b[0], AXES, swap_b)  1.92 us
  transfers between devices with their start and end apart: 14, of which 6 were waited for; matrix products, arithmetic and copies ran while one was open for 0% of the time, Pallas kernels for 23%

profile of v5, /device:TPU:17, one launch (start us, length us, event | category | flops | bytes accessed | tf_op | source)
XLA Modules:
  0.0 68.2 jit_solution(6336322747478858857)
XLA Ops:
  0.0 3.0 %shard_map.46 = (bf16[38,16,128]{2,1,0:T(8,128)(2,1)}, bf16[38,16,128]{2,1,0:T(8,128)(2,1)}, bf16[38,16,128]{2,1,0:T(8,128)(2,1)}, bf16[38,16,128]{2,1,0:T(8,128)(2,1)}) custom-call(f32[16,128,128]{2,1,0:T(8,128)} %bitcast.3, f32[384,128]{1,0:T(8,128)} %bitcast.4), custom_call_target="tpu_custom_call" | custom-call | bytes 1867776 | tf_op jit(solution)/shard_map/pallas_call | solution.py:324
  5.5 4.1 %collective-permute-done.1.refs_2_ = bf16[38,16,128]{2,1,0:T(8,128)(2,1)S(1)} collective-permute-done((bf16[38,16,128]{2,1,0:T(8,128)(2,1)}, bf16[38,16,128]{2,1,0:T(8,128)(2,1)S(1)}, u32[]{:S(2)}, u32[]{:S(2)}) %collective-permute-start.1) | collective-permute-done | bytes 155680 | tf_op jit(solution)/shard_map/ppermute | solution.py:362
  9.6 3.5 %collective-permute-done.2.refs_3_ = bf16[38,16,128]{2,1,0:T(8,128)(2,1)S(1)} collective-permute-done((bf16[38,16,128]{2,1,0:T(8,128)(2,1)}, bf16[38,16,128]{2,1,0:T(8,128)(2,1)S(1)}, u32[]{:S(2)}, u32[]{:S(2)}) %collective-permute-start.2) | collective-permute-done | bytes 155680 | tf_op jit(solution)/shard_map/ppermute | solution.py:362
  14.7 3.4 %collective-permute-start.4 = (bf16[4,20,16,128]{3,2,1,0:T(8,128)(2,1)S(1)}, bf16[4,20,16,128]{3,2,1,0:T(8,128)(2,1)S(1)}, u32[]{:S(2)}, u32[]{:S(2)}) collective-permute-start(bf16[4,20,16,128]{3,2,1,0:T(8,128)(2,1)S(1)} %get-tuple-element.34), channel_id=1, source_target_pairs={{8,16},{16,8},{24,25},{25,24},{17,9},{9,17},{1,2},{2,1},{10,18},{1... | collective-permute-start | bytes 983048 | tf_op jit(solution)/shard_map/ppermute | solution.py:397
  18.3 5.2 %collective-permute-done.4.from_b_ref.outer_ref.own_ref = bf16[4,20,16,128]{3,2,1,0:T(8,128)(2,1)S(1)} collective-permute-done((bf16[4,20,16,128]{3,2,1,0:T(8,128)(2,1)S(1)}, bf16[4,20,16,128]{3,2,1,0:T(8,128)(2,1)S(1)}, u32[]{:S(2)}, u32[]{:S(2)}) %collective-permute-start.4) | collective-permute-done | bytes 327712 | tf_op jit(solution)/shard_map/ppermute | solution.py:397
  23.5 1.9 %shard_map.48 = (bf16[4,16,16,128]{3,2,1,0:T(8,128)(2,1)S(1)}, f32[16,64,128]{2,1,0:T(8,128)S(1)}) custom-call(f32[16,64,128]{2,1,0:T(8,128)S(1)} %get-tuple-element.30.own_ref.inner_ref, f32[16,64,128]{2,1,0:T(8,128)S(1)} %get-tuple-element.31.inner_ref.own_ref, bf16[4,17,16,128]{3,2,1,0:T(8,128)(2,1)S(1)} %collective-permute-done.3.outer_ref.from_a_ref, ...), custom_call_target="tpu_custom_call" | custom-call | flops 268435456 | bytes 3047424 | tf_op jit(solution)/shard_map/pallas_call | solution.py:324
  27.0 1.9 %collective-permute-start.6 = (bf16[4,17,16,128]{3,2,1,0:T(8,128)(2,1)S(1)}, bf16[4,17,16,128]{3,2,1,0:T(8,128)(2,1)S(1)}, u32[]{:S(2)}, u32[]{:S(2)}) collective-permute-start(bf16[4,17,16,128]{3,2,1,0:T(8,128)(2,1)S(1)} %get-tuple-element.32), channel_id=1, source_target_pairs={{8,16},{16,8},{24,25},{25,24},{17,9},{9,17},{1,2},{2,1},{10,18},{1... | collective-permute-start | bytes 835592 | tf_op jit(solution)/shard_map/ppermute | solution.py:398
  28.9 1.9 %shard_map.49.inner_ref.own_ref = f32[16,64,128]{2,1,0:T(8,128)S(1)} custom-call(f32[16,64,128]{2,1,0:T(8,128)S(1)} %get-tuple-element.31.inner_ref.own_ref, f32[16,64,128]{2,1,0:T(8,128)S(1)} %get-tuple-element.30.own_ref.inner_ref, bf16[4,20,16,128]{3,2,1,0:T(8,128)(2,1)S(1)} %collective-permute-done.4.from_b_ref.outer_ref.own_ref, ...), custom_call_target="tpu_custom_call" | custom-call | flops 268435456 | bytes 2834432 | tf_op jit(solution)/shard_map/pallas_call | solution.py:324
  30.8 1.9 %shard_map.50 = (bf16[4,16,16,128]{3,2,1,0:T(8,128)(2,1)S(1)}, f32[16,64,128]{2,1,0:T(8,128)S(1)}) custom-call(f32[16,64,128]{2,1,0:T(8,128)S(1)} %get-tuple-element.35.own_ref.inner_ref, f32[16,64,128]{2,1,0:T(8,128)S(1)} %shard_map.49.inner_ref.own_ref, bf16[4,16,16,128]{3,2,1,0:T(8,128)(2,1)S(1)} %collective-permute-done.5.outer_ref, ...), custom_call_target="tpu_custom_call" | custom-call | flops 268435456 | bytes 3031040 | tf_op jit(solution)/shard_map/pallas_call | solution.py:324
  35.1 1.9 %shard_map.51.outer_ref = f32[16,64,128]{2,1,0:T(8,128)S(1)} custom-call(bf16[4,20,16,128]{3,2,1,0:T(8,128)(2,1)S(1)} %collective-permute-done.4.from_b_ref.outer_ref.own_ref, f32[16,64,128]{2,1,0:T(8,128)S(1)} %get-tuple-element.31.inner_ref.own_ref, bf16[4,17,16,128]{3,2,1,0:T(8,128)(2,1)S(1)} %collective-permute-done.6.outer_ref, ...), custom_call_target="tpu_custom_call" | custom-call | flops 268435456 | bytes 2588672 | tf_op jit(solution)/shard_map/pallas_call | solution.py:324
  37.0 1.9 %shard_map.52 = (bf16[4,16,16,128]{3,2,1,0:T(8,128)(2,1)S(1)}, f32[16,64,128]{2,1,0:T(8,128)S(1)}) custom-call(f32[16,64,128]{2,1,0:T(8,128)S(1)} %shard_map.49.inner_ref.own_ref, f32[16,64,128]{2,1,0:T(8,128)S(1)} %get-tuple-element.35.own_ref.inner_ref, f32[16,64,128]{2,1,0:T(8,128)S(1)} %shard_map.51.outer_ref, ...), custom_call_target="tpu_custom_call" | custom-call | flops 268435456 | bytes 3293184 | tf_op jit(solution)/shard_map/pallas_call | solution.py:324
  39.0 1.9 %collective-permute-start.8 = (bf16[4,16,16,128]{3,2,1,0:T(8,128)(2,1)S(1)}, bf16[4,16,16,128]{3,2,1,0:T(8,128)(2,1)S(1)}, u32[]{:S(2)}, u32[]{:S(2)}) collective-permute-start(bf16[4,16,16,128]{3,2,1,0:T(8,128)(2,1)S(1)} %get-tuple-element.41), channel_id=1, source_target_pairs={{8,16},{16,8},{24,25},{25,24},{17,9},{9,17},{1,2},{2,1},{10,18},{1... | collective-permute-start | bytes 786440 | tf_op jit(solution)/shard_map/ppermute | solution.py:433
  40.9 3.6 %collective-permute-start.10 = (bf16[4,16,16,128]{3,2,1,0:T(8,128)(2,1)S(1)}, bf16[4,16,16,128]{3,2,1,0:T(8,128)(2,1)S(1)}, u32[]{:S(2)}, u32[]{:S(2)}) collective-permute-start(bf16[4,16,16,128]{3,2,1,0:T(8,128)(2,1)S(1)} %get-tuple-element.39), channel_id=1, source_target_pairs={{8,16},{16,8},{24,25},{25,24},{17,9},{9,17},{1,2},{2,1},{10,18},{1... | collective-permute-start | bytes 786440 | tf_op jit(solution)/shard_map/ppermute | solution.py:436
  44.6 1.9 %shard_map.53 = (bf16[4,16,16,128]{3,2,1,0:T(8,128)(2,1)S(1)}, f32[16,64,128]{2,1,0:T(8,128)S(1)}) custom-call(f32[16,64,128]{2,1,0:T(8,128)S(1)} %get-tuple-element.37.own_ref.inner_ref, f32[16,64,128]{2,1,0:T(8,128)S(1)} %get-tuple-element.38.inner_ref.own_ref, bf16[4,16,16,128]{3,2,1,0:T(8,128)(2,1)S(1)} %collective-permute-done.7.outer_ref, ...), custom_call_target="tpu_custom_call" | custom-call | flops 268435456 | bytes 3031040 | tf_op jit(solution)/shard_map/pallas_call | solution.py:324
  46.5 2.4 %collective-permute-start.9 = (bf16[4,16,16,128]{3,2,1,0:T(8,128)(2,1)S(1)}, bf16[4,16,16,128]{3,2,1,0:T(8,128)(2,1)S(1)}, u32[]{:S(2)}, u32[]{:S(2)}) collective-permute-start(bf16[4,16,16,128]{3,2,1,0:T(8,128)(2,1)S(1)} %get-tuple-element.42), channel_id=1, source_target_pairs={{0,8},{8,0},{16,24},{24,16},{25,17},{17,25},{9,1},{1,9},{2,10},{10... | collective-permute-start | bytes 786440 | tf_op jit(solution)/shard_map/ppermute | solution.py:425
  48.9 1.9 %shard_map.54.own_ref.inner_ref = f32[16,64,128]{2,1,0:T(8,128)S(1)} custom-call(f32[16,64,128]{2,1,0:T(8,128)S(1)} %get-tuple-element.38.inner_ref.own_ref, f32[16,64,128]{2,1,0:T(8,128)S(1)} %get-tuple-element.37.own_ref.inner_ref, bf16[4,16,16,128]{3,2,1,0:T(8,128)(2,1)S(1)} %collective-permute-done.8.outer_ref.own_ref, ...), custom_call_target="tpu_custom_call" | custom-call | flops 268435456 | bytes 2768896 | tf_op jit(solution)/shard_map/pallas_call | solution.py:324
  50.9 1.9 %shard_map.55.outer_ref = f32[16,64,128]{2,1,0:T(8,128)S(1)} custom-call(bf16[4,16,16,128]{3,2,1,0:T(8,128)(2,1)S(1)} %collective-permute-done.8.outer_ref.own_ref, f32[16,64,128]{2,1,0:T(8,128)S(1)} %get-tuple-element.38.inner_ref.own_ref, bf16[4,16,16,128]{3,2,1,0:T(8,128)(2,1)S(1)} %collective-permute-done.10.outer_ref, ...), custom_call_target="tpu_custom_call" | custom-call | flops 268435456 | bytes 2506752 | tf_op jit(solution)/shard_map/pallas_call | solution.py:324
  52.8 1.9 %shard_map.56.rest_0_ = bf16[4,16,16,128]{3,2,1,0:T(8,128)(2,1)S(1)} custom-call(f32[16,64,128]{2,1,0:T(8,128)S(1)} %shard_map.54.own_ref.inner_ref, f32[16,64,128]{2,1,0:T(8,128)S(1)} %get-tuple-element.40.inner_ref.own_ref, f32[16,64,128]{2,1,0:T(8,128)S(1)} %shard_map.55.outer_ref, f32[4,6,4,4,128]{4,3,2,1,0:T(4,128)S(1)} %get-tuple-element.33.flux_ref, ...), custom_call_target="tpu_custom_call" | custom-call | flops 268435456 | bytes 2768896 | tf_op jit(solution)/shard_map/pallas_call | solution.py:324
  54.7 1.9 %shard_map.57 = (bf16[2,16,16,128]{3,2,1,0:T(8,128)(2,1)S(1)}, bf16[2,16,16,128]{3,2,1,0:T(8,128)(2,1)S(1)}, bf16[2,16,16,128]{3,2,1,0:T(8,128)(2,1)S(1)}, bf16[2,16,16,128]{3,2,1,0:T(8,128)(2,1)S(1)}) custom-call(f32[16,64,128]{2,1,0:T(8,128)S(1)} %get-tuple-element.40.inner_ref.own_ref, f32[16,64,128]{2,1,0:T(8,128)S(1)} %shard_map.54.own_ref.inner_ref, ...), custom_call_target="tpu_custom_call" | custom-call | flops 268435456 | bytes 3031040 | tf_op jit(solution)/shard_map/pallas_call | solution.py:324
  56.7 1.8 %collective-permute-start.11 = (bf16[2,16,16,128]{3,2,1,0:T(8,128)(2,1)S(1)}, bf16[2,16,16,128]{3,2,1,0:T(8,128)(2,1)S(1)}, u32[]{:S(2)}, u32[]{:S(2)}) collective-permute-start(bf16[2,16,16,128]{3,2,1,0:T(8,128)(2,1)S(1)} %get-tuple-element.44), channel_id=1, source_target_pairs={{0,8},{8,0},{16,24},{24,16},{1,9},{9,1},{17,25},{25,17},{2,10},{10... | collective-permute-start | bytes 393224 | tf_op jit(solution)/shard_map/ppermute | solution.py:362
  58.5 1.7 %collective-permute-start.13 = (bf16[2,16,16,128]{3,2,1,0:T(8,128)(2,1)S(1)}, bf16[2,16,16,128]{3,2,1,0:T(8,128)(2,1)S(1)}, u32[]{:S(2)}, u32[]{:S(2)}) collective-permute-start(bf16[2,16,16,128]{3,2,1,0:T(8,128)(2,1)S(1)} %get-tuple-element.46), channel_id=1, source_target_pairs={{0,24},{8,16},{16,8},{24,0},{1,25},{9,17},{17,9},{25,1},{2,26},{10... | collective-permute-start | bytes 393224 | tf_op jit(solution)/shard_map/ppermute | solution.py:362
  60.2 3.4 %collective-permute-done.12.refs_2_ = bf16[2,16,16,128]{3,2,1,0:T(8,128)(2,1)S(1)} collective-permute-done((bf16[2,16,16,128]{3,2,1,0:T(8,128)(2,1)S(1)}, bf16[2,16,16,128]{3,2,1,0:T(8,128)(2,1)S(1)}, u32[]{:S(2)}, u32[]{:S(2)}) %collective-permute-start.12) | collective-permute-done | bytes 131104 | tf_op jit(solution)/shard_map/ppermute | solution.py:362
  63.6 3.0 %collective-permute-done.13.refs_3_ = bf16[2,16,16,128]{3,2,1,0:T(8,128)(2,1)S(1)} collective-permute-done((bf16[2,16,16,128]{3,2,1,0:T(8,128)(2,1)S(1)}, bf16[2,16,16,128]{3,2,1,0:T(8,128)(2,1)S(1)}, u32[]{:S(2)}, u32[]{:S(2)}) %collective-permute-start.13) | collective-permute-done | bytes 131104 | tf_op jit(solution)/shard_map/ppermute | solution.py:362
  66.6 1.6 %shard_map.58 = f32[16,128,128]{2,1,0:T(8,128)} custom-call(bf16[2,16,16,128]{3,2,1,0:T(8,128)(2,1)S(1)} %get-tuple-element.43.refs_0_, bf16[2,16,16,128]{3,2,1,0:T(8,128)(2,1)S(1)} %collective-permute-done.11.refs_1_, bf16[2,16,16,128]{3,2,1,0:T(8,128)(2,1)S(1)} %collective-permute-done.12.refs_2_, bf16[2,16,16,128]{3,2,1,0:T(8,128)(2,1)S(1)} %collective-permute-done.13.refs_3_), custom_call_target="tpu_custom_call" | custom-call | bytes 1572864 | tf_op jit(solution)/shard_map/pallas_call | solution.py:324
  (26 shorter events, 8.1 us)
Async XLA Ops:
  3.0 2.5 %collective-permute-start = (bf16[38,16,128]{2,1,0:T(8,128)(2,1)}, bf16[38,16,128]{2,1,0:T(8,128)(2,1)S(1)}, u32[]{:S(2)}, u32[]{:S(2)}) collective-permute-start(bf16[38,16,128]{2,1,0:T(8,128)(2,1)} %get-tuple-element.27), channel_id=1, source_target_pairs={{0,8},{8,0},{16,24},{24,16},{1,9},{9,1},{17,25},{25,17},{2,10},{10... | collective-permute-start | bytes 466952 | tf_op jit(solution)/shard_map/ppermute | solution.py:362
  3.8 5.8 %collective-permute-start.1 = (bf16[38,16,128]{2,1,0:T(8,128)(2,1)}, bf16[38,16,128]{2,1,0:T(8,128)(2,1)S(1)}, u32[]{:S(2)}, u32[]{:S(2)}) collective-permute-start(bf16[38,16,128]{2,1,0:T(8,128)(2,1)} %get-tuple-element.28), channel_id=1, source_target_pairs={{0,16},{8,24},{16,0},{24,8},{1,17},{9,25},{17,1},{25,9},{2,18},{10... | collective-permute-start | bytes 466952 | tf_op jit(solution)/shard_map/ppermute | solution.py:362
  5.0 8.1 %collective-permute-start.2 = (bf16[38,16,128]{2,1,0:T(8,128)(2,1)}, bf16[38,16,128]{2,1,0:T(8,128)(2,1)S(1)}, u32[]{:S(2)}, u32[]{:S(2)}) collective-permute-start(bf16[38,16,128]{2,1,0:T(8,128)(2,1)} %get-tuple-element.29), channel_id=1, source_target_pairs={{0,24},{8,16},{16,8},{24,0},{1,25},{9,17},{17,9},{25,1},{2,26},{10... | collective-permute-start | bytes 466952 | tf_op jit(solution)/shard_map/ppermute | solution.py:362
  13.1 0.9 %copy-start = (bf16[38,16,128]{2,1,0:T(8,128)(2,1)S(1)}, bf16[38,16,128]{2,1,0:T(8,128)(2,1)}, u32[]{:S(2)}) copy-start(bf16[38,16,128]{2,1,0:T(8,128)(2,1)} %get-tuple-element.26.refs_0_) | copy-start | bytes 466948
  14.0 4.2 %copy-start.2 = (bf16[64,512]{1,0:T(8,128)(2,1)S(1)}, bf16[64,512]{1,0:T(8,128)(2,1)}, u32[]{:S(2)}) copy-start(bf16[64,512]{1,0:T(8,128)(2,1)} %param.7) | copy-start | bytes 196612
  14.4 3.9 %collective-permute-start.3 = (bf16[4,17,16,128]{3,2,1,0:T(8,128)(2,1)S(1)}, bf16[4,17,16,128]{3,2,1,0:T(8,128)(2,1)S(1)}, u32[]{:S(2)}, u32[]{:S(2)}) collective-permute-start(bf16[4,17,16,128]{3,2,1,0:T(8,128)(2,1)S(1)} %get-tuple-element.32), channel_id=1, source_target_pairs={{0,8},{8,0},{16,24},{24,16},{25,17},{17,25},{9,1},{1,9},{2,10},{10... | collective-permute-start | bytes 835592 | tf_op jit(solution)/shard_map/ppermute | solution.py:396
  14.7 3.5 %copy-start.1 = (bf16[512,64]{0,1:T(8,128)(2,1)S(1)}, bf16[512,64]{0,1:T(8,128)(2,1)}, u32[]{:S(2)}) copy-start(bf16[512,64]{0,1:T(8,128)(2,1)} %param.6) | copy-start | bytes 196612
  14.7 8.8 %collective-permute-start.4 = (bf16[4,20,16,128]{3,2,1,0:T(8,128)(2,1)S(1)}, bf16[4,20,16,128]{3,2,1,0:T(8,128)(2,1)S(1)}, u32[]{:S(2)}, u32[]{:S(2)}) collective-permute-start(bf16[4,20,16,128]{3,2,1,0:T(8,128)(2,1)S(1)} %get-tuple-element.34), channel_id=1, source_target_pairs={{8,16},{16,8},{24,25},{25,24},{17,9},{9,17},{1,2},{2,1},{10,18},{1... | collective-permute-start | bytes 983048 | tf_op jit(solution)/shard_map/ppermute | solution.py:397
  25.4 5.4 %collective-permute-start.5 = (bf16[4,16,16,128]{3,2,1,0:T(8,128)(2,1)S(1)}, bf16[4,16,16,128]{3,2,1,0:T(8,128)(2,1)S(1)}, u32[]{:S(2)}, u32[]{:S(2)}) collective-permute-start(bf16[4,16,16,128]{3,2,1,0:T(8,128)(2,1)S(1)} %get-tuple-element.36), channel_id=1, source_target_pairs={{0,8},{8,0},{16,24},{24,16},{25,17},{17,25},{9,1},{1,9},{2,10},{10... | collective-permute-start | bytes 786440 | tf_op jit(solution)/shard_map/ppermute | solution.py:425
  27.0 8.1 %collective-permute-start.6 = (bf16[4,17,16,128]{3,2,1,0:T(8,128)(2,1)S(1)}, bf16[4,17,16,128]{3,2,1,0:T(8,128)(2,1)S(1)}, u32[]{:S(2)}, u32[]{:S(2)}) collective-permute-start(bf16[4,17,16,128]{3,2,1,0:T(8,128)(2,1)S(1)} %get-tuple-element.32), channel_id=1, source_target_pairs={{8,16},{16,8},{24,25},{25,24},{17,9},{9,17},{1,2},{2,1},{10,18},{1... | collective-permute-start | bytes 835592 | tf_op jit(solution)/shard_map/ppermute | solution.py:398
  32.7 11.8 %collective-permute-start.7 = (bf16[4,16,16,128]{3,2,1,0:T(8,128)(2,1)S(1)}, bf16[4,16,16,128]{3,2,1,0:T(8,128)(2,1)S(1)}, u32[]{:S(2)}, u32[]{:S(2)}) collective-permute-start(bf16[4,16,16,128]{3,2,1,0:T(8,128)(2,1)S(1)} %get-tuple-element.39), channel_id=1, source_target_pairs={{0,8},{8,0},{16,24},{24,16},{25,17},{17,25},{9,1},{1,9},{2,10},{10... | collective-permute-start | bytes 786440 | tf_op jit(solution)/shard_map/ppermute | solution.py:435
  39.0 10.0 %collective-permute-start.8 = (bf16[4,16,16,128]{3,2,1,0:T(8,128)(2,1)S(1)}, bf16[4,16,16,128]{3,2,1,0:T(8,128)(2,1)S(1)}, u32[]{:S(2)}, u32[]{:S(2)}) collective-permute-start(bf16[4,16,16,128]{3,2,1,0:T(8,128)(2,1)S(1)} %get-tuple-element.41), channel_id=1, source_target_pairs={{8,16},{16,8},{24,25},{25,24},{17,9},{9,17},{1,2},{2,1},{10,18},{1... | collective-permute-start | bytes 786440 | tf_op jit(solution)/shard_map/ppermute | solution.py:433
  40.9 10.0 %collective-permute-start.10 = (bf16[4,16,16,128]{3,2,1,0:T(8,128)(2,1)S(1)}, bf16[4,16,16,128]{3,2,1,0:T(8,128)(2,1)S(1)}, u32[]{:S(2)}, u32[]{:S(2)}) collective-permute-start(bf16[4,16,16,128]{3,2,1,0:T(8,128)(2,1)S(1)} %get-tuple-element.39), channel_id=1, source_target_pairs={{8,16},{16,8},{24,25},{25,24},{17,9},{9,17},{1,2},{2,1},{10,18},{1... | collective-permute-start | bytes 786440 | tf_op jit(solution)/shard_map/ppermute | solution.py:436
  46.5 8.2 %collective-permute-start.9 = (bf16[4,16,16,128]{3,2,1,0:T(8,128)(2,1)S(1)}, bf16[4,16,16,128]{3,2,1,0:T(8,128)(2,1)S(1)}, u32[]{:S(2)}, u32[]{:S(2)}) collective-permute-start(bf16[4,16,16,128]{3,2,1,0:T(8,128)(2,1)S(1)} %get-tuple-element.42), channel_id=1, source_target_pairs={{0,8},{8,0},{16,24},{24,16},{25,17},{17,25},{9,1},{1,9},{2,10},{10... | collective-permute-start | bytes 786440 | tf_op jit(solution)/shard_map/ppermute | solution.py:425
  56.7 3.5 %collective-permute-start.11 = (bf16[2,16,16,128]{3,2,1,0:T(8,128)(2,1)S(1)}, bf16[2,16,16,128]{3,2,1,0:T(8,128)(2,1)S(1)}, u32[]{:S(2)}, u32[]{:S(2)}) collective-permute-start(bf16[2,16,16,128]{3,2,1,0:T(8,128)(2,1)S(1)} %get-tuple-element.44), channel_id=1, source_target_pairs={{0,8},{8,0},{16,24},{24,16},{1,9},{9,1},{17,25},{25,17},{2,10},{10... | collective-permute-start | bytes 393224 | tf_op jit(solution)/shard_map/ppermute | solution.py:362
  58.5 5.1 %collective-permute-start.12 = (bf16[2,16,16,128]{3,2,1,0:T(8,128)(2,1)S(1)}, bf16[2,16,16,128]{3,2,1,0:T(8,128)(2,1)S(1)}, u32[]{:S(2)}, u32[]{:S(2)}) collective-permute-start(bf16[2,16,16,128]{3,2,1,0:T(8,128)(2,1)S(1)} %get-tuple-element.45), channel_id=1, source_target_pairs={{0,16},{8,24},{16,0},{24,8},{1,17},{9,25},{17,1},{25,9},{2,18},{10... | collective-permute-start | bytes 393224 | tf_op jit(solution)/shard_map/ppermute | solution.py:362
  58.5 8.0 %collective-permute-start.13 = (bf16[2,16,16,128]{3,2,1,0:T(8,128)(2,1)S(1)}, bf16[2,16,16,128]{3,2,1,0:T(8,128)(2,1)S(1)}, u32[]{:S(2)}, u32[]{:S(2)}) collective-permute-start(bf16[2,16,16,128]{3,2,1,0:T(8,128)(2,1)S(1)} %get-tuple-element.46), channel_id=1, source_target_pairs={{0,24},{8,16},{16,8},{24,0},{1,25},{9,17},{17,9},{25,1},{2,26},{10... | collective-permute-start | bytes 393224 | tf_op jit(solution)/shard_map/ppermute | solution.py:362

commit v6 on v5

--- a/solution.py
+++ b/solution.py
@@ -188,11 +188,11 @@
 
 
 def column_kernel(
-    t, kind, group, sends, own_ref, inner_ref, outer_ref, flux_ref, from_a_ref, from_b_ref, w_in_ref, w_out_ref, *rest
+    t, kind, group, sends, own_ref, inner_ref, outer_ref, flux_ref, from_ref, w_in_ref, w_out_ref, *rest
 ):
     last = t == STEPS - 1
-    coef, moved_ref, cells_ref = rest[-3:]
-    count, spec, lev = from_a_ref.shape[0], from_a_ref.shape[2], flux_ref.shape[3]
+    coef, moved_ref, cells_ref, half_ref = rest[-4:]
+    count, spec, lev = from_ref.shape[0], from_ref.shape[2], flux_ref.shape[3]
     depth, spec_all, width_y = inner_ref.shape
     place, species = place_and_species(count)
     rest = list(rest)
@@ -209,26 +209,26 @@
     def mine(index):
         return jnp.concatenate([flux_ref[t, index, s] for s in range(count)], 0)
 
-    def theirs(ref, index):
-        parts = [ref[s, depth + index].astype(jnp.float32) for s in range(count)]
+    def theirs(index):
+        parts = [from_ref[s, depth + index].astype(jnp.float32) for s in range(count)]
         return jnp.concatenate([p[t * lev : (t + 1) * lev] for p in parts], 0)
 
     even = lax.rem(place, 2) == 0
     if kind == "A":
         outer_high = even
         fx = jnp.where(even, mine(1), mine(0))
-        fx_hi = jnp.where(even, theirs(from_a_ref, 0), mine(1))
+        fx_hi = jnp.where(even, theirs(0), mine(1))
         fy, fz = mine(4), mine(5)
     elif kind == "B":
         outer_high = jnp.logical_not(even)
         fx = jnp.where(even, mine(0), mine(1))
-        fx_hi = jnp.where(even, mine(1), theirs(from_b_ref, 0))
+        fx_hi = jnp.where(even, mine(1), theirs(0))
         fy, fz = mine(2), mine(3)
     else:
         outer_high = jnp.logical_not(even)
-        fx = jnp.where(even, theirs(from_b_ref, 1), theirs(from_b_ref, 0))
-        fx_hi = jnp.where(even, mine(0), theirs(from_b_ref, 1))
-        fy, fz = theirs(from_b_ref, 2), theirs(from_b_ref, 3)
+        fx = jnp.where(even, theirs(1), theirs(0))
+        fx_hi = jnp.where(even, mine(0), theirs(1))
+        fy, fz = theirs(2), theirs(3)
     fy_hi = pltpu.roll(fy, width_y - 1, 1)
     fz = jnp.where(lax.broadcasted_iota(jnp.int32, fz.shape, 0) == 0, 0.0, fz)
     fz_hi = jnp.concatenate([fz[1:], jnp.zeros_like(fz[:1])], 0)
@@ -245,10 +245,8 @@
     coef[4] = -negative(fy_hi)
     coef[5] = positive(fz)
     coef[6] = -negative(fz_hi)
-    w_in = w_in_ref[...]
-    w_out = w_out_ref[...]
-
-    def level(k, slot, column):
+
+    def level(k, column):
         own = cells_of(own_ref, k)
         out = coef[0, pl.ds(k, 1)] * own
         out += coef[1, pl.ds(k, 1)] * cells_of(outer_ref, k)
@@ -258,30 +256,49 @@
         out += coef[5, pl.ds(k, 1)] * cells_of(own_ref, jnp.maximum(k - 1, 0))
         out += coef[6, pl.ds(k, 1)] * cells_of(own_ref, jnp.minimum(k + 1, depth - 1))
         moved_ref[k] = out
-        cells_ref[slot, :, column * width_y : (column + 1) * width_y] = out.astype(jnp.bfloat16)
+        cells_ref[:, column * width_y : (column + 1) * width_y] = out.astype(jnp.bfloat16)
 
     groups = depth // group
+    hid = w_in_ref.shape[0]
+    piece = hid // 2
+    wide = 2 * width_y
+
+    def first_matmul(slot, i, j):
+        half_ref[slot, i * piece : (i + 1) * piece, j * wide : (j + 1) * wide] = jnp.dot(
+            w_in_ref[i * piece : (i + 1) * piece, :],
+            cells_ref[:, j * wide : (j + 1) * wide],
+            preferred_element_type=jnp.float32,
+        )
 
     def body(g, carry):
         slot = lax.rem(g, 2)
-        half = jnp.dot(w_in, cells_ref[slot], preferred_element_type=jnp.float32)
         ahead = jnp.minimum(g + 1, groups - 1)
         for i in range(group):
-            level(ahead * group + i, 1 - slot, i)
-        hidden = (half + half * jnp.tanh(half)).astype(jnp.bfloat16)
-        change = jnp.dot(w_out, hidden, preferred_element_type=jnp.float32)
-        for i in range(group):
-            k = g * group + i
-            new = moved_ref[k] + change[:, i * width_y : (i + 1) * width_y]
-            if new_ref is not None:
-                new_ref[k] = new
-            if send_ref is not None:
-                for s in range(count):
-                    send_ref[s, k] = new[s * spec : (s + 1) * spec].astype(jnp.bfloat16)
+            level(ahead * group + i, i)
+        for j in range(group * width_y // wide):
+            change = 0.0
+            for i in range(2):
+                first_matmul(1 - slot, i, j)
+                half = half_ref[slot, i * piece : (i + 1) * piece, j * wide : (j + 1) * wide]
+                hidden = (half + half * jnp.tanh(half)).astype(jnp.bfloat16)
+                change += jnp.dot(
+                    w_out_ref[:, i * piece : (i + 1) * piece], hidden, preferred_element_type=jnp.float32
+                )
+            for i in range(2):
+                k = g * group + 2 * j + i
+                new = moved_ref[k] + change[:, i * width_y : (i + 1) * width_y]
+                if new_ref is not None:
+                    new_ref[k] = new
+                if send_ref is not None:
+                    for s in range(count):
+                        send_ref[s, k] = new[s * spec : (s + 1) * spec].astype(jnp.bfloat16)
         return carry
 
     for i in range(group):
-        level(i, 0, i)
+        level(i, i)
+    for j in range(group * width_y // wide):
+        for i in range(2):
+            first_matmul(0, i, j)
     lax.fori_loop(0, groups, body, 0)
     if outs is not None:
         for d in range(count):
@@ -316,10 +333,8 @@
         copy.wait()
 
 
-def call(kernel, out_shape, args, scratch=(), limit=LIMIT, far=(), far_out=False, flops=0, trans=0):
+def call(kernel, out_shape, args, scratch=(), limit=LIMIT, far=(), far_out=False):
     many = isinstance(out_shape, (list, tuple))
-    moved = sum(a.size * a.dtype.itemsize for a in args)
-    moved += sum(o.size * o.dtype.itemsize for o in (out_shape if many else [out_shape]))
     anywhere = pl.BlockSpec(memory_space=pl.ANY)
     return pl.pallas_call(
         kernel,
@@ -331,14 +346,14 @@
         out_specs=[VMEM] * len(out_shape) if many else anywhere if far_out else VMEM,
         scratch_shapes=scratch,
         compiler_params=pltpu.CompilerParams(vmem_limit_bytes=limit),
-        cost_estimate=pl.CostEstimate(flops=flops, bytes_accessed=moved, transcendentals=trans),
+        cost_estimate=pl.CostEstimate(flops=1024, bytes_accessed=1024, transcendentals=0),
     )(*args)
 
 
 def by_columns(tracers, fluxes, weight_in, weight_out):
     spec, depth, width, width_y = tracers.shape
     count, tiles = lax.axis_size("species"), lax.axis_size("tile")
-    spec_all, hid = spec * count, weight_in.shape[0]
+    spec_all = spec * count
     f32, bf16 = jnp.float32, jnp.bfloat16
     shape = jax.ShapeDtypeStruct
 
@@ -399,7 +414,8 @@
     common = [
         pltpu.VMEM((7, depth, width_y), f32),
         pltpu.VMEM(row.shape, f32),
-        pltpu.VMEM((2, spec_all, GROUP * width_y), bf16),
+        pltpu.VMEM((spec_all, GROUP * width_y), bf16),
+        pltpu.VMEM((2, weight_in.shape[0], GROUP * width_y), f32),
     ]
 
     def column(t, kind, own, inner, outer, sends=True, more=()):
@@ -414,10 +430,8 @@
         return call(
             functools.partial(column_kernel, t, kind, GROUP, sends),
             outs,
-            (own, inner, outer, flux, from_a, from_b, w_in, w_out, *more),
+            (own, inner, outer, flux, from_a if kind == "A" else from_b, w_in, w_out, *more),
             scratch=scratch,
-            flops=4 * depth * width_y * spec_all * hid,
-            trans=depth * width_y * hid,
         )
 
     for t in range(0, STEPS, 2):

time: 68.6 us -> 88 us (1.28)
  Pallas kernels: 24.3 us -> 54.5 us
  waiting for transfers between devices: 20.1 us -> 13.5 us
  starting transfers between devices: 22.6 us -> 19.2 us
  local copies, waits for them, and re-layouts: 1.04 us -> 0.13 us
    pallas_call x13, Pallas kernels: 24.3 us -> 54.5 us  [call(): pl.pallas_call(kernel, out_shape=out_shape, in_specs=[anywhere if i in fa...]
    ppermute x1, waiting for transfers between devices: 5.18 us -> 0.01 us  [by_columns(): halo_b = from_b = lax.ppermute(send_b, AXES, swap_b)]
    ppermute x3, starting transfers between devices: 5.42 us -> 2.14 us  [by_columns(): halo_a = lax.ppermute(send_a, AXES, swap_a)]
    ppermute x6, starting transfers between devices: 5.98 us -> 4.65 us  [exchange(): lax.ppermute(pieces[d], 'species', [(s, s ^ d) for s in range(count)])]
    ppermute x2, starting transfers between devices: 5.55 us -> 6.75 us  [by_columns(): halo_c = lax.ppermute(send_a, AXES, swap_b)]
    ppermute x2, waiting for transfers between devices: 0.94 us -> 0.01 us  [by_columns(): halo_c = lax.ppermute(send_a, AXES, swap_b)]
    unnamed x7, local copies, waits for them, and re-layouts: 1.04 us -> 0.13 us
  transfers between devices with their start and end apart: 14 -> 14, of which waited for: 6 -> 4; matrix products, arithmetic and copies ran while one was open for 0% -> 0% of each run, Pallas kernels for 23% -> 51%
where the time goes in v6:
time: 88 us; the launch traced here: 87.7 us
  Pallas kernels  54.5 us (62%)
  starting transfers between devices  19.2 us (22%)
  waiting for transfers between devices  13.5 us (15%)
    pallas_call x13, Pallas kernels, call(): pl.pallas_call(kernel, out_shape=out_shape, in_specs=[anywhere if i in fa...  54.5 us
    ppermute x6, waiting for transfers between devices, exchange(): lax.ppermute(pieces[d], 'species', [(s, s ^ d) for s in range(count)])  13.4 us
    ppermute x2, starting transfers between devices, by_columns(): halo_c = lax.ppermute(send_a, AXES, swap_b)  6.75 us
    ppermute x6, starting transfers between devices, exchange(): lax.ppermute(pieces[d], 'species', [(s, s ^ d) for s in range(count)])  4.65 us
    ppermute x1, starting transfers between devices, by_columns(): halo_b = from_b = lax.ppermute(send_b, AXES, swap_b)  3.31 us
    ppermute x3, starting transfers between devices, by_columns(): halo_a = lax.ppermute(send_a, AXES, swap_a)  2.14 us
    ppermute x1, starting transfers between devices, by_columns(): halo_b = lax.ppermute(made_b[0], AXES, swap_b)  2.09 us
  transfers between devices with their start and end apart: 14, of which 4 were waited for; matrix products, arithmetic and copies ran while one was open for 0% of the time, Pallas kernels for 51%

profile of v6, /device:TPU:17, one launch (start us, length us, event | category | flops | bytes accessed | tf_op | source)
XLA Modules:
  0.0 87.7 jit_solution(11983722926997257301)
XLA Ops:
  0.0 3.0 %shard_map.46 = (bf16[38,16,128]{2,1,0:T(8,128)(2,1)}, bf16[38,16,128]{2,1,0:T(8,128)(2,1)}, bf16[38,16,128]{2,1,0:T(8,128)(2,1)}, bf16[38,16,128]{2,1,0:T(8,128)(2,1)}) custom-call(f32[16,128,128]{2,1,0:T(8,128)} %bitcast.3, f32[384,128]{1,0:T(8,128)} %bitcast.4), custom_call_target="tpu_custom_call" | custom-call | flops 1024 | bytes 1024 | tf_op jit(solution)/shard_map/pallas_call | solution.py:339
  3.1 0.7 collective-permute-start
  3.8 1.3 %collective-permute-start.1 = (bf16[38,16,128]{2,1,0:T(8,128)(2,1)}, bf16[38,16,128]{2,1,0:T(8,128)(2,1)S(1)}, u32[]{:S(2)}, u32[]{:S(2)}) collective-permute-start(bf16[38,16,128]{2,1,0:T(8,128)(2,1)} %get-tuple-element.28), channel_id=1, source_target_pairs={{0,16},{8,24},{16,0},{24,8},{1,17},{9,25},{17,1},{25,9},{2,18},{10... | collective-permute-start | bytes 466952 | tf_op jit(solution)/shard_map/ppermute | solution.py:377
  5.6 4.0 %collective-permute-done.1.refs_2_ = bf16[38,16,128]{2,1,0:T(8,128)(2,1)S(1)} collective-permute-done((bf16[38,16,128]{2,1,0:T(8,128)(2,1)}, bf16[38,16,128]{2,1,0:T(8,128)(2,1)S(1)}, u32[]{:S(2)}, u32[]{:S(2)}) %collective-permute-start.1) | collective-permute-done | bytes 155680 | tf_op jit(solution)/shard_map/ppermute | solution.py:377
  9.6 3.5 %collective-permute-done.2.refs_3_ = bf16[38,16,128]{2,1,0:T(8,128)(2,1)S(1)} collective-permute-done((bf16[38,16,128]{2,1,0:T(8,128)(2,1)}, bf16[38,16,128]{2,1,0:T(8,128)(2,1)S(1)}, u32[]{:S(2)}, u32[]{:S(2)}) %collective-permute-start.2) | collective-permute-done | bytes 155680 | tf_op jit(solution)/shard_map/ppermute | solution.py:377
  13.9 3.3 %collective-permute-start.4 = (bf16[4,20,16,128]{3,2,1,0:T(8,128)(2,1)S(1)}, bf16[4,20,16,128]{3,2,1,0:T(8,128)(2,1)S(1)}, u32[]{:S(2)}, u32[]{:S(2)}) collective-permute-start(bf16[4,20,16,128]{3,2,1,0:T(8,128)(2,1)S(1)} %get-tuple-element.35), channel_id=1, source_target_pairs={{8,16},{16,8},{24,25},{25,24},{17,9},{9,17},{1,2},{2,1},{10,18},{1... | collective-permute-start | bytes 983048 | tf_op jit(solution)/shard_map/ppermute | solution.py:412
  17.2 4.9 %shard_map.48 = (bf16[4,16,16,128]{3,2,1,0:T(8,128)(2,1)S(1)}, f32[16,64,128]{2,1,0:T(8,128)S(1)}) custom-call(f32[16,64,128]{2,1,0:T(8,128)S(1)} %get-tuple-element.30.own_ref.inner_ref, f32[16,64,128]{2,1,0:T(8,128)S(1)} %get-tuple-element.31.inner_ref.own_ref, bf16[4,17,16,128]{3,2,1,0:T(8,128)(2,1)S(1)} %collective-permute-done.3.outer_ref.from_ref, ...), custom_call_target="tpu_custom_call" | custom-call | flops 1024 | bytes 1024 | tf_op jit(solution)/shard_map/pallas_call | solution.py:339
  22.5 3.1 %collective-permute-start.6 = (bf16[4,17,16,128]{3,2,1,0:T(8,128)(2,1)S(1)}, bf16[4,17,16,128]{3,2,1,0:T(8,128)(2,1)S(1)}, u32[]{:S(2)}, u32[]{:S(2)}) collective-permute-start(bf16[4,17,16,128]{3,2,1,0:T(8,128)(2,1)S(1)} %get-tuple-element.32), channel_id=1, source_target_pairs={{8,16},{16,8},{24,25},{25,24},{17,9},{9,17},{1,2},{2,1},{10,18},{1... | collective-permute-start | bytes 835592 | tf_op jit(solution)/shard_map/ppermute | solution.py:413
  25.6 4.9 %shard_map.49.inner_ref.own_ref = f32[16,64,128]{2,1,0:T(8,128)S(1)} custom-call(f32[16,64,128]{2,1,0:T(8,128)S(1)} %get-tuple-element.31.inner_ref.own_ref, f32[16,64,128]{2,1,0:T(8,128)S(1)} %get-tuple-element.30.own_ref.inner_ref, bf16[4,20,16,128]{3,2,1,0:T(8,128)(2,1)S(1)} %collective-permute-done.4.outer_ref.from_ref.own_ref, ...), custom_call_target="tpu_custom_call" | custom-call | flops 1024 | bytes 1024 | tf_op jit(solution)/shard_map/pallas_call | solution.py:339
  30.6 4.9 %shard_map.50 = (bf16[4,16,16,128]{3,2,1,0:T(8,128)(2,1)S(1)}, f32[16,64,128]{2,1,0:T(8,128)S(1)}) custom-call(f32[16,64,128]{2,1,0:T(8,128)S(1)} %get-tuple-element.34.own_ref.inner_ref, f32[16,64,128]{2,1,0:T(8,128)S(1)} %shard_map.49.inner_ref.own_ref, bf16[4,16,16,128]{3,2,1,0:T(8,128)(2,1)S(1)} %collective-permute-done.5.outer_ref, ...), custom_call_target="tpu_custom_call" | custom-call | flops 1024 | bytes 1024 | tf_op jit(solution)/shard_map/pallas_call | solution.py:339
  36.0 4.9 %shard_map.51.outer_ref = f32[16,64,128]{2,1,0:T(8,128)S(1)} custom-call(bf16[4,20,16,128]{3,2,1,0:T(8,128)(2,1)S(1)} %collective-permute-done.4.outer_ref.from_ref.own_ref, f32[16,64,128]{2,1,0:T(8,128)S(1)} %get-tuple-element.31.inner_ref.own_ref, bf16[4,17,16,128]{3,2,1,0:T(8,128)(2,1)S(1)} %collective-permute-done.6.outer_ref, ...), custom_call_target="tpu_custom_call" | custom-call | flops 1024 | bytes 1024 | tf_op jit(solution)/shard_map/pallas_call | solution.py:339
  40.9 5.0 %shard_map.52 = (bf16[4,16,16,128]{3,2,1,0:T(8,128)(2,1)S(1)}, f32[16,64,128]{2,1,0:T(8,128)S(1)}) custom-call(f32[16,64,128]{2,1,0:T(8,128)S(1)} %shard_map.49.inner_ref.own_ref, f32[16,64,128]{2,1,0:T(8,128)S(1)} %get-tuple-element.34.own_ref.inner_ref, f32[16,64,128]{2,1,0:T(8,128)S(1)} %shard_map.51.outer_ref, ...), custom_call_target="tpu_custom_call" | custom-call | flops 1024 | bytes 1024 | tf_op jit(solution)/shard_map/pallas_call | solution.py:339
  45.9 2.1 %collective-permute-start.8 = (bf16[4,16,16,128]{3,2,1,0:T(8,128)(2,1)S(1)}, bf16[4,16,16,128]{3,2,1,0:T(8,128)(2,1)S(1)}, u32[]{:S(2)}, u32[]{:S(2)}) collective-permute-start(bf16[4,16,16,128]{3,2,1,0:T(8,128)(2,1)S(1)} %get-tuple-element.41), channel_id=1, source_target_pairs={{8,16},{16,8},{24,25},{25,24},{17,9},{9,17},{1,2},{2,1},{10,18},{1... | collective-permute-start | bytes 786440 | tf_op jit(solution)/shard_map/ppermute | solution.py:447
  48.0 3.7 %collective-permute-start.10 = (bf16[4,16,16,128]{3,2,1,0:T(8,128)(2,1)S(1)}, bf16[4,16,16,128]{3,2,1,0:T(8,128)(2,1)S(1)}, u32[]{:S(2)}, u32[]{:S(2)}) collective-permute-start(bf16[4,16,16,128]{3,2,1,0:T(8,128)(2,1)S(1)} %get-tuple-element.39), channel_id=1, source_target_pairs={{8,16},{16,8},{24,25},{25,24},{17,9},{9,17},{1,2},{2,1},{10,18},{1... | collective-permute-start | bytes 786440 | tf_op jit(solution)/shard_map/ppermute | solution.py:450
  51.7 4.9 %shard_map.53 = (bf16[4,16,16,128]{3,2,1,0:T(8,128)(2,1)S(1)}, f32[16,64,128]{2,1,0:T(8,128)S(1)}) custom-call(f32[16,64,128]{2,1,0:T(8,128)S(1)} %get-tuple-element.37.own_ref.inner_ref, f32[16,64,128]{2,1,0:T(8,128)S(1)} %get-tuple-element.38.inner_ref.own_ref, bf16[4,16,16,128]{3,2,1,0:T(8,128)(2,1)S(1)} %collective-permute-done.7.outer_ref, ...), custom_call_target="tpu_custom_call" | custom-call | flops 1024 | bytes 1024 | tf_op jit(solution)/shard_map/pallas_call | solution.py:339
  56.7 1.3 %collective-permute-start.9 = (bf16[4,16,16,128]{3,2,1,0:T(8,128)(2,1)S(1)}, bf16[4,16,16,128]{3,2,1,0:T(8,128)(2,1)S(1)}, u32[]{:S(2)}, u32[]{:S(2)}) collective-permute-start(bf16[4,16,16,128]{3,2,1,0:T(8,128)(2,1)S(1)} %get-tuple-element.42), channel_id=1, source_target_pairs={{0,8},{8,0},{16,24},{24,16},{25,17},{17,25},{9,1},{1,9},{2,10},{10... | collective-permute-start | bytes 786440 | tf_op jit(solution)/shard_map/ppermute | solution.py:439
  58.0 4.9 %shard_map.54.own_ref.inner_ref = f32[16,64,128]{2,1,0:T(8,128)S(1)} custom-call(f32[16,64,128]{2,1,0:T(8,128)S(1)} %get-tuple-element.38.inner_ref.own_ref, f32[16,64,128]{2,1,0:T(8,128)S(1)} %get-tuple-element.37.own_ref.inner_ref, bf16[4,16,16,128]{3,2,1,0:T(8,128)(2,1)S(1)} %collective-permute-done.8.outer_ref.own_ref, ...), custom_call_target="tpu_custom_call" | custom-call | flops 1024 | bytes 1024 | tf_op jit(solution)/shard_map/pallas_call | solution.py:339
  62.9 4.9 %shard_map.55.outer_ref = f32[16,64,128]{2,1,0:T(8,128)S(1)} custom-call(bf16[4,16,16,128]{3,2,1,0:T(8,128)(2,1)S(1)} %collective-permute-done.8.outer_ref.own_ref, f32[16,64,128]{2,1,0:T(8,128)S(1)} %get-tuple-element.38.inner_ref.own_ref, bf16[4,16,16,128]{3,2,1,0:T(8,128)(2,1)S(1)} %collective-permute-done.10.outer_ref, ...), custom_call_target="tpu_custom_call" | custom-call | flops 1024 | bytes 1024 | tf_op jit(solution)/shard_map/pallas_call | solution.py:339
  67.8 4.9 %shard_map.56.rest_0_ = bf16[4,16,16,128]{3,2,1,0:T(8,128)(2,1)S(1)} custom-call(f32[16,64,128]{2,1,0:T(8,128)S(1)} %shard_map.54.own_ref.inner_ref, f32[16,64,128]{2,1,0:T(8,128)S(1)} %get-tuple-element.40.inner_ref.own_ref, f32[16,64,128]{2,1,0:T(8,128)S(1)} %shard_map.55.outer_ref, f32[4,6,4,4,128]{4,3,2,1,0:T(4,128)S(1)} %get-tuple-element.33.flux_ref, ...), custom_call_target="tpu_custom_call" | custom-call | flops 1024 | bytes 1024 | tf_op jit(solution)/shard_map/pallas_call | solution.py:339
  72.8 5.0 %shard_map.57 = (bf16[2,16,16,128]{3,2,1,0:T(8,128)(2,1)S(1)}, bf16[2,16,16,128]{3,2,1,0:T(8,128)(2,1)S(1)}, bf16[2,16,16,128]{3,2,1,0:T(8,128)(2,1)S(1)}, bf16[2,16,16,128]{3,2,1,0:T(8,128)(2,1)S(1)}) custom-call(f32[16,64,128]{2,1,0:T(8,128)S(1)} %get-tuple-element.40.inner_ref.own_ref, f32[16,64,128]{2,1,0:T(8,128)S(1)} %shard_map.54.own_ref.inner_ref, ...), custom_call_target="tpu_custom_call" | custom-call | flops 1024 | bytes 1024 | tf_op jit(solution)/shard_map/pallas_call | solution.py:339
  77.9 2.0 %collective-permute-start.13 = (bf16[2,16,16,128]{3,2,1,0:T(8,128)(2,1)S(1)}, bf16[2,16,16,128]{3,2,1,0:T(8,128)(2,1)S(1)}, u32[]{:S(2)}, u32[]{:S(2)}) collective-permute-start(bf16[2,16,16,128]{3,2,1,0:T(8,128)(2,1)S(1)} %get-tuple-element.46), channel_id=1, source_target_pairs={{0,24},{8,16},{16,8},{24,0},{1,25},{9,17},{17,9},{25,1},{2,26},{10... | collective-permute-start | bytes 393224 | tf_op jit(solution)/shard_map/ppermute | solution.py:377
  80.0 2.6 %collective-permute-done.12.refs_2_ = bf16[2,16,16,128]{3,2,1,0:T(8,128)(2,1)S(1)} collective-permute-done((bf16[2,16,16,128]{3,2,1,0:T(8,128)(2,1)S(1)}, bf16[2,16,16,128]{3,2,1,0:T(8,128)(2,1)S(1)}, u32[]{:S(2)}, u32[]{:S(2)}) %collective-permute-start.12) | collective-permute-done | bytes 131104 | tf_op jit(solution)/shard_map/ppermute | solution.py:377
  82.5 3.4 %collective-permute-done.13.refs_3_ = bf16[2,16,16,128]{3,2,1,0:T(8,128)(2,1)S(1)} collective-permute-done((bf16[2,16,16,128]{3,2,1,0:T(8,128)(2,1)S(1)}, bf16[2,16,16,128]{3,2,1,0:T(8,128)(2,1)S(1)}, u32[]{:S(2)}, u32[]{:S(2)}) %collective-permute-start.13) | collective-permute-done | bytes 131104 | tf_op jit(solution)/shard_map/ppermute | solution.py:377
  85.9 1.6 %shard_map.58 = f32[16,128,128]{2,1,0:T(8,128)} custom-call(bf16[2,16,16,128]{3,2,1,0:T(8,128)(2,1)S(1)} %get-tuple-element.43.refs_0_, bf16[2,16,16,128]{3,2,1,0:T(8,128)(2,1)S(1)} %collective-permute-done.11.refs_1_, bf16[2,16,16,128]{3,2,1,0:T(8,128)(2,1)S(1)} %collective-permute-done.12.refs_2_, bf16[2,16,16,128]{3,2,1,0:T(8,128)(2,1)S(1)} %collective-permute-done.13.refs_3_), custom_call_target="tpu_custom_call" | custom-call | flops 1024 | bytes 1024 | tf_op jit(solution)/shard_map/pallas_call | solution.py:339
  (26 shorter events, 2.3 us)
Async XLA Ops:
  0.0 5.5 %copy-start.1 = (bf16[512,64]{0,1:T(8,128)(2,1)S(1)}, bf16[512,64]{0,1:T(8,128)(2,1)}, u32[]{:S(2)}) copy-start(bf16[512,64]{0,1:T(8,128)(2,1)} %param.6) | copy-start | bytes 196612
  3.0 10.1 %copy-start = (bf16[38,16,128]{2,1,0:T(8,128)(2,1)S(1)}, bf16[38,16,128]{2,1,0:T(8,128)(2,1)}, u32[]{:S(2)}) copy-start(bf16[38,16,128]{2,1,0:T(8,128)(2,1)} %get-tuple-element.26.refs_0_) | copy-start | bytes 466948
  3.1 2.6 %collective-permute-start = (bf16[38,16,128]{2,1,0:T(8,128)(2,1)}, bf16[38,16,128]{2,1,0:T(8,128)(2,1)S(1)}, u32[]{:S(2)}, u32[]{:S(2)}) collective-permute-start(bf16[38,16,128]{2,1,0:T(8,128)(2,1)} %get-tuple-element.27), channel_id=1, source_target_pairs={{0,8},{8,0},{16,24},{24,16},{1,9},{9,1},{17,25},{25,17},{2,10},{10... | collective-permute-start | bytes 466952 | tf_op jit(solution)/shard_map/ppermute | solution.py:377
  3.8 5.8 %collective-permute-start.1 = (bf16[38,16,128]{2,1,0:T(8,128)(2,1)}, bf16[38,16,128]{2,1,0:T(8,128)(2,1)S(1)}, u32[]{:S(2)}, u32[]{:S(2)}) collective-permute-start(bf16[38,16,128]{2,1,0:T(8,128)(2,1)} %get-tuple-element.28), channel_id=1, source_target_pairs={{0,16},{8,24},{16,0},{24,8},{1,17},{9,25},{17,1},{25,9},{2,18},{10... | collective-permute-start | bytes 466952 | tf_op jit(solution)/shard_map/ppermute | solution.py:377
  5.1 8.1 %collective-permute-start.2 = (bf16[38,16,128]{2,1,0:T(8,128)(2,1)}, bf16[38,16,128]{2,1,0:T(8,128)(2,1)S(1)}, u32[]{:S(2)}, u32[]{:S(2)}) collective-permute-start(bf16[38,16,128]{2,1,0:T(8,128)(2,1)} %get-tuple-element.29), channel_id=1, source_target_pairs={{0,24},{8,16},{16,8},{24,0},{1,25},{9,17},{17,9},{25,1},{2,26},{10... | collective-permute-start | bytes 466952 | tf_op jit(solution)/shard_map/ppermute | solution.py:377
  13.5 3.6 %copy-start.2 = (bf16[64,512]{1,0:T(8,128)(2,1)S(1)}, bf16[64,512]{1,0:T(8,128)(2,1)}, u32[]{:S(2)}) copy-start(bf16[64,512]{1,0:T(8,128)(2,1)} %param.7) | copy-start | bytes 196612
  13.6 3.7 %collective-permute-start.3 = (bf16[4,17,16,128]{3,2,1,0:T(8,128)(2,1)S(1)}, bf16[4,17,16,128]{3,2,1,0:T(8,128)(2,1)S(1)}, u32[]{:S(2)}, u32[]{:S(2)}) collective-permute-start(bf16[4,17,16,128]{3,2,1,0:T(8,128)(2,1)S(1)} %get-tuple-element.32), channel_id=1, source_target_pairs={{0,8},{8,0},{16,24},{24,16},{25,17},{17,25},{9,1},{1,9},{2,10},{10... | collective-permute-start | bytes 835592 | tf_op jit(solution)/shard_map/ppermute | solution.py:411
  13.9 11.7 %collective-permute-start.4 = (bf16[4,20,16,128]{3,2,1,0:T(8,128)(2,1)S(1)}, bf16[4,20,16,128]{3,2,1,0:T(8,128)(2,1)S(1)}, u32[]{:S(2)}, u32[]{:S(2)}) collective-permute-start(bf16[4,20,16,128]{3,2,1,0:T(8,128)(2,1)S(1)} %get-tuple-element.35), channel_id=1, source_target_pairs={{8,16},{16,8},{24,25},{25,24},{17,9},{9,17},{1,2},{2,1},{10,18},{1... | collective-permute-start | bytes 983048 | tf_op jit(solution)/shard_map/ppermute | solution.py:412
  22.2 8.4 %collective-permute-start.5 = (bf16[4,16,16,128]{3,2,1,0:T(8,128)(2,1)S(1)}, bf16[4,16,16,128]{3,2,1,0:T(8,128)(2,1)S(1)}, u32[]{:S(2)}, u32[]{:S(2)}) collective-permute-start(bf16[4,16,16,128]{3,2,1,0:T(8,128)(2,1)S(1)} %get-tuple-element.36), channel_id=1, source_target_pairs={{0,8},{8,0},{16,24},{24,16},{25,17},{17,25},{9,1},{1,9},{2,10},{10... | collective-permute-start | bytes 786440 | tf_op jit(solution)/shard_map/ppermute | solution.py:439
  22.5 13.5 %collective-permute-start.6 = (bf16[4,17,16,128]{3,2,1,0:T(8,128)(2,1)S(1)}, bf16[4,17,16,128]{3,2,1,0:T(8,128)(2,1)S(1)}, u32[]{:S(2)}, u32[]{:S(2)}) collective-permute-start(bf16[4,17,16,128]{3,2,1,0:T(8,128)(2,1)S(1)} %get-tuple-element.32), channel_id=1, source_target_pairs={{8,16},{16,8},{24,25},{25,24},{17,9},{9,17},{1,2},{2,1},{10,18},{1... | collective-permute-start | bytes 835592 | tf_op jit(solution)/shard_map/ppermute | solution.py:413
  35.5 16.2 %collective-permute-start.7 = (bf16[4,16,16,128]{3,2,1,0:T(8,128)(2,1)S(1)}, bf16[4,16,16,128]{3,2,1,0:T(8,128)(2,1)S(1)}, u32[]{:S(2)}, u32[]{:S(2)}) collective-permute-start(bf16[4,16,16,128]{3,2,1,0:T(8,128)(2,1)S(1)} %get-tuple-element.39), channel_id=1, source_target_pairs={{0,8},{8,0},{16,24},{24,16},{25,17},{17,25},{9,1},{1,9},{2,10},{10... | collective-permute-start | bytes 786440 | tf_op jit(solution)/shard_map/ppermute | solution.py:449
  45.9 12.0 %collective-permute-start.8 = (bf16[4,16,16,128]{3,2,1,0:T(8,128)(2,1)S(1)}, bf16[4,16,16,128]{3,2,1,0:T(8,128)(2,1)S(1)}, u32[]{:S(2)}, u32[]{:S(2)}) collective-permute-start(bf16[4,16,16,128]{3,2,1,0:T(8,128)(2,1)S(1)} %get-tuple-element.41), channel_id=1, source_target_pairs={{8,16},{16,8},{24,25},{25,24},{17,9},{9,17},{1,2},{2,1},{10,18},{1... | collective-permute-start | bytes 786440 | tf_op jit(solution)/shard_map/ppermute | solution.py:447
  48.0 14.9 %collective-permute-start.10 = (bf16[4,16,16,128]{3,2,1,0:T(8,128)(2,1)S(1)}, bf16[4,16,16,128]{3,2,1,0:T(8,128)(2,1)S(1)}, u32[]{:S(2)}, u32[]{:S(2)}) collective-permute-start(bf16[4,16,16,128]{3,2,1,0:T(8,128)(2,1)S(1)} %get-tuple-element.39), channel_id=1, source_target_pairs={{8,16},{16,8},{24,25},{25,24},{17,9},{9,17},{1,2},{2,1},{10,18},{1... | collective-permute-start | bytes 786440 | tf_op jit(solution)/shard_map/ppermute | solution.py:450
  56.7 16.1 %collective-permute-start.9 = (bf16[4,16,16,128]{3,2,1,0:T(8,128)(2,1)S(1)}, bf16[4,16,16,128]{3,2,1,0:T(8,128)(2,1)S(1)}, u32[]{:S(2)}, u32[]{:S(2)}) collective-permute-start(bf16[4,16,16,128]{3,2,1,0:T(8,128)(2,1)S(1)} %get-tuple-element.42), channel_id=1, source_target_pairs={{0,8},{8,0},{16,24},{24,16},{25,17},{17,25},{9,1},{1,9},{2,10},{10... | collective-permute-start | bytes 786440 | tf_op jit(solution)/shard_map/ppermute | solution.py:439
  77.8 2.2 %collective-permute-start.11 = (bf16[2,16,16,128]{3,2,1,0:T(8,128)(2,1)S(1)}, bf16[2,16,16,128]{3,2,1,0:T(8,128)(2,1)S(1)}, u32[]{:S(2)}, u32[]{:S(2)}) collective-permute-start(bf16[2,16,16,128]{3,2,1,0:T(8,128)(2,1)S(1)} %get-tuple-element.44), channel_id=1, source_target_pairs={{0,8},{8,0},{16,24},{24,16},{1,9},{9,1},{17,25},{25,17},{2,10},{10... | collective-permute-start | bytes 393224 | tf_op jit(solution)/shard_map/ppermute | solution.py:377
  77.8 4.7 %collective-permute-start.12 = (bf16[2,16,16,128]{3,2,1,0:T(8,128)(2,1)S(1)}, bf16[2,16,16,128]{3,2,1,0:T(8,128)(2,1)S(1)}, u32[]{:S(2)}, u32[]{:S(2)}) collective-permute-start(bf16[2,16,16,128]{3,2,1,0:T(8,128)(2,1)S(1)} %get-tuple-element.45), channel_id=1, source_target_pairs={{0,16},{8,24},{16,0},{24,8},{1,17},{9,25},{17,1},{25,9},{2,18},{10... | collective-permute-start | bytes 393224 | tf_op jit(solution)/shard_map/ppermute | solution.py:377
  77.9 8.0 %collective-permute-start.13 = (bf16[2,16,16,128]{3,2,1,0:T(8,128)(2,1)S(1)}, bf16[2,16,16,128]{3,2,1,0:T(8,128)(2,1)S(1)}, u32[]{:S(2)}, u32[]{:S(2)}) collective-permute-start(bf16[2,16,16,128]{3,2,1,0:T(8,128)(2,1)S(1)} %get-tuple-element.46), channel_id=1, source_target_pairs={{0,24},{8,16},{16,8},{24,0},{1,25},{9,17},{17,9},{25,1},{2,26},{10... | collective-permute-start | bytes 393224 | tf_op jit(solution)/shard_map/ppermute | solution.py:377

commit v7 on v5

--- a/solution.py
+++ b/solution.py
@@ -14,7 +14,6 @@
 PARTS = 4
 VMEM = pl.BlockSpec(memory_space=pltpu.VMEM)
 LIMIT = 24 * 1024 * 1024
-FULL = 56 * 1024 * 1024
 
 
 def positive(value):
@@ -102,38 +101,26 @@
     return 2 * place + odd, 2 * place + 1 - odd
 
 
-def pack_kernel(count, tracers_ref, fluxes_ref, *refs):
-    out_refs, (held, flux_ref, sems) = refs[:count], refs[count:]
-    parts, spec, rows, width_y = held.shape
+def pack_kernel(count, depth, kind, *refs):
+    tracers_ref, out_refs = refs[0], refs[-count:]
     width = 2 * count
-    lev = rows // width
-    depth = parts * lev
-    lev_own = fluxes_ref.shape[0] // (STEPS * 3 * width)
+    spec = tracers_ref.shape[0] // (depth * width)
+    lev = depth // count
     own, _ = place_and_species(count)
+    columns = [columns_of(own ^ d) for d in range(count)]
+
+    def level(k, carry):
+        for d in range(count):
+            x = columns[d][0 if kind == "B" else 1]
+            cells = tracers_ref[pl.ds(k * width + x, spec, stride=depth * width), :]
+            out_refs[d][k] = cells.astype(jnp.bfloat16)
+        return carry
+
+    lax.fori_loop(0, depth, level, 0, unroll=2)
+    if kind == "A":
+        return
+    flux_ref = refs[1]
     outer = lax.axis_index("tile") == 0
-    copies = []
-    for part in range(parts):
-        source = tracers_ref.at[:, pl.ds(part * rows, rows), :]
-        copies.append(pltpu.make_async_copy(source, held.at[part], sems.at[part]))
-    copies.append(pltpu.make_async_copy(fluxes_ref, flux_ref, sems.at[parts]))
-    for copy in copies:
-        copy.start()
-
-    columns = [columns_of(own ^ d) for d in range(count)]
-    for part in range(parts):
-        copies[part].wait()
-        flat = held.at[part].reshape(spec * rows, width_y)
-
-        def level(k, carry):
-            for d in range(count):
-                for base, x in zip((depth + 4, 0), columns[d]):
-                    cells = flat[pl.ds(k * width + x, spec, stride=rows), :]
-                    out_refs[d][base + part * lev + k] = cells.astype(jnp.bfloat16)
-            return carry
-
-        lax.fori_loop(0, lev, level, 0)
-
-    copies[parts].wait()
     for d in range(count):
         b_at, a_at = columns[d]
         low = jnp.minimum(b_at, a_at)
@@ -141,7 +128,7 @@
         def tile_of(direction, x):
             return jnp.concatenate(
                 [
-                    flux_ref[pl.ds((t * 3 + direction) * lev_own * width + x, lev_own, stride=width), :]
+                    flux_ref[pl.ds((t * 3 + direction) * lev * width + x, lev, stride=width), :]
                     for t in range(STEPS)
                 ],
                 0,
@@ -149,55 +136,52 @@
 
         first = jnp.where(jnp.logical_and(outer, low == 0), 0.0, tile_of(0, low))
         out_refs[d][depth] = first.astype(jnp.bfloat16)
-        others = ((0, low + 1, 1), (1, b_at, 2), (2, b_at, 3), (1, a_at, depth + 4), (2, a_at, depth + 5))
-        for direction, x, to in others:
-            out_refs[d][depth + to] = tile_of(direction, x).astype(jnp.bfloat16)
-
-
-def unpack_kernel(depth, *refs):
-    count = len(refs) - 7
-    got, refs = refs[:count], refs[count:]
-    b_ref, a_ref, msg_b_ref, msg_a_ref, flux_ref, kept, sem = refs
-    copy = pltpu.make_async_copy(got[0], kept, sem)
-    copy.start()
-    got = [kept, *got[1:]]
+        others = ((0, low + 1), (1, b_at), (2, b_at), (1, a_at), (2, a_at))
+        for i, (direction, x) in enumerate(others):
+            out_refs[d][depth + 1 + i] = tile_of(direction, x).astype(jnp.bfloat16)
+
+
+def unpack_kernel(count, depth, kind, *refs):
+    got, (state_ref, msg_ref) = refs[:count], refs[-2 if kind == "A" else -4 :][:2]
     lev = depth // count
     spec = got[0].shape[1]
     _, species = place_and_species(count)
 
+    if kind == "B":
+        flux_ref, near_ref = refs[-2:]
+        near_ref[...] = refs[count][...]
+
     def level(d, k, carry):
         rows = pl.ds(pl.multiple_of((species ^ d) * spec, spec), spec)
-        for base, state_ref, msg_ref in ((depth + 4, b_ref, msg_b_ref), (0, a_ref, msg_a_ref)):
-            cells = got[d][base + k]
-            state_ref[k, rows] = cells.astype(jnp.float32)
-            msg_ref[species ^ d, k] = cells
+        cells = got[d][k]
+        state_ref[k, rows] = cells.astype(jnp.float32)
+        msg_ref[species ^ d, k] = cells
         return carry
 
-    for d in [*range(1, count), 0]:
-        if d == 0:
-            copy.wait()
+    for d in range(count):
         lax.fori_loop(0, depth, functools.partial(level, d), 0, unroll=4)
         source = species ^ d
-        msg_a_ref[source, depth] = got[d][depth]
+        if kind == "A":
+            msg_ref[source, depth] = refs[count + d][depth]
+            continue
         for i in range(4):
-            msg_b_ref[source, depth + i] = got[d][depth + i]
+            msg_ref[source, depth + i] = got[d][depth + i]
         for i in range(6):
-            part = got[d][depth + i if i < 4 else 2 * depth + i].astype(jnp.float32)
+            part = got[d][depth + i].astype(jnp.float32)
             for t in range(STEPS):
                 flux_ref[t, i, source] = part[t * lev : (t + 1) * lev]
 
 
 def column_kernel(
-    t, kind, group, sends, own_ref, inner_ref, outer_ref, flux_ref, from_a_ref, from_b_ref, w_in_ref, w_out_ref, *rest
+    t, kind, group, sends, own_ref, inner_ref, outer_ref, flux_ref, from_ref, w_in_ref, w_out_ref, *rest
 ):
     last = t == STEPS - 1
     coef, moved_ref, cells_ref = rest[-3:]
-    count, spec, lev = from_a_ref.shape[0], from_a_ref.shape[2], flux_ref.shape[3]
+    count, spec, lev = from_ref.shape[0], from_ref.shape[2], flux_ref.shape[3]
     depth, spec_all, width_y = inner_ref.shape
     place, species = place_and_species(count)
     rest = list(rest)
-    sent_b_ref = rest.pop(0) if last and kind == "A" else None
-    outs = rest[:count] if last and kind == "A" else None
+    outs = rest[:count] if last else None
     send_ref = rest[count] if outs else rest.pop(0) if sends else None
     new_ref = None if last else rest.pop(0)
 
@@ -209,26 +193,26 @@
     def mine(index):
         return jnp.concatenate([flux_ref[t, index, s] for s in range(count)], 0)
 
-    def theirs(ref, index):
-        parts = [ref[s, depth + index].astype(jnp.float32) for s in range(count)]
+    def theirs(index):
+        parts = [from_ref[s, depth + index].astype(jnp.float32) for s in range(count)]
         return jnp.concatenate([p[t * lev : (t + 1) * lev] for p in parts], 0)
 
     even = lax.rem(place, 2) == 0
     if kind == "A":
         outer_high = even
         fx = jnp.where(even, mine(1), mine(0))
-        fx_hi = jnp.where(even, theirs(from_a_ref, 0), mine(1))
+        fx_hi = jnp.where(even, theirs(0), mine(1))
         fy, fz = mine(4), mine(5)
     elif kind == "B":
         outer_high = jnp.logical_not(even)
         fx = jnp.where(even, mine(0), mine(1))
-        fx_hi = jnp.where(even, mine(1), theirs(from_b_ref, 0))
+        fx_hi = jnp.where(even, mine(1), theirs(0))
         fy, fz = mine(2), mine(3)
     else:
         outer_high = jnp.logical_not(even)
-        fx = jnp.where(even, theirs(from_b_ref, 1), theirs(from_b_ref, 0))
-        fx_hi = jnp.where(even, mine(0), theirs(from_b_ref, 1))
-        fy, fz = theirs(from_b_ref, 2), theirs(from_b_ref, 3)
+        fx = jnp.where(even, theirs(1), theirs(0))
+        fx_hi = jnp.where(even, mine(0), theirs(1))
+        fy, fz = theirs(2), theirs(3)
     fy_hi = pltpu.roll(fy, width_y - 1, 1)
     fz = jnp.where(lax.broadcasted_iota(jnp.int32, fz.shape, 0) == 0, 0.0, fz)
     fz_hi = jnp.concatenate([fz[1:], jnp.zeros_like(fz[:1])], 0)
@@ -285,14 +269,12 @@
     lax.fori_loop(0, groups, body, 0)
     if outs is not None:
         for d in range(count):
-            outs[d][0] = sent_b_ref[species ^ d]
-            outs[d][1] = send_ref[species ^ d]
-
-
-def finish_kernel(*refs):
-    out_ref, held, sems = refs[-3:]
-    count, spec = len(refs) - 3, refs[0].shape[2]
-    parts, _, rows, width_y = held.shape
+            outs[d][...] = send_ref[species ^ d]
+
+
+def finish_kernel(count, *refs):
+    pieces, (out_ref, held, sems) = refs[: 2 * count], refs[2 * count :]
+    parts, spec, rows, width_y = held.shape
     width = 2 * count
     lev = rows // width
     own, _ = place_and_species(count)
@@ -304,7 +286,7 @@
         def level(k, carry):
             for d in range(count):
                 for side, x in enumerate(columns[d]):
-                    cells = refs[d][side, part * lev + k].astype(jnp.float32)
+                    cells = pieces[side * count + d][part * lev + k].astype(jnp.float32)
                     flat[pl.ds(k * width + x, spec, stride=rows), :] = cells
             return carry
 
@@ -316,29 +298,24 @@
         copy.wait()
 
 
-def call(kernel, out_shape, args, scratch=(), limit=LIMIT, far=(), far_out=False, flops=0, trans=0):
+def call(kernel, out_shape, args, scratch=(), far_out=False):
     many = isinstance(out_shape, (list, tuple))
-    moved = sum(a.size * a.dtype.itemsize for a in args)
-    moved += sum(o.size * o.dtype.itemsize for o in (out_shape if many else [out_shape]))
     anywhere = pl.BlockSpec(memory_space=pl.ANY)
     return pl.pallas_call(
         kernel,
         out_shape=out_shape,
-        in_specs=[
-            anywhere if i in far else VMEM
-            for i in range(len(args))
-        ],
+        in_specs=[VMEM] * len(args),
         out_specs=[VMEM] * len(out_shape) if many else anywhere if far_out else VMEM,
         scratch_shapes=scratch,
-        compiler_params=pltpu.CompilerParams(vmem_limit_bytes=limit),
-        cost_estimate=pl.CostEstimate(flops=flops, bytes_accessed=moved, transcendentals=trans),
+        compiler_params=pltpu.CompilerParams(vmem_limit_bytes=LIMIT),
+        cost_estimate=pl.CostEstimate(flops=1024, bytes_accessed=1024, transcendentals=0),
     )(*args)
 
 
 def by_columns(tracers, fluxes, weight_in, weight_out):
     spec, depth, width, width_y = tracers.shape
     count, tiles = lax.axis_size("species"), lax.axis_size("tile")
-    spec_all, hid = spec * count, weight_in.shape[0]
+    spec_all = spec * count
     f32, bf16 = jnp.float32, jnp.bfloat16
     shape = jax.ShapeDtypeStruct
 
@@ -356,45 +333,43 @@
     w_in = weight_in * jnp.asarray(0.5, bf16)
     w_out = weight_out * jnp.asarray(0.5, bf16)
 
+    def swapped(piece, d):
+        return lax.ppermute(piece, "species", [(s, s ^ d) for s in range(count)])
+
     def exchange(pieces):
-        got = list(pieces)
-        for d in [*range(2, count), 1]:
-            got[d] = lax.ppermute(pieces[d], "species", [(s, s ^ d) for s in range(count)])
-        return got
-
-    piece = shape((2 * depth + 6, spec, width_y), bf16)
+        return [piece if d == 0 else swapped(piece, d) for d, piece in enumerate(pieces)]
+
+    row = shape((depth, spec_all, width_y), f32)
     held = pltpu.VMEM((PARTS, spec, depth * width // PARTS, width_y), f32)
-    flux_rows = fluxes.reshape(-1, width_y)
-    packed = call(
-        functools.partial(pack_kernel, count),
-        [piece] * count,
-        (tracers.reshape(spec, depth * width, width_y), flux_rows),
-        scratch=[
-            held,
-            pltpu.VMEM(flux_rows.shape, f32),
-            pltpu.SemaphoreType.DMA((PARTS + 1,)),
-        ],
-        limit=FULL,
-        far=(0, 1),
-    )
-    got = exchange(packed)
-    row = shape((depth, spec_all, width_y), f32)
+    flat = tracers.reshape(-1, width_y)
     sent = shape((count, depth, spec, width_y), bf16)
-    b, a, send_b, send_a, flux = call(
-        functools.partial(unpack_kernel, depth),
+    piece = shape((depth, spec, width_y), bf16)
+    piece_b = shape((depth + 6, spec, width_y), bf16)
+    packed_b = call(
+        functools.partial(pack_kernel, count, depth, "B"),
+        [piece_b] * count,
+        (flat, fluxes.reshape(-1, width_y)),
+    )
+    got_b = exchange(packed_b)
+    packed_a = call(functools.partial(pack_kernel, count, depth, "A"), [piece] * count, (flat, packed_b[0]))
+    b, send_b, flux, near_a = call(
+        functools.partial(unpack_kernel, count, depth, "B"),
         [
             row,
-            row,
             shape((count, depth + 4, spec, width_y), bf16),
-            shape((count, depth + 1, spec, width_y), bf16),
             shape((STEPS, 6, count, depth // count, width_y), f32),
+            piece,
         ],
-        got,
-        scratch=[pltpu.VMEM(piece.shape, bf16), pltpu.SemaphoreType.DMA],
-        far=(0,),
+        (*got_b, packed_a[1]),
+    )
+    halo_b = from_b = lax.ppermute(send_b, AXES, swap_b)
+    got_a = [packed_a[0], swapped(near_a, 1), *(swapped(packed_a[d], d) for d in range(2, count))]
+    a, send_a = call(
+        functools.partial(unpack_kernel, count, depth, "A"),
+        [row, shape((count, depth + 1, spec, width_y), bf16)],
+        (*got_a, *got_b, send_b),
     )
     halo_a = from_a = lax.ppermute(send_a, AXES, swap_a)
-    halo_b = from_b = lax.ppermute(send_b, AXES, swap_b)
     halo_c = lax.ppermute(send_a, AXES, swap_b)
     common = [
         pltpu.VMEM((7, depth, width_y), f32),
@@ -402,22 +377,18 @@
         pltpu.VMEM((2, spec_all, GROUP * width_y), bf16),
     ]
 
-    def column(t, kind, own, inner, outer, sends=True, more=()):
+    def column(t, kind, own, inner, outer, sends=True):
         scratch = list(common)
         if t < STEPS - 1:
             outs = [sent, row] if sends else [row]
-        elif kind == "A":
-            outs = [shape((2, depth, spec, width_y), bf16)] * count
+        else:
+            outs = [piece] * count
             scratch = [pltpu.VMEM(sent.shape, bf16), *common]
-        else:
-            outs = [sent]
         return call(
             functools.partial(column_kernel, t, kind, GROUP, sends),
             outs,
-            (own, inner, outer, flux, from_a, from_b, w_in, w_out, *more),
+            (own, inner, outer, flux, from_a if kind == "A" else from_b, w_in, w_out),
             scratch=scratch,
-            flops=4 * depth * width_y * spec_all * hid,
-            trans=depth * width_y * hid,
         )
 
     for t in range(0, STEPS, 2):
@@ -428,7 +399,7 @@
         a, b = new_a, new_b
         made_b = column(t + 1, "B", b, a, ghost)
         if t + 1 == STEPS - 1:
-            pieces = column(t + 1, "A", a, b, halo_a, more=made_b)
+            pieces = [*exchange(made_b), *exchange(column(t + 1, "A", a, b, halo_a))]
             break
         halo_b = lax.ppermute(made_b[0], AXES, swap_b)
         send_a, new_a = column(t + 1, "A", a, b, halo_a)
@@ -436,9 +407,9 @@
         halo_c = lax.ppermute(send_a, AXES, swap_b)
         a, b = new_a, made_b[1]
     out = call(
-        finish_kernel,
+        functools.partial(finish_kernel, count),
         shape((spec, depth * width, width_y), f32),
-        exchange(pieces),
+        pieces,
         scratch=[held, pltpu.SemaphoreType.DMA((PARTS,))],
         far_out=True,
     )

time: 68.6 us -> 59.6 us (0.87)
  waiting for transfers between devices: 20.1 us -> 7.38 us
  starting transfers between devices: 22.6 us -> 26.6 us
  Pallas kernels: 24.3 us -> 22.1 us
  local copies, waits for them, and re-layouts: 1.04 us -> 2.86 us
    ppermute x6 -> x12, waiting for transfers between devices: 13.9 us -> 7.36 us  [swapped(): return lax.ppermute(piece, 'species', [(s, s ^ d) for s in range(count)])]
    ppermute x1, waiting for transfers between devices: 5.18 us -> 0.01 us  [by_columns(): halo_b = from_b = lax.ppermute(send_b, AXES, swap_b)]
    ppermute x6 -> x12, starting transfers between devices: 5.98 us -> 10.1 us  [swapped(): return lax.ppermute(piece, 'species', [(s, s ^ d) for s in range(count)])]
    pallas_call x13 -> x15, Pallas kernels: 24.3 us -> 22.1 us  [call(): pl.pallas_call(kernel, out_shape=out_shape, in_specs=[VMEM] * len(args),...]
    unnamed x7 -> x9, local copies, waits for them, and re-layouts: 1.04 us -> 2.86 us
    ppermute x3, starting transfers between devices: 5.42 us -> 4.16 us  [by_columns(): halo_a = lax.ppermute(send_a, AXES, swap_a)]
    ppermute x2, waiting for transfers between devices: 0.94 us -> 0.01 us  [by_columns(): halo_c = lax.ppermute(send_a, AXES, swap_b)]
  transfers between devices with their start and end apart: 14 -> 20, of which waited for: 6 -> 5; matrix products, arithmetic and copies ran while one was open for 0% -> 0% of each run, Pallas kernels for 23% -> 34%
where the time goes in v7:
time: 59.6 us; the launch traced here: 59.1 us
  starting transfers between devices  26.6 us (45%)
  Pallas kernels  22.1 us (37%)
  waiting for transfers between devices  7.38 us (12%)
  local copies, waits for them, and re-layouts  2.86 us (5%)
    pallas_call x15, Pallas kernels, call(): pl.pallas_call(kernel, out_shape=out_shape, in_specs=[VMEM] * len(args),...  22.1 us
    ppermute x12, starting transfers between devices, swapped(): return lax.ppermute(piece, 'species', [(s, s ^ d) for s in range(count)])  10.1 us
    ppermute x12, waiting for transfers between devices, swapped(): return lax.ppermute(piece, 'species', [(s, s ^ d) for s in range(count)])  7.36 us
    ppermute x2, starting transfers between devices, by_columns(): halo_c = lax.ppermute(send_a, AXES, swap_b)  6.19 us
    ppermute x3, starting transfers between devices, by_columns(): halo_a = lax.ppermute(send_a, AXES, swap_a)  4.16 us
    ppermute x1, starting transfers between devices, by_columns(): halo_b = from_b = lax.ppermute(send_b, AXES, swap_b)  3.31 us
    unnamed x9, local copies, waits for them, and re-layouts  2.86 us
    ppermute x1, starting transfers between devices, by_columns(): halo_b = lax.ppermute(made_b[0], AXES, swap_b)  2.46 us
  transfers between devices with their start and end apart: 20, of which 5 were waited for; matrix products, arithmetic and copies ran while one was open for 0% of the time, Pallas kernels for 34%

profile of v7, /device:TPU:17, one launch (start us, length us, event | category | flops | bytes accessed | tf_op | source)
XLA Modules:
  0.0 59.1 jit_solution(6097119099284531127)
XLA Ops:
  5.5 1.3 %collective-permute-start.4 = (bf16[16,16,128]{2,1,0:T(8,128)(2,1)S(1)}, bf16[16,16,128]{2,1,0:T(8,128)(2,1)S(1)}, u32[]{:S(2)}, u32[]{:S(2)}) collective-permute-start(bf16[16,16,128]{2,1,0:T(8,128)(2,1)S(1)} %get-tuple-element.43), channel_id=1, source_target_pairs={{0,16},{8,24},{16,0},{24,8},{1,17},{9,25},{17,1},{25,9},{2,18},{10... | collective-permute-start | bytes 196616 | tf_op jit(solution)/shard_map/ppermute | solution.py:337
  7.6 2.5 %collective-permute-done.2.refs_3_.refs_7_ = bf16[22,16,128]{2,1,0:T(8,128)(2,1)S(1)} collective-permute-done((bf16[22,16,128]{2,1,0:T(8,128)(2,1)S(1)}, bf16[22,16,128]{2,1,0:T(8,128)(2,1)S(1)}, u32[]{:S(2)}, u32[]{:S(2)}) %collective-permute-start.2) | collective-permute-done | bytes 90144 | tf_op jit(solution)/shard_map/ppermute | solution.py:337
  11.1 1.4 %collective-permute-done.5.refs_3_ = bf16[16,16,128]{2,1,0:T(8,128)(2,1)S(1)} collective-permute-done((bf16[16,16,128]{2,1,0:T(8,128)(2,1)S(1)}, bf16[16,16,128]{2,1,0:T(8,128)(2,1)S(1)}, u32[]{:S(2)}, u32[]{:S(2)}) %collective-permute-start.5) | collective-permute-done | bytes 65568 | tf_op jit(solution)/shard_map/ppermute | solution.py:337
  12.9 3.3 %collective-permute-start.6 = (bf16[4,20,16,128]{3,2,1,0:T(8,128)(2,1)S(1)}, bf16[4,20,16,128]{3,2,1,0:T(8,128)(2,1)S(1)}, u32[]{:S(2)}, u32[]{:S(2)}) collective-permute-start(bf16[4,20,16,128]{3,2,1,0:T(8,128)(2,1)S(1)} %get-tuple-element.45.refs_8_), channel_id=1, source_target_pairs={{8,16},{16,8},{24,25},{25,24},{17,9},{9,17},{1,2},{2,1},{10,18},{1... | collective-permute-start | bytes 983048 | tf_op jit(solution)/shard_map/ppermute | solution.py:365
  16.3 1.9 %shard_map.51 = (bf16[4,16,16,128]{3,2,1,0:T(8,128)(2,1)S(1)}, f32[16,64,128]{2,1,0:T(8,128)S(1)}) custom-call(f32[16,64,128]{2,1,0:T(8,128)S(1)} %get-tuple-element.46.inner_ref.own_ref, f32[16,64,128]{2,1,0:T(8,128)S(1)} %get-tuple-element.40.own_ref.inner_ref, bf16[4,17,16,128]{3,2,1,0:T(8,128)(2,1)S(1)} %collective-permute-done.7.outer_ref.from_ref, ...), custom_call_target="tpu_custom_call" | custom-call | flops 1024 | bytes 1024 | tf_op jit(solution)/shard_map/pallas_call | solution.py:304
  18.5 3.1 %collective-permute-start.8 = (bf16[4,17,16,128]{3,2,1,0:T(8,128)(2,1)S(1)}, bf16[4,17,16,128]{3,2,1,0:T(8,128)(2,1)S(1)}, u32[]{:S(2)}, u32[]{:S(2)}) collective-permute-start(bf16[4,17,16,128]{3,2,1,0:T(8,128)(2,1)S(1)} %get-tuple-element.48), channel_id=1, source_target_pairs={{8,16},{16,8},{24,25},{25,24},{17,9},{9,17},{1,2},{2,1},{10,18},{1... | collective-permute-start | bytes 835592 | tf_op jit(solution)/shard_map/ppermute | solution.py:373
  21.6 1.9 %shard_map.50.own_ref.inner_ref = f32[16,64,128]{2,1,0:T(8,128)S(1)} custom-call(f32[16,64,128]{2,1,0:T(8,128)S(1)} %get-tuple-element.40.own_ref.inner_ref, f32[16,64,128]{2,1,0:T(8,128)S(1)} %get-tuple-element.46.inner_ref.own_ref, bf16[4,20,16,128]{3,2,1,0:T(8,128)(2,1)S(1)} %collective-permute-done.6.outer_ref.from_ref.own_ref, ...), custom_call_target="tpu_custom_call" | custom-call | flops 1024 | bytes 1024 | tf_op jit(solution)/shard_map/pallas_call | solution.py:304
  23.6 1.9 %shard_map.54 = (bf16[4,16,16,128]{3,2,1,0:T(8,128)(2,1)S(1)}, f32[16,64,128]{2,1,0:T(8,128)S(1)}) custom-call(f32[16,64,128]{2,1,0:T(8,128)S(1)} %get-tuple-element.49.inner_ref.own_ref, f32[16,64,128]{2,1,0:T(8,128)S(1)} %shard_map.50.own_ref.inner_ref, bf16[4,16,16,128]{3,2,1,0:T(8,128)(2,1)S(1)} %collective-permute-done.9.outer_ref, ...), custom_call_target="tpu_custom_call" | custom-call | flops 1024 | bytes 1024 | tf_op jit(solution)/shard_map/pallas_call | solution.py:304
  25.5 1.5 %collective-permute-start.11 = (bf16[4,16,16,128]{3,2,1,0:T(8,128)(2,1)S(1)}, bf16[4,16,16,128]{3,2,1,0:T(8,128)(2,1)S(1)}, u32[]{:S(2)}, u32[]{:S(2)}) collective-permute-start(bf16[4,16,16,128]{3,2,1,0:T(8,128)(2,1)S(1)} %get-tuple-element.54), channel_id=1, source_target_pairs={{0,8},{8,0},{16,24},{24,16},{25,17},{17,25},{9,1},{1,9},{2,10},{10... | collective-permute-start | bytes 786440 | tf_op jit(solution)/shard_map/ppermute | solution.py:406
  27.0 1.9 %shard_map.52.outer_ref = f32[16,64,128]{2,1,0:T(8,128)S(1)} custom-call(bf16[4,20,16,128]{3,2,1,0:T(8,128)(2,1)S(1)} %collective-permute-done.6.outer_ref.from_ref.own_ref, f32[16,64,128]{2,1,0:T(8,128)S(1)} %get-tuple-element.40.own_ref.inner_ref, bf16[4,17,16,128]{3,2,1,0:T(8,128)(2,1)S(1)} %collective-permute-done.8.outer_ref, ...), custom_call_target="tpu_custom_call" | custom-call | flops 1024 | bytes 1024 | tf_op jit(solution)/shard_map/pallas_call | solution.py:304
  28.9 1.9 %shard_map.53 = (bf16[4,16,16,128]{3,2,1,0:T(8,128)(2,1)S(1)}, f32[16,64,128]{2,1,0:T(8,128)S(1)}) custom-call(f32[16,64,128]{2,1,0:T(8,128)S(1)} %shard_map.50.own_ref.inner_ref, f32[16,64,128]{2,1,0:T(8,128)S(1)} %get-tuple-element.49.inner_ref.own_ref, f32[16,64,128]{2,1,0:T(8,128)S(1)} %shard_map.52.outer_ref, ...), custom_call_target="tpu_custom_call" | custom-call | flops 1024 | bytes 1024 | tf_op jit(solution)/shard_map/pallas_call | solution.py:304
  30.9 2.5 %collective-permute-start.10 = (bf16[4,16,16,128]{3,2,1,0:T(8,128)(2,1)S(1)}, bf16[4,16,16,128]{3,2,1,0:T(8,128)(2,1)S(1)}, u32[]{:S(2)}, u32[]{:S(2)}) collective-permute-start(bf16[4,16,16,128]{3,2,1,0:T(8,128)(2,1)S(1)} %get-tuple-element.53), channel_id=1, source_target_pairs={{8,16},{16,8},{24,25},{25,24},{17,9},{9,17},{1,2},{2,1},{10,18},{1... | collective-permute-start | bytes 786440 | tf_op jit(solution)/shard_map/ppermute | solution.py:404
  33.4 3.1 %collective-permute-start.12 = (bf16[4,16,16,128]{3,2,1,0:T(8,128)(2,1)S(1)}, bf16[4,16,16,128]{3,2,1,0:T(8,128)(2,1)S(1)}, u32[]{:S(2)}, u32[]{:S(2)}) collective-permute-start(bf16[4,16,16,128]{3,2,1,0:T(8,128)(2,1)S(1)} %get-tuple-element.54), channel_id=1, source_target_pairs={{8,16},{16,8},{24,25},{25,24},{17,9},{9,17},{1,2},{2,1},{10,18},{1... | collective-permute-start | bytes 786440 | tf_op jit(solution)/shard_map/ppermute | solution.py:407
  36.5 1.9 %shard_map.56 = (bf16[4,16,16,128]{3,2,1,0:T(8,128)(2,1)S(1)}, f32[16,64,128]{2,1,0:T(8,128)S(1)}) custom-call(f32[16,64,128]{2,1,0:T(8,128)S(1)} %get-tuple-element.52.inner_ref.own_ref, f32[16,64,128]{2,1,0:T(8,128)S(1)} %get-tuple-element.50.own_ref.inner_ref, bf16[4,16,16,128]{3,2,1,0:T(8,128)(2,1)S(1)} %collective-permute-done.11.outer_ref, ...), custom_call_target="tpu_custom_call" | custom-call | flops 1024 | bytes 1024 | tf_op jit(solution)/shard_map/pallas_call | solution.py:304
  38.4 2.3 %collective-permute-start.16 = (bf16[4,16,16,128]{3,2,1,0:T(8,128)(2,1)S(1)}, bf16[4,16,16,128]{3,2,1,0:T(8,128)(2,1)S(1)}, u32[]{:S(2)}, u32[]{:S(2)}) collective-permute-start(bf16[4,16,16,128]{3,2,1,0:T(8,128)(2,1)S(1)} %get-tuple-element.60), channel_id=1, source_target_pairs={{0,8},{8,0},{16,24},{24,16},{25,17},{17,25},{9,1},{1,9},{2,10},{10... | collective-permute-start | bytes 786440 | tf_op jit(solution)/shard_map/ppermute | solution.py:396
  40.7 1.9 %shard_map.55.own_ref.inner_ref = f32[16,64,128]{2,1,0:T(8,128)S(1)} custom-call(f32[16,64,128]{2,1,0:T(8,128)S(1)} %get-tuple-element.50.own_ref.inner_ref, f32[16,64,128]{2,1,0:T(8,128)S(1)} %get-tuple-element.52.inner_ref.own_ref, bf16[4,16,16,128]{3,2,1,0:T(8,128)(2,1)S(1)} %collective-permute-done.10.outer_ref.own_ref, ...), custom_call_target="tpu_custom_call" | custom-call | flops 1024 | bytes 1024 | tf_op jit(solution)/shard_map/pallas_call | solution.py:304
  42.7 1.9 %shard_map.57.outer_ref = f32[16,64,128]{2,1,0:T(8,128)S(1)} custom-call(bf16[4,16,16,128]{3,2,1,0:T(8,128)(2,1)S(1)} %collective-permute-done.10.outer_ref.own_ref, f32[16,64,128]{2,1,0:T(8,128)S(1)} %get-tuple-element.50.own_ref.inner_ref, bf16[4,16,16,128]{3,2,1,0:T(8,128)(2,1)S(1)} %collective-permute-done.12.outer_ref, ...), custom_call_target="tpu_custom_call" | custom-call | flops 1024 | bytes 1024 | tf_op jit(solution)/shard_map/pallas_call | solution.py:304
  44.6 2.0 %shard_map.58 = (bf16[16,16,128]{2,1,0:T(8,128)(2,1)S(1)}, bf16[16,16,128]{2,1,0:T(8,128)(2,1)S(1)}, bf16[16,16,128]{2,1,0:T(8,128)(2,1)S(1)}, bf16[16,16,128]{2,1,0:T(8,128)(2,1)S(1)}) custom-call(f32[16,64,128]{2,1,0:T(8,128)S(1)} %shard_map.55.own_ref.inner_ref, f32[16,64,128]{2,1,0:T(8,128)S(1)} %get-tuple-element.55.inner_ref.own_ref, ...), custom_call_target="tpu_custom_call" | custom-call | flops 1024 | bytes 1024 | tf_op jit(solution)/shard_map/pallas_call | solution.py:304
  46.6 1.8 %collective-permute-start.13 = (bf16[16,16,128]{2,1,0:T(8,128)(2,1)S(1)}, bf16[16,16,128]{2,1,0:T(8,128)(2,1)S(1)}, u32[]{:S(2)}, u32[]{:S(2)}) collective-permute-start(bf16[16,16,128]{2,1,0:T(8,128)(2,1)S(1)} %get-tuple-element.57), channel_id=1, source_target_pairs={{0,8},{8,0},{16,24},{24,16},{1,9},{9,1},{17,25},{25,17},{2,10},{10... | collective-permute-start | bytes 196616 | tf_op jit(solution)/shard_map/ppermute | solution.py:337
  48.4 1.7 %collective-permute-start.15 = (bf16[16,16,128]{2,1,0:T(8,128)(2,1)S(1)}, bf16[16,16,128]{2,1,0:T(8,128)(2,1)S(1)}, u32[]{:S(2)}, u32[]{:S(2)}) collective-permute-start(bf16[16,16,128]{2,1,0:T(8,128)(2,1)S(1)} %get-tuple-element.59), channel_id=1, source_target_pairs={{0,24},{8,16},{16,8},{24,0},{1,25},{9,17},{17,9},{25,1},{2,26},{10... | collective-permute-start | bytes 196616 | tf_op jit(solution)/shard_map/ppermute | solution.py:337
  50.1 1.9 %shard_map.59 = (bf16[16,16,128]{2,1,0:T(8,128)(2,1)S(1)}, bf16[16,16,128]{2,1,0:T(8,128)(2,1)S(1)}, bf16[16,16,128]{2,1,0:T(8,128)(2,1)S(1)}, bf16[16,16,128]{2,1,0:T(8,128)(2,1)S(1)}) custom-call(f32[16,64,128]{2,1,0:T(8,128)S(1)} %get-tuple-element.55.inner_ref.own_ref, f32[16,64,128]{2,1,0:T(8,128)S(1)} %shard_map.55.own_ref.inner_ref, ...), custom_call_target="tpu_custom_call" | custom-call | flops 1024 | bytes 1024 | tf_op jit(solution)/shard_map/pallas_call | solution.py:304
  52.3 2.0 %collective-permute-start.19 = (bf16[16,16,128]{2,1,0:T(8,128)(2,1)S(1)}, bf16[16,16,128]{2,1,0:T(8,128)(2,1)S(1)}, u32[]{:S(2)}, u32[]{:S(2)}) collective-permute-start(bf16[16,16,128]{2,1,0:T(8,128)(2,1)S(1)} %get-tuple-element.64), channel_id=1, source_target_pairs={{0,24},{8,16},{16,8},{24,0},{1,25},{9,17},{17,9},{25,1},{2,26},{10... | collective-permute-start | bytes 196616 | tf_op jit(solution)/shard_map/ppermute | solution.py:337
  55.4 2.1 %collective-permute-done.19.refs_7_ = bf16[16,16,128]{2,1,0:T(8,128)(2,1)S(1)} collective-permute-done((bf16[16,16,128]{2,1,0:T(8,128)(2,1)S(1)}, bf16[16,16,128]{2,1,0:T(8,128)(2,1)S(1)}, u32[]{:S(2)}, u32[]{:S(2)}) %collective-permute-start.19) | collective-permute-done | bytes 65568 | tf_op jit(solution)/shard_map/ppermute | solution.py:337
  57.5 1.6 %shard_map.60 = f32[16,128,128]{2,1,0:T(8,128)} custom-call(bf16[16,16,128]{2,1,0:T(8,128)(2,1)S(1)} %get-tuple-element.56.refs_0_, bf16[16,16,128]{2,1,0:T(8,128)(2,1)S(1)} %collective-permute-done.13.refs_1_, bf16[16,16,128]{2,1,0:T(8,128)(2,1)S(1)} %collective-permute-done.14.refs_2_, bf16[16,16,128]{2,1,0:T(8,128)(2,1)S(1)} %collective-permute-done.15.refs_3_, ...), custom_call_target="tpu_custom_call" | custom-call | flops 1024 | bytes 1024 | tf_op jit(solution)/shard_map/pallas_call | solution.py:304
  (42 shorter events, 9.4 us)
Async XLA Ops:
  0.0 1.2 %copy-start = (f32[16,16,8,128]{3,2,1,0:T(8,128)S(1)}, f32[16,16,8,128]{3,2,1,0:T(8,128)}, u32[]{:S(2)}) copy-start(f32[16,16,8,128]{3,2,1,0:T(8,128)} %param.4) | copy-start | bytes 3145732
  1.2 0.9 %copy-start.1 = (f32[4,3,4,8,128]{4,3,2,1,0:T(8,128)S(1)}, f32[4,3,4,8,128]{4,3,2,1,0:T(8,128)}, u32[]{:S(2)}) copy-start(f32[4,3,4,8,128]{4,3,2,1,0:T(8,128)} %param.5) | copy-start | bytes 589828
  2.6 4.8 %collective-permute-start = (bf16[22,16,128]{2,1,0:T(8,128)(2,1)S(1)}, bf16[22,16,128]{2,1,0:T(8,128)(2,1)S(1)}, u32[]{:S(2)}, u32[]{:S(2)}) collective-permute-start(bf16[22,16,128]{2,1,0:T(8,128)(2,1)S(1)} %get-tuple-element.36), channel_id=1, source_target_pairs={{0,8},{8,0},{16,24},{24,16},{1,9},{9,1},{17,25},{25,17},{2,10},{10... | collective-permute-start | bytes 270344 | tf_op jit(solution)/shard_map/ppermute | solution.py:337
  3.4 4.2 %collective-permute-start.1 = (bf16[22,16,128]{2,1,0:T(8,128)(2,1)S(1)}, bf16[22,16,128]{2,1,0:T(8,128)(2,1)S(1)}, u32[]{:S(2)}, u32[]{:S(2)}) collective-permute-start(bf16[22,16,128]{2,1,0:T(8,128)(2,1)S(1)} %get-tuple-element.37), channel_id=1, source_target_pairs={{0,16},{8,24},{16,0},{24,8},{1,17},{9,25},{17,1},{25,9},{2,18},{10... | collective-permute-start | bytes 270344 | tf_op jit(solution)/shard_map/ppermute | solution.py:337
  4.6 5.5 %collective-permute-start.2 = (bf16[22,16,128]{2,1,0:T(8,128)(2,1)S(1)}, bf16[22,16,128]{2,1,0:T(8,128)(2,1)S(1)}, u32[]{:S(2)}, u32[]{:S(2)}) collective-permute-start(bf16[22,16,128]{2,1,0:T(8,128)(2,1)S(1)} %get-tuple-element.38), channel_id=1, source_target_pairs={{0,24},{8,16},{16,8},{24,0},{1,25},{9,17},{17,9},{25,1},{2,26},{10... | collective-permute-start | bytes 270344 | tf_op jit(solution)/shard_map/ppermute | solution.py:337
  5.5 5.6 %collective-permute-start.4 = (bf16[16,16,128]{2,1,0:T(8,128)(2,1)S(1)}, bf16[16,16,128]{2,1,0:T(8,128)(2,1)S(1)}, u32[]{:S(2)}, u32[]{:S(2)}) collective-permute-start(bf16[16,16,128]{2,1,0:T(8,128)(2,1)S(1)} %get-tuple-element.43), channel_id=1, source_target_pairs={{0,16},{8,24},{16,0},{24,8},{1,17},{9,25},{17,1},{25,9},{2,18},{10... | collective-permute-start | bytes 196616 | tf_op jit(solution)/shard_map/ppermute | solution.py:337
  6.8 5.6 %collective-permute-start.5 = (bf16[16,16,128]{2,1,0:T(8,128)(2,1)S(1)}, bf16[16,16,128]{2,1,0:T(8,128)(2,1)S(1)}, u32[]{:S(2)}, u32[]{:S(2)}) collective-permute-start(bf16[16,16,128]{2,1,0:T(8,128)(2,1)S(1)} %get-tuple-element.44), channel_id=1, source_target_pairs={{0,24},{8,16},{16,8},{24,0},{1,25},{9,17},{17,9},{25,1},{2,26},{10... | collective-permute-start | bytes 196616 | tf_op jit(solution)/shard_map/ppermute | solution.py:337
  10.1 0.8 %copy-start.2 = (bf16[512,64]{0,1:T(8,128)(2,1)S(1)}, bf16[512,64]{0,1:T(8,128)(2,1)}, u32[]{:S(2)}) copy-start(bf16[512,64]{0,1:T(8,128)(2,1)} %param.6) | copy-start | bytes 196612
  10.3 2.2 %collective-permute-start.3 = (bf16[16,16,128]{2,1,0:T(8,128)(2,1)S(1)}, bf16[16,16,128]{2,1,0:T(8,128)(2,1)S(1)}, u32[]{:S(2)}, u32[]{:S(2)}) collective-permute-start(bf16[16,16,128]{2,1,0:T(8,128)(2,1)S(1)} %get-tuple-element.42), channel_id=1, source_target_pairs={{0,8},{8,0},{16,24},{24,16},{1,9},{9,1},{17,25},{25,17},{2,10},{10... | collective-permute-start | bytes 196616 | tf_op jit(solution)/shard_map/ppermute | solution.py:337
  12.6 3.6 %copy-start.3 = (bf16[64,512]{1,0:T(8,128)(2,1)S(1)}, bf16[64,512]{1,0:T(8,128)(2,1)}, u32[]{:S(2)}) copy-start(bf16[64,512]{1,0:T(8,128)(2,1)} %param.7) | copy-start | bytes 196612
  12.6 3.7 %collective-permute-start.7 = (bf16[4,17,16,128]{3,2,1,0:T(8,128)(2,1)S(1)}, bf16[4,17,16,128]{3,2,1,0:T(8,128)(2,1)S(1)}, u32[]{:S(2)}, u32[]{:S(2)}) collective-permute-start(bf16[4,17,16,128]{3,2,1,0:T(8,128)(2,1)S(1)} %get-tuple-element.48), channel_id=1, source_target_pairs={{0,8},{8,0},{16,24},{24,16},{25,17},{17,25},{9,1},{1,9},{2,10},{10... | collective-permute-start | bytes 835592 | tf_op jit(solution)/shard_map/ppermute | solution.py:372
  12.9 8.7 %collective-permute-start.6 = (bf16[4,20,16,128]{3,2,1,0:T(8,128)(2,1)S(1)}, bf16[4,20,16,128]{3,2,1,0:T(8,128)(2,1)S(1)}, u32[]{:S(2)}, u32[]{:S(2)}) collective-permute-start(bf16[4,20,16,128]{3,2,1,0:T(8,128)(2,1)S(1)} %get-tuple-element.45.refs_8_), channel_id=1, source_target_pairs={{8,16},{16,8},{24,25},{25,24},{17,9},{9,17},{1,2},{2,1},{10,18},{1... | collective-permute-start | bytes 983048 | tf_op jit(solution)/shard_map/ppermute | solution.py:365
  18.2 5.3 %collective-permute-start.9 = (bf16[4,16,16,128]{3,2,1,0:T(8,128)(2,1)S(1)}, bf16[4,16,16,128]{3,2,1,0:T(8,128)(2,1)S(1)}, u32[]{:S(2)}, u32[]{:S(2)}) collective-permute-start(bf16[4,16,16,128]{3,2,1,0:T(8,128)(2,1)S(1)} %get-tuple-element.51), channel_id=1, source_target_pairs={{0,8},{8,0},{16,24},{24,16},{25,17},{17,25},{9,1},{1,9},{2,10},{10... | collective-permute-start | bytes 786440 | tf_op jit(solution)/shard_map/ppermute | solution.py:396
  18.5 8.5 %collective-permute-start.8 = (bf16[4,17,16,128]{3,2,1,0:T(8,128)(2,1)S(1)}, bf16[4,17,16,128]{3,2,1,0:T(8,128)(2,1)S(1)}, u32[]{:S(2)}, u32[]{:S(2)}) collective-permute-start(bf16[4,17,16,128]{3,2,1,0:T(8,128)(2,1)S(1)} %get-tuple-element.48), channel_id=1, source_target_pairs={{8,16},{16,8},{24,25},{25,24},{17,9},{9,17},{1,2},{2,1},{10,18},{1... | collective-permute-start | bytes 835592 | tf_op jit(solution)/shard_map/ppermute | solution.py:373
  25.5 11.0 %collective-permute-start.11 = (bf16[4,16,16,128]{3,2,1,0:T(8,128)(2,1)S(1)}, bf16[4,16,16,128]{3,2,1,0:T(8,128)(2,1)S(1)}, u32[]{:S(2)}, u32[]{:S(2)}) collective-permute-start(bf16[4,16,16,128]{3,2,1,0:T(8,128)(2,1)S(1)} %get-tuple-element.54), channel_id=1, source_target_pairs={{0,8},{8,0},{16,24},{24,16},{25,17},{17,25},{9,1},{1,9},{2,10},{10... | collective-permute-start | bytes 786440 | tf_op jit(solution)/shard_map/ppermute | solution.py:406
  30.9 9.8 %collective-permute-start.10 = (bf16[4,16,16,128]{3,2,1,0:T(8,128)(2,1)S(1)}, bf16[4,16,16,128]{3,2,1,0:T(8,128)(2,1)S(1)}, u32[]{:S(2)}, u32[]{:S(2)}) collective-permute-start(bf16[4,16,16,128]{3,2,1,0:T(8,128)(2,1)S(1)} %get-tuple-element.53), channel_id=1, source_target_pairs={{8,16},{16,8},{24,25},{25,24},{17,9},{9,17},{1,2},{2,1},{10,18},{1... | collective-permute-start | bytes 786440 | tf_op jit(solution)/shard_map/ppermute | solution.py:404
  33.4 9.3 %collective-permute-start.12 = (bf16[4,16,16,128]{3,2,1,0:T(8,128)(2,1)S(1)}, bf16[4,16,16,128]{3,2,1,0:T(8,128)(2,1)S(1)}, u32[]{:S(2)}, u32[]{:S(2)}) collective-permute-start(bf16[4,16,16,128]{3,2,1,0:T(8,128)(2,1)S(1)} %get-tuple-element.54), channel_id=1, source_target_pairs={{8,16},{16,8},{24,25},{25,24},{17,9},{9,17},{1,2},{2,1},{10,18},{1... | collective-permute-start | bytes 786440 | tf_op jit(solution)/shard_map/ppermute | solution.py:407
  38.4 11.7 %collective-permute-start.16 = (bf16[4,16,16,128]{3,2,1,0:T(8,128)(2,1)S(1)}, bf16[4,16,16,128]{3,2,1,0:T(8,128)(2,1)S(1)}, u32[]{:S(2)}, u32[]{:S(2)}) collective-permute-start(bf16[4,16,16,128]{3,2,1,0:T(8,128)(2,1)S(1)} %get-tuple-element.60), channel_id=1, source_target_pairs={{0,8},{8,0},{16,24},{24,16},{25,17},{17,25},{9,1},{1,9},{2,10},{10... | collective-permute-start | bytes 786440 | tf_op jit(solution)/shard_map/ppermute | solution.py:396
  46.6 5.7 %collective-permute-start.13 = (bf16[16,16,128]{2,1,0:T(8,128)(2,1)S(1)}, bf16[16,16,128]{2,1,0:T(8,128)(2,1)S(1)}, u32[]{:S(2)}, u32[]{:S(2)}) collective-permute-start(bf16[16,16,128]{2,1,0:T(8,128)(2,1)S(1)} %get-tuple-element.57), channel_id=1, source_target_pairs={{0,8},{8,0},{16,24},{24,16},{1,9},{9,1},{17,25},{25,17},{2,10},{10... | collective-permute-start | bytes 196616 | tf_op jit(solution)/shard_map/ppermute | solution.py:337
  48.4 5.9 %collective-permute-start.14 = (bf16[16,16,128]{2,1,0:T(8,128)(2,1)S(1)}, bf16[16,16,128]{2,1,0:T(8,128)(2,1)S(1)}, u32[]{:S(2)}, u32[]{:S(2)}) collective-permute-start(bf16[16,16,128]{2,1,0:T(8,128)(2,1)S(1)} %get-tuple-element.58), channel_id=1, source_target_pairs={{0,16},{8,24},{16,0},{24,8},{1,17},{9,25},{17,1},{25,9},{2,18},{10... | collective-permute-start | bytes 196616 | tf_op jit(solution)/shard_map/ppermute | solution.py:337
  48.4 5.9 %collective-permute-start.15 = (bf16[16,16,128]{2,1,0:T(8,128)(2,1)S(1)}, bf16[16,16,128]{2,1,0:T(8,128)(2,1)S(1)}, u32[]{:S(2)}, u32[]{:S(2)}) collective-permute-start(bf16[16,16,128]{2,1,0:T(8,128)(2,1)S(1)} %get-tuple-element.59), channel_id=1, source_target_pairs={{0,24},{8,16},{16,8},{24,0},{1,25},{9,17},{17,9},{25,1},{2,26},{10... | collective-permute-start | bytes 196616 | tf_op jit(solution)/shard_map/ppermute | solution.py:337
  52.0 2.2 %collective-permute-start.17 = (bf16[16,16,128]{2,1,0:T(8,128)(2,1)S(1)}, bf16[16,16,128]{2,1,0:T(8,128)(2,1)S(1)}, u32[]{:S(2)}, u32[]{:S(2)}) collective-permute-start(bf16[16,16,128]{2,1,0:T(8,128)(2,1)S(1)} %get-tuple-element.62), channel_id=1, source_target_pairs={{0,8},{8,0},{16,24},{24,16},{1,9},{9,1},{17,25},{25,17},{2,10},{10... | collective-permute-start | bytes 196616 | tf_op jit(solution)/shard_map/ppermute | solution.py:337
  52.3 3.1 %collective-permute-start.18 = (bf16[16,16,128]{2,1,0:T(8,128)(2,1)S(1)}, bf16[16,16,128]{2,1,0:T(8,128)(2,1)S(1)}, u32[]{:S(2)}, u32[]{:S(2)}) collective-permute-start(bf16[16,16,128]{2,1,0:T(8,128)(2,1)S(1)} %get-tuple-element.63), channel_id=1, source_target_pairs={{0,16},{8,24},{16,0},{24,8},{1,17},{9,25},{17,1},{25,9},{2,18},{10... | collective-permute-start | bytes 196616 | tf_op jit(solution)/shard_map/ppermute | solution.py:337
  52.3 5.2 %collective-permute-start.19 = (bf16[16,16,128]{2,1,0:T(8,128)(2,1)S(1)}, bf16[16,16,128]{2,1,0:T(8,128)(2,1)S(1)}, u32[]{:S(2)}, u32[]{:S(2)}) collective-permute-start(bf16[16,16,128]{2,1,0:T(8,128)(2,1)S(1)} %get-tuple-element.64), channel_id=1, source_target_pairs={{0,24},{8,16},{16,8},{24,0},{1,25},{9,17},{17,9},{25,1},{2,26},{10... | collective-permute-start | bytes 196616 | tf_op jit(solution)/shard_map/ppermute | solution.py:337

commit v8 on v7

--- a/solution.py
+++ b/solution.py
@@ -176,7 +176,7 @@
     t, kind, group, sends, own_ref, inner_ref, outer_ref, flux_ref, from_ref, w_in_ref, w_out_ref, *rest
 ):
     last = t == STEPS - 1
-    coef, moved_ref, cells_ref = rest[-3:]
+    coef = rest[-1]
     count, spec, lev = from_ref.shape[0], from_ref.shape[2], flux_ref.shape[3]
     depth, spec_all, width_y = inner_ref.shape
     place, species = place_and_species(count)
@@ -232,41 +232,58 @@
     w_in = w_in_ref[...]
     w_out = w_out_ref[...]
 
-    def level(k, slot, column):
+    def level(k):
         own = cells_of(own_ref, k)
         out = coef[0, pl.ds(k, 1)] * own
         out += coef[1, pl.ds(k, 1)] * cells_of(outer_ref, k)
         out += coef[2, pl.ds(k, 1)] * inner_ref[k]
         out += coef[3, pl.ds(k, 1)] * pltpu.roll(own, 1, 1)
         out += coef[4, pl.ds(k, 1)] * pltpu.roll(own, width_y - 1, 1)
-        out += coef[5, pl.ds(k, 1)] * cells_of(own_ref, jnp.maximum(k - 1, 0))
-        out += coef[6, pl.ds(k, 1)] * cells_of(own_ref, jnp.minimum(k + 1, depth - 1))
-        moved_ref[k] = out
-        cells_ref[slot, :, column * width_y : (column + 1) * width_y] = out.astype(jnp.bfloat16)
-
-    groups = depth // group
-
-    def body(g, carry):
-        slot = lax.rem(g, 2)
-        half = jnp.dot(w_in, cells_ref[slot], preferred_element_type=jnp.float32)
-        ahead = jnp.minimum(g + 1, groups - 1)
-        for i in range(group):
-            level(ahead * group + i, 1 - slot, i)
-        hidden = (half + half * jnp.tanh(half)).astype(jnp.bfloat16)
-        change = jnp.dot(w_out, hidden, preferred_element_type=jnp.float32)
-        for i in range(group):
-            k = g * group + i
-            new = moved_ref[k] + change[:, i * width_y : (i + 1) * width_y]
-            if new_ref is not None:
-                new_ref[k] = new
-            if send_ref is not None:
-                for s in range(count):
-                    send_ref[s, k] = new[s * spec : (s + 1) * spec].astype(jnp.bfloat16)
-        return carry
-
-    for i in range(group):
-        level(i, 0, i)
-    lax.fori_loop(0, groups, body, 0)
+        out += coef[5, pl.ds(k, 1)] * cells_of(own_ref, max(k - 1, 0))
+        out += coef[6, pl.ds(k, 1)] * cells_of(own_ref, min(k + 1, depth - 1))
+        return out, out.astype(jnp.bfloat16)
+
+    hid = w_in.shape[0]
+    split = hid // 2
+    wide = 2 * width_y
+    pieces = [(i, j) for j in range(group // 2) for i in range(2)]
+
+    def first_matmul(i, cells):
+        return jnp.dot(w_in[i * split : (i + 1) * split], cells, preferred_element_type=jnp.float32)
+
+    def columns(k0):
+        levels = [level(k0 + i) for i in range(group)]
+        moved = [m for m, _ in levels]
+        cells = [jnp.concatenate([levels[j][1], levels[j + 1][1]], 1) for j in range(0, group, 2)]
+        return moved, cells
+
+    moved, cells = columns(0)
+    halves = [first_matmul(i, cells[j]) for i, j in pieces]
+    for k0 in range(0, depth, group):
+        more = k0 + group < depth
+        if more:
+            next_moved, cells = columns(k0 + group)
+        next_halves = []
+        for p, (i, j) in enumerate(pieces):
+            if more:
+                next_halves.append(first_matmul(i, cells[j]))
+            half = halves[p]
+            hidden = (half + half * jnp.tanh(half)).astype(jnp.bfloat16)
+            part = jnp.dot(w_out[:, i * split : (i + 1) * split], hidden, preferred_element_type=jnp.float32)
+            change = part if i == 0 else change + part
+            if i == 0:
+                continue
+            for n in range(2):
+                k = k0 + 2 * j + n
+                new = moved[2 * j + n] + change[:, n * width_y : (n + 1) * width_y]
+                if new_ref is not None:
+                    new_ref[k] = new
+                if send_ref is not None:
+                    for s in range(count):
+                        send_ref[s, k] = new[s * spec : (s + 1) * spec].astype(jnp.bfloat16)
+        halves = next_halves
+        if more:
+            moved = next_moved
     if outs is not None:
         for d in range(count):
             outs[d][...] = send_ref[species ^ d]
@@ -373,8 +390,6 @@
     halo_c = lax.ppermute(send_a, AXES, swap_b)
     common = [
         pltpu.VMEM((7, depth, width_y), f32),
-        pltpu.VMEM(row.shape, f32),
-        pltpu.VMEM((2, spec_all, GROUP * width_y), bf16),
     ]
 
     def column(t, kind, own, inner, outer, sends=True):

time: 59.6 us -> 55.9 us (0.938)
  Pallas kernels: 22.1 us -> 15.5 us
  starting transfers between devices: 26.6 us -> 28.2 us
  waiting for transfers between devices: 7.38 us -> 8.36 us
    pallas_call x15, Pallas kernels: 22.1 us -> 15.5 us  [call(): pl.pallas_call(kernel, out_shape=out_shape, in_specs=[VMEM] * len(args),...]
    ppermute x12, starting transfers between devices: 10.1 us -> 11.2 us  [swapped(): return lax.ppermute(piece, 'species', [(s, s ^ d) for s in range(count)])]
    ppermute x1, waiting for transfers between devices: 0.01 us -> 0.65 us  [by_columns(): halo_b = from_b = lax.ppermute(send_b, AXES, swap_b)]
  transfers between devices with their start and end apart: 20 -> 20, of which waited for: 5 -> 7; matrix products, arithmetic and copies ran while one was open for 0% -> 0% of each run, Pallas kernels for 34% -> 24%
where the time goes in v8:
time: 55.9 us; the launch traced here: 55.4 us
  starting transfers between devices  28.2 us (50%)
  Pallas kernels  15.5 us (28%)
  waiting for transfers between devices  8.36 us (15%)
  local copies, waits for them, and re-layouts  2.86 us (5%)
    pallas_call x15, Pallas kernels, call(): pl.pallas_call(kernel, out_shape=out_shape, in_specs=[VMEM] * len(args),...  15.5 us
    ppermute x12, starting transfers between devices, swapped(): return lax.ppermute(piece, 'species', [(s, s ^ d) for s in range(count)])  11.2 us
    ppermute x12, waiting for transfers between devices, swapped(): return lax.ppermute(piece, 'species', [(s, s ^ d) for s in range(count)])  7.36 us
    ppermute x2, starting transfers between devices, by_columns(): halo_c = lax.ppermute(send_a, AXES, swap_b)  6.03 us
    ppermute x3, starting transfers between devices, by_columns(): halo_a = lax.ppermute(send_a, AXES, swap_a)  4.5 us
    ppermute x1, starting transfers between devices, by_columns(): halo_b = from_b = lax.ppermute(send_b, AXES, swap_b)  3.31 us
    unnamed x9, local copies, waits for them, and re-layouts  2.86 us
    ppermute x1, starting transfers between devices, by_columns(): halo_b = lax.ppermute(made_b[0], AXES, swap_b)  2.81 us
  transfers between devices with their start and end apart: 20, of which 7 were waited for; matrix products, arithmetic and copies ran while one was open for 0% of the time, Pallas kernels for 24%

profile of v8, /device:TPU:17, one launch (start us, length us, event | category | flops | bytes accessed | tf_op | source)
XLA Modules:
  0.0 55.4 jit_solution(280942184860294740)
XLA Ops:
  5.5 1.3 %collective-permute-start.4 = (bf16[16,16,128]{2,1,0:T(8,128)(2,1)S(1)}, bf16[16,16,128]{2,1,0:T(8,128)(2,1)S(1)}, u32[]{:S(2)}, u32[]{:S(2)}) collective-permute-start(bf16[16,16,128]{2,1,0:T(8,128)(2,1)S(1)} %get-tuple-element.43), channel_id=1, source_target_pairs={{0,16},{8,24},{16,0},{24,8},{1,17},{9,25},{17,1},{25,9},{2,18},{10... | collective-permute-start | bytes 196616 | tf_op jit(solution)/shard_map/ppermute | solution.py:354
  7.6 2.5 %collective-permute-done.2.refs_3_.refs_7_ = bf16[22,16,128]{2,1,0:T(8,128)(2,1)S(1)} collective-permute-done((bf16[22,16,128]{2,1,0:T(8,128)(2,1)S(1)}, bf16[22,16,128]{2,1,0:T(8,128)(2,1)S(1)}, u32[]{:S(2)}, u32[]{:S(2)}) %collective-permute-start.2) | collective-permute-done | bytes 90144 | tf_op jit(solution)/shard_map/ppermute | solution.py:354
  11.1 1.4 %collective-permute-done.5.refs_3_ = bf16[16,16,128]{2,1,0:T(8,128)(2,1)S(1)} collective-permute-done((bf16[16,16,128]{2,1,0:T(8,128)(2,1)S(1)}, bf16[16,16,128]{2,1,0:T(8,128)(2,1)S(1)}, u32[]{:S(2)}, u32[]{:S(2)}) %collective-permute-start.5) | collective-permute-done | bytes 65568 | tf_op jit(solution)/shard_map/ppermute | solution.py:354
  12.9 3.3 %collective-permute-start.6 = (bf16[4,20,16,128]{3,2,1,0:T(8,128)(2,1)S(1)}, bf16[4,20,16,128]{3,2,1,0:T(8,128)(2,1)S(1)}, u32[]{:S(2)}, u32[]{:S(2)}) collective-permute-start(bf16[4,20,16,128]{3,2,1,0:T(8,128)(2,1)S(1)} %get-tuple-element.45.refs_8_), channel_id=1, source_target_pairs={{8,16},{16,8},{24,25},{25,24},{17,9},{9,17},{1,2},{2,1},{10,18},{1... | collective-permute-start | bytes 983048 | tf_op jit(solution)/shard_map/ppermute | solution.py:382
  16.3 1.3 %shard_map.51 = (bf16[4,16,16,128]{3,2,1,0:T(8,128)(2,1)S(1)}, f32[16,64,128]{2,1,0:T(8,128)S(1)}) custom-call(f32[16,64,128]{2,1,0:T(8,128)S(1)} %get-tuple-element.46.inner_ref.own_ref, f32[16,64,128]{2,1,0:T(8,128)S(1)} %get-tuple-element.40.own_ref.inner_ref, bf16[4,17,16,128]{3,2,1,0:T(8,128)(2,1)S(1)} %collective-permute-done.7.outer_ref.from_ref, ...), custom_call_target="tpu_custom_call" | custom-call | flops 1024 | bytes 1024 | tf_op jit(solution)/shard_map/pallas_call | solution.py:321
  17.9 3.1 %collective-permute-start.8 = (bf16[4,17,16,128]{3,2,1,0:T(8,128)(2,1)S(1)}, bf16[4,17,16,128]{3,2,1,0:T(8,128)(2,1)S(1)}, u32[]{:S(2)}, u32[]{:S(2)}) collective-permute-start(bf16[4,17,16,128]{3,2,1,0:T(8,128)(2,1)S(1)} %get-tuple-element.48), channel_id=1, source_target_pairs={{8,16},{16,8},{24,25},{25,24},{17,9},{9,17},{1,2},{2,1},{10,18},{1... | collective-permute-start | bytes 835592 | tf_op jit(solution)/shard_map/ppermute | solution.py:390
  21.6 1.3 %shard_map.50.own_ref.inner_ref = f32[16,64,128]{2,1,0:T(8,128)S(1)} custom-call(f32[16,64,128]{2,1,0:T(8,128)S(1)} %get-tuple-element.40.own_ref.inner_ref, f32[16,64,128]{2,1,0:T(8,128)S(1)} %get-tuple-element.46.inner_ref.own_ref, bf16[4,20,16,128]{3,2,1,0:T(8,128)(2,1)S(1)} %collective-permute-done.6.outer_ref.from_ref.own_ref, ...), custom_call_target="tpu_custom_call" | custom-call | flops 1024 | bytes 1024 | tf_op jit(solution)/shard_map/pallas_call | solution.py:321
  22.9 1.3 %shard_map.54 = (bf16[4,16,16,128]{3,2,1,0:T(8,128)(2,1)S(1)}, f32[16,64,128]{2,1,0:T(8,128)S(1)}) custom-call(f32[16,64,128]{2,1,0:T(8,128)S(1)} %get-tuple-element.49.inner_ref.own_ref, f32[16,64,128]{2,1,0:T(8,128)S(1)} %shard_map.50.own_ref.inner_ref, bf16[4,16,16,128]{3,2,1,0:T(8,128)(2,1)S(1)} %collective-permute-done.9.outer_ref, ...), custom_call_target="tpu_custom_call" | custom-call | flops 1024 | bytes 1024 | tf_op jit(solution)/shard_map/pallas_call | solution.py:321
  24.2 1.5 %collective-permute-start.11 = (bf16[4,16,16,128]{3,2,1,0:T(8,128)(2,1)S(1)}, bf16[4,16,16,128]{3,2,1,0:T(8,128)(2,1)S(1)}, u32[]{:S(2)}, u32[]{:S(2)}) collective-permute-start(bf16[4,16,16,128]{3,2,1,0:T(8,128)(2,1)S(1)} %get-tuple-element.54), channel_id=1, source_target_pairs={{0,8},{8,0},{16,24},{24,16},{25,17},{17,25},{9,1},{1,9},{2,10},{10... | collective-permute-start | bytes 786440 | tf_op jit(solution)/shard_map/ppermute | solution.py:421
  26.0 1.3 %shard_map.52.outer_ref = f32[16,64,128]{2,1,0:T(8,128)S(1)} custom-call(bf16[4,20,16,128]{3,2,1,0:T(8,128)(2,1)S(1)} %collective-permute-done.6.outer_ref.from_ref.own_ref, f32[16,64,128]{2,1,0:T(8,128)S(1)} %get-tuple-element.40.own_ref.inner_ref, bf16[4,17,16,128]{3,2,1,0:T(8,128)(2,1)S(1)} %collective-permute-done.8.outer_ref, ...), custom_call_target="tpu_custom_call" | custom-call | flops 1024 | bytes 1024 | tf_op jit(solution)/shard_map/pallas_call | solution.py:321
  27.3 1.3 %shard_map.53 = (bf16[4,16,16,128]{3,2,1,0:T(8,128)(2,1)S(1)}, f32[16,64,128]{2,1,0:T(8,128)S(1)}) custom-call(f32[16,64,128]{2,1,0:T(8,128)S(1)} %shard_map.50.own_ref.inner_ref, f32[16,64,128]{2,1,0:T(8,128)S(1)} %get-tuple-element.49.inner_ref.own_ref, f32[16,64,128]{2,1,0:T(8,128)S(1)} %shard_map.52.outer_ref, ...), custom_call_target="tpu_custom_call" | custom-call | flops 1024 | bytes 1024 | tf_op jit(solution)/shard_map/pallas_call | solution.py:321
  28.6 2.8 %collective-permute-start.10 = (bf16[4,16,16,128]{3,2,1,0:T(8,128)(2,1)S(1)}, bf16[4,16,16,128]{3,2,1,0:T(8,128)(2,1)S(1)}, u32[]{:S(2)}, u32[]{:S(2)}) collective-permute-start(bf16[4,16,16,128]{3,2,1,0:T(8,128)(2,1)S(1)} %get-tuple-element.53), channel_id=1, source_target_pairs={{8,16},{16,8},{24,25},{25,24},{17,9},{9,17},{1,2},{2,1},{10,18},{1... | collective-permute-start | bytes 786440 | tf_op jit(solution)/shard_map/ppermute | solution.py:419
  31.4 2.9 %collective-permute-start.12 = (bf16[4,16,16,128]{3,2,1,0:T(8,128)(2,1)S(1)}, bf16[4,16,16,128]{3,2,1,0:T(8,128)(2,1)S(1)}, u32[]{:S(2)}, u32[]{:S(2)}) collective-permute-start(bf16[4,16,16,128]{3,2,1,0:T(8,128)(2,1)S(1)} %get-tuple-element.54), channel_id=1, source_target_pairs={{8,16},{16,8},{24,25},{25,24},{17,9},{9,17},{1,2},{2,1},{10,18},{1... | collective-permute-start | bytes 786440 | tf_op jit(solution)/shard_map/ppermute | solution.py:422
  34.4 1.3 %shard_map.56 = (bf16[4,16,16,128]{3,2,1,0:T(8,128)(2,1)S(1)}, f32[16,64,128]{2,1,0:T(8,128)S(1)}) custom-call(f32[16,64,128]{2,1,0:T(8,128)S(1)} %get-tuple-element.52.inner_ref.own_ref, f32[16,64,128]{2,1,0:T(8,128)S(1)} %get-tuple-element.50.own_ref.inner_ref, bf16[4,16,16,128]{3,2,1,0:T(8,128)(2,1)S(1)} %collective-permute-done.11.outer_ref, ...), custom_call_target="tpu_custom_call" | custom-call | flops 1024 | bytes 1024 | tf_op jit(solution)/shard_map/pallas_call | solution.py:321
  35.6 2.7 %collective-permute-start.16 = (bf16[4,16,16,128]{3,2,1,0:T(8,128)(2,1)S(1)}, bf16[4,16,16,128]{3,2,1,0:T(8,128)(2,1)S(1)}, u32[]{:S(2)}, u32[]{:S(2)}) collective-permute-start(bf16[4,16,16,128]{3,2,1,0:T(8,128)(2,1)S(1)} %get-tuple-element.60), channel_id=1, source_target_pairs={{0,8},{8,0},{16,24},{24,16},{25,17},{17,25},{9,1},{1,9},{2,10},{10... | collective-permute-start | bytes 786440 | tf_op jit(solution)/shard_map/ppermute | solution.py:411
  38.3 1.3 %shard_map.55.own_ref.inner_ref = f32[16,64,128]{2,1,0:T(8,128)S(1)} custom-call(f32[16,64,128]{2,1,0:T(8,128)S(1)} %get-tuple-element.50.own_ref.inner_ref, f32[16,64,128]{2,1,0:T(8,128)S(1)} %get-tuple-element.52.inner_ref.own_ref, bf16[4,16,16,128]{3,2,1,0:T(8,128)(2,1)S(1)} %collective-permute-done.10.outer_ref.own_ref, ...), custom_call_target="tpu_custom_call" | custom-call | flops 1024 | bytes 1024 | tf_op jit(solution)/shard_map/pallas_call | solution.py:321
  39.6 1.3 %shard_map.57.outer_ref = f32[16,64,128]{2,1,0:T(8,128)S(1)} custom-call(bf16[4,16,16,128]{3,2,1,0:T(8,128)(2,1)S(1)} %collective-permute-done.10.outer_ref.own_ref, f32[16,64,128]{2,1,0:T(8,128)S(1)} %get-tuple-element.50.own_ref.inner_ref, bf16[4,16,16,128]{3,2,1,0:T(8,128)(2,1)S(1)} %collective-permute-done.12.outer_ref, ...), custom_call_target="tpu_custom_call" | custom-call | flops 1024 | bytes 1024 | tf_op jit(solution)/shard_map/pallas_call | solution.py:321
  40.9 1.3 %shard_map.58 = (bf16[16,16,128]{2,1,0:T(8,128)(2,1)S(1)}, bf16[16,16,128]{2,1,0:T(8,128)(2,1)S(1)}, bf16[16,16,128]{2,1,0:T(8,128)(2,1)S(1)}, bf16[16,16,128]{2,1,0:T(8,128)(2,1)S(1)}) custom-call(f32[16,64,128]{2,1,0:T(8,128)S(1)} %shard_map.55.own_ref.inner_ref, f32[16,64,128]{2,1,0:T(8,128)S(1)} %get-tuple-element.55.inner_ref.own_ref, ...), custom_call_target="tpu_custom_call" | custom-call | flops 1024 | bytes 1024 | tf_op jit(solution)/shard_map/pallas_call | solution.py:321
  42.2 2.9 %collective-permute-start.13 = (bf16[16,16,128]{2,1,0:T(8,128)(2,1)S(1)}, bf16[16,16,128]{2,1,0:T(8,128)(2,1)S(1)}, u32[]{:S(2)}, u32[]{:S(2)}) collective-permute-start(bf16[16,16,128]{2,1,0:T(8,128)(2,1)S(1)} %get-tuple-element.57), channel_id=1, source_target_pairs={{0,8},{8,0},{16,24},{24,16},{1,9},{9,1},{17,25},{25,17},{2,10},{10... | collective-permute-start | bytes 196616 | tf_op jit(solution)/shard_map/ppermute | solution.py:354
  45.2 1.7 %collective-permute-start.15 = (bf16[16,16,128]{2,1,0:T(8,128)(2,1)S(1)}, bf16[16,16,128]{2,1,0:T(8,128)(2,1)S(1)}, u32[]{:S(2)}, u32[]{:S(2)}) collective-permute-start(bf16[16,16,128]{2,1,0:T(8,128)(2,1)S(1)} %get-tuple-element.59), channel_id=1, source_target_pairs={{0,24},{8,16},{16,8},{24,0},{1,25},{9,17},{17,9},{25,1},{2,26},{10... | collective-permute-start | bytes 196616 | tf_op jit(solution)/shard_map/ppermute | solution.py:354
  46.9 1.3 %shard_map.59 = (bf16[16,16,128]{2,1,0:T(8,128)(2,1)S(1)}, bf16[16,16,128]{2,1,0:T(8,128)(2,1)S(1)}, bf16[16,16,128]{2,1,0:T(8,128)(2,1)S(1)}, bf16[16,16,128]{2,1,0:T(8,128)(2,1)S(1)}) custom-call(f32[16,64,128]{2,1,0:T(8,128)S(1)} %get-tuple-element.55.inner_ref.own_ref, f32[16,64,128]{2,1,0:T(8,128)S(1)} %shard_map.55.own_ref.inner_ref, ...), custom_call_target="tpu_custom_call" | custom-call | flops 1024 | bytes 1024 | tf_op jit(solution)/shard_map/pallas_call | solution.py:321
  48.4 2.0 %collective-permute-start.19 = (bf16[16,16,128]{2,1,0:T(8,128)(2,1)S(1)}, bf16[16,16,128]{2,1,0:T(8,128)(2,1)S(1)}, u32[]{:S(2)}, u32[]{:S(2)}) collective-permute-start(bf16[16,16,128]{2,1,0:T(8,128)(2,1)S(1)} %get-tuple-element.64), channel_id=1, source_target_pairs={{0,24},{8,16},{16,8},{24,0},{1,25},{9,17},{17,9},{25,1},{2,26},{10... | collective-permute-start | bytes 196616 | tf_op jit(solution)/shard_map/ppermute | solution.py:354
  51.5 2.1 %collective-permute-done.19.refs_7_ = bf16[16,16,128]{2,1,0:T(8,128)(2,1)S(1)} collective-permute-done((bf16[16,16,128]{2,1,0:T(8,128)(2,1)S(1)}, bf16[16,16,128]{2,1,0:T(8,128)(2,1)S(1)}, u32[]{:S(2)}, u32[]{:S(2)}) %collective-permute-start.19) | collective-permute-done | bytes 65568 | tf_op jit(solution)/shard_map/ppermute | solution.py:354
  53.6 1.6 %shard_map.60 = f32[16,128,128]{2,1,0:T(8,128)} custom-call(bf16[16,16,128]{2,1,0:T(8,128)(2,1)S(1)} %get-tuple-element.56.refs_0_, bf16[16,16,128]{2,1,0:T(8,128)(2,1)S(1)} %collective-permute-done.13.refs_1_, bf16[16,16,128]{2,1,0:T(8,128)(2,1)S(1)} %collective-permute-done.14.refs_2_, bf16[16,16,128]{2,1,0:T(8,128)(2,1)S(1)} %collective-permute-done.15.refs_3_, ...), custom_call_target="tpu_custom_call" | custom-call | flops 1024 | bytes 1024 | tf_op jit(solution)/shard_map/pallas_call | solution.py:321
  (42 shorter events, 10.4 us)
Async XLA Ops:
  0.0 1.2 %copy-start = (f32[16,16,8,128]{3,2,1,0:T(8,128)S(1)}, f32[16,16,8,128]{3,2,1,0:T(8,128)}, u32[]{:S(2)}) copy-start(f32[16,16,8,128]{3,2,1,0:T(8,128)} %param.4) | copy-start | bytes 3145732
  1.2 0.9 %copy-start.1 = (f32[4,3,4,8,128]{4,3,2,1,0:T(8,128)S(1)}, f32[4,3,4,8,128]{4,3,2,1,0:T(8,128)}, u32[]{:S(2)}) copy-start(f32[4,3,4,8,128]{4,3,2,1,0:T(8,128)} %param.5) | copy-start | bytes 589828
  2.6 4.8 %collective-permute-start = (bf16[22,16,128]{2,1,0:T(8,128)(2,1)S(1)}, bf16[22,16,128]{2,1,0:T(8,128)(2,1)S(1)}, u32[]{:S(2)}, u32[]{:S(2)}) collective-permute-start(bf16[22,16,128]{2,1,0:T(8,128)(2,1)S(1)} %get-tuple-element.36), channel_id=1, source_target_pairs={{0,8},{8,0},{16,24},{24,16},{1,9},{9,1},{17,25},{25,17},{2,10},{10... | collective-permute-start | bytes 270344 | tf_op jit(solution)/shard_map/ppermute | solution.py:354
  3.4 4.2 %collective-permute-start.1 = (bf16[22,16,128]{2,1,0:T(8,128)(2,1)S(1)}, bf16[22,16,128]{2,1,0:T(8,128)(2,1)S(1)}, u32[]{:S(2)}, u32[]{:S(2)}) collective-permute-start(bf16[22,16,128]{2,1,0:T(8,128)(2,1)S(1)} %get-tuple-element.37), channel_id=1, source_target_pairs={{0,16},{8,24},{16,0},{24,8},{1,17},{9,25},{17,1},{25,9},{2,18},{10... | collective-permute-start | bytes 270344 | tf_op jit(solution)/shard_map/ppermute | solution.py:354
  4.6 5.5 %collective-permute-start.2 = (bf16[22,16,128]{2,1,0:T(8,128)(2,1)S(1)}, bf16[22,16,128]{2,1,0:T(8,128)(2,1)S(1)}, u32[]{:S(2)}, u32[]{:S(2)}) collective-permute-start(bf16[22,16,128]{2,1,0:T(8,128)(2,1)S(1)} %get-tuple-element.38), channel_id=1, source_target_pairs={{0,24},{8,16},{16,8},{24,0},{1,25},{9,17},{17,9},{25,1},{2,26},{10... | collective-permute-start | bytes 270344 | tf_op jit(solution)/shard_map/ppermute | solution.py:354
  5.5 5.6 %collective-permute-start.4 = (bf16[16,16,128]{2,1,0:T(8,128)(2,1)S(1)}, bf16[16,16,128]{2,1,0:T(8,128)(2,1)S(1)}, u32[]{:S(2)}, u32[]{:S(2)}) collective-permute-start(bf16[16,16,128]{2,1,0:T(8,128)(2,1)S(1)} %get-tuple-element.43), channel_id=1, source_target_pairs={{0,16},{8,24},{16,0},{24,8},{1,17},{9,25},{17,1},{25,9},{2,18},{10... | collective-permute-start | bytes 196616 | tf_op jit(solution)/shard_map/ppermute | solution.py:354
  6.8 5.6 %collective-permute-start.5 = (bf16[16,16,128]{2,1,0:T(8,128)(2,1)S(1)}, bf16[16,16,128]{2,1,0:T(8,128)(2,1)S(1)}, u32[]{:S(2)}, u32[]{:S(2)}) collective-permute-start(bf16[16,16,128]{2,1,0:T(8,128)(2,1)S(1)} %get-tuple-element.44), channel_id=1, source_target_pairs={{0,24},{8,16},{16,8},{24,0},{1,25},{9,17},{17,9},{25,1},{2,26},{10... | collective-permute-start | bytes 196616 | tf_op jit(solution)/shard_map/ppermute | solution.py:354
  10.1 0.8 %copy-start.2 = (bf16[512,64]{0,1:T(8,128)(2,1)S(1)}, bf16[512,64]{0,1:T(8,128)(2,1)}, u32[]{:S(2)}) copy-start(bf16[512,64]{0,1:T(8,128)(2,1)} %param.6) | copy-start | bytes 196612
  10.3 2.2 %collective-permute-start.3 = (bf16[16,16,128]{2,1,0:T(8,128)(2,1)S(1)}, bf16[16,16,128]{2,1,0:T(8,128)(2,1)S(1)}, u32[]{:S(2)}, u32[]{:S(2)}) collective-permute-start(bf16[16,16,128]{2,1,0:T(8,128)(2,1)S(1)} %get-tuple-element.42), channel_id=1, source_target_pairs={{0,8},{8,0},{16,24},{24,16},{1,9},{9,1},{17,25},{25,17},{2,10},{10... | collective-permute-start | bytes 196616 | tf_op jit(solution)/shard_map/ppermute | solution.py:354
  12.6 3.6 %copy-start.3 = (bf16[64,512]{1,0:T(8,128)(2,1)S(1)}, bf16[64,512]{1,0:T(8,128)(2,1)}, u32[]{:S(2)}) copy-start(bf16[64,512]{1,0:T(8,128)(2,1)} %param.7) | copy-start | bytes 196612
  12.6 3.7 %collective-permute-start.7 = (bf16[4,17,16,128]{3,2,1,0:T(8,128)(2,1)S(1)}, bf16[4,17,16,128]{3,2,1,0:T(8,128)(2,1)S(1)}, u32[]{:S(2)}, u32[]{:S(2)}) collective-permute-start(bf16[4,17,16,128]{3,2,1,0:T(8,128)(2,1)S(1)} %get-tuple-element.48), channel_id=1, source_target_pairs={{0,8},{8,0},{16,24},{24,16},{25,17},{17,25},{9,1},{1,9},{2,10},{10... | collective-permute-start | bytes 835592 | tf_op jit(solution)/shard_map/ppermute | solution.py:389
  12.9 8.7 %collective-permute-start.6 = (bf16[4,20,16,128]{3,2,1,0:T(8,128)(2,1)S(1)}, bf16[4,20,16,128]{3,2,1,0:T(8,128)(2,1)S(1)}, u32[]{:S(2)}, u32[]{:S(2)}) collective-permute-start(bf16[4,20,16,128]{3,2,1,0:T(8,128)(2,1)S(1)} %get-tuple-element.45.refs_8_), channel_id=1, source_target_pairs={{8,16},{16,8},{24,25},{25,24},{17,9},{9,17},{1,2},{2,1},{10,18},{1... | collective-permute-start | bytes 983048 | tf_op jit(solution)/shard_map/ppermute | solution.py:382
  17.6 5.3 %collective-permute-start.9 = (bf16[4,16,16,128]{3,2,1,0:T(8,128)(2,1)S(1)}, bf16[4,16,16,128]{3,2,1,0:T(8,128)(2,1)S(1)}, u32[]{:S(2)}, u32[]{:S(2)}) collective-permute-start(bf16[4,16,16,128]{3,2,1,0:T(8,128)(2,1)S(1)} %get-tuple-element.51), channel_id=1, source_target_pairs={{0,8},{8,0},{16,24},{24,16},{25,17},{17,25},{9,1},{1,9},{2,10},{10... | collective-permute-start | bytes 786440 | tf_op jit(solution)/shard_map/ppermute | solution.py:411
  17.9 8.1 %collective-permute-start.8 = (bf16[4,17,16,128]{3,2,1,0:T(8,128)(2,1)S(1)}, bf16[4,17,16,128]{3,2,1,0:T(8,128)(2,1)S(1)}, u32[]{:S(2)}, u32[]{:S(2)}) collective-permute-start(bf16[4,17,16,128]{3,2,1,0:T(8,128)(2,1)S(1)} %get-tuple-element.48), channel_id=1, source_target_pairs={{8,16},{16,8},{24,25},{25,24},{17,9},{9,17},{1,2},{2,1},{10,18},{1... | collective-permute-start | bytes 835592 | tf_op jit(solution)/shard_map/ppermute | solution.py:390
  24.2 10.2 %collective-permute-start.11 = (bf16[4,16,16,128]{3,2,1,0:T(8,128)(2,1)S(1)}, bf16[4,16,16,128]{3,2,1,0:T(8,128)(2,1)S(1)}, u32[]{:S(2)}, u32[]{:S(2)}) collective-permute-start(bf16[4,16,16,128]{3,2,1,0:T(8,128)(2,1)S(1)} %get-tuple-element.54), channel_id=1, source_target_pairs={{0,8},{8,0},{16,24},{24,16},{25,17},{17,25},{9,1},{1,9},{2,10},{10... | collective-permute-start | bytes 786440 | tf_op jit(solution)/shard_map/ppermute | solution.py:421
  28.6 9.7 %collective-permute-start.10 = (bf16[4,16,16,128]{3,2,1,0:T(8,128)(2,1)S(1)}, bf16[4,16,16,128]{3,2,1,0:T(8,128)(2,1)S(1)}, u32[]{:S(2)}, u32[]{:S(2)}) collective-permute-start(bf16[4,16,16,128]{3,2,1,0:T(8,128)(2,1)S(1)} %get-tuple-element.53), channel_id=1, source_target_pairs={{8,16},{16,8},{24,25},{25,24},{17,9},{9,17},{1,2},{2,1},{10,18},{1... | collective-permute-start | bytes 786440 | tf_op jit(solution)/shard_map/ppermute | solution.py:419
  31.4 8.2 %collective-permute-start.12 = (bf16[4,16,16,128]{3,2,1,0:T(8,128)(2,1)S(1)}, bf16[4,16,16,128]{3,2,1,0:T(8,128)(2,1)S(1)}, u32[]{:S(2)}, u32[]{:S(2)}) collective-permute-start(bf16[4,16,16,128]{3,2,1,0:T(8,128)(2,1)S(1)} %get-tuple-element.54), channel_id=1, source_target_pairs={{8,16},{16,8},{24,25},{25,24},{17,9},{9,17},{1,2},{2,1},{10,18},{1... | collective-permute-start | bytes 786440 | tf_op jit(solution)/shard_map/ppermute | solution.py:422
  35.6 11.2 %collective-permute-start.16 = (bf16[4,16,16,128]{3,2,1,0:T(8,128)(2,1)S(1)}, bf16[4,16,16,128]{3,2,1,0:T(8,128)(2,1)S(1)}, u32[]{:S(2)}, u32[]{:S(2)}) collective-permute-start(bf16[4,16,16,128]{3,2,1,0:T(8,128)(2,1)S(1)} %get-tuple-element.60), channel_id=1, source_target_pairs={{0,8},{8,0},{16,24},{24,16},{25,17},{17,25},{9,1},{1,9},{2,10},{10... | collective-permute-start | bytes 786440 | tf_op jit(solution)/shard_map/ppermute | solution.py:411
  42.2 6.2 %collective-permute-start.13 = (bf16[16,16,128]{2,1,0:T(8,128)(2,1)S(1)}, bf16[16,16,128]{2,1,0:T(8,128)(2,1)S(1)}, u32[]{:S(2)}, u32[]{:S(2)}) collective-permute-start(bf16[16,16,128]{2,1,0:T(8,128)(2,1)S(1)} %get-tuple-element.57), channel_id=1, source_target_pairs={{0,8},{8,0},{16,24},{24,16},{1,9},{9,1},{17,25},{25,17},{2,10},{10... | collective-permute-start | bytes 196616 | tf_op jit(solution)/shard_map/ppermute | solution.py:354
  45.1 5.2 %collective-permute-start.14 = (bf16[16,16,128]{2,1,0:T(8,128)(2,1)S(1)}, bf16[16,16,128]{2,1,0:T(8,128)(2,1)S(1)}, u32[]{:S(2)}, u32[]{:S(2)}) collective-permute-start(bf16[16,16,128]{2,1,0:T(8,128)(2,1)S(1)} %get-tuple-element.58), channel_id=1, source_target_pairs={{0,16},{8,24},{16,0},{24,8},{1,17},{9,25},{17,1},{25,9},{2,18},{10... | collective-permute-start | bytes 196616 | tf_op jit(solution)/shard_map/ppermute | solution.py:354
  45.2 5.2 %collective-permute-start.15 = (bf16[16,16,128]{2,1,0:T(8,128)(2,1)S(1)}, bf16[16,16,128]{2,1,0:T(8,128)(2,1)S(1)}, u32[]{:S(2)}, u32[]{:S(2)}) collective-permute-start(bf16[16,16,128]{2,1,0:T(8,128)(2,1)S(1)} %get-tuple-element.59), channel_id=1, source_target_pairs={{0,24},{8,16},{16,8},{24,0},{1,25},{9,17},{17,9},{25,1},{2,26},{10... | collective-permute-start | bytes 196616 | tf_op jit(solution)/shard_map/ppermute | solution.py:354
  48.1 2.2 %collective-permute-start.17 = (bf16[16,16,128]{2,1,0:T(8,128)(2,1)S(1)}, bf16[16,16,128]{2,1,0:T(8,128)(2,1)S(1)}, u32[]{:S(2)}, u32[]{:S(2)}) collective-permute-start(bf16[16,16,128]{2,1,0:T(8,128)(2,1)S(1)} %get-tuple-element.62), channel_id=1, source_target_pairs={{0,8},{8,0},{16,24},{24,16},{1,9},{9,1},{17,25},{25,17},{2,10},{10... | collective-permute-start | bytes 196616 | tf_op jit(solution)/shard_map/ppermute | solution.py:354
  48.4 3.1 %collective-permute-start.18 = (bf16[16,16,128]{2,1,0:T(8,128)(2,1)S(1)}, bf16[16,16,128]{2,1,0:T(8,128)(2,1)S(1)}, u32[]{:S(2)}, u32[]{:S(2)}) collective-permute-start(bf16[16,16,128]{2,1,0:T(8,128)(2,1)S(1)} %get-tuple-element.63), channel_id=1, source_target_pairs={{0,16},{8,24},{16,0},{24,8},{1,17},{9,25},{17,1},{25,9},{2,18},{10... | collective-permute-start | bytes 196616 | tf_op jit(solution)/shard_map/ppermute | solution.py:354
  48.4 5.2 %collective-permute-start.19 = (bf16[16,16,128]{2,1,0:T(8,128)(2,1)S(1)}, bf16[16,16,128]{2,1,0:T(8,128)(2,1)S(1)}, u32[]{:S(2)}, u32[]{:S(2)}) collective-permute-start(bf16[16,16,128]{2,1,0:T(8,128)(2,1)S(1)} %get-tuple-element.64), channel_id=1, source_target_pairs={{0,24},{8,16},{16,8},{24,0},{1,25},{9,17},{17,9},{25,1},{2,26},{10... | collective-permute-start | bytes 196616 | tf_op jit(solution)/shard_map/ppermute | solution.py:354

commit v9 on v8

--- a/solution.py
+++ b/solution.py
@@ -11,7 +11,7 @@
 AXES = ("species", "tile")
 PACK = 16
 GROUP = 4
-PARTS = 4
+PARTS = 8
 VMEM = pl.BlockSpec(memory_space=pltpu.VMEM)
 LIMIT = 24 * 1024 * 1024
 
@@ -120,7 +120,6 @@
     if kind == "A":
         return
     flux_ref = refs[1]
-    outer = lax.axis_index("tile") == 0
     for d in range(count):
         b_at, a_at = columns[d]
         low = jnp.minimum(b_at, a_at)
@@ -134,11 +133,9 @@
                 0,
             )
 
-        first = jnp.where(jnp.logical_and(outer, low == 0), 0.0, tile_of(0, low))
-        out_refs[d][depth] = first.astype(jnp.bfloat16)
-        others = ((0, low + 1), (1, b_at), (2, b_at), (1, a_at), (2, a_at))
-        for i, (direction, x) in enumerate(others):
-            out_refs[d][depth + 1 + i] = tile_of(direction, x).astype(jnp.bfloat16)
+        tiles = ((0, low), (0, low + 1), (1, b_at), (2, b_at), (1, a_at), (2, a_at))
+        for i, (direction, x) in enumerate(tiles):
+            out_refs[d][depth + i] = tile_of(direction, x).astype(jnp.bfloat16)
 
 
 def unpack_kernel(count, depth, kind, *refs):
@@ -325,7 +322,7 @@
         out_specs=[VMEM] * len(out_shape) if many else anywhere if far_out else VMEM,
         scratch_shapes=scratch,
         compiler_params=pltpu.CompilerParams(vmem_limit_bytes=LIMIT),
-        cost_estimate=pl.CostEstimate(flops=1024, bytes_accessed=1024, transcendentals=0),
+        cost_estimate=pl.CostEstimate(flops=10**10, bytes_accessed=10**6, transcendentals=0),
     )(*args)
 
 
@@ -359,6 +356,9 @@
     row = shape((depth, spec_all, width_y), f32)
     held = pltpu.VMEM((PARTS, spec, depth * width // PARTS, width_y), f32)
     flat = tracers.reshape(-1, width_y)
+    column_at = lax.axis_index("tile") * width + lax.broadcasted_iota(jnp.int32, fluxes.shape, 3)
+    closed = jnp.logical_and(column_at == 0, lax.broadcasted_iota(jnp.int32, fluxes.shape, 1) == 0)
+    fluxes = jnp.where(closed, 0.0, fluxes)
     sent = shape((count, depth, spec, width_y), bf16)
     piece = shape((depth, spec, width_y), bf16)
     piece_b = shape((depth + 6, spec, width_y), bf16)

time: 55.9 us -> 53 us (0.948)
  starting transfers between devices: 28.2 us -> 26.6 us
  other arithmetic: 0.02 us -> 1.05 us
  local copies, waits for them, and re-layouts: 2.86 us -> 1.93 us
  waiting for transfers between devices: 8.36 us -> 7.61 us
    ppermute x12, waiting for transfers between devices: 7.36 us -> 5.82 us  [swapped(): return lax.ppermute(piece, 'species', [(s, s ^ d) for s in range(count)])]
    ppermute x1, waiting for transfers between devices: 0.65 us -> 1.77 us  [by_columns(): halo_b = from_b = lax.ppermute(send_b, AXES, swap_b)]
    select_n x0 -> x1, other arithmetic: none -> 1.01 us  [by_columns(): fluxes = jnp.where(closed, 0.0, fluxes)]
    unnamed x9 -> x7, local copies, waits for them, and re-layouts: 2.86 us -> 1.93 us
    ppermute x1, starting transfers between devices: 2.81 us -> 1.92 us  [by_columns(): halo_b = lax.ppermute(made_b[0], AXES, swap_b)]
    ppermute x1, starting transfers between devices: 0.3 us -> 1.15 us  [by_columns(): halo_a = from_a = lax.ppermute(send_a, AXES, swap_a)]
    ppermute x3, starting transfers between devices: 4.5 us -> 3.71 us  [by_columns(): halo_a = lax.ppermute(send_a, AXES, swap_a)]
    ppermute x12, starting transfers between devices: 11.2 us -> 10.5 us  [swapped(): return lax.ppermute(piece, 'species', [(s, s ^ d) for s in range(count)])]
  transfers between devices with their start and end apart: 20 -> 20, of which waited for: 7 -> 4; matrix products, arithmetic and copies ran while one was open for 0% -> 0% of each run, Pallas kernels for 24% -> 26%
where the time goes in v9:
time: 53 us; the launch traced here: 52.7 us
  starting transfers between devices  26.6 us (50%)
  Pallas kernels  15.1 us (28%)
  waiting for transfers between devices  7.61 us (14%)
  local copies, waits for them, and re-layouts  1.93 us (4%)
  other arithmetic  1.05 us (2%)
    pallas_call x15, Pallas kernels, call(): pl.pallas_call(kernel, out_shape=out_shape, in_specs=[VMEM] * len(args),...  15.1 us
    ppermute x12, starting transfers between devices, swapped(): return lax.ppermute(piece, 'species', [(s, s ^ d) for s in range(count)])  10.5 us
    ppermute x2, starting transfers between devices, by_columns(): halo_c = lax.ppermute(send_a, AXES, swap_b)  6.44 us
    ppermute x12, waiting for transfers between devices, swapped(): return lax.ppermute(piece, 'species', [(s, s ^ d) for s in range(count)])  5.82 us
    ppermute x3, starting transfers between devices, by_columns(): halo_a = lax.ppermute(send_a, AXES, swap_a)  3.71 us
    ppermute x1, starting transfers between devices, by_columns(): halo_b = from_b = lax.ppermute(send_b, AXES, swap_b)  2.94 us
    unnamed x7, local copies, waits for them, and re-layouts  1.93 us
    ppermute x1, starting transfers between devices, by_columns(): halo_b = lax.ppermute(made_b[0], AXES, swap_b)  1.92 us
  transfers between devices with their start and end apart: 20, of which 4 were waited for; matrix products, arithmetic and copies ran while one was open for 0% of the time, Pallas kernels for 26%

profile of v9, /device:TPU:17, one launch (start us, length us, event | category | flops | bytes accessed | tf_op | source)
XLA Modules:
  0.0 52.7 jit_solution(10338184919372440409)
XLA Ops:
  1.0 1.2 %copy-done = f32[16,16,8,128]{3,2,1,0:T(8,128)S(1)} copy-done((f32[16,16,8,128]{3,2,1,0:T(8,128)S(1)}, f32[16,16,8,128]{3,2,1,0:T(8,128)}, u32[]{:S(2)}) %copy-start) | copy-done | bytes 1048600
  3.5 1.3 %collective-permute-start.1 = (bf16[22,16,128]{2,1,0:T(8,128)(2,1)S(1)}, bf16[22,16,128]{2,1,0:T(8,128)(2,1)S(1)}, u32[]{:S(2)}, u32[]{:S(2)}) collective-permute-start(bf16[22,16,128]{2,1,0:T(8,128)(2,1)S(1)} %get-tuple-element.37), channel_id=1, source_target_pairs={{0,16},{8,24},{16,0},{24,8},{1,17},{9,25},{17,1},{25,9},{2,18},{10... | collective-permute-start | bytes 270344 | tf_op jit(solution)/shard_map/ppermute | solution.py:351
  5.6 1.3 %collective-permute-start.4 = (bf16[16,16,128]{2,1,0:T(8,128)(2,1)S(1)}, bf16[16,16,128]{2,1,0:T(8,128)(2,1)S(1)}, u32[]{:S(2)}, u32[]{:S(2)}) collective-permute-start(bf16[16,16,128]{2,1,0:T(8,128)(2,1)S(1)} %get-tuple-element.43), channel_id=1, source_target_pairs={{0,16},{8,24},{16,0},{24,8},{1,17},{9,25},{17,1},{25,9},{2,18},{10... | collective-permute-start | bytes 196616 | tf_op jit(solution)/shard_map/ppermute | solution.py:351
  7.7 2.5 %collective-permute-done.2.refs_3_.refs_7_ = bf16[22,16,128]{2,1,0:T(8,128)(2,1)S(1)} collective-permute-done((bf16[22,16,128]{2,1,0:T(8,128)(2,1)S(1)}, bf16[22,16,128]{2,1,0:T(8,128)(2,1)S(1)}, u32[]{:S(2)}, u32[]{:S(2)}) %collective-permute-start.2) | collective-permute-done | bytes 90144 | tf_op jit(solution)/shard_map/ppermute | solution.py:351
  11.1 2.9 %collective-permute-start.6 = (bf16[4,20,16,128]{3,2,1,0:T(8,128)(2,1)S(1)}, bf16[4,20,16,128]{3,2,1,0:T(8,128)(2,1)S(1)}, u32[]{:S(2)}, u32[]{:S(2)}) collective-permute-start(bf16[4,20,16,128]{3,2,1,0:T(8,128)(2,1)S(1)} %get-tuple-element.45.refs_8_), channel_id=1, source_target_pairs={{8,16},{16,8},{24,25},{25,24},{17,9},{9,17},{1,2},{2,1},{10,18},{1... | collective-permute-start | bytes 983048 | tf_op jit(solution)/shard_map/ppermute | solution.py:382
  14.2 2.6 %collective-permute-start.8 = (bf16[4,17,16,128]{3,2,1,0:T(8,128)(2,1)S(1)}, bf16[4,17,16,128]{3,2,1,0:T(8,128)(2,1)S(1)}, u32[]{:S(2)}, u32[]{:S(2)}) collective-permute-start(bf16[4,17,16,128]{3,2,1,0:T(8,128)(2,1)S(1)} %get-tuple-element.48), channel_id=1, source_target_pairs={{8,16},{16,8},{24,25},{25,24},{17,9},{9,17},{1,2},{2,1},{10,18},{1... | collective-permute-start | bytes 835592 | tf_op jit(solution)/shard_map/ppermute | solution.py:390
  18.0 1.8 %collective-permute-done.6.outer_ref.from_ref.own_ref = bf16[4,20,16,128]{3,2,1,0:T(8,128)(2,1)S(1)} collective-permute-done((bf16[4,20,16,128]{3,2,1,0:T(8,128)(2,1)S(1)}, bf16[4,20,16,128]{3,2,1,0:T(8,128)(2,1)S(1)}, u32[]{:S(2)}, u32[]{:S(2)}) %collective-permute-start.6) | collective-permute-done | bytes 327712 | tf_op jit(solution)/shard_map/ppermute | solution.py:382
  19.8 1.3 %shard_map.50.own_ref.inner_ref = f32[16,64,128]{2,1,0:T(8,128)S(1)} custom-call(f32[16,64,128]{2,1,0:T(8,128)S(1)} %get-tuple-element.40.own_ref.inner_ref, f32[16,64,128]{2,1,0:T(8,128)S(1)} %get-tuple-element.46.inner_ref.own_ref, bf16[4,20,16,128]{3,2,1,0:T(8,128)(2,1)S(1)} %collective-permute-done.6.outer_ref.from_ref.own_ref, ...), custom_call_target="tpu_custom_call" | custom-call | flops 10000000000 | bytes 1000000 | tf_op jit(solution)/shard_map/pallas_call | solution.py:318
  21.0 1.3 %shard_map.51 = (bf16[4,16,16,128]{3,2,1,0:T(8,128)(2,1)S(1)}, f32[16,64,128]{2,1,0:T(8,128)S(1)}) custom-call(f32[16,64,128]{2,1,0:T(8,128)S(1)} %get-tuple-element.46.inner_ref.own_ref, f32[16,64,128]{2,1,0:T(8,128)S(1)} %get-tuple-element.40.own_ref.inner_ref, bf16[4,17,16,128]{3,2,1,0:T(8,128)(2,1)S(1)} %collective-permute-done.7.outer_ref.from_ref, ...), custom_call_target="tpu_custom_call" | custom-call | flops 10000000000 | bytes 1000000 | tf_op jit(solution)/shard_map/pallas_call | solution.py:318
  23.5 1.3 %shard_map.52.outer_ref = f32[16,64,128]{2,1,0:T(8,128)S(1)} custom-call(bf16[4,20,16,128]{3,2,1,0:T(8,128)(2,1)S(1)} %collective-permute-done.6.outer_ref.from_ref.own_ref, f32[16,64,128]{2,1,0:T(8,128)S(1)} %get-tuple-element.40.own_ref.inner_ref, bf16[4,17,16,128]{3,2,1,0:T(8,128)(2,1)S(1)} %collective-permute-done.8.outer_ref, ...), custom_call_target="tpu_custom_call" | custom-call | flops 10000000000 | bytes 1000000 | tf_op jit(solution)/shard_map/pallas_call | solution.py:318
  24.8 1.3 %shard_map.53 = (bf16[4,16,16,128]{3,2,1,0:T(8,128)(2,1)S(1)}, f32[16,64,128]{2,1,0:T(8,128)S(1)}) custom-call(f32[16,64,128]{2,1,0:T(8,128)S(1)} %shard_map.50.own_ref.inner_ref, f32[16,64,128]{2,1,0:T(8,128)S(1)} %get-tuple-element.49.inner_ref.own_ref, f32[16,64,128]{2,1,0:T(8,128)S(1)} %shard_map.52.outer_ref, ...), custom_call_target="tpu_custom_call" | custom-call | flops 10000000000 | bytes 1000000 | tf_op jit(solution)/shard_map/pallas_call | solution.py:318
  26.0 1.9 %collective-permute-start.10 = (bf16[4,16,16,128]{3,2,1,0:T(8,128)(2,1)S(1)}, bf16[4,16,16,128]{3,2,1,0:T(8,128)(2,1)S(1)}, u32[]{:S(2)}, u32[]{:S(2)}) collective-permute-start(bf16[4,16,16,128]{3,2,1,0:T(8,128)(2,1)S(1)} %get-tuple-element.53), channel_id=1, source_target_pairs={{8,16},{16,8},{24,25},{25,24},{17,9},{9,17},{1,2},{2,1},{10,18},{1... | collective-permute-start | bytes 786440 | tf_op jit(solution)/shard_map/ppermute | solution.py:419
  28.0 1.3 %shard_map.54 = (bf16[4,16,16,128]{3,2,1,0:T(8,128)(2,1)S(1)}, f32[16,64,128]{2,1,0:T(8,128)S(1)}) custom-call(f32[16,64,128]{2,1,0:T(8,128)S(1)} %get-tuple-element.49.inner_ref.own_ref, f32[16,64,128]{2,1,0:T(8,128)S(1)} %shard_map.50.own_ref.inner_ref, bf16[4,16,16,128]{3,2,1,0:T(8,128)(2,1)S(1)} %collective-permute-done.9.outer_ref, ...), custom_call_target="tpu_custom_call" | custom-call | flops 10000000000 | bytes 1000000 | tf_op jit(solution)/shard_map/pallas_call | solution.py:318
  29.3 3.8 %collective-permute-start.12 = (bf16[4,16,16,128]{3,2,1,0:T(8,128)(2,1)S(1)}, bf16[4,16,16,128]{3,2,1,0:T(8,128)(2,1)S(1)}, u32[]{:S(2)}, u32[]{:S(2)}) collective-permute-start(bf16[4,16,16,128]{3,2,1,0:T(8,128)(2,1)S(1)} %get-tuple-element.54), channel_id=1, source_target_pairs={{8,16},{16,8},{24,25},{25,24},{17,9},{9,17},{1,2},{2,1},{10,18},{1... | collective-permute-start | bytes 786440 | tf_op jit(solution)/shard_map/ppermute | solution.py:422
  33.1 1.6 %collective-permute-start.11 = (bf16[4,16,16,128]{3,2,1,0:T(8,128)(2,1)S(1)}, bf16[4,16,16,128]{3,2,1,0:T(8,128)(2,1)S(1)}, u32[]{:S(2)}, u32[]{:S(2)}) collective-permute-start(bf16[4,16,16,128]{3,2,1,0:T(8,128)(2,1)S(1)} %get-tuple-element.54), channel_id=1, source_target_pairs={{0,8},{8,0},{16,24},{24,16},{25,17},{17,25},{9,1},{1,9},{2,10},{10... | collective-permute-start | bytes 786440 | tf_op jit(solution)/shard_map/ppermute | solution.py:421
  34.7 1.3 %shard_map.55.own_ref.inner_ref = f32[16,64,128]{2,1,0:T(8,128)S(1)} custom-call(f32[16,64,128]{2,1,0:T(8,128)S(1)} %get-tuple-element.50.own_ref.inner_ref, f32[16,64,128]{2,1,0:T(8,128)S(1)} %get-tuple-element.52.inner_ref.own_ref, bf16[4,16,16,128]{3,2,1,0:T(8,128)(2,1)S(1)} %collective-permute-done.10.outer_ref.own_ref, ...), custom_call_target="tpu_custom_call" | custom-call | flops 10000000000 | bytes 1000000 | tf_op jit(solution)/shard_map/pallas_call | solution.py:318
  36.0 1.3 %shard_map.56 = (bf16[4,16,16,128]{3,2,1,0:T(8,128)(2,1)S(1)}, f32[16,64,128]{2,1,0:T(8,128)S(1)}) custom-call(f32[16,64,128]{2,1,0:T(8,128)S(1)} %get-tuple-element.52.inner_ref.own_ref, f32[16,64,128]{2,1,0:T(8,128)S(1)} %get-tuple-element.50.own_ref.inner_ref, bf16[4,16,16,128]{3,2,1,0:T(8,128)(2,1)S(1)} %collective-permute-done.11.outer_ref, ...), custom_call_target="tpu_custom_call" | custom-call | flops 10000000000 | bytes 1000000 | tf_op jit(solution)/shard_map/pallas_call | solution.py:318
  38.2 1.3 %shard_map.57.outer_ref = f32[16,64,128]{2,1,0:T(8,128)S(1)} custom-call(bf16[4,16,16,128]{3,2,1,0:T(8,128)(2,1)S(1)} %collective-permute-done.10.outer_ref.own_ref, f32[16,64,128]{2,1,0:T(8,128)S(1)} %get-tuple-element.50.own_ref.inner_ref, bf16[4,16,16,128]{3,2,1,0:T(8,128)(2,1)S(1)} %collective-permute-done.12.outer_ref, ...), custom_call_target="tpu_custom_call" | custom-call | flops 10000000000 | bytes 1000000 | tf_op jit(solution)/shard_map/pallas_call | solution.py:318
  39.5 1.3 %shard_map.58 = (bf16[16,16,128]{2,1,0:T(8,128)(2,1)S(1)}, bf16[16,16,128]{2,1,0:T(8,128)(2,1)S(1)}, bf16[16,16,128]{2,1,0:T(8,128)(2,1)S(1)}, bf16[16,16,128]{2,1,0:T(8,128)(2,1)S(1)}) custom-call(f32[16,64,128]{2,1,0:T(8,128)S(1)} %shard_map.55.own_ref.inner_ref, f32[16,64,128]{2,1,0:T(8,128)S(1)} %get-tuple-element.55.inner_ref.own_ref, ...), custom_call_target="tpu_custom_call" | custom-call | flops 10000000000 | bytes 1000000 | tf_op jit(solution)/shard_map/pallas_call | solution.py:318
  40.8 2.2 %collective-permute-start.13 = (bf16[16,16,128]{2,1,0:T(8,128)(2,1)S(1)}, bf16[16,16,128]{2,1,0:T(8,128)(2,1)S(1)}, u32[]{:S(2)}, u32[]{:S(2)}) collective-permute-start(bf16[16,16,128]{2,1,0:T(8,128)(2,1)S(1)} %get-tuple-element.57), channel_id=1, source_target_pairs={{0,8},{8,0},{16,24},{24,16},{1,9},{9,1},{17,25},{25,17},{2,10},{10... | collective-permute-start | bytes 196616 | tf_op jit(solution)/shard_map/ppermute | solution.py:351
  42.9 1.7 %collective-permute-start.15 = (bf16[16,16,128]{2,1,0:T(8,128)(2,1)S(1)}, bf16[16,16,128]{2,1,0:T(8,128)(2,1)S(1)}, u32[]{:S(2)}, u32[]{:S(2)}) collective-permute-start(bf16[16,16,128]{2,1,0:T(8,128)(2,1)S(1)} %get-tuple-element.59), channel_id=1, source_target_pairs={{0,24},{8,16},{16,8},{24,0},{1,25},{9,17},{17,9},{25,1},{2,26},{10... | collective-permute-start | bytes 196616 | tf_op jit(solution)/shard_map/ppermute | solution.py:351
  44.7 1.3 %shard_map.59 = (bf16[16,16,128]{2,1,0:T(8,128)(2,1)S(1)}, bf16[16,16,128]{2,1,0:T(8,128)(2,1)S(1)}, bf16[16,16,128]{2,1,0:T(8,128)(2,1)S(1)}, bf16[16,16,128]{2,1,0:T(8,128)(2,1)S(1)}) custom-call(f32[16,64,128]{2,1,0:T(8,128)S(1)} %get-tuple-element.55.inner_ref.own_ref, f32[16,64,128]{2,1,0:T(8,128)S(1)} %shard_map.55.own_ref.inner_ref, ...), custom_call_target="tpu_custom_call" | custom-call | flops 10000000000 | bytes 1000000 | tf_op jit(solution)/shard_map/pallas_call | solution.py:318
  46.2 1.9 %collective-permute-start.19 = (bf16[16,16,128]{2,1,0:T(8,128)(2,1)S(1)}, bf16[16,16,128]{2,1,0:T(8,128)(2,1)S(1)}, u32[]{:S(2)}, u32[]{:S(2)}) collective-permute-start(bf16[16,16,128]{2,1,0:T(8,128)(2,1)S(1)} %get-tuple-element.64), channel_id=1, source_target_pairs={{0,24},{8,16},{16,8},{24,0},{1,25},{9,17},{17,9},{25,1},{2,26},{10... | collective-permute-start | bytes 196616 | tf_op jit(solution)/shard_map/ppermute | solution.py:351
  49.3 2.1 %collective-permute-done.19.refs_7_ = bf16[16,16,128]{2,1,0:T(8,128)(2,1)S(1)} collective-permute-done((bf16[16,16,128]{2,1,0:T(8,128)(2,1)S(1)}, bf16[16,16,128]{2,1,0:T(8,128)(2,1)S(1)}, u32[]{:S(2)}, u32[]{:S(2)}) %collective-permute-start.19) | collective-permute-done | bytes 65568 | tf_op jit(solution)/shard_map/ppermute | solution.py:351
  (43 shorter events, 10.6 us)
Async XLA Ops:
  1.0 1.2 %copy-start = (f32[16,16,8,128]{3,2,1,0:T(8,128)S(1)}, f32[16,16,8,128]{3,2,1,0:T(8,128)}, u32[]{:S(2)}) copy-start(f32[16,16,8,128]{3,2,1,0:T(8,128)} %param.4) | copy-start | bytes 3145732
  2.7 4.9 %collective-permute-start = (bf16[22,16,128]{2,1,0:T(8,128)(2,1)S(1)}, bf16[22,16,128]{2,1,0:T(8,128)(2,1)S(1)}, u32[]{:S(2)}, u32[]{:S(2)}) collective-permute-start(bf16[22,16,128]{2,1,0:T(8,128)(2,1)S(1)} %get-tuple-element.36), channel_id=1, source_target_pairs={{0,8},{8,0},{16,24},{24,16},{1,9},{9,1},{17,25},{25,17},{2,10},{10... | collective-permute-start | bytes 270344 | tf_op jit(solution)/shard_map/ppermute | solution.py:351
  3.5 4.2 %collective-permute-start.1 = (bf16[22,16,128]{2,1,0:T(8,128)(2,1)S(1)}, bf16[22,16,128]{2,1,0:T(8,128)(2,1)S(1)}, u32[]{:S(2)}, u32[]{:S(2)}) collective-permute-start(bf16[22,16,128]{2,1,0:T(8,128)(2,1)S(1)} %get-tuple-element.37), channel_id=1, source_target_pairs={{0,16},{8,24},{16,0},{24,8},{1,17},{9,25},{17,1},{25,9},{2,18},{10... | collective-permute-start | bytes 270344 | tf_op jit(solution)/shard_map/ppermute | solution.py:351
  4.7 5.5 %collective-permute-start.2 = (bf16[22,16,128]{2,1,0:T(8,128)(2,1)S(1)}, bf16[22,16,128]{2,1,0:T(8,128)(2,1)S(1)}, u32[]{:S(2)}, u32[]{:S(2)}) collective-permute-start(bf16[22,16,128]{2,1,0:T(8,128)(2,1)S(1)} %get-tuple-element.38), channel_id=1, source_target_pairs={{0,24},{8,16},{16,8},{24,0},{1,25},{9,17},{17,9},{25,1},{2,26},{10... | collective-permute-start | bytes 270344 | tf_op jit(solution)/shard_map/ppermute | solution.py:351
  5.2 2.3 %copy-start.1 = (bf16[512,64]{0,1:T(8,128)(2,1)S(1)}, bf16[512,64]{0,1:T(8,128)(2,1)}, u32[]{:S(2)}) copy-start(bf16[512,64]{0,1:T(8,128)(2,1)} %param.6) | copy-start | bytes 196612
  5.6 8.4 %collective-permute-start.4 = (bf16[16,16,128]{2,1,0:T(8,128)(2,1)S(1)}, bf16[16,16,128]{2,1,0:T(8,128)(2,1)S(1)}, u32[]{:S(2)}, u32[]{:S(2)}) collective-permute-start(bf16[16,16,128]{2,1,0:T(8,128)(2,1)S(1)} %get-tuple-element.43), channel_id=1, source_target_pairs={{0,16},{8,24},{16,0},{24,8},{1,17},{9,25},{17,1},{25,9},{2,18},{10... | collective-permute-start | bytes 196616 | tf_op jit(solution)/shard_map/ppermute | solution.py:351
  6.9 7.1 %collective-permute-start.5 = (bf16[16,16,128]{2,1,0:T(8,128)(2,1)S(1)}, bf16[16,16,128]{2,1,0:T(8,128)(2,1)S(1)}, u32[]{:S(2)}, u32[]{:S(2)}) collective-permute-start(bf16[16,16,128]{2,1,0:T(8,128)(2,1)S(1)} %get-tuple-element.44), channel_id=1, source_target_pairs={{0,24},{8,16},{16,8},{24,0},{1,25},{9,17},{17,9},{25,1},{2,26},{10... | collective-permute-start | bytes 196616 | tf_op jit(solution)/shard_map/ppermute | solution.py:351
  10.2 0.8 %copy-start.2 = (bf16[64,512]{1,0:T(8,128)(2,1)S(1)}, bf16[64,512]{1,0:T(8,128)(2,1)}, u32[]{:S(2)}) copy-start(bf16[64,512]{1,0:T(8,128)(2,1)} %param.7) | copy-start | bytes 196612
  10.4 3.7 %collective-permute-start.3 = (bf16[16,16,128]{2,1,0:T(8,128)(2,1)S(1)}, bf16[16,16,128]{2,1,0:T(8,128)(2,1)S(1)}, u32[]{:S(2)}, u32[]{:S(2)}) collective-permute-start(bf16[16,16,128]{2,1,0:T(8,128)(2,1)S(1)} %get-tuple-element.42), channel_id=1, source_target_pairs={{0,8},{8,0},{16,24},{24,16},{1,9},{9,1},{17,25},{25,17},{2,10},{10... | collective-permute-start | bytes 196616 | tf_op jit(solution)/shard_map/ppermute | solution.py:351
  11.1 8.7 %collective-permute-start.6 = (bf16[4,20,16,128]{3,2,1,0:T(8,128)(2,1)S(1)}, bf16[4,20,16,128]{3,2,1,0:T(8,128)(2,1)S(1)}, u32[]{:S(2)}, u32[]{:S(2)}) collective-permute-start(bf16[4,20,16,128]{3,2,1,0:T(8,128)(2,1)S(1)} %get-tuple-element.45.refs_8_), channel_id=1, source_target_pairs={{8,16},{16,8},{24,25},{25,24},{17,9},{9,17},{1,2},{2,1},{10,18},{1... | collective-permute-start | bytes 983048 | tf_op jit(solution)/shard_map/ppermute | solution.py:382
  14.2 9.3 %collective-permute-start.8 = (bf16[4,17,16,128]{3,2,1,0:T(8,128)(2,1)S(1)}, bf16[4,17,16,128]{3,2,1,0:T(8,128)(2,1)S(1)}, u32[]{:S(2)}, u32[]{:S(2)}) collective-permute-start(bf16[4,17,16,128]{3,2,1,0:T(8,128)(2,1)S(1)} %get-tuple-element.48), channel_id=1, source_target_pairs={{8,16},{16,8},{24,25},{25,24},{17,9},{9,17},{1,2},{2,1},{10,18},{1... | collective-permute-start | bytes 835592 | tf_op jit(solution)/shard_map/ppermute | solution.py:390
  16.8 4.2 %collective-permute-start.7 = (bf16[4,17,16,128]{3,2,1,0:T(8,128)(2,1)S(1)}, bf16[4,17,16,128]{3,2,1,0:T(8,128)(2,1)S(1)}, u32[]{:S(2)}, u32[]{:S(2)}) collective-permute-start(bf16[4,17,16,128]{3,2,1,0:T(8,128)(2,1)S(1)} %get-tuple-element.48), channel_id=1, source_target_pairs={{0,8},{8,0},{16,24},{24,16},{25,17},{17,25},{9,1},{1,9},{2,10},{10... | collective-permute-start | bytes 835592 | tf_op jit(solution)/shard_map/ppermute | solution.py:389
  22.3 5.7 %collective-permute-start.9 = (bf16[4,16,16,128]{3,2,1,0:T(8,128)(2,1)S(1)}, bf16[4,16,16,128]{3,2,1,0:T(8,128)(2,1)S(1)}, u32[]{:S(2)}, u32[]{:S(2)}) collective-permute-start(bf16[4,16,16,128]{3,2,1,0:T(8,128)(2,1)S(1)} %get-tuple-element.51), channel_id=1, source_target_pairs={{0,8},{8,0},{16,24},{24,16},{25,17},{17,25},{9,1},{1,9},{2,10},{10... | collective-permute-start | bytes 786440 | tf_op jit(solution)/shard_map/ppermute | solution.py:411
  26.0 8.7 %collective-permute-start.10 = (bf16[4,16,16,128]{3,2,1,0:T(8,128)(2,1)S(1)}, bf16[4,16,16,128]{3,2,1,0:T(8,128)(2,1)S(1)}, u32[]{:S(2)}, u32[]{:S(2)}) collective-permute-start(bf16[4,16,16,128]{3,2,1,0:T(8,128)(2,1)S(1)} %get-tuple-element.53), channel_id=1, source_target_pairs={{8,16},{16,8},{24,25},{25,24},{17,9},{9,17},{1,2},{2,1},{10,18},{1... | collective-permute-start | bytes 786440 | tf_op jit(solution)/shard_map/ppermute | solution.py:419
  29.3 8.9 %collective-permute-start.12 = (bf16[4,16,16,128]{3,2,1,0:T(8,128)(2,1)S(1)}, bf16[4,16,16,128]{3,2,1,0:T(8,128)(2,1)S(1)}, u32[]{:S(2)}, u32[]{:S(2)}) collective-permute-start(bf16[4,16,16,128]{3,2,1,0:T(8,128)(2,1)S(1)} %get-tuple-element.54), channel_id=1, source_target_pairs={{8,16},{16,8},{24,25},{25,24},{17,9},{9,17},{1,2},{2,1},{10,18},{1... | collective-permute-start | bytes 786440 | tf_op jit(solution)/shard_map/ppermute | solution.py:422
  33.1 2.9 %collective-permute-start.11 = (bf16[4,16,16,128]{3,2,1,0:T(8,128)(2,1)S(1)}, bf16[4,16,16,128]{3,2,1,0:T(8,128)(2,1)S(1)}, u32[]{:S(2)}, u32[]{:S(2)}) collective-permute-start(bf16[4,16,16,128]{3,2,1,0:T(8,128)(2,1)S(1)} %get-tuple-element.54), channel_id=1, source_target_pairs={{0,8},{8,0},{16,24},{24,16},{25,17},{17,25},{9,1},{1,9},{2,10},{10... | collective-permute-start | bytes 786440 | tf_op jit(solution)/shard_map/ppermute | solution.py:421
  37.3 7.4 %collective-permute-start.16 = (bf16[4,16,16,128]{3,2,1,0:T(8,128)(2,1)S(1)}, bf16[4,16,16,128]{3,2,1,0:T(8,128)(2,1)S(1)}, u32[]{:S(2)}, u32[]{:S(2)}) collective-permute-start(bf16[4,16,16,128]{3,2,1,0:T(8,128)(2,1)S(1)} %get-tuple-element.60), channel_id=1, source_target_pairs={{0,8},{8,0},{16,24},{24,16},{25,17},{17,25},{9,1},{1,9},{2,10},{10... | collective-permute-start | bytes 786440 | tf_op jit(solution)/shard_map/ppermute | solution.py:411
  40.8 5.4 %collective-permute-start.13 = (bf16[16,16,128]{2,1,0:T(8,128)(2,1)S(1)}, bf16[16,16,128]{2,1,0:T(8,128)(2,1)S(1)}, u32[]{:S(2)}, u32[]{:S(2)}) collective-permute-start(bf16[16,16,128]{2,1,0:T(8,128)(2,1)S(1)} %get-tuple-element.57), channel_id=1, source_target_pairs={{0,8},{8,0},{16,24},{24,16},{1,9},{9,1},{17,25},{25,17},{2,10},{10... | collective-permute-start | bytes 196616 | tf_op jit(solution)/shard_map/ppermute | solution.py:351
  42.9 5.2 %collective-permute-start.14 = (bf16[16,16,128]{2,1,0:T(8,128)(2,1)S(1)}, bf16[16,16,128]{2,1,0:T(8,128)(2,1)S(1)}, u32[]{:S(2)}, u32[]{:S(2)}) collective-permute-start(bf16[16,16,128]{2,1,0:T(8,128)(2,1)S(1)} %get-tuple-element.58), channel_id=1, source_target_pairs={{0,16},{8,24},{16,0},{24,8},{1,17},{9,25},{17,1},{25,9},{2,18},{10... | collective-permute-start | bytes 196616 | tf_op jit(solution)/shard_map/ppermute | solution.py:351
  42.9 5.2 %collective-permute-start.15 = (bf16[16,16,128]{2,1,0:T(8,128)(2,1)S(1)}, bf16[16,16,128]{2,1,0:T(8,128)(2,1)S(1)}, u32[]{:S(2)}, u32[]{:S(2)}) collective-permute-start(bf16[16,16,128]{2,1,0:T(8,128)(2,1)S(1)} %get-tuple-element.59), channel_id=1, source_target_pairs={{0,24},{8,16},{16,8},{24,0},{1,25},{9,17},{17,9},{25,1},{2,26},{10... | collective-permute-start | bytes 196616 | tf_op jit(solution)/shard_map/ppermute | solution.py:351
  45.9 2.2 %collective-permute-start.17 = (bf16[16,16,128]{2,1,0:T(8,128)(2,1)S(1)}, bf16[16,16,128]{2,1,0:T(8,128)(2,1)S(1)}, u32[]{:S(2)}, u32[]{:S(2)}) collective-permute-start(bf16[16,16,128]{2,1,0:T(8,128)(2,1)S(1)} %get-tuple-element.62), channel_id=1, source_target_pairs={{0,8},{8,0},{16,24},{24,16},{1,9},{9,1},{17,25},{25,17},{2,10},{10... | collective-permute-start | bytes 196616 | tf_op jit(solution)/shard_map/ppermute | solution.py:351
  46.2 3.1 %collective-permute-start.18 = (bf16[16,16,128]{2,1,0:T(8,128)(2,1)S(1)}, bf16[16,16,128]{2,1,0:T(8,128)(2,1)S(1)}, u32[]{:S(2)}, u32[]{:S(2)}) collective-permute-start(bf16[16,16,128]{2,1,0:T(8,128)(2,1)S(1)} %get-tuple-element.63), channel_id=1, source_target_pairs={{0,16},{8,24},{16,0},{24,8},{1,17},{9,25},{17,1},{25,9},{2,18},{10... | collective-permute-start | bytes 196616 | tf_op jit(solution)/shard_map/ppermute | solution.py:351
  46.2 5.2 %collective-permute-start.19 = (bf16[16,16,128]{2,1,0:T(8,128)(2,1)S(1)}, bf16[16,16,128]{2,1,0:T(8,128)(2,1)S(1)}, u32[]{:S(2)}, u32[]{:S(2)}) collective-permute-start(bf16[16,16,128]{2,1,0:T(8,128)(2,1)S(1)} %get-tuple-element.64), channel_id=1, source_target_pairs={{0,24},{8,16},{16,8},{24,0},{1,25},{9,17},{17,9},{25,1},{2,26},{10... | collective-permute-start | bytes 196616 | tf_op jit(solution)/shard_map/ppermute | solution.py:351

commit v10 on v9

--- a/solution.py
+++ b/solution.py
@@ -12,6 +12,8 @@
 PACK = 16
 GROUP = 4
 PARTS = 8
+COLUMN_COST = 10**10
+A0_COST = 1024
 VMEM = pl.BlockSpec(memory_space=pltpu.VMEM)
 LIMIT = 24 * 1024 * 1024
 
@@ -170,14 +172,14 @@
 
 
 def column_kernel(
-    t, kind, group, sends, own_ref, inner_ref, outer_ref, flux_ref, from_ref, w_in_ref, w_out_ref, *rest
+    t, kind, group, sends, behind, own_ref, inner_ref, outer_ref, flux_ref, from_ref, w_in_ref, w_out_ref, *rest
 ):
     last = t == STEPS - 1
     coef = rest[-1]
     count, spec, lev = from_ref.shape[0], from_ref.shape[2], flux_ref.shape[3]
     depth, spec_all, width_y = inner_ref.shape
     place, species = place_and_species(count)
-    rest = list(rest)
+    rest = list(rest)[behind:]
     outs = rest[:count] if last else None
     send_ref = rest[count] if outs else rest.pop(0) if sends else None
     new_ref = None if last else rest.pop(0)
@@ -312,7 +314,7 @@
         copy.wait()
 
 
-def call(kernel, out_shape, args, scratch=(), far_out=False):
+def call(kernel, out_shape, args, scratch=(), far_out=False, cost=COLUMN_COST):
     many = isinstance(out_shape, (list, tuple))
     anywhere = pl.BlockSpec(memory_space=pl.ANY)
     return pl.pallas_call(
@@ -322,7 +324,7 @@
         out_specs=[VMEM] * len(out_shape) if many else anywhere if far_out else VMEM,
         scratch_shapes=scratch,
         compiler_params=pltpu.CompilerParams(vmem_limit_bytes=LIMIT),
-        cost_estimate=pl.CostEstimate(flops=10**10, bytes_accessed=10**6, transcendentals=0),
+        cost_estimate=pl.CostEstimate(flops=cost, bytes_accessed=cost // 10**4, transcendentals=0),
     )(*args)
 
 
@@ -392,7 +394,7 @@
         pltpu.VMEM((7, depth, width_y), f32),
     ]
 
-    def column(t, kind, own, inner, outer, sends=True):
+    def column(t, kind, own, inner, outer, sends=True, after=()):
         scratch = list(common)
         if t < STEPS - 1:
             outs = [sent, row] if sends else [row]
@@ -400,27 +402,27 @@
             outs = [piece] * count
             scratch = [pltpu.VMEM(sent.shape, bf16), *common]
         return call(
-            functools.partial(column_kernel, t, kind, GROUP, sends),
+            functools.partial(column_kernel, t, kind, GROUP, sends, len(after)),
             outs,
-            (own, inner, outer, flux, from_a if kind == "A" else from_b, w_in, w_out),
+            (own, inner, outer, flux, from_a if kind == "A" else from_b, w_in, w_out, *after),
+            cost=A0_COST if kind == "A" and t == 0 else COLUMN_COST,
             scratch=scratch,
         )
 
     for t in range(0, STEPS, 2):
         send_a, new_a = column(t, "A", a, b, halo_a)
         halo_a = lax.ppermute(send_a, AXES, swap_a)
-        (new_b,) = column(t, "B", b, a, halo_b, sends=False)
-        (ghost,) = column(t, "G", halo_b, b, halo_c, sends=False)
-        a, b = new_a, new_b
-        made_b = column(t + 1, "B", b, a, ghost)
+        (new_b,) = column(t, "B", b, a, halo_b, sends=False, after=(send_a,) if t == 0 else ())
+        made_a = column(t + 1, "A", new_a, new_b, halo_a)
+        (ghost,) = column(t, "G", halo_b, b, halo_c, sends=False, after=made_a[:1])
+        made_b = column(t + 1, "B", new_b, new_a, ghost)
         if t + 1 == STEPS - 1:
-            pieces = [*exchange(made_b), *exchange(column(t + 1, "A", a, b, halo_a))]
+            pieces = [*exchange(made_b), *exchange(made_a)]
             break
-        halo_b = lax.ppermute(made_b[0], AXES, swap_b)
-        send_a, new_a = column(t + 1, "A", a, b, halo_a)
+        (send_b, b), (send_a, a) = made_b, made_a
+        halo_b = lax.ppermute(send_b, AXES, swap_b)
         halo_a = lax.ppermute(send_a, AXES, swap_a)
         halo_c = lax.ppermute(send_a, AXES, swap_b)
-        a, b = new_a, made_b[1]
     out = call(
         functools.partial(finish_kernel, count),
         shape((spec, depth * width, width_y), f32),

time: 53 us -> 52.6 us (level)
  starting transfers between devices: 26.6 us -> 24.8 us
  waiting for transfers between devices: 7.61 us -> 8.95 us
    ppermute x1, waiting for transfers between devices: 0.01 us -> 2.95 us  [by_columns(): halo_b = lax.ppermute(send_b, AXES, swap_b)]
    ppermute x2, starting transfers between devices: 6.44 us -> 4.51 us  [by_columns(): halo_c = lax.ppermute(send_a, AXES, swap_b)]
    ppermute x1, waiting for transfers between devices: 1.77 us -> 0.01 us  [by_columns(): halo_b = from_b = lax.ppermute(send_b, AXES, swap_b)]
    ppermute x3, starting transfers between devices: 3.71 us -> 4.79 us  [by_columns(): halo_a = lax.ppermute(send_a, AXES, swap_a)]
    ppermute x12, starting transfers between devices: 10.5 us -> 9.56 us  [swapped(): return lax.ppermute(piece, 'species', [(s, s ^ d) for s in range(count)])]
    ppermute x1, starting transfers between devices: 1.15 us -> 0.32 us  [by_columns(): halo_a = from_a = lax.ppermute(send_a, AXES, swap_a)]
    ppermute x1, starting transfers between devices: 2.94 us -> 3.52 us  [by_columns(): halo_b = from_b = lax.ppermute(send_b, AXES, swap_b)]
  transfers between devices with their start and end apart: 20 -> 20, of which waited for: 4 -> 5; matrix products, arithmetic and copies ran while one was open for 0% -> 0% of each run, Pallas kernels for 26% -> 26%
where the time goes in v10:
time: 52.6 us; the launch traced here: 52.2 us
  starting transfers between devices  24.8 us (47%)
  Pallas kernels  15.1 us (29%)
  waiting for transfers between devices  8.95 us (17%)
  local copies, waits for them, and re-layouts  1.85 us (4%)
  other arithmetic  1.05 us (2%)
    pallas_call x15, Pallas kernels, call(): pl.pallas_call(kernel, out_shape=out_shape, in_specs=[VMEM] * len(args),...  15.1 us
    ppermute x12, starting transfers between devices, swapped(): return lax.ppermute(piece, 'species', [(s, s ^ d) for s in range(count)])  9.56 us
    ppermute x12, waiting for transfers between devices, swapped(): return lax.ppermute(piece, 'species', [(s, s ^ d) for s in range(count)])  5.97 us
    ppermute x3, starting transfers between devices, by_columns(): halo_a = lax.ppermute(send_a, AXES, swap_a)  4.79 us
    ppermute x2, starting transfers between devices, by_columns(): halo_c = lax.ppermute(send_a, AXES, swap_b)  4.51 us
    ppermute x1, starting transfers between devices, by_columns(): halo_b = from_b = lax.ppermute(send_b, AXES, swap_b)  3.52 us
    ppermute x1, waiting for transfers between devices, by_columns(): halo_b = lax.ppermute(send_b, AXES, swap_b)  2.95 us
    ppermute x1, starting transfers between devices, by_columns(): halo_b = lax.ppermute(send_b, AXES, swap_b)  2.1 us
  transfers between devices with their start and end apart: 20, of which 5 were waited for; matrix products, arithmetic and copies ran while one was open for 0% of the time, Pallas kernels for 26%

profile of v10, /device:TPU:17, one launch (start us, length us, event | category | flops | bytes accessed | tf_op | source)
XLA Modules:
  0.0 52.2 jit_solution(11389415609345900018)
XLA Ops:
  5.6 1.3 %collective-permute-start.4 = (bf16[16,16,128]{2,1,0:T(8,128)(2,1)S(1)}, bf16[16,16,128]{2,1,0:T(8,128)(2,1)S(1)}, u32[]{:S(2)}, u32[]{:S(2)}) collective-permute-start(bf16[16,16,128]{2,1,0:T(8,128)(2,1)S(1)} %get-tuple-element.43), channel_id=1, source_target_pairs={{0,16},{8,24},{16,0},{24,8},{1,17},{9,25},{17,1},{25,9},{2,18},{10... | collective-permute-start | bytes 196616 | tf_op jit(solution)/shard_map/ppermute | solution.py:353
  7.7 2.5 %collective-permute-done.2.refs_3_.refs_7_ = bf16[22,16,128]{2,1,0:T(8,128)(2,1)S(1)} collective-permute-done((bf16[22,16,128]{2,1,0:T(8,128)(2,1)S(1)}, bf16[22,16,128]{2,1,0:T(8,128)(2,1)S(1)}, u32[]{:S(2)}, u32[]{:S(2)}) %collective-permute-start.2) | collective-permute-done | bytes 90144 | tf_op jit(solution)/shard_map/ppermute | solution.py:353
  10.5 3.5 %collective-permute-start.6 = (bf16[4,20,16,128]{3,2,1,0:T(8,128)(2,1)S(1)}, bf16[4,20,16,128]{3,2,1,0:T(8,128)(2,1)S(1)}, u32[]{:S(2)}, u32[]{:S(2)}) collective-permute-start(bf16[4,20,16,128]{3,2,1,0:T(8,128)(2,1)S(1)} %get-tuple-element.45.refs_8_), channel_id=1, source_target_pairs={{8,16},{16,8},{24,25},{25,24},{17,9},{9,17},{1,2},{2,1},{10,18},{1... | collective-permute-start | bytes 983048 | tf_op jit(solution)/shard_map/ppermute | solution.py:384
  15.2 2.4 %collective-permute-start.8 = (bf16[4,17,16,128]{3,2,1,0:T(8,128)(2,1)S(1)}, bf16[4,17,16,128]{3,2,1,0:T(8,128)(2,1)S(1)}, u32[]{:S(2)}, u32[]{:S(2)}) collective-permute-start(bf16[4,17,16,128]{3,2,1,0:T(8,128)(2,1)S(1)} %get-tuple-element.48), channel_id=1, source_target_pairs={{8,16},{16,8},{24,25},{25,24},{17,9},{9,17},{1,2},{2,1},{10,18},{1... | collective-permute-start | bytes 835592 | tf_op jit(solution)/shard_map/ppermute | solution.py:392
  17.6 1.3 %shard_map.50 = (bf16[4,16,16,128]{3,2,1,0:T(8,128)(2,1)S(1)}, f32[16,64,128]{2,1,0:T(8,128)S(1)}) custom-call(f32[16,64,128]{2,1,0:T(8,128)S(1)} %get-tuple-element.46.own_ref.inner_ref, f32[16,64,128]{2,1,0:T(8,128)S(1)} %get-tuple-element.40.inner_ref.own_ref, bf16[4,17,16,128]{3,2,1,0:T(8,128)(2,1)S(1)} %collective-permute-done.7.outer_ref.from_ref, ...), custom_call_target="tpu_custom_call" | custom-call | flops 1024 | tf_op jit(solution)/shard_map/pallas_call | solution.py:320
  18.9 1.4 %collective-permute-start.9 = (bf16[4,16,16,128]{3,2,1,0:T(8,128)(2,1)S(1)}, bf16[4,16,16,128]{3,2,1,0:T(8,128)(2,1)S(1)}, u32[]{:S(2)}, u32[]{:S(2)}) collective-permute-start(bf16[4,16,16,128]{3,2,1,0:T(8,128)(2,1)S(1)} %get-tuple-element.49.rest_0_), channel_id=1, source_target_pairs={{0,8},{8,0},{16,24},{24,16},{25,17},{17,25},{9,1},{1,9},{2,10},{10... | collective-permute-start | bytes 786440 | tf_op jit(solution)/shard_map/ppermute | solution.py:414
  20.3 1.3 %shard_map.51.inner_ref.own_ref = f32[16,64,128]{2,1,0:T(8,128)S(1)} custom-call(f32[16,64,128]{2,1,0:T(8,128)S(1)} %get-tuple-element.40.inner_ref.own_ref, f32[16,64,128]{2,1,0:T(8,128)S(1)} %get-tuple-element.46.own_ref.inner_ref, bf16[4,20,16,128]{3,2,1,0:T(8,128)(2,1)S(1)} %collective-permute-done.6.outer_ref.from_ref.own_ref, ...), custom_call_target="tpu_custom_call" | custom-call | flops 10000000000 | bytes 1000000 | tf_op jit(solution)/shard_map/pallas_call | solution.py:320
  21.5 1.3 %shard_map.52 = (bf16[4,16,16,128]{3,2,1,0:T(8,128)(2,1)S(1)}, f32[16,64,128]{2,1,0:T(8,128)S(1)}) custom-call(f32[16,64,128]{2,1,0:T(8,128)S(1)} %get-tuple-element.50.own_ref.inner_ref, f32[16,64,128]{2,1,0:T(8,128)S(1)} %shard_map.51.inner_ref.own_ref, bf16[4,16,16,128]{3,2,1,0:T(8,128)(2,1)S(1)} %collective-permute-done.9.outer_ref, ...), custom_call_target="tpu_custom_call" | custom-call | flops 10000000000 | bytes 1000000 | tf_op jit(solution)/shard_map/pallas_call | solution.py:320
  22.8 2.1 %collective-permute-start.12 = (bf16[4,16,16,128]{3,2,1,0:T(8,128)(2,1)S(1)}, bf16[4,16,16,128]{3,2,1,0:T(8,128)(2,1)S(1)}, u32[]{:S(2)}, u32[]{:S(2)}) collective-permute-start(bf16[4,16,16,128]{3,2,1,0:T(8,128)(2,1)S(1)} %get-tuple-element.51.rest_0_), channel_id=1, source_target_pairs={{8,16},{16,8},{24,25},{25,24},{17,9},{9,17},{1,2},{2,1},{10,18},{1... | collective-permute-start | bytes 786440 | tf_op jit(solution)/shard_map/ppermute | solution.py:425
  24.9 1.8 %collective-permute-start.11 = (bf16[4,16,16,128]{3,2,1,0:T(8,128)(2,1)S(1)}, bf16[4,16,16,128]{3,2,1,0:T(8,128)(2,1)S(1)}, u32[]{:S(2)}, u32[]{:S(2)}) collective-permute-start(bf16[4,16,16,128]{3,2,1,0:T(8,128)(2,1)S(1)} %get-tuple-element.51.rest_0_), channel_id=1, source_target_pairs={{0,8},{8,0},{16,24},{24,16},{25,17},{17,25},{9,1},{1,9},{2,10},{10... | collective-permute-start | bytes 786440 | tf_op jit(solution)/shard_map/ppermute | solution.py:424
  26.7 1.3 %shard_map.53.outer_ref = f32[16,64,128]{2,1,0:T(8,128)S(1)} custom-call(bf16[4,20,16,128]{3,2,1,0:T(8,128)(2,1)S(1)} %collective-permute-done.6.outer_ref.from_ref.own_ref, f32[16,64,128]{2,1,0:T(8,128)S(1)} %get-tuple-element.40.inner_ref.own_ref, bf16[4,17,16,128]{3,2,1,0:T(8,128)(2,1)S(1)} %collective-permute-done.8.outer_ref, ...), custom_call_target="tpu_custom_call" | custom-call | flops 10000000000 | bytes 1000000 | tf_op jit(solution)/shard_map/pallas_call | solution.py:320
  28.0 1.3 %shard_map.54 = (bf16[4,16,16,128]{3,2,1,0:T(8,128)(2,1)S(1)}, f32[16,64,128]{2,1,0:T(8,128)S(1)}) custom-call(f32[16,64,128]{2,1,0:T(8,128)S(1)} %shard_map.51.inner_ref.own_ref, f32[16,64,128]{2,1,0:T(8,128)S(1)} %get-tuple-element.50.own_ref.inner_ref, f32[16,64,128]{2,1,0:T(8,128)S(1)} %shard_map.53.outer_ref, ...), custom_call_target="tpu_custom_call" | custom-call | flops 10000000000 | bytes 1000000 | tf_op jit(solution)/shard_map/pallas_call | solution.py:320
  29.3 2.1 %collective-permute-start.10 = (bf16[4,16,16,128]{3,2,1,0:T(8,128)(2,1)S(1)}, bf16[4,16,16,128]{3,2,1,0:T(8,128)(2,1)S(1)}, u32[]{:S(2)}, u32[]{:S(2)}) collective-permute-start(bf16[4,16,16,128]{3,2,1,0:T(8,128)(2,1)S(1)} %get-tuple-element.54), channel_id=1, source_target_pairs={{8,16},{16,8},{24,25},{25,24},{17,9},{9,17},{1,2},{2,1},{10,18},{1... | collective-permute-start | bytes 786440 | tf_op jit(solution)/shard_map/ppermute | solution.py:423
  31.4 1.3 %shard_map.56 = (bf16[4,16,16,128]{3,2,1,0:T(8,128)(2,1)S(1)}, f32[16,64,128]{2,1,0:T(8,128)S(1)}) custom-call(f32[16,64,128]{2,1,0:T(8,128)S(1)} %get-tuple-element.53.inner_ref.own_ref, f32[16,64,128]{2,1,0:T(8,128)S(1)} %get-tuple-element.52.own_ref.inner_ref, bf16[4,16,16,128]{3,2,1,0:T(8,128)(2,1)S(1)} %collective-permute-done.11.outer_ref, ...), custom_call_target="tpu_custom_call" | custom-call | flops 10000000000 | bytes 1000000 | tf_op jit(solution)/shard_map/pallas_call | solution.py:320
  32.7 1.6 %collective-permute-start.13 = (bf16[4,16,16,128]{3,2,1,0:T(8,128)(2,1)S(1)}, bf16[4,16,16,128]{3,2,1,0:T(8,128)(2,1)S(1)}, u32[]{:S(2)}, u32[]{:S(2)}) collective-permute-start(bf16[4,16,16,128]{3,2,1,0:T(8,128)(2,1)S(1)} %get-tuple-element.56), channel_id=1, source_target_pairs={{0,8},{8,0},{16,24},{24,16},{25,17},{17,25},{9,1},{1,9},{2,10},{10... | collective-permute-start | bytes 786440 | tf_op jit(solution)/shard_map/ppermute | solution.py:414
  34.3 3.0 %collective-permute-done.10.outer_ref.own_ref = bf16[4,16,16,128]{3,2,1,0:T(8,128)(2,1)S(1)} collective-permute-done((bf16[4,16,16,128]{3,2,1,0:T(8,128)(2,1)S(1)}, bf16[4,16,16,128]{3,2,1,0:T(8,128)(2,1)S(1)}, u32[]{:S(2)}, u32[]{:S(2)}) %collective-permute-start.10) | collective-permute-done | bytes 262176 | tf_op jit(solution)/shard_map/ppermute | solution.py:423
  37.3 1.3 %shard_map.55.inner_ref.own_ref = f32[16,64,128]{2,1,0:T(8,128)S(1)} custom-call(f32[16,64,128]{2,1,0:T(8,128)S(1)} %get-tuple-element.52.own_ref.inner_ref, f32[16,64,128]{2,1,0:T(8,128)S(1)} %get-tuple-element.53.inner_ref.own_ref, bf16[4,16,16,128]{3,2,1,0:T(8,128)(2,1)S(1)} %collective-permute-done.10.outer_ref.own_ref, ...), custom_call_target="tpu_custom_call" | custom-call | flops 10000000000 | bytes 1000000 | tf_op jit(solution)/shard_map/pallas_call | solution.py:320
  38.6 1.3 %shard_map.57 = (bf16[16,16,128]{2,1,0:T(8,128)(2,1)S(1)}, bf16[16,16,128]{2,1,0:T(8,128)(2,1)S(1)}, bf16[16,16,128]{2,1,0:T(8,128)(2,1)S(1)}, bf16[16,16,128]{2,1,0:T(8,128)(2,1)S(1)}) custom-call(f32[16,64,128]{2,1,0:T(8,128)S(1)} %get-tuple-element.55.own_ref.inner_ref, f32[16,64,128]{2,1,0:T(8,128)S(1)} %shard_map.55.inner_ref.own_ref, ...), custom_call_target="tpu_custom_call" | custom-call | flops 10000000000 | bytes 1000000 | tf_op jit(solution)/shard_map/pallas_call | solution.py:320
  39.8 1.3 %collective-permute-start.17 = (bf16[16,16,128]{2,1,0:T(8,128)(2,1)S(1)}, bf16[16,16,128]{2,1,0:T(8,128)(2,1)S(1)}, u32[]{:S(2)}, u32[]{:S(2)}) collective-permute-start(bf16[16,16,128]{2,1,0:T(8,128)(2,1)S(1)} %get-tuple-element.62), channel_id=1, source_target_pairs={{0,8},{8,0},{16,24},{24,16},{1,9},{9,1},{17,25},{25,17},{2,10},{10... | collective-permute-start | bytes 196616 | tf_op jit(solution)/shard_map/ppermute | solution.py:353
  41.1 1.7 %collective-permute-start.19 = (bf16[16,16,128]{2,1,0:T(8,128)(2,1)S(1)}, bf16[16,16,128]{2,1,0:T(8,128)(2,1)S(1)}, u32[]{:S(2)}, u32[]{:S(2)}) collective-permute-start(bf16[16,16,128]{2,1,0:T(8,128)(2,1)S(1)} %get-tuple-element.64), channel_id=1, source_target_pairs={{0,24},{8,16},{16,8},{24,0},{1,25},{9,17},{17,9},{25,1},{2,26},{10... | collective-permute-start | bytes 196616 | tf_op jit(solution)/shard_map/ppermute | solution.py:353
  42.8 1.3 %shard_map.58.outer_ref = f32[16,64,128]{2,1,0:T(8,128)S(1)} custom-call(bf16[4,16,16,128]{3,2,1,0:T(8,128)(2,1)S(1)} %collective-permute-done.10.outer_ref.own_ref, f32[16,64,128]{2,1,0:T(8,128)S(1)} %get-tuple-element.52.own_ref.inner_ref, bf16[4,16,16,128]{3,2,1,0:T(8,128)(2,1)S(1)} %collective-permute-done.12.outer_ref, ...), custom_call_target="tpu_custom_call" | custom-call | flops 10000000000 | bytes 1000000 | tf_op jit(solution)/shard_map/pallas_call | solution.py:320
  44.1 1.3 %shard_map.59 = (bf16[16,16,128]{2,1,0:T(8,128)(2,1)S(1)}, bf16[16,16,128]{2,1,0:T(8,128)(2,1)S(1)}, bf16[16,16,128]{2,1,0:T(8,128)(2,1)S(1)}, bf16[16,16,128]{2,1,0:T(8,128)(2,1)S(1)}) custom-call(f32[16,64,128]{2,1,0:T(8,128)S(1)} %shard_map.55.inner_ref.own_ref, f32[16,64,128]{2,1,0:T(8,128)S(1)} %get-tuple-element.55.own_ref.inner_ref, ...), custom_call_target="tpu_custom_call" | custom-call | flops 10000000000 | bytes 1000000 | tf_op jit(solution)/shard_map/pallas_call | solution.py:320
  45.7 2.0 %collective-permute-start.16 = (bf16[16,16,128]{2,1,0:T(8,128)(2,1)S(1)}, bf16[16,16,128]{2,1,0:T(8,128)(2,1)S(1)}, u32[]{:S(2)}, u32[]{:S(2)}) collective-permute-start(bf16[16,16,128]{2,1,0:T(8,128)(2,1)S(1)} %get-tuple-element.61), channel_id=1, source_target_pairs={{0,24},{8,16},{16,8},{24,0},{1,25},{9,17},{17,9},{25,1},{2,26},{10... | collective-permute-start | bytes 196616 | tf_op jit(solution)/shard_map/ppermute | solution.py:353
  48.8 2.1 %collective-permute-done.16.refs_3_ = bf16[16,16,128]{2,1,0:T(8,128)(2,1)S(1)} collective-permute-done((bf16[16,16,128]{2,1,0:T(8,128)(2,1)S(1)}, bf16[16,16,128]{2,1,0:T(8,128)(2,1)S(1)}, u32[]{:S(2)}, u32[]{:S(2)}) %collective-permute-start.16) | collective-permute-done | bytes 65568 | tf_op jit(solution)/shard_map/ppermute | solution.py:353
  (43 shorter events, 10.2 us)
Async XLA Ops:
  1.0 1.2 %copy-start = (f32[16,16,8,128]{3,2,1,0:T(8,128)S(1)}, f32[16,16,8,128]{3,2,1,0:T(8,128)}, u32[]{:S(2)}) copy-start(f32[16,16,8,128]{3,2,1,0:T(8,128)} %param.4) | copy-start | bytes 3145732
  2.7 4.8 %collective-permute-start = (bf16[22,16,128]{2,1,0:T(8,128)(2,1)S(1)}, bf16[22,16,128]{2,1,0:T(8,128)(2,1)S(1)}, u32[]{:S(2)}, u32[]{:S(2)}) collective-permute-start(bf16[22,16,128]{2,1,0:T(8,128)(2,1)S(1)} %get-tuple-element.36), channel_id=1, source_target_pairs={{0,8},{8,0},{16,24},{24,16},{1,9},{9,1},{17,25},{25,17},{2,10},{10... | collective-permute-start | bytes 270344 | tf_op jit(solution)/shard_map/ppermute | solution.py:353
  3.5 4.2 %collective-permute-start.1 = (bf16[22,16,128]{2,1,0:T(8,128)(2,1)S(1)}, bf16[22,16,128]{2,1,0:T(8,128)(2,1)S(1)}, u32[]{:S(2)}, u32[]{:S(2)}) collective-permute-start(bf16[22,16,128]{2,1,0:T(8,128)(2,1)S(1)} %get-tuple-element.37), channel_id=1, source_target_pairs={{0,16},{8,24},{16,0},{24,8},{1,17},{9,25},{17,1},{25,9},{2,18},{10... | collective-permute-start | bytes 270344 | tf_op jit(solution)/shard_map/ppermute | solution.py:353
  4.7 5.5 %collective-permute-start.2 = (bf16[22,16,128]{2,1,0:T(8,128)(2,1)S(1)}, bf16[22,16,128]{2,1,0:T(8,128)(2,1)S(1)}, u32[]{:S(2)}, u32[]{:S(2)}) collective-permute-start(bf16[22,16,128]{2,1,0:T(8,128)(2,1)S(1)} %get-tuple-element.38), channel_id=1, source_target_pairs={{0,24},{8,16},{16,8},{24,0},{1,25},{9,17},{17,9},{25,1},{2,26},{10... | collective-permute-start | bytes 270344 | tf_op jit(solution)/shard_map/ppermute | solution.py:353
  5.6 8.4 %collective-permute-start.4 = (bf16[16,16,128]{2,1,0:T(8,128)(2,1)S(1)}, bf16[16,16,128]{2,1,0:T(8,128)(2,1)S(1)}, u32[]{:S(2)}, u32[]{:S(2)}) collective-permute-start(bf16[16,16,128]{2,1,0:T(8,128)(2,1)S(1)} %get-tuple-element.43), channel_id=1, source_target_pairs={{0,16},{8,24},{16,0},{24,8},{1,17},{9,25},{17,1},{25,9},{2,18},{10... | collective-permute-start | bytes 196616 | tf_op jit(solution)/shard_map/ppermute | solution.py:353
  6.9 7.1 %collective-permute-start.5 = (bf16[16,16,128]{2,1,0:T(8,128)(2,1)S(1)}, bf16[16,16,128]{2,1,0:T(8,128)(2,1)S(1)}, u32[]{:S(2)}, u32[]{:S(2)}) collective-permute-start(bf16[16,16,128]{2,1,0:T(8,128)(2,1)S(1)} %get-tuple-element.44), channel_id=1, source_target_pairs={{0,24},{8,16},{16,8},{24,0},{1,25},{9,17},{17,9},{25,1},{2,26},{10... | collective-permute-start | bytes 196616 | tf_op jit(solution)/shard_map/ppermute | solution.py:353
  10.4 3.6 %collective-permute-start.3 = (bf16[16,16,128]{2,1,0:T(8,128)(2,1)S(1)}, bf16[16,16,128]{2,1,0:T(8,128)(2,1)S(1)}, u32[]{:S(2)}, u32[]{:S(2)}) collective-permute-start(bf16[16,16,128]{2,1,0:T(8,128)(2,1)S(1)} %get-tuple-element.42), channel_id=1, source_target_pairs={{0,8},{8,0},{16,24},{24,16},{1,9},{9,1},{17,25},{25,17},{2,10},{10... | collective-permute-start | bytes 196616 | tf_op jit(solution)/shard_map/ppermute | solution.py:353
  10.5 9.8 %collective-permute-start.6 = (bf16[4,20,16,128]{3,2,1,0:T(8,128)(2,1)S(1)}, bf16[4,20,16,128]{3,2,1,0:T(8,128)(2,1)S(1)}, u32[]{:S(2)}, u32[]{:S(2)}) collective-permute-start(bf16[4,20,16,128]{3,2,1,0:T(8,128)(2,1)S(1)} %get-tuple-element.45.refs_8_), channel_id=1, source_target_pairs={{8,16},{16,8},{24,25},{25,24},{17,9},{9,17},{1,2},{2,1},{10,18},{1... | collective-permute-start | bytes 983048 | tf_op jit(solution)/shard_map/ppermute | solution.py:384
  14.0 0.8 %copy-start.2 = (bf16[64,512]{1,0:T(8,128)(2,1)S(1)}, bf16[64,512]{1,0:T(8,128)(2,1)}, u32[]{:S(2)}) copy-start(bf16[64,512]{1,0:T(8,128)(2,1)} %param.7) | copy-start | bytes 196612
  14.2 0.8 %copy-start.1 = (bf16[512,64]{0,1:T(8,128)(2,1)S(1)}, bf16[512,64]{0,1:T(8,128)(2,1)}, u32[]{:S(2)}) copy-start(bf16[512,64]{0,1:T(8,128)(2,1)} %param.6) | copy-start | bytes 196612
  14.2 3.4 %collective-permute-start.7 = (bf16[4,17,16,128]{3,2,1,0:T(8,128)(2,1)S(1)}, bf16[4,17,16,128]{3,2,1,0:T(8,128)(2,1)S(1)}, u32[]{:S(2)}, u32[]{:S(2)}) collective-permute-start(bf16[4,17,16,128]{3,2,1,0:T(8,128)(2,1)S(1)} %get-tuple-element.48), channel_id=1, source_target_pairs={{0,8},{8,0},{16,24},{24,16},{25,17},{17,25},{9,1},{1,9},{2,10},{10... | collective-permute-start | bytes 835592 | tf_op jit(solution)/shard_map/ppermute | solution.py:391
  15.2 11.5 %collective-permute-start.8 = (bf16[4,17,16,128]{3,2,1,0:T(8,128)(2,1)S(1)}, bf16[4,17,16,128]{3,2,1,0:T(8,128)(2,1)S(1)}, u32[]{:S(2)}, u32[]{:S(2)}) collective-permute-start(bf16[4,17,16,128]{3,2,1,0:T(8,128)(2,1)S(1)} %get-tuple-element.48), channel_id=1, source_target_pairs={{8,16},{16,8},{24,25},{25,24},{17,9},{9,17},{1,2},{2,1},{10,18},{1... | collective-permute-start | bytes 835592 | tf_op jit(solution)/shard_map/ppermute | solution.py:392
  18.9 2.7 %collective-permute-start.9 = (bf16[4,16,16,128]{3,2,1,0:T(8,128)(2,1)S(1)}, bf16[4,16,16,128]{3,2,1,0:T(8,128)(2,1)S(1)}, u32[]{:S(2)}, u32[]{:S(2)}) collective-permute-start(bf16[4,16,16,128]{3,2,1,0:T(8,128)(2,1)S(1)} %get-tuple-element.49.rest_0_), channel_id=1, source_target_pairs={{0,8},{8,0},{16,24},{24,16},{25,17},{17,25},{9,1},{1,9},{2,10},{10... | collective-permute-start | bytes 786440 | tf_op jit(solution)/shard_map/ppermute | solution.py:414
  22.8 20.0 %collective-permute-start.12 = (bf16[4,16,16,128]{3,2,1,0:T(8,128)(2,1)S(1)}, bf16[4,16,16,128]{3,2,1,0:T(8,128)(2,1)S(1)}, u32[]{:S(2)}, u32[]{:S(2)}) collective-permute-start(bf16[4,16,16,128]{3,2,1,0:T(8,128)(2,1)S(1)} %get-tuple-element.51.rest_0_), channel_id=1, source_target_pairs={{8,16},{16,8},{24,25},{25,24},{17,9},{9,17},{1,2},{2,1},{10,18},{1... | collective-permute-start | bytes 786440 | tf_op jit(solution)/shard_map/ppermute | solution.py:425
  24.9 6.5 %collective-permute-start.11 = (bf16[4,16,16,128]{3,2,1,0:T(8,128)(2,1)S(1)}, bf16[4,16,16,128]{3,2,1,0:T(8,128)(2,1)S(1)}, u32[]{:S(2)}, u32[]{:S(2)}) collective-permute-start(bf16[4,16,16,128]{3,2,1,0:T(8,128)(2,1)S(1)} %get-tuple-element.51.rest_0_), channel_id=1, source_target_pairs={{0,8},{8,0},{16,24},{24,16},{25,17},{17,25},{9,1},{1,9},{2,10},{10... | collective-permute-start | bytes 786440 | tf_op jit(solution)/shard_map/ppermute | solution.py:424
  29.3 8.0 %collective-permute-start.10 = (bf16[4,16,16,128]{3,2,1,0:T(8,128)(2,1)S(1)}, bf16[4,16,16,128]{3,2,1,0:T(8,128)(2,1)S(1)}, u32[]{:S(2)}, u32[]{:S(2)}) collective-permute-start(bf16[4,16,16,128]{3,2,1,0:T(8,128)(2,1)S(1)} %get-tuple-element.54), channel_id=1, source_target_pairs={{8,16},{16,8},{24,25},{25,24},{17,9},{9,17},{1,2},{2,1},{10,18},{1... | collective-permute-start | bytes 786440 | tf_op jit(solution)/shard_map/ppermute | solution.py:423
  32.7 5.9 %collective-permute-start.13 = (bf16[4,16,16,128]{3,2,1,0:T(8,128)(2,1)S(1)}, bf16[4,16,16,128]{3,2,1,0:T(8,128)(2,1)S(1)}, u32[]{:S(2)}, u32[]{:S(2)}) collective-permute-start(bf16[4,16,16,128]{3,2,1,0:T(8,128)(2,1)S(1)} %get-tuple-element.56), channel_id=1, source_target_pairs={{0,8},{8,0},{16,24},{24,16},{25,17},{17,25},{9,1},{1,9},{2,10},{10... | collective-permute-start | bytes 786440 | tf_op jit(solution)/shard_map/ppermute | solution.py:414
  39.8 5.8 %collective-permute-start.17 = (bf16[16,16,128]{2,1,0:T(8,128)(2,1)S(1)}, bf16[16,16,128]{2,1,0:T(8,128)(2,1)S(1)}, u32[]{:S(2)}, u32[]{:S(2)}) collective-permute-start(bf16[16,16,128]{2,1,0:T(8,128)(2,1)S(1)} %get-tuple-element.62), channel_id=1, source_target_pairs={{0,8},{8,0},{16,24},{24,16},{1,9},{9,1},{17,25},{25,17},{2,10},{10... | collective-permute-start | bytes 196616 | tf_op jit(solution)/shard_map/ppermute | solution.py:353
  41.1 6.5 %collective-permute-start.18 = (bf16[16,16,128]{2,1,0:T(8,128)(2,1)S(1)}, bf16[16,16,128]{2,1,0:T(8,128)(2,1)S(1)}, u32[]{:S(2)}, u32[]{:S(2)}) collective-permute-start(bf16[16,16,128]{2,1,0:T(8,128)(2,1)S(1)} %get-tuple-element.63), channel_id=1, source_target_pairs={{0,16},{8,24},{16,0},{24,8},{1,17},{9,25},{17,1},{25,9},{2,18},{10... | collective-permute-start | bytes 196616 | tf_op jit(solution)/shard_map/ppermute | solution.py:353
  41.1 6.5 %collective-permute-start.19 = (bf16[16,16,128]{2,1,0:T(8,128)(2,1)S(1)}, bf16[16,16,128]{2,1,0:T(8,128)(2,1)S(1)}, u32[]{:S(2)}, u32[]{:S(2)}) collective-permute-start(bf16[16,16,128]{2,1,0:T(8,128)(2,1)S(1)} %get-tuple-element.64), channel_id=1, source_target_pairs={{0,24},{8,16},{16,8},{24,0},{1,25},{9,17},{17,9},{25,1},{2,26},{10... | collective-permute-start | bytes 196616 | tf_op jit(solution)/shard_map/ppermute | solution.py:353
  45.4 2.2 %collective-permute-start.14 = (bf16[16,16,128]{2,1,0:T(8,128)(2,1)S(1)}, bf16[16,16,128]{2,1,0:T(8,128)(2,1)S(1)}, u32[]{:S(2)}, u32[]{:S(2)}) collective-permute-start(bf16[16,16,128]{2,1,0:T(8,128)(2,1)S(1)} %get-tuple-element.59), channel_id=1, source_target_pairs={{0,8},{8,0},{16,24},{24,16},{1,9},{9,1},{17,25},{25,17},{2,10},{10... | collective-permute-start | bytes 196616 | tf_op jit(solution)/shard_map/ppermute | solution.py:353
  45.6 3.1 %collective-permute-start.15 = (bf16[16,16,128]{2,1,0:T(8,128)(2,1)S(1)}, bf16[16,16,128]{2,1,0:T(8,128)(2,1)S(1)}, u32[]{:S(2)}, u32[]{:S(2)}) collective-permute-start(bf16[16,16,128]{2,1,0:T(8,128)(2,1)S(1)} %get-tuple-element.60), channel_id=1, source_target_pairs={{0,16},{8,24},{16,0},{24,8},{1,17},{9,25},{17,1},{25,9},{2,18},{10... | collective-permute-start | bytes 196616 | tf_op jit(solution)/shard_map/ppermute | solution.py:353
  45.7 5.2 %collective-permute-start.16 = (bf16[16,16,128]{2,1,0:T(8,128)(2,1)S(1)}, bf16[16,16,128]{2,1,0:T(8,128)(2,1)S(1)}, u32[]{:S(2)}, u32[]{:S(2)}) collective-permute-start(bf16[16,16,128]{2,1,0:T(8,128)(2,1)S(1)} %get-tuple-element.61), channel_id=1, source_target_pairs={{0,24},{8,16},{16,8},{24,0},{1,25},{9,17},{17,9},{25,1},{2,26},{10... | collective-permute-start | bytes 196616 | tf_op jit(solution)/shard_map/ppermute | solution.py:353

commit v11 on v10

--- a/solution.py
+++ b/solution.py
@@ -183,6 +183,7 @@
     outs = rest[:count] if last else None
     send_ref = rest[count] if outs else rest.pop(0) if sends else None
     new_ref = None if last else rest.pop(0)
+    old_ref = rest.pop(0) if kind == "A" and t == 0 else None
 
     def cells_of(ref, k):
         if ref.shape == inner_ref.shape:
@@ -233,6 +234,9 @@
 
     def level(k):
         own = cells_of(own_ref, k)
+        if old_ref is not None:
+            for s in range(count):
+                old_ref[s, k] = own[s * spec : (s + 1) * spec].astype(jnp.bfloat16)
         out = coef[0, pl.ds(k, 1)] * own
         out += coef[1, pl.ds(k, 1)] * cells_of(outer_ref, k)
         out += coef[2, pl.ds(k, 1)] * inner_ref[k]
@@ -267,7 +271,8 @@
             if more:
                 next_halves.append(first_matmul(i, cells[j]))
             half = halves[p]
-            hidden = (half + half * jnp.tanh(half)).astype(jnp.bfloat16)
+            half = half.astype(jnp.bfloat16)
+            hidden = half + half * jnp.tanh(half)
             part = jnp.dot(w_out[:, i * split : (i + 1) * split], hidden, preferred_element_type=jnp.float32)
             change = part if i == 0 else change + part
             if i == 0:
@@ -389,7 +394,6 @@
         (*got_a, *got_b, send_b),
     )
     halo_a = from_a = lax.ppermute(send_a, AXES, swap_a)
-    halo_c = lax.ppermute(send_a, AXES, swap_b)
     common = [
         pltpu.VMEM((7, depth, width_y), f32),
     ]
@@ -397,7 +401,7 @@
     def column(t, kind, own, inner, outer, sends=True, after=()):
         scratch = list(common)
         if t < STEPS - 1:
-            outs = [sent, row] if sends else [row]
+            outs = ([sent, row] if sends else [row]) + ([sent] if kind == "A" and t == 0 else [])
         else:
             outs = [piece] * count
             scratch = [pltpu.VMEM(sent.shape, bf16), *common]
@@ -410,8 +414,10 @@
         )
 
     for t in range(0, STEPS, 2):
-        send_a, new_a = column(t, "A", a, b, halo_a)
+        send_a, new_a, *old_a = column(t, "A", a, b, halo_a)
         halo_a = lax.ppermute(send_a, AXES, swap_a)
+        if t == 0:
+            halo_c = lax.ppermute(old_a[0], AXES, swap_b)
         (new_b,) = column(t, "B", b, a, halo_b, sends=False, after=(send_a,) if t == 0 else ())
         made_a = column(t + 1, "A", new_a, new_b, halo_a)
         (ghost,) = column(t, "G", halo_b, b, halo_c, sends=False, after=made_a[:1])

time: 52.6 us -> 53 us (level)
  waiting for transfers between devices: 8.95 us -> 9.59 us
    ppermute x0 -> x1, starting transfers between devices: none -> 2.77 us  [by_columns(): halo_c = lax.ppermute(old_a[0], AXES, swap_b)]
    ppermute x2 -> x1, starting transfers between devices: 4.51 us -> 2.09 us  [by_columns(): halo_c = lax.ppermute(send_a, AXES, swap_b)]
    ppermute x3, starting transfers between devices: 4.79 us -> 3.98 us  [by_columns(): halo_a = lax.ppermute(send_a, AXES, swap_a)]
    ppermute x1, waiting for transfers between devices: 0.01 us -> 0.64 us  [by_columns(): halo_a = from_a = lax.ppermute(send_a, AXES, swap_a)]
  transfers between devices with their start and end apart: 20 -> 20, of which waited for: 5 -> 6; matrix products, arithmetic and copies ran while one was open for 0% -> 0% of each run, Pallas kernels for 26% -> 26%
where the time goes in v11:
time: 53 us; the launch traced here: 52.6 us
  starting transfers between devices  24.5 us (46%)
  Pallas kernels  15.1 us (28%)
  waiting for transfers between devices  9.59 us (18%)
  local copies, waits for them, and re-layouts  1.85 us (3%)
  other arithmetic  1.05 us (2%)
    pallas_call x15, Pallas kernels, call(): pl.pallas_call(kernel, out_shape=out_shape, in_specs=[VMEM] * len(args),...  15.1 us
    ppermute x12, starting transfers between devices, swapped(): return lax.ppermute(piece, 'species', [(s, s ^ d) for s in range(count)])  9.57 us
    ppermute x12, waiting for transfers between devices, swapped(): return lax.ppermute(piece, 'species', [(s, s ^ d) for s in range(count)])  5.98 us
    ppermute x3, starting transfers between devices, by_columns(): halo_a = lax.ppermute(send_a, AXES, swap_a)  3.98 us
    ppermute x1, starting transfers between devices, by_columns(): halo_b = from_b = lax.ppermute(send_b, AXES, swap_b)  3.52 us
    ppermute x1, waiting for transfers between devices, by_columns(): halo_b = lax.ppermute(send_b, AXES, swap_b)  2.96 us
    ppermute x1, starting transfers between devices, by_columns(): halo_c = lax.ppermute(old_a[0], AXES, swap_b)  2.77 us
    ppermute x1, starting transfers between devices, by_columns(): halo_b = lax.ppermute(send_b, AXES, swap_b)  2.25 us
  transfers between devices with their start and end apart: 20, of which 6 were waited for; matrix products, arithmetic and copies ran while one was open for 0% of the time, Pallas kernels for 26%

profile of v11, /device:TPU:17, one launch (start us, length us, event | category | flops | bytes accessed | tf_op | source)
XLA Modules:
  0.0 52.6 jit_solution(2562205809242219941)
XLA Ops:
  3.5 1.3 %collective-permute-start.1 = (bf16[22,16,128]{2,1,0:T(8,128)(2,1)S(1)}, bf16[22,16,128]{2,1,0:T(8,128)(2,1)S(1)}, u32[]{:S(2)}, u32[]{:S(2)}) collective-permute-start(bf16[22,16,128]{2,1,0:T(8,128)(2,1)S(1)} %get-tuple-element.38), channel_id=1, source_target_pairs={{0,16},{8,24},{16,0},{24,8},{1,17},{9,25},{17,1},{25,9},{2,18},{10... | collective-permute-start | bytes 270344 | tf_op jit(solution)/shard_map/ppermute | solution.py:358
  5.6 1.3 %collective-permute-start.4 = (bf16[16,16,128]{2,1,0:T(8,128)(2,1)S(1)}, bf16[16,16,128]{2,1,0:T(8,128)(2,1)S(1)}, u32[]{:S(2)}, u32[]{:S(2)}) collective-permute-start(bf16[16,16,128]{2,1,0:T(8,128)(2,1)S(1)} %get-tuple-element.44), channel_id=1, source_target_pairs={{0,16},{8,24},{16,0},{24,8},{1,17},{9,25},{17,1},{25,9},{2,18},{10... | collective-permute-start | bytes 196616 | tf_op jit(solution)/shard_map/ppermute | solution.py:358
  7.7 2.5 %collective-permute-done.2.refs_3_.refs_7_ = bf16[22,16,128]{2,1,0:T(8,128)(2,1)S(1)} collective-permute-done((bf16[22,16,128]{2,1,0:T(8,128)(2,1)S(1)}, bf16[22,16,128]{2,1,0:T(8,128)(2,1)S(1)}, u32[]{:S(2)}, u32[]{:S(2)}) %collective-permute-start.2) | collective-permute-done | bytes 90144 | tf_op jit(solution)/shard_map/ppermute | solution.py:358
  10.5 3.5 %collective-permute-start.6 = (bf16[4,20,16,128]{3,2,1,0:T(8,128)(2,1)S(1)}, bf16[4,20,16,128]{3,2,1,0:T(8,128)(2,1)S(1)}, u32[]{:S(2)}, u32[]{:S(2)}) collective-permute-start(bf16[4,20,16,128]{3,2,1,0:T(8,128)(2,1)S(1)} %get-tuple-element.46.refs_8_), channel_id=1, source_target_pairs={{8,16},{16,8},{24,25},{25,24},{17,9},{9,17},{1,2},{2,1},{10,18},{1... | collective-permute-start | bytes 983048 | tf_op jit(solution)/shard_map/ppermute | solution.py:389
  15.8 1.3 %shard_map.50 = (bf16[4,16,16,128]{3,2,1,0:T(8,128)(2,1)S(1)}, f32[16,64,128]{2,1,0:T(8,128)S(1)}, bf16[4,16,16,128]{3,2,1,0:T(8,128)(2,1)S(1)}) custom-call(f32[16,64,128]{2,1,0:T(8,128)S(1)} %get-tuple-element.47.own_ref.inner_ref, f32[16,64,128]{2,1,0:T(8,128)S(1)} %get-tuple-element.41.inner_ref.own_ref, ...), custom_call_target="tpu_custom_call" | custom-call | flops 1024 | tf_op jit(solution)/shard_map/pallas_call | solution.py:325
  17.1 2.8 %collective-permute-start.8 = (bf16[4,16,16,128]{3,2,1,0:T(8,128)(2,1)S(1)}, bf16[4,16,16,128]{3,2,1,0:T(8,128)(2,1)S(1)}, u32[]{:S(2)}, u32[]{:S(2)}) collective-permute-start(bf16[4,16,16,128]{3,2,1,0:T(8,128)(2,1)S(1)} %get-tuple-element.52), channel_id=1, source_target_pairs={{8,16},{16,8},{24,25},{25,24},{17,9},{9,17},{1,2},{2,1},{10,18},{1... | collective-permute-start | bytes 786440 | tf_op jit(solution)/shard_map/ppermute | solution.py:420
  20.9 1.3 %shard_map.51.inner_ref.own_ref = f32[16,64,128]{2,1,0:T(8,128)S(1)} custom-call(f32[16,64,128]{2,1,0:T(8,128)S(1)} %get-tuple-element.41.inner_ref.own_ref, f32[16,64,128]{2,1,0:T(8,128)S(1)} %get-tuple-element.47.own_ref.inner_ref, bf16[4,20,16,128]{3,2,1,0:T(8,128)(2,1)S(1)} %collective-permute-done.6.outer_ref.from_ref.own_ref, ...), custom_call_target="tpu_custom_call" | custom-call | flops 10000000000 | bytes 1000000 | tf_op jit(solution)/shard_map/pallas_call | solution.py:325
  22.2 1.3 %shard_map.52 = (bf16[4,16,16,128]{3,2,1,0:T(8,128)(2,1)S(1)}, f32[16,64,128]{2,1,0:T(8,128)S(1)}) custom-call(f32[16,64,128]{2,1,0:T(8,128)S(1)} %get-tuple-element.51.own_ref.inner_ref, f32[16,64,128]{2,1,0:T(8,128)S(1)} %shard_map.51.inner_ref.own_ref, bf16[4,16,16,128]{3,2,1,0:T(8,128)(2,1)S(1)} %collective-permute-done.9.outer_ref, ...), custom_call_target="tpu_custom_call" | custom-call | flops 10000000000 | bytes 1000000 | tf_op jit(solution)/shard_map/pallas_call | solution.py:325
  23.5 2.1 %collective-permute-start.12 = (bf16[4,16,16,128]{3,2,1,0:T(8,128)(2,1)S(1)}, bf16[4,16,16,128]{3,2,1,0:T(8,128)(2,1)S(1)}, u32[]{:S(2)}, u32[]{:S(2)}) collective-permute-start(bf16[4,16,16,128]{3,2,1,0:T(8,128)(2,1)S(1)} %get-tuple-element.53.rest_0_), channel_id=1, source_target_pairs={{8,16},{16,8},{24,25},{25,24},{17,9},{9,17},{1,2},{2,1},{10,18},{1... | collective-permute-start | bytes 786440 | tf_op jit(solution)/shard_map/ppermute | solution.py:431
  25.6 1.5 %collective-permute-start.11 = (bf16[4,16,16,128]{3,2,1,0:T(8,128)(2,1)S(1)}, bf16[4,16,16,128]{3,2,1,0:T(8,128)(2,1)S(1)}, u32[]{:S(2)}, u32[]{:S(2)}) collective-permute-start(bf16[4,16,16,128]{3,2,1,0:T(8,128)(2,1)S(1)} %get-tuple-element.53.rest_0_), channel_id=1, source_target_pairs={{0,8},{8,0},{16,24},{24,16},{25,17},{17,25},{9,1},{1,9},{2,10},{10... | collective-permute-start | bytes 786440 | tf_op jit(solution)/shard_map/ppermute | solution.py:430
  27.1 1.3 %shard_map.53.outer_ref = f32[16,64,128]{2,1,0:T(8,128)S(1)} custom-call(bf16[4,20,16,128]{3,2,1,0:T(8,128)(2,1)S(1)} %collective-permute-done.6.outer_ref.from_ref.own_ref, f32[16,64,128]{2,1,0:T(8,128)S(1)} %get-tuple-element.41.inner_ref.own_ref, bf16[4,16,16,128]{3,2,1,0:T(8,128)(2,1)S(1)} %collective-permute-done.8.outer_ref, ...), custom_call_target="tpu_custom_call" | custom-call | flops 10000000000 | bytes 1000000 | tf_op jit(solution)/shard_map/pallas_call | solution.py:325
  28.4 1.3 %shard_map.54 = (bf16[4,16,16,128]{3,2,1,0:T(8,128)(2,1)S(1)}, f32[16,64,128]{2,1,0:T(8,128)S(1)}) custom-call(f32[16,64,128]{2,1,0:T(8,128)S(1)} %shard_map.51.inner_ref.own_ref, f32[16,64,128]{2,1,0:T(8,128)S(1)} %get-tuple-element.51.own_ref.inner_ref, f32[16,64,128]{2,1,0:T(8,128)S(1)} %shard_map.53.outer_ref, ...), custom_call_target="tpu_custom_call" | custom-call | flops 10000000000 | bytes 1000000 | tf_op jit(solution)/shard_map/pallas_call | solution.py:325
  29.7 2.3 %collective-permute-start.10 = (bf16[4,16,16,128]{3,2,1,0:T(8,128)(2,1)S(1)}, bf16[4,16,16,128]{3,2,1,0:T(8,128)(2,1)S(1)}, u32[]{:S(2)}, u32[]{:S(2)}) collective-permute-start(bf16[4,16,16,128]{3,2,1,0:T(8,128)(2,1)S(1)} %get-tuple-element.56), channel_id=1, source_target_pairs={{8,16},{16,8},{24,25},{25,24},{17,9},{9,17},{1,2},{2,1},{10,18},{1... | collective-permute-start | bytes 786440 | tf_op jit(solution)/shard_map/ppermute | solution.py:429
  31.9 1.3 %shard_map.56 = (bf16[4,16,16,128]{3,2,1,0:T(8,128)(2,1)S(1)}, f32[16,64,128]{2,1,0:T(8,128)S(1)}) custom-call(f32[16,64,128]{2,1,0:T(8,128)S(1)} %get-tuple-element.55.inner_ref.own_ref, f32[16,64,128]{2,1,0:T(8,128)S(1)} %get-tuple-element.54.own_ref.inner_ref, bf16[4,16,16,128]{3,2,1,0:T(8,128)(2,1)S(1)} %collective-permute-done.11.outer_ref, ...), custom_call_target="tpu_custom_call" | custom-call | flops 10000000000 | bytes 1000000 | tf_op jit(solution)/shard_map/pallas_call | solution.py:325
  33.2 1.5 %collective-permute-start.13 = (bf16[4,16,16,128]{3,2,1,0:T(8,128)(2,1)S(1)}, bf16[4,16,16,128]{3,2,1,0:T(8,128)(2,1)S(1)}, u32[]{:S(2)}, u32[]{:S(2)}) collective-permute-start(bf16[4,16,16,128]{3,2,1,0:T(8,128)(2,1)S(1)} %get-tuple-element.58), channel_id=1, source_target_pairs={{0,8},{8,0},{16,24},{24,16},{25,17},{17,25},{9,1},{1,9},{2,10},{10... | collective-permute-start | bytes 786440 | tf_op jit(solution)/shard_map/ppermute | solution.py:418
  34.7 3.0 %collective-permute-done.10.outer_ref.own_ref = bf16[4,16,16,128]{3,2,1,0:T(8,128)(2,1)S(1)} collective-permute-done((bf16[4,16,16,128]{3,2,1,0:T(8,128)(2,1)S(1)}, bf16[4,16,16,128]{3,2,1,0:T(8,128)(2,1)S(1)}, u32[]{:S(2)}, u32[]{:S(2)}) %collective-permute-start.10) | collective-permute-done | bytes 262176 | tf_op jit(solution)/shard_map/ppermute | solution.py:429
  37.6 1.3 %shard_map.55.inner_ref.own_ref = f32[16,64,128]{2,1,0:T(8,128)S(1)} custom-call(f32[16,64,128]{2,1,0:T(8,128)S(1)} %get-tuple-element.54.own_ref.inner_ref, f32[16,64,128]{2,1,0:T(8,128)S(1)} %get-tuple-element.55.inner_ref.own_ref, bf16[4,16,16,128]{3,2,1,0:T(8,128)(2,1)S(1)} %collective-permute-done.10.outer_ref.own_ref, ...), custom_call_target="tpu_custom_call" | custom-call | flops 10000000000 | bytes 1000000 | tf_op jit(solution)/shard_map/pallas_call | solution.py:325
  38.9 1.3 %shard_map.57 = (bf16[16,16,128]{2,1,0:T(8,128)(2,1)S(1)}, bf16[16,16,128]{2,1,0:T(8,128)(2,1)S(1)}, bf16[16,16,128]{2,1,0:T(8,128)(2,1)S(1)}, bf16[16,16,128]{2,1,0:T(8,128)(2,1)S(1)}) custom-call(f32[16,64,128]{2,1,0:T(8,128)S(1)} %get-tuple-element.57.own_ref.inner_ref, f32[16,64,128]{2,1,0:T(8,128)S(1)} %shard_map.55.inner_ref.own_ref, ...), custom_call_target="tpu_custom_call" | custom-call | flops 10000000000 | bytes 1000000 | tf_op jit(solution)/shard_map/pallas_call | solution.py:325
  40.2 1.3 %collective-permute-start.17 = (bf16[16,16,128]{2,1,0:T(8,128)(2,1)S(1)}, bf16[16,16,128]{2,1,0:T(8,128)(2,1)S(1)}, u32[]{:S(2)}, u32[]{:S(2)}) collective-permute-start(bf16[16,16,128]{2,1,0:T(8,128)(2,1)S(1)} %get-tuple-element.64), channel_id=1, source_target_pairs={{0,8},{8,0},{16,24},{24,16},{1,9},{9,1},{17,25},{25,17},{2,10},{10... | collective-permute-start | bytes 196616 | tf_op jit(solution)/shard_map/ppermute | solution.py:358
  41.5 1.7 %collective-permute-start.19 = (bf16[16,16,128]{2,1,0:T(8,128)(2,1)S(1)}, bf16[16,16,128]{2,1,0:T(8,128)(2,1)S(1)}, u32[]{:S(2)}, u32[]{:S(2)}) collective-permute-start(bf16[16,16,128]{2,1,0:T(8,128)(2,1)S(1)} %get-tuple-element.66), channel_id=1, source_target_pairs={{0,24},{8,16},{16,8},{24,0},{1,25},{9,17},{17,9},{25,1},{2,26},{10... | collective-permute-start | bytes 196616 | tf_op jit(solution)/shard_map/ppermute | solution.py:358
  43.2 1.3 %shard_map.58.outer_ref = f32[16,64,128]{2,1,0:T(8,128)S(1)} custom-call(bf16[4,16,16,128]{3,2,1,0:T(8,128)(2,1)S(1)} %collective-permute-done.10.outer_ref.own_ref, f32[16,64,128]{2,1,0:T(8,128)S(1)} %get-tuple-element.54.own_ref.inner_ref, bf16[4,16,16,128]{3,2,1,0:T(8,128)(2,1)S(1)} %collective-permute-done.12.outer_ref, ...), custom_call_target="tpu_custom_call" | custom-call | flops 10000000000 | bytes 1000000 | tf_op jit(solution)/shard_map/pallas_call | solution.py:325
  44.5 1.3 %shard_map.59 = (bf16[16,16,128]{2,1,0:T(8,128)(2,1)S(1)}, bf16[16,16,128]{2,1,0:T(8,128)(2,1)S(1)}, bf16[16,16,128]{2,1,0:T(8,128)(2,1)S(1)}, bf16[16,16,128]{2,1,0:T(8,128)(2,1)S(1)}) custom-call(f32[16,64,128]{2,1,0:T(8,128)S(1)} %shard_map.55.inner_ref.own_ref, f32[16,64,128]{2,1,0:T(8,128)S(1)} %get-tuple-element.57.own_ref.inner_ref, ...), custom_call_target="tpu_custom_call" | custom-call | flops 10000000000 | bytes 1000000 | tf_op jit(solution)/shard_map/pallas_call | solution.py:325
  46.1 2.0 %collective-permute-start.16 = (bf16[16,16,128]{2,1,0:T(8,128)(2,1)S(1)}, bf16[16,16,128]{2,1,0:T(8,128)(2,1)S(1)}, u32[]{:S(2)}, u32[]{:S(2)}) collective-permute-start(bf16[16,16,128]{2,1,0:T(8,128)(2,1)S(1)} %get-tuple-element.63), channel_id=1, source_target_pairs={{0,24},{8,16},{16,8},{24,0},{1,25},{9,17},{17,9},{25,1},{2,26},{10... | collective-permute-start | bytes 196616 | tf_op jit(solution)/shard_map/ppermute | solution.py:358
  49.2 2.1 %collective-permute-done.16.refs_3_ = bf16[16,16,128]{2,1,0:T(8,128)(2,1)S(1)} collective-permute-done((bf16[16,16,128]{2,1,0:T(8,128)(2,1)S(1)}, bf16[16,16,128]{2,1,0:T(8,128)(2,1)S(1)}, u32[]{:S(2)}, u32[]{:S(2)}) %collective-permute-start.16) | collective-permute-done | bytes 65568 | tf_op jit(solution)/shard_map/ppermute | solution.py:358
  (43 shorter events, 10.6 us)
Async XLA Ops:
  1.0 1.2 %copy-start = (f32[16,16,8,128]{3,2,1,0:T(8,128)S(1)}, f32[16,16,8,128]{3,2,1,0:T(8,128)}, u32[]{:S(2)}) copy-start(f32[16,16,8,128]{3,2,1,0:T(8,128)} %param.4) | copy-start | bytes 3145732
  2.7 4.8 %collective-permute-start = (bf16[22,16,128]{2,1,0:T(8,128)(2,1)S(1)}, bf16[22,16,128]{2,1,0:T(8,128)(2,1)S(1)}, u32[]{:S(2)}, u32[]{:S(2)}) collective-permute-start(bf16[22,16,128]{2,1,0:T(8,128)(2,1)S(1)} %get-tuple-element.37), channel_id=1, source_target_pairs={{0,8},{8,0},{16,24},{24,16},{1,9},{9,1},{17,25},{25,17},{2,10},{10... | collective-permute-start | bytes 270344 | tf_op jit(solution)/shard_map/ppermute | solution.py:358
  3.5 4.2 %collective-permute-start.1 = (bf16[22,16,128]{2,1,0:T(8,128)(2,1)S(1)}, bf16[22,16,128]{2,1,0:T(8,128)(2,1)S(1)}, u32[]{:S(2)}, u32[]{:S(2)}) collective-permute-start(bf16[22,16,128]{2,1,0:T(8,128)(2,1)S(1)} %get-tuple-element.38), channel_id=1, source_target_pairs={{0,16},{8,24},{16,0},{24,8},{1,17},{9,25},{17,1},{25,9},{2,18},{10... | collective-permute-start | bytes 270344 | tf_op jit(solution)/shard_map/ppermute | solution.py:358
  4.7 5.5 %collective-permute-start.2 = (bf16[22,16,128]{2,1,0:T(8,128)(2,1)S(1)}, bf16[22,16,128]{2,1,0:T(8,128)(2,1)S(1)}, u32[]{:S(2)}, u32[]{:S(2)}) collective-permute-start(bf16[22,16,128]{2,1,0:T(8,128)(2,1)S(1)} %get-tuple-element.39), channel_id=1, source_target_pairs={{0,24},{8,16},{16,8},{24,0},{1,25},{9,17},{17,9},{25,1},{2,26},{10... | collective-permute-start | bytes 270344 | tf_op jit(solution)/shard_map/ppermute | solution.py:358
  5.6 8.4 %collective-permute-start.4 = (bf16[16,16,128]{2,1,0:T(8,128)(2,1)S(1)}, bf16[16,16,128]{2,1,0:T(8,128)(2,1)S(1)}, u32[]{:S(2)}, u32[]{:S(2)}) collective-permute-start(bf16[16,16,128]{2,1,0:T(8,128)(2,1)S(1)} %get-tuple-element.44), channel_id=1, source_target_pairs={{0,16},{8,24},{16,0},{24,8},{1,17},{9,25},{17,1},{25,9},{2,18},{10... | collective-permute-start | bytes 196616 | tf_op jit(solution)/shard_map/ppermute | solution.py:358
  6.9 7.1 %collective-permute-start.5 = (bf16[16,16,128]{2,1,0:T(8,128)(2,1)S(1)}, bf16[16,16,128]{2,1,0:T(8,128)(2,1)S(1)}, u32[]{:S(2)}, u32[]{:S(2)}) collective-permute-start(bf16[16,16,128]{2,1,0:T(8,128)(2,1)S(1)} %get-tuple-element.45), channel_id=1, source_target_pairs={{0,24},{8,16},{16,8},{24,0},{1,25},{9,17},{17,9},{25,1},{2,26},{10... | collective-permute-start | bytes 196616 | tf_op jit(solution)/shard_map/ppermute | solution.py:358
  10.4 3.6 %collective-permute-start.3 = (bf16[16,16,128]{2,1,0:T(8,128)(2,1)S(1)}, bf16[16,16,128]{2,1,0:T(8,128)(2,1)S(1)}, u32[]{:S(2)}, u32[]{:S(2)}) collective-permute-start(bf16[16,16,128]{2,1,0:T(8,128)(2,1)S(1)} %get-tuple-element.43), channel_id=1, source_target_pairs={{0,8},{8,0},{16,24},{24,16},{1,9},{9,1},{17,25},{25,17},{2,10},{10... | collective-permute-start | bytes 196616 | tf_op jit(solution)/shard_map/ppermute | solution.py:358
  10.5 10.4 %collective-permute-start.6 = (bf16[4,20,16,128]{3,2,1,0:T(8,128)(2,1)S(1)}, bf16[4,20,16,128]{3,2,1,0:T(8,128)(2,1)S(1)}, u32[]{:S(2)}, u32[]{:S(2)}) collective-permute-start(bf16[4,20,16,128]{3,2,1,0:T(8,128)(2,1)S(1)} %get-tuple-element.46.refs_8_), channel_id=1, source_target_pairs={{8,16},{16,8},{24,25},{25,24},{17,9},{9,17},{1,2},{2,1},{10,18},{1... | collective-permute-start | bytes 983048 | tf_op jit(solution)/shard_map/ppermute | solution.py:389
  14.0 0.8 %copy-start.2 = (bf16[64,512]{1,0:T(8,128)(2,1)S(1)}, bf16[64,512]{1,0:T(8,128)(2,1)}, u32[]{:S(2)}) copy-start(bf16[64,512]{1,0:T(8,128)(2,1)} %param.7) | copy-start | bytes 196612
  14.2 0.8 %copy-start.1 = (bf16[512,64]{0,1:T(8,128)(2,1)S(1)}, bf16[512,64]{0,1:T(8,128)(2,1)}, u32[]{:S(2)}) copy-start(bf16[512,64]{0,1:T(8,128)(2,1)} %param.6) | copy-start | bytes 196612
  14.2 1.6 %collective-permute-start.7 = (bf16[4,17,16,128]{3,2,1,0:T(8,128)(2,1)S(1)}, bf16[4,17,16,128]{3,2,1,0:T(8,128)(2,1)S(1)}, u32[]{:S(2)}, u32[]{:S(2)}) collective-permute-start(bf16[4,17,16,128]{3,2,1,0:T(8,128)(2,1)S(1)} %get-tuple-element.49), channel_id=1, source_target_pairs={{0,8},{8,0},{16,24},{24,16},{25,17},{17,25},{9,1},{1,9},{2,10},{10... | collective-permute-start | bytes 835592 | tf_op jit(solution)/shard_map/ppermute | solution.py:396
  17.1 10.0 %collective-permute-start.8 = (bf16[4,16,16,128]{3,2,1,0:T(8,128)(2,1)S(1)}, bf16[4,16,16,128]{3,2,1,0:T(8,128)(2,1)S(1)}, u32[]{:S(2)}, u32[]{:S(2)}) collective-permute-start(bf16[4,16,16,128]{3,2,1,0:T(8,128)(2,1)S(1)} %get-tuple-element.52), channel_id=1, source_target_pairs={{8,16},{16,8},{24,25},{25,24},{17,9},{9,17},{1,2},{2,1},{10,18},{1... | collective-permute-start | bytes 786440 | tf_op jit(solution)/shard_map/ppermute | solution.py:420
  19.9 2.3 %collective-permute-start.9 = (bf16[4,16,16,128]{3,2,1,0:T(8,128)(2,1)S(1)}, bf16[4,16,16,128]{3,2,1,0:T(8,128)(2,1)S(1)}, u32[]{:S(2)}, u32[]{:S(2)}) collective-permute-start(bf16[4,16,16,128]{3,2,1,0:T(8,128)(2,1)S(1)} %get-tuple-element.50.rest_0_), channel_id=1, source_target_pairs={{0,8},{8,0},{16,24},{24,16},{25,17},{17,25},{9,1},{1,9},{2,10},{10... | collective-permute-start | bytes 786440 | tf_op jit(solution)/shard_map/ppermute | solution.py:418
  23.5 19.7 %collective-permute-start.12 = (bf16[4,16,16,128]{3,2,1,0:T(8,128)(2,1)S(1)}, bf16[4,16,16,128]{3,2,1,0:T(8,128)(2,1)S(1)}, u32[]{:S(2)}, u32[]{:S(2)}) collective-permute-start(bf16[4,16,16,128]{3,2,1,0:T(8,128)(2,1)S(1)} %get-tuple-element.53.rest_0_), channel_id=1, source_target_pairs={{8,16},{16,8},{24,25},{25,24},{17,9},{9,17},{1,2},{2,1},{10,18},{1... | collective-permute-start | bytes 786440 | tf_op jit(solution)/shard_map/ppermute | solution.py:431
  25.6 6.3 %collective-permute-start.11 = (bf16[4,16,16,128]{3,2,1,0:T(8,128)(2,1)S(1)}, bf16[4,16,16,128]{3,2,1,0:T(8,128)(2,1)S(1)}, u32[]{:S(2)}, u32[]{:S(2)}) collective-permute-start(bf16[4,16,16,128]{3,2,1,0:T(8,128)(2,1)S(1)} %get-tuple-element.53.rest_0_), channel_id=1, source_target_pairs={{0,8},{8,0},{16,24},{24,16},{25,17},{17,25},{9,1},{1,9},{2,10},{10... | collective-permute-start | bytes 786440 | tf_op jit(solution)/shard_map/ppermute | solution.py:430
  29.7 8.0 %collective-permute-start.10 = (bf16[4,16,16,128]{3,2,1,0:T(8,128)(2,1)S(1)}, bf16[4,16,16,128]{3,2,1,0:T(8,128)(2,1)S(1)}, u32[]{:S(2)}, u32[]{:S(2)}) collective-permute-start(bf16[4,16,16,128]{3,2,1,0:T(8,128)(2,1)S(1)} %get-tuple-element.56), channel_id=1, source_target_pairs={{8,16},{16,8},{24,25},{25,24},{17,9},{9,17},{1,2},{2,1},{10,18},{1... | collective-permute-start | bytes 786440 | tf_op jit(solution)/shard_map/ppermute | solution.py:429
  33.2 5.7 %collective-permute-start.13 = (bf16[4,16,16,128]{3,2,1,0:T(8,128)(2,1)S(1)}, bf16[4,16,16,128]{3,2,1,0:T(8,128)(2,1)S(1)}, u32[]{:S(2)}, u32[]{:S(2)}) collective-permute-start(bf16[4,16,16,128]{3,2,1,0:T(8,128)(2,1)S(1)} %get-tuple-element.58), channel_id=1, source_target_pairs={{0,8},{8,0},{16,24},{24,16},{25,17},{17,25},{9,1},{1,9},{2,10},{10... | collective-permute-start | bytes 786440 | tf_op jit(solution)/shard_map/ppermute | solution.py:418
  40.2 5.8 %collective-permute-start.17 = (bf16[16,16,128]{2,1,0:T(8,128)(2,1)S(1)}, bf16[16,16,128]{2,1,0:T(8,128)(2,1)S(1)}, u32[]{:S(2)}, u32[]{:S(2)}) collective-permute-start(bf16[16,16,128]{2,1,0:T(8,128)(2,1)S(1)} %get-tuple-element.64), channel_id=1, source_target_pairs={{0,8},{8,0},{16,24},{24,16},{1,9},{9,1},{17,25},{25,17},{2,10},{10... | collective-permute-start | bytes 196616 | tf_op jit(solution)/shard_map/ppermute | solution.py:358
  41.5 6.5 %collective-permute-start.18 = (bf16[16,16,128]{2,1,0:T(8,128)(2,1)S(1)}, bf16[16,16,128]{2,1,0:T(8,128)(2,1)S(1)}, u32[]{:S(2)}, u32[]{:S(2)}) collective-permute-start(bf16[16,16,128]{2,1,0:T(8,128)(2,1)S(1)} %get-tuple-element.65), channel_id=1, source_target_pairs={{0,16},{8,24},{16,0},{24,8},{1,17},{9,25},{17,1},{25,9},{2,18},{10... | collective-permute-start | bytes 196616 | tf_op jit(solution)/shard_map/ppermute | solution.py:358
  41.5 6.5 %collective-permute-start.19 = (bf16[16,16,128]{2,1,0:T(8,128)(2,1)S(1)}, bf16[16,16,128]{2,1,0:T(8,128)(2,1)S(1)}, u32[]{:S(2)}, u32[]{:S(2)}) collective-permute-start(bf16[16,16,128]{2,1,0:T(8,128)(2,1)S(1)} %get-tuple-element.66), channel_id=1, source_target_pairs={{0,24},{8,16},{16,8},{24,0},{1,25},{9,17},{17,9},{25,1},{2,26},{10... | collective-permute-start | bytes 196616 | tf_op jit(solution)/shard_map/ppermute | solution.py:358
  45.8 2.2 %collective-permute-start.14 = (bf16[16,16,128]{2,1,0:T(8,128)(2,1)S(1)}, bf16[16,16,128]{2,1,0:T(8,128)(2,1)S(1)}, u32[]{:S(2)}, u32[]{:S(2)}) collective-permute-start(bf16[16,16,128]{2,1,0:T(8,128)(2,1)S(1)} %get-tuple-element.61), channel_id=1, source_target_pairs={{0,8},{8,0},{16,24},{24,16},{1,9},{9,1},{17,25},{25,17},{2,10},{10... | collective-permute-start | bytes 196616 | tf_op jit(solution)/shard_map/ppermute | solution.py:358
  46.0 3.1 %collective-permute-start.15 = (bf16[16,16,128]{2,1,0:T(8,128)(2,1)S(1)}, bf16[16,16,128]{2,1,0:T(8,128)(2,1)S(1)}, u32[]{:S(2)}, u32[]{:S(2)}) collective-permute-start(bf16[16,16,128]{2,1,0:T(8,128)(2,1)S(1)} %get-tuple-element.62), channel_id=1, source_target_pairs={{0,16},{8,24},{16,0},{24,8},{1,17},{9,25},{17,1},{25,9},{2,18},{10... | collective-permute-start | bytes 196616 | tf_op jit(solution)/shard_map/ppermute | solution.py:358
  46.1 5.2 %collective-permute-start.16 = (bf16[16,16,128]{2,1,0:T(8,128)(2,1)S(1)}, bf16[16,16,128]{2,1,0:T(8,128)(2,1)S(1)}, u32[]{:S(2)}, u32[]{:S(2)}) collective-permute-start(bf16[16,16,128]{2,1,0:T(8,128)(2,1)S(1)} %get-tuple-element.63), channel_id=1, source_target_pairs={{0,24},{8,16},{16,8},{24,0},{1,25},{9,17},{17,9},{25,1},{2,26},{10... | collective-permute-start | bytes 196616 | tf_op jit(solution)/shard_map/ppermute | solution.py:358

commit v12 on v10

--- a/solution.py
+++ b/solution.py
@@ -379,7 +379,7 @@
             shape((STEPS, 6, count, depth // count, width_y), f32),
             piece,
         ],
-        (*got_b, packed_a[1]),
+        (*got_b, packed_a[1], w_in, w_out),
     )
     halo_b = from_b = lax.ppermute(send_b, AXES, swap_b)
     got_a = [packed_a[0], swapped(near_a, 1), *(swapped(packed_a[d], d) for d in range(2, count))]

time: 52.6 us -> 52.6 us (level)
  waiting for transfers between devices: 8.95 us -> 7.94 us
  starting transfers between devices: 24.8 us -> 25.5 us
    ppermute x2, starting transfers between devices: 4.51 us -> 5.88 us  [by_columns(): halo_c = lax.ppermute(send_a, AXES, swap_b)]
    ppermute x12, waiting for transfers between devices: 5.97 us -> 4.97 us  [swapped(): return lax.ppermute(piece, 'species', [(s, s ^ d) for s in range(count)])]
    ppermute x3, starting transfers between devices: 4.79 us -> 4.14 us  [by_columns(): halo_a = lax.ppermute(send_a, AXES, swap_a)]
  transfers between devices with their start and end apart: 20 -> 20, of which waited for: 5 -> 4; matrix products, arithmetic and copies ran while one was open for 0% -> 0% of each run, Pallas kernels for 26% -> 26%
where the time goes in v12:
time: 52.6 us; the launch traced here: 52.2 us
  starting transfers between devices  25.5 us (48%)
  Pallas kernels  15.1 us (29%)
  waiting for transfers between devices  7.94 us (15%)
  local copies, waits for them, and re-layouts  2.16 us (4%)
  other arithmetic  1.05 us (2%)
    pallas_call x15, Pallas kernels, call(): pl.pallas_call(kernel, out_shape=out_shape, in_specs=[VMEM] * len(args),...  15.1 us
    ppermute x12, starting transfers between devices, swapped(): return lax.ppermute(piece, 'species', [(s, s ^ d) for s in range(count)])  9.57 us
    ppermute x2, starting transfers between devices, by_columns(): halo_c = lax.ppermute(send_a, AXES, swap_b)  5.88 us
    ppermute x12, waiting for transfers between devices, swapped(): return lax.ppermute(piece, 'species', [(s, s ^ d) for s in range(count)])  4.97 us
    ppermute x3, starting transfers between devices, by_columns(): halo_a = lax.ppermute(send_a, AXES, swap_a)  4.14 us
    ppermute x1, starting transfers between devices, by_columns(): halo_b = from_b = lax.ppermute(send_b, AXES, swap_b)  3.52 us
    ppermute x1, waiting for transfers between devices, by_columns(): halo_b = lax.ppermute(send_b, AXES, swap_b)  2.95 us
    unnamed x7, local copies, waits for them, and re-layouts  2.16 us
  transfers between devices with their start and end apart: 20, of which 4 were waited for; matrix products, arithmetic and copies ran while one was open for 0% of the time, Pallas kernels for 26%

profile of v12, /device:TPU:17, one launch (start us, length us, event | category | flops | bytes accessed | tf_op | source)
XLA Modules:
  0.0 52.2 jit_solution(4860133218063980363)
XLA Ops:
  3.5 1.3 %collective-permute-start.1 = (bf16[22,16,128]{2,1,0:T(8,128)(2,1)S(1)}, bf16[22,16,128]{2,1,0:T(8,128)(2,1)S(1)}, u32[]{:S(2)}, u32[]{:S(2)}) collective-permute-start(bf16[22,16,128]{2,1,0:T(8,128)(2,1)S(1)} %get-tuple-element.37), channel_id=1, source_target_pairs={{0,16},{8,24},{16,0},{24,8},{1,17},{9,25},{17,1},{25,9},{2,18},{10... | collective-permute-start | bytes 270344 | tf_op jit(solution)/shard_map/ppermute | solution.py:353
  5.6 1.3 %collective-permute-start.4 = (bf16[16,16,128]{2,1,0:T(8,128)(2,1)S(1)}, bf16[16,16,128]{2,1,0:T(8,128)(2,1)S(1)}, u32[]{:S(2)}, u32[]{:S(2)}) collective-permute-start(bf16[16,16,128]{2,1,0:T(8,128)(2,1)S(1)} %get-tuple-element.43), channel_id=1, source_target_pairs={{0,16},{8,24},{16,0},{24,8},{1,17},{9,25},{17,1},{25,9},{2,18},{10... | collective-permute-start | bytes 196616 | tf_op jit(solution)/shard_map/ppermute | solution.py:353
  8.5 1.7 %collective-permute-done.2.refs_3_.refs_7_ = bf16[22,16,128]{2,1,0:T(8,128)(2,1)S(1)} collective-permute-done((bf16[22,16,128]{2,1,0:T(8,128)(2,1)S(1)}, bf16[22,16,128]{2,1,0:T(8,128)(2,1)S(1)}, u32[]{:S(2)}, u32[]{:S(2)}) %collective-permute-start.2) | collective-permute-done | bytes 90144 | tf_op jit(solution)/shard_map/ppermute | solution.py:353
  10.5 3.5 %collective-permute-start.6 = (bf16[4,20,16,128]{3,2,1,0:T(8,128)(2,1)S(1)}, bf16[4,20,16,128]{3,2,1,0:T(8,128)(2,1)S(1)}, u32[]{:S(2)}, u32[]{:S(2)}) collective-permute-start(bf16[4,20,16,128]{3,2,1,0:T(8,128)(2,1)S(1)} %get-tuple-element.45.refs_8_), channel_id=1, source_target_pairs={{8,16},{16,8},{24,25},{25,24},{17,9},{9,17},{1,2},{2,1},{10,18},{1... | collective-permute-start | bytes 983048 | tf_op jit(solution)/shard_map/ppermute | solution.py:384
  14.5 2.9 %collective-permute-start.8 = (bf16[4,17,16,128]{3,2,1,0:T(8,128)(2,1)S(1)}, bf16[4,17,16,128]{3,2,1,0:T(8,128)(2,1)S(1)}, u32[]{:S(2)}, u32[]{:S(2)}) collective-permute-start(bf16[4,17,16,128]{3,2,1,0:T(8,128)(2,1)S(1)} %get-tuple-element.48), channel_id=1, source_target_pairs={{8,16},{16,8},{24,25},{25,24},{17,9},{9,17},{1,2},{2,1},{10,18},{1... | collective-permute-start | bytes 835592 | tf_op jit(solution)/shard_map/ppermute | solution.py:392
  17.4 1.3 %shard_map.50 = (bf16[4,16,16,128]{3,2,1,0:T(8,128)(2,1)S(1)}, f32[16,64,128]{2,1,0:T(8,128)S(1)}) custom-call(f32[16,64,128]{2,1,0:T(8,128)S(1)} %get-tuple-element.46.own_ref.inner_ref, f32[16,64,128]{2,1,0:T(8,128)S(1)} %get-tuple-element.40.inner_ref.own_ref, bf16[4,17,16,128]{3,2,1,0:T(8,128)(2,1)S(1)} %collective-permute-done.7.outer_ref.from_ref, ...), custom_call_target="tpu_custom_call" | custom-call | flops 1024 | tf_op jit(solution)/shard_map/pallas_call | solution.py:320
  19.4 1.3 %shard_map.51.inner_ref.own_ref = f32[16,64,128]{2,1,0:T(8,128)S(1)} custom-call(f32[16,64,128]{2,1,0:T(8,128)S(1)} %get-tuple-element.40.inner_ref.own_ref, f32[16,64,128]{2,1,0:T(8,128)S(1)} %get-tuple-element.46.own_ref.inner_ref, bf16[4,20,16,128]{3,2,1,0:T(8,128)(2,1)S(1)} %collective-permute-done.6.outer_ref.from_ref.own_ref, ...), custom_call_target="tpu_custom_call" | custom-call | flops 10000000000 | bytes 1000000 | tf_op jit(solution)/shard_map/pallas_call | solution.py:320
  20.7 1.3 %shard_map.52 = (bf16[4,16,16,128]{3,2,1,0:T(8,128)(2,1)S(1)}, f32[16,64,128]{2,1,0:T(8,128)S(1)}) custom-call(f32[16,64,128]{2,1,0:T(8,128)S(1)} %get-tuple-element.50.own_ref.inner_ref, f32[16,64,128]{2,1,0:T(8,128)S(1)} %shard_map.51.inner_ref.own_ref, bf16[4,16,16,128]{3,2,1,0:T(8,128)(2,1)S(1)} %collective-permute-done.9.outer_ref, ...), custom_call_target="tpu_custom_call" | custom-call | flops 10000000000 | bytes 1000000 | tf_op jit(solution)/shard_map/pallas_call | solution.py:320
  21.9 3.0 %collective-permute-start.12 = (bf16[4,16,16,128]{3,2,1,0:T(8,128)(2,1)S(1)}, bf16[4,16,16,128]{3,2,1,0:T(8,128)(2,1)S(1)}, u32[]{:S(2)}, u32[]{:S(2)}) collective-permute-start(bf16[4,16,16,128]{3,2,1,0:T(8,128)(2,1)S(1)} %get-tuple-element.51.rest_0_), channel_id=1, source_target_pairs={{8,16},{16,8},{24,25},{25,24},{17,9},{9,17},{1,2},{2,1},{10,18},{1... | collective-permute-start | bytes 786440 | tf_op jit(solution)/shard_map/ppermute | solution.py:425
  24.9 1.8 %collective-permute-start.11 = (bf16[4,16,16,128]{3,2,1,0:T(8,128)(2,1)S(1)}, bf16[4,16,16,128]{3,2,1,0:T(8,128)(2,1)S(1)}, u32[]{:S(2)}, u32[]{:S(2)}) collective-permute-start(bf16[4,16,16,128]{3,2,1,0:T(8,128)(2,1)S(1)} %get-tuple-element.51.rest_0_), channel_id=1, source_target_pairs={{0,8},{8,0},{16,24},{24,16},{25,17},{17,25},{9,1},{1,9},{2,10},{10... | collective-permute-start | bytes 786440 | tf_op jit(solution)/shard_map/ppermute | solution.py:424
  26.7 1.3 %shard_map.53.outer_ref = f32[16,64,128]{2,1,0:T(8,128)S(1)} custom-call(bf16[4,20,16,128]{3,2,1,0:T(8,128)(2,1)S(1)} %collective-permute-done.6.outer_ref.from_ref.own_ref, f32[16,64,128]{2,1,0:T(8,128)S(1)} %get-tuple-element.40.inner_ref.own_ref, bf16[4,17,16,128]{3,2,1,0:T(8,128)(2,1)S(1)} %collective-permute-done.8.outer_ref, ...), custom_call_target="tpu_custom_call" | custom-call | flops 10000000000 | bytes 1000000 | tf_op jit(solution)/shard_map/pallas_call | solution.py:320
  28.0 1.3 %shard_map.54 = (bf16[4,16,16,128]{3,2,1,0:T(8,128)(2,1)S(1)}, f32[16,64,128]{2,1,0:T(8,128)S(1)}) custom-call(f32[16,64,128]{2,1,0:T(8,128)S(1)} %shard_map.51.inner_ref.own_ref, f32[16,64,128]{2,1,0:T(8,128)S(1)} %get-tuple-element.50.own_ref.inner_ref, f32[16,64,128]{2,1,0:T(8,128)S(1)} %shard_map.53.outer_ref, ...), custom_call_target="tpu_custom_call" | custom-call | flops 10000000000 | bytes 1000000 | tf_op jit(solution)/shard_map/pallas_call | solution.py:320
  29.3 2.1 %collective-permute-start.10 = (bf16[4,16,16,128]{3,2,1,0:T(8,128)(2,1)S(1)}, bf16[4,16,16,128]{3,2,1,0:T(8,128)(2,1)S(1)}, u32[]{:S(2)}, u32[]{:S(2)}) collective-permute-start(bf16[4,16,16,128]{3,2,1,0:T(8,128)(2,1)S(1)} %get-tuple-element.54), channel_id=1, source_target_pairs={{8,16},{16,8},{24,25},{25,24},{17,9},{9,17},{1,2},{2,1},{10,18},{1... | collective-permute-start | bytes 786440 | tf_op jit(solution)/shard_map/ppermute | solution.py:423
  31.4 1.3 %shard_map.56 = (bf16[4,16,16,128]{3,2,1,0:T(8,128)(2,1)S(1)}, f32[16,64,128]{2,1,0:T(8,128)S(1)}) custom-call(f32[16,64,128]{2,1,0:T(8,128)S(1)} %get-tuple-element.53.inner_ref.own_ref, f32[16,64,128]{2,1,0:T(8,128)S(1)} %get-tuple-element.52.own_ref.inner_ref, bf16[4,16,16,128]{3,2,1,0:T(8,128)(2,1)S(1)} %collective-permute-done.11.outer_ref, ...), custom_call_target="tpu_custom_call" | custom-call | flops 10000000000 | bytes 1000000 | tf_op jit(solution)/shard_map/pallas_call | solution.py:320
  32.7 1.6 %collective-permute-start.13 = (bf16[4,16,16,128]{3,2,1,0:T(8,128)(2,1)S(1)}, bf16[4,16,16,128]{3,2,1,0:T(8,128)(2,1)S(1)}, u32[]{:S(2)}, u32[]{:S(2)}) collective-permute-start(bf16[4,16,16,128]{3,2,1,0:T(8,128)(2,1)S(1)} %get-tuple-element.56), channel_id=1, source_target_pairs={{0,8},{8,0},{16,24},{24,16},{25,17},{17,25},{9,1},{1,9},{2,10},{10... | collective-permute-start | bytes 786440 | tf_op jit(solution)/shard_map/ppermute | solution.py:414
  34.3 2.9 %collective-permute-done.10.outer_ref.own_ref = bf16[4,16,16,128]{3,2,1,0:T(8,128)(2,1)S(1)} collective-permute-done((bf16[4,16,16,128]{3,2,1,0:T(8,128)(2,1)S(1)}, bf16[4,16,16,128]{3,2,1,0:T(8,128)(2,1)S(1)}, u32[]{:S(2)}, u32[]{:S(2)}) %collective-permute-start.10) | collective-permute-done | bytes 262176 | tf_op jit(solution)/shard_map/ppermute | solution.py:423
  37.3 1.3 %shard_map.55.inner_ref.own_ref = f32[16,64,128]{2,1,0:T(8,128)S(1)} custom-call(f32[16,64,128]{2,1,0:T(8,128)S(1)} %get-tuple-element.52.own_ref.inner_ref, f32[16,64,128]{2,1,0:T(8,128)S(1)} %get-tuple-element.53.inner_ref.own_ref, bf16[4,16,16,128]{3,2,1,0:T(8,128)(2,1)S(1)} %collective-permute-done.10.outer_ref.own_ref, ...), custom_call_target="tpu_custom_call" | custom-call | flops 10000000000 | bytes 1000000 | tf_op jit(solution)/shard_map/pallas_call | solution.py:320
  38.6 1.3 %shard_map.57 = (bf16[16,16,128]{2,1,0:T(8,128)(2,1)S(1)}, bf16[16,16,128]{2,1,0:T(8,128)(2,1)S(1)}, bf16[16,16,128]{2,1,0:T(8,128)(2,1)S(1)}, bf16[16,16,128]{2,1,0:T(8,128)(2,1)S(1)}) custom-call(f32[16,64,128]{2,1,0:T(8,128)S(1)} %get-tuple-element.55.own_ref.inner_ref, f32[16,64,128]{2,1,0:T(8,128)S(1)} %shard_map.55.inner_ref.own_ref, ...), custom_call_target="tpu_custom_call" | custom-call | flops 10000000000 | bytes 1000000 | tf_op jit(solution)/shard_map/pallas_call | solution.py:320
  39.9 1.3 %collective-permute-start.17 = (bf16[16,16,128]{2,1,0:T(8,128)(2,1)S(1)}, bf16[16,16,128]{2,1,0:T(8,128)(2,1)S(1)}, u32[]{:S(2)}, u32[]{:S(2)}) collective-permute-start(bf16[16,16,128]{2,1,0:T(8,128)(2,1)S(1)} %get-tuple-element.62), channel_id=1, source_target_pairs={{0,8},{8,0},{16,24},{24,16},{1,9},{9,1},{17,25},{25,17},{2,10},{10... | collective-permute-start | bytes 196616 | tf_op jit(solution)/shard_map/ppermute | solution.py:353
  41.1 1.7 %collective-permute-start.19 = (bf16[16,16,128]{2,1,0:T(8,128)(2,1)S(1)}, bf16[16,16,128]{2,1,0:T(8,128)(2,1)S(1)}, u32[]{:S(2)}, u32[]{:S(2)}) collective-permute-start(bf16[16,16,128]{2,1,0:T(8,128)(2,1)S(1)} %get-tuple-element.64), channel_id=1, source_target_pairs={{0,24},{8,16},{16,8},{24,0},{1,25},{9,17},{17,9},{25,1},{2,26},{10... | collective-permute-start | bytes 196616 | tf_op jit(solution)/shard_map/ppermute | solution.py:353
  42.8 1.3 %shard_map.58.outer_ref = f32[16,64,128]{2,1,0:T(8,128)S(1)} custom-call(bf16[4,16,16,128]{3,2,1,0:T(8,128)(2,1)S(1)} %collective-permute-done.10.outer_ref.own_ref, f32[16,64,128]{2,1,0:T(8,128)S(1)} %get-tuple-element.52.own_ref.inner_ref, bf16[4,16,16,128]{3,2,1,0:T(8,128)(2,1)S(1)} %collective-permute-done.12.outer_ref, ...), custom_call_target="tpu_custom_call" | custom-call | flops 10000000000 | bytes 1000000 | tf_op jit(solution)/shard_map/pallas_call | solution.py:320
  44.1 1.3 %shard_map.59 = (bf16[16,16,128]{2,1,0:T(8,128)(2,1)S(1)}, bf16[16,16,128]{2,1,0:T(8,128)(2,1)S(1)}, bf16[16,16,128]{2,1,0:T(8,128)(2,1)S(1)}, bf16[16,16,128]{2,1,0:T(8,128)(2,1)S(1)}) custom-call(f32[16,64,128]{2,1,0:T(8,128)S(1)} %shard_map.55.inner_ref.own_ref, f32[16,64,128]{2,1,0:T(8,128)S(1)} %get-tuple-element.55.own_ref.inner_ref, ...), custom_call_target="tpu_custom_call" | custom-call | flops 10000000000 | bytes 1000000 | tf_op jit(solution)/shard_map/pallas_call | solution.py:320
  45.7 2.0 %collective-permute-start.16 = (bf16[16,16,128]{2,1,0:T(8,128)(2,1)S(1)}, bf16[16,16,128]{2,1,0:T(8,128)(2,1)S(1)}, u32[]{:S(2)}, u32[]{:S(2)}) collective-permute-start(bf16[16,16,128]{2,1,0:T(8,128)(2,1)S(1)} %get-tuple-element.61), channel_id=1, source_target_pairs={{0,24},{8,16},{16,8},{24,0},{1,25},{9,17},{17,9},{25,1},{2,26},{10... | collective-permute-start | bytes 196616 | tf_op jit(solution)/shard_map/ppermute | solution.py:353
  48.8 2.1 %collective-permute-done.16.refs_3_ = bf16[16,16,128]{2,1,0:T(8,128)(2,1)S(1)} collective-permute-done((bf16[16,16,128]{2,1,0:T(8,128)(2,1)S(1)}, bf16[16,16,128]{2,1,0:T(8,128)(2,1)S(1)}, u32[]{:S(2)}, u32[]{:S(2)}) %collective-permute-start.16) | collective-permute-done | bytes 65568 | tf_op jit(solution)/shard_map/ppermute | solution.py:353
  (43 shorter events, 9.8 us)
Async XLA Ops:
  1.0 1.2 %copy-start = (f32[16,16,8,128]{3,2,1,0:T(8,128)S(1)}, f32[16,16,8,128]{3,2,1,0:T(8,128)}, u32[]{:S(2)}) copy-start(f32[16,16,8,128]{3,2,1,0:T(8,128)} %param.4) | copy-start | bytes 3145732
  2.7 5.7 %collective-permute-start = (bf16[22,16,128]{2,1,0:T(8,128)(2,1)S(1)}, bf16[22,16,128]{2,1,0:T(8,128)(2,1)S(1)}, u32[]{:S(2)}, u32[]{:S(2)}) collective-permute-start(bf16[22,16,128]{2,1,0:T(8,128)(2,1)S(1)} %get-tuple-element.36), channel_id=1, source_target_pairs={{0,8},{8,0},{16,24},{24,16},{1,9},{9,1},{17,25},{25,17},{2,10},{10... | collective-permute-start | bytes 270344 | tf_op jit(solution)/shard_map/ppermute | solution.py:353
  3.5 5.0 %collective-permute-start.1 = (bf16[22,16,128]{2,1,0:T(8,128)(2,1)S(1)}, bf16[22,16,128]{2,1,0:T(8,128)(2,1)S(1)}, u32[]{:S(2)}, u32[]{:S(2)}) collective-permute-start(bf16[22,16,128]{2,1,0:T(8,128)(2,1)S(1)} %get-tuple-element.37), channel_id=1, source_target_pairs={{0,16},{8,24},{16,0},{24,8},{1,17},{9,25},{17,1},{25,9},{2,18},{10... | collective-permute-start | bytes 270344 | tf_op jit(solution)/shard_map/ppermute | solution.py:353
  4.7 5.5 %collective-permute-start.2 = (bf16[22,16,128]{2,1,0:T(8,128)(2,1)S(1)}, bf16[22,16,128]{2,1,0:T(8,128)(2,1)S(1)}, u32[]{:S(2)}, u32[]{:S(2)}) collective-permute-start(bf16[22,16,128]{2,1,0:T(8,128)(2,1)S(1)} %get-tuple-element.38), channel_id=1, source_target_pairs={{0,24},{8,16},{16,8},{24,0},{1,25},{9,17},{17,9},{25,1},{2,26},{10... | collective-permute-start | bytes 270344 | tf_op jit(solution)/shard_map/ppermute | solution.py:353
  5.2 2.3 %copy-start.1 = (bf16[512,64]{0,1:T(8,128)(2,1)S(1)}, bf16[512,64]{0,1:T(8,128)(2,1)}, u32[]{:S(2)}) copy-start(bf16[512,64]{0,1:T(8,128)(2,1)} %param.6) | copy-start | bytes 196612
  5.6 8.4 %collective-permute-start.4 = (bf16[16,16,128]{2,1,0:T(8,128)(2,1)S(1)}, bf16[16,16,128]{2,1,0:T(8,128)(2,1)S(1)}, u32[]{:S(2)}, u32[]{:S(2)}) collective-permute-start(bf16[16,16,128]{2,1,0:T(8,128)(2,1)S(1)} %get-tuple-element.43), channel_id=1, source_target_pairs={{0,16},{8,24},{16,0},{24,8},{1,17},{9,25},{17,1},{25,9},{2,18},{10... | collective-permute-start | bytes 196616 | tf_op jit(solution)/shard_map/ppermute | solution.py:353
  6.9 7.1 %collective-permute-start.5 = (bf16[16,16,128]{2,1,0:T(8,128)(2,1)S(1)}, bf16[16,16,128]{2,1,0:T(8,128)(2,1)S(1)}, u32[]{:S(2)}, u32[]{:S(2)}) collective-permute-start(bf16[16,16,128]{2,1,0:T(8,128)(2,1)S(1)} %get-tuple-element.44), channel_id=1, source_target_pairs={{0,24},{8,16},{16,8},{24,0},{1,25},{9,17},{17,9},{25,1},{2,26},{10... | collective-permute-start | bytes 196616 | tf_op jit(solution)/shard_map/ppermute | solution.py:353
  7.6 0.8 %copy-start.2 = (bf16[64,512]{1,0:T(8,128)(2,1)S(1)}, bf16[64,512]{1,0:T(8,128)(2,1)}, u32[]{:S(2)}) copy-start(bf16[64,512]{1,0:T(8,128)(2,1)} %param.7) | copy-start | bytes 196612
  10.4 3.6 %collective-permute-start.3 = (bf16[16,16,128]{2,1,0:T(8,128)(2,1)S(1)}, bf16[16,16,128]{2,1,0:T(8,128)(2,1)S(1)}, u32[]{:S(2)}, u32[]{:S(2)}) collective-permute-start(bf16[16,16,128]{2,1,0:T(8,128)(2,1)S(1)} %get-tuple-element.42), channel_id=1, source_target_pairs={{0,8},{8,0},{16,24},{24,16},{1,9},{9,1},{17,25},{25,17},{2,10},{10... | collective-permute-start | bytes 196616 | tf_op jit(solution)/shard_map/ppermute | solution.py:353
  10.5 8.9 %collective-permute-start.6 = (bf16[4,20,16,128]{3,2,1,0:T(8,128)(2,1)S(1)}, bf16[4,20,16,128]{3,2,1,0:T(8,128)(2,1)S(1)}, u32[]{:S(2)}, u32[]{:S(2)}) collective-permute-start(bf16[4,20,16,128]{3,2,1,0:T(8,128)(2,1)S(1)} %get-tuple-element.45.refs_8_), channel_id=1, source_target_pairs={{8,16},{16,8},{24,25},{25,24},{17,9},{9,17},{1,2},{2,1},{10,18},{1... | collective-permute-start | bytes 983048 | tf_op jit(solution)/shard_map/ppermute | solution.py:384
  14.2 3.2 %collective-permute-start.7 = (bf16[4,17,16,128]{3,2,1,0:T(8,128)(2,1)S(1)}, bf16[4,17,16,128]{3,2,1,0:T(8,128)(2,1)S(1)}, u32[]{:S(2)}, u32[]{:S(2)}) collective-permute-start(bf16[4,17,16,128]{3,2,1,0:T(8,128)(2,1)S(1)} %get-tuple-element.48), channel_id=1, source_target_pairs={{0,8},{8,0},{16,24},{24,16},{25,17},{17,25},{9,1},{1,9},{2,10},{10... | collective-permute-start | bytes 835592 | tf_op jit(solution)/shard_map/ppermute | solution.py:391
  14.5 12.2 %collective-permute-start.8 = (bf16[4,17,16,128]{3,2,1,0:T(8,128)(2,1)S(1)}, bf16[4,17,16,128]{3,2,1,0:T(8,128)(2,1)S(1)}, u32[]{:S(2)}, u32[]{:S(2)}) collective-permute-start(bf16[4,17,16,128]{3,2,1,0:T(8,128)(2,1)S(1)} %get-tuple-element.48), channel_id=1, source_target_pairs={{8,16},{16,8},{24,25},{25,24},{17,9},{9,17},{1,2},{2,1},{10,18},{1... | collective-permute-start | bytes 835592 | tf_op jit(solution)/shard_map/ppermute | solution.py:392
  18.7 2.0 %collective-permute-start.9 = (bf16[4,16,16,128]{3,2,1,0:T(8,128)(2,1)S(1)}, bf16[4,16,16,128]{3,2,1,0:T(8,128)(2,1)S(1)}, u32[]{:S(2)}, u32[]{:S(2)}) collective-permute-start(bf16[4,16,16,128]{3,2,1,0:T(8,128)(2,1)S(1)} %get-tuple-element.49.rest_0_), channel_id=1, source_target_pairs={{0,8},{8,0},{16,24},{24,16},{25,17},{17,25},{9,1},{1,9},{2,10},{10... | collective-permute-start | bytes 786440 | tf_op jit(solution)/shard_map/ppermute | solution.py:414
  21.9 20.9 %collective-permute-start.12 = (bf16[4,16,16,128]{3,2,1,0:T(8,128)(2,1)S(1)}, bf16[4,16,16,128]{3,2,1,0:T(8,128)(2,1)S(1)}, u32[]{:S(2)}, u32[]{:S(2)}) collective-permute-start(bf16[4,16,16,128]{3,2,1,0:T(8,128)(2,1)S(1)} %get-tuple-element.51.rest_0_), channel_id=1, source_target_pairs={{8,16},{16,8},{24,25},{25,24},{17,9},{9,17},{1,2},{2,1},{10,18},{1... | collective-permute-start | bytes 786440 | tf_op jit(solution)/shard_map/ppermute | solution.py:425
  24.9 6.5 %collective-permute-start.11 = (bf16[4,16,16,128]{3,2,1,0:T(8,128)(2,1)S(1)}, bf16[4,16,16,128]{3,2,1,0:T(8,128)(2,1)S(1)}, u32[]{:S(2)}, u32[]{:S(2)}) collective-permute-start(bf16[4,16,16,128]{3,2,1,0:T(8,128)(2,1)S(1)} %get-tuple-element.51.rest_0_), channel_id=1, source_target_pairs={{0,8},{8,0},{16,24},{24,16},{25,17},{17,25},{9,1},{1,9},{2,10},{10... | collective-permute-start | bytes 786440 | tf_op jit(solution)/shard_map/ppermute | solution.py:424
  29.3 8.0 %collective-permute-start.10 = (bf16[4,16,16,128]{3,2,1,0:T(8,128)(2,1)S(1)}, bf16[4,16,16,128]{3,2,1,0:T(8,128)(2,1)S(1)}, u32[]{:S(2)}, u32[]{:S(2)}) collective-permute-start(bf16[4,16,16,128]{3,2,1,0:T(8,128)(2,1)S(1)} %get-tuple-element.54), channel_id=1, source_target_pairs={{8,16},{16,8},{24,25},{25,24},{17,9},{9,17},{1,2},{2,1},{10,18},{1... | collective-permute-start | bytes 786440 | tf_op jit(solution)/shard_map/ppermute | solution.py:423
  32.7 5.9 %collective-permute-start.13 = (bf16[4,16,16,128]{3,2,1,0:T(8,128)(2,1)S(1)}, bf16[4,16,16,128]{3,2,1,0:T(8,128)(2,1)S(1)}, u32[]{:S(2)}, u32[]{:S(2)}) collective-permute-start(bf16[4,16,16,128]{3,2,1,0:T(8,128)(2,1)S(1)} %get-tuple-element.56), channel_id=1, source_target_pairs={{0,8},{8,0},{16,24},{24,16},{25,17},{17,25},{9,1},{1,9},{2,10},{10... | collective-permute-start | bytes 786440 | tf_op jit(solution)/shard_map/ppermute | solution.py:414
  39.9 5.8 %collective-permute-start.17 = (bf16[16,16,128]{2,1,0:T(8,128)(2,1)S(1)}, bf16[16,16,128]{2,1,0:T(8,128)(2,1)S(1)}, u32[]{:S(2)}, u32[]{:S(2)}) collective-permute-start(bf16[16,16,128]{2,1,0:T(8,128)(2,1)S(1)} %get-tuple-element.62), channel_id=1, source_target_pairs={{0,8},{8,0},{16,24},{24,16},{1,9},{9,1},{17,25},{25,17},{2,10},{10... | collective-permute-start | bytes 196616 | tf_op jit(solution)/shard_map/ppermute | solution.py:353
  41.1 6.5 %collective-permute-start.18 = (bf16[16,16,128]{2,1,0:T(8,128)(2,1)S(1)}, bf16[16,16,128]{2,1,0:T(8,128)(2,1)S(1)}, u32[]{:S(2)}, u32[]{:S(2)}) collective-permute-start(bf16[16,16,128]{2,1,0:T(8,128)(2,1)S(1)} %get-tuple-element.63), channel_id=1, source_target_pairs={{0,16},{8,24},{16,0},{24,8},{1,17},{9,25},{17,1},{25,9},{2,18},{10... | collective-permute-start | bytes 196616 | tf_op jit(solution)/shard_map/ppermute | solution.py:353
  41.1 6.5 %collective-permute-start.19 = (bf16[16,16,128]{2,1,0:T(8,128)(2,1)S(1)}, bf16[16,16,128]{2,1,0:T(8,128)(2,1)S(1)}, u32[]{:S(2)}, u32[]{:S(2)}) collective-permute-start(bf16[16,16,128]{2,1,0:T(8,128)(2,1)S(1)} %get-tuple-element.64), channel_id=1, source_target_pairs={{0,24},{8,16},{16,8},{24,0},{1,25},{9,17},{17,9},{25,1},{2,26},{10... | collective-permute-start | bytes 196616 | tf_op jit(solution)/shard_map/ppermute | solution.py:353
  45.4 2.2 %collective-permute-start.14 = (bf16[16,16,128]{2,1,0:T(8,128)(2,1)S(1)}, bf16[16,16,128]{2,1,0:T(8,128)(2,1)S(1)}, u32[]{:S(2)}, u32[]{:S(2)}) collective-permute-start(bf16[16,16,128]{2,1,0:T(8,128)(2,1)S(1)} %get-tuple-element.59), channel_id=1, source_target_pairs={{0,8},{8,0},{16,24},{24,16},{1,9},{9,1},{17,25},{25,17},{2,10},{10... | collective-permute-start | bytes 196616 | tf_op jit(solution)/shard_map/ppermute | solution.py:353
  45.7 3.1 %collective-permute-start.15 = (bf16[16,16,128]{2,1,0:T(8,128)(2,1)S(1)}, bf16[16,16,128]{2,1,0:T(8,128)(2,1)S(1)}, u32[]{:S(2)}, u32[]{:S(2)}) collective-permute-start(bf16[16,16,128]{2,1,0:T(8,128)(2,1)S(1)} %get-tuple-element.60), channel_id=1, source_target_pairs={{0,16},{8,24},{16,0},{24,8},{1,17},{9,25},{17,1},{25,9},{2,18},{10... | collective-permute-start | bytes 196616 | tf_op jit(solution)/shard_map/ppermute | solution.py:353
  45.7 5.2 %collective-permute-start.16 = (bf16[16,16,128]{2,1,0:T(8,128)(2,1)S(1)}, bf16[16,16,128]{2,1,0:T(8,128)(2,1)S(1)}, u32[]{:S(2)}, u32[]{:S(2)}) collective-permute-start(bf16[16,16,128]{2,1,0:T(8,128)(2,1)S(1)} %get-tuple-element.61), channel_id=1, source_target_pairs={{0,24},{8,16},{16,8},{24,0},{1,25},{9,17},{17,9},{25,1},{2,26},{10... | collective-permute-start | bytes 196616 | tf_op jit(solution)/shard_map/ppermute | solution.py:353
